TPU v7x, 32 devices: a whole 2x2x4 slice. The times are simulated.
32 devices in a mesh: wide: 8 (over y, x, core), narrow: 4 (over z).
Axes of the slice: x: 2, y: 2, z: 4, core: 2. Of those that a mesh axis runs over, the one named last changes fastest.
Arguments:
- char_ids: int32 [8192, 50], P(('wide', 'narrow')), may hold values from 0 to 261
- bank_order: int32 [8], replicated, may hold values from 0 to 7, each once
- char_table: bfloat16 [262, 16], replicated, may hold values from -4 to 4
- conv_w1: bfloat16 [16, 32], replicated, may hold values from -1.5 to 1.5
- conv_w2: bfloat16 [32, 32], replicated, may hold values from -1 to 1
- conv_w3: bfloat16 [48, 64], replicated, may hold values from -0.875 to 0.875
- conv_w4: bfloat16 [64, 128], replicated, may hold values from -0.75 to 0.75
- conv_w5: bfloat16 [80, 256], replicated, may hold values from -0.625 to 0.625
- conv_w6: bfloat16 [96, 512], replicated, may hold values from -0.625 to 0.625
- conv_w7: bfloat16 [112, 1024], replicated, may hold values from -0.5 to 0.5
- conv_bias: bfloat16 [2048], replicated, may hold values from -3 to 3
- highway_w1: bfloat16 [2048, 4096], P(None, ('wide', 'narrow')), may hold values from -0.125 to 0.125
- highway_b1: bfloat16 [4096], P(('wide', 'narrow')), may hold values from -3 to 3
- highway_w2: bfloat16 [2048, 4096], P(None, ('wide', 'narrow')), may hold values from -0.125 to 0.125
- highway_b2: bfloat16 [4096], P(('wide', 'narrow')), may hold values from -3 to 3
- proj_weight: bfloat16 [2048, 512], P(None, ('wide', 'narrow')), may hold values from -0.125 to 0.125
- proj_bias: bfloat16 [512], P(('wide', 'narrow')), may hold values from -3 to 3
- cotangent: bfloat16 [8192, 512], P(('wide', 'narrow')), may hold values from -6 to 6
Outputs:
- encoded: bfloat16 [8192, 512], P(('wide', 'narrow'))
- grad_char_table: float32 [262, 16], replicated
- grad_conv_w1: float32 [16, 32], replicated
- grad_conv_w2: float32 [32, 32], replicated
- grad_conv_w3: float32 [48, 64], replicated
- grad_conv_w4: float32 [64, 128], replicated
- grad_conv_w5: float32 [80, 256], replicated
- grad_conv_w6: float32 [96, 512], replicated
- grad_conv_w7: float32 [112, 1024], replicated
- grad_conv_bias: float32 [2048], replicated
- grad_highway_w1: float32 [2048, 4096], P(None, ('wide', 'narrow'))
- grad_highway_b1: float32 [4096], P(('wide', 'narrow'))
- grad_highway_w2: float32 [2048, 4096], P(None, ('wide', 'narrow'))
- grad_highway_b2: float32 [4096], P(('wide', 'narrow'))
- grad_proj_weight: float32 [2048, 512], P(None, ('wide', 'narrow'))
- grad_proj_bias: float32 [512], P(('wide', 'narrow'))
Inputs may be any that keep to these rules, and one draw needn't show every extreme that they name: `bank_order`: each bank number appears once.
All inputs are finite; a program needn't handle non-finite values.
Results may differ from a plain program's by a relative error of at most 0.0063.
Values may be sent and summed in bfloat16 or wider, within the bound.
No kernel may reach another device: no remote copies, remote signals or barrier semaphores. Data moves between devices by JAX's collectives and lax.ppermute only.
A program may use at most 256 MiB of HBM per device.

v0:
```python
import math

import jax
import jax.numpy as jnp
from jax import lax
from jax.sharding import PartitionSpec as P

bank_widths = (1, 2, 3, 4, 5, 6, 7, 7)
bank_parts = (1, 1, 2, 4, 8, 16, 16, 16)


def for_sending(x):

    def short(part):
        return part.astype(jnp.bfloat16) if part.dtype == jnp.float32 else part

    return jax.tree.map(short, x)


def bank_layout(base_count):
    layout = []
    natural = 0
    for number in range(8):
        filters = bank_parts[number] * base_count
        leading = 16 * base_count if number == 7 else 0
        layout.append((bank_widths[number], leading, filters, natural))
        natural += filters
    return layout


def bank_starts(bank_order, layout):
    counts = jnp.array([entry[2] for entry in layout], jnp.int32)
    matches = (bank_order[:, None] == lax.iota(jnp.int32, 8)[None, :]).astype(jnp.int32)
    placed = jnp.sum(matches * counts[None, :], axis=1)
    before = jnp.cumsum(placed) - placed
    return jnp.sum(matches * before[:, None], axis=0)


def one_hot(char_rows, vocab_count, number_type):
    return (char_rows[:, :, None] == lax.iota(jnp.int32, vocab_count)[None, None, :]).astype(
        number_type
    )


def embed_chars(char_rows, char_table):
    table_hits = one_hot(char_rows, char_table.shape[0], jnp.bfloat16)
    return jnp.einsum(
        "bcv,ve->bce", table_hits, char_table, preferred_element_type=jnp.float32
    ).astype(jnp.bfloat16)


def sliding(embedded, kernel):
    places = embedded.shape[1] - kernel + 1
    return jnp.concatenate(
        [embedded[:, offset : offset + places] for offset in range(kernel)], axis=2
    )


def pool_stats(conv_out):
    highest = jnp.max(conv_out, axis=1)
    summed = jnp.sum(jnp.exp(conv_out - highest[:, None, :]), axis=1)
    return highest + jnp.log(summed)


def bank_act(embedded, weight, bias_part, kernel):
    windowed = sliding(embedded, kernel)
    conv_out = jnp.einsum("bpc,cf->bpf", windowed, weight, preferred_element_type=jnp.float32)
    pooled = pool_stats(conv_out) - math.log(windowed.shape[1])
    return jax.nn.silu(pooled + bias_part)


def bank_back(embedded, weight, bias_part, kernel, d_act):
    windowed = sliding(embedded, kernel)
    conv_out = jnp.einsum("bpc,cf->bpf", windowed, weight, preferred_element_type=jnp.float32)
    logsum = pool_stats(conv_out)
    before_act = logsum - math.log(windowed.shape[1]) + bias_part
    sigmoid_at = jax.nn.sigmoid(before_act)
    d_before = d_act * sigmoid_at * (1.0 + before_act * (1.0 - sigmoid_at))
    d_conv = (d_before[:, None, :] * jnp.exp(conv_out - logsum[:, None, :])).astype(jnp.bfloat16)
    d_weight = jnp.einsum("bpc,bpf->cf", windowed, d_conv, preferred_element_type=jnp.float32)
    d_window = jnp.einsum("bpf,cf->bpc", d_conv, weight, preferred_element_type=jnp.float32)
    emb_width = embedded.shape[2]
    d_embedded = jnp.zeros(embedded.shape, jnp.float32)
    for offset in range(kernel):
        d_slice = d_window[:, :, offset * emb_width : (offset + 1) * emb_width]
        d_embedded = d_embedded + jnp.pad(d_slice, ((0, 0), (offset, kernel - 1 - offset), (0, 0)))
    return (d_weight, jnp.sum(d_before, axis=0), d_embedded)


def bank_features(char_rows, char_table, weights, conv_bias, chosen, layout, out_width):
    total_rows = char_rows.shape[0]
    block_size = math.gcd(total_rows, 512)

    def one_block(block_rows):
        embedded = embed_chars(block_rows, char_table)
        pieces = []
        for number in chosen:
            kernel, leading, filters, natural = layout[number]
            weight = weights[kernel - 1][:, leading : leading + filters]
            pieces.append(
                bank_act(
                    embedded,
                    weight,
                    conv_bias[natural : natural + filters].astype(jnp.float32),
                    kernel,
                )
            )
        joined = jnp.concatenate(pieces, axis=1)
        return jnp.pad(joined, ((0, 0), (0, out_width - joined.shape[1]))).astype(jnp.bfloat16)

    stacked = lax.map(
        one_block, char_rows.reshape(total_rows // block_size, block_size, char_rows.shape[1])
    )
    return stacked.reshape(total_rows, out_width)


def bank_grads(char_rows, char_table, weights, conv_bias, chosen, layout, d_source):
    total_rows = char_rows.shape[0]
    block_size = math.gcd(total_rows, 512)
    vocab_count = char_table.shape[0]

    def one_block(carried, block_pair):
        block_rows, d_block = block_pair
        embedded = embed_chars(block_rows, char_table)
        grad_weights = list(carried[0])
        grad_bias = carried[1]
        d_embedded = jnp.zeros(embedded.shape, jnp.float32)
        column = 0
        for number in chosen:
            kernel, leading, filters, natural = layout[number]
            weight = weights[kernel - 1][:, leading : leading + filters]
            d_act = d_block[:, column : column + filters].astype(jnp.float32)
            column += filters
            d_weight, d_bias, d_part = bank_back(
                embedded,
                weight,
                conv_bias[natural : natural + filters].astype(jnp.float32),
                kernel,
                d_act,
            )
            grad_weights[kernel - 1] = (
                grad_weights[kernel - 1].at[:, leading : leading + filters].add(d_weight)
            )
            grad_bias = grad_bias.at[natural : natural + filters].add(d_bias)
            d_embedded = d_embedded + d_part
        table_hits = one_hot(block_rows, vocab_count, jnp.float32)
        grad_table = carried[2] + jnp.einsum(
            "bcv,bce->ve", table_hits, d_embedded, precision=lax.Precision.HIGHEST
        )
        return ((tuple(grad_weights), grad_bias, grad_table), None)

    initial = (
        tuple((jnp.zeros(weight.shape, jnp.float32) for weight in weights)),
        jnp.zeros(conv_bias.shape, jnp.float32),
        jnp.zeros(char_table.shape, jnp.float32),
    )
    block_count = total_rows // block_size
    result, unused = lax.scan(
        one_block,
        initial,
        (
            char_rows.reshape(block_count, block_size, char_rows.shape[1]),
            d_source.reshape(block_count, block_size, d_source.shape[1]),
        ),
    )
    return result


def make_forward(chosen, char_table, weights, conv_bias, layout, slot_width):

    def compute(char_rows):
        return bank_features(char_rows, char_table, weights, conv_bias, chosen, layout, slot_width)

    return compute


def make_backward(chosen, char_table, weights, conv_bias, layout):

    def compute(char_rows, d_source):
        return bank_grads(char_rows, char_table, weights, conv_bias, chosen, layout, d_source)

    return compute


def place_banks(source, starts, located, layout, feature_count):
    features = jnp.zeros((source.shape[0], feature_count), jnp.bfloat16)
    for number in range(8):
        filters = layout[number][2]
        features = lax.dynamic_update_slice_in_dim(
            features, source[:, located[number] : located[number] + filters], starts[number], 1
        )
    return features


def take_banks(d_features, starts, located, layout, source_width):
    spread = jnp.zeros((d_features.shape[0], source_width), jnp.bfloat16)
    for number in range(8):
        filters = layout[number][2]
        spread = spread.at[:, located[number] : located[number] + filters].set(
            lax.dynamic_slice_in_dim(d_features, starts[number], filters, 1)
        )
    return spread


def highway_forward(inputs, weight, bias_row, feature_count):
    project = jnp.dot(inputs, weight, preferred_element_type=jnp.float32) + bias_row.astype(
        jnp.float32
    )
    gating = jax.nn.sigmoid(project[:, feature_count:])
    blended = gating * inputs.astype(jnp.float32) + (1.0 - gating) * jax.nn.silu(
        project[:, :feature_count]
    )
    return (blended, project)


def highway_back(inputs, weight, project, d_output, feature_count):
    carried = inputs.astype(jnp.float32)
    linear = project[:, :feature_count]
    gating = jax.nn.sigmoid(project[:, feature_count:])
    sigmoid_at = jax.nn.sigmoid(linear)
    d_linear = d_output * (1.0 - gating) * sigmoid_at * (1.0 + linear * (1.0 - sigmoid_at))
    d_gating = d_output * (carried - linear * sigmoid_at) * gating * (1.0 - gating)
    d_project = jnp.concatenate([d_linear, d_gating], axis=1).astype(jnp.bfloat16)
    grad_weight = jnp.einsum("tf,tg->fg", inputs, d_project, preferred_element_type=jnp.float32)
    grad_bias = jnp.sum(d_project.astype(jnp.float32), axis=0)
    d_inputs = (
        jnp.einsum("tg,fg->tf", d_project, weight, preferred_element_type=jnp.float32)
        + gating * d_output
    )
    return (d_inputs, grad_weight, grad_bias)


def local(
    char_ids,
    bank_order,
    char_table,
    conv_w1,
    conv_w2,
    conv_w3,
    conv_w4,
    conv_w5,
    conv_w6,
    conv_w7,
    conv_bias,
    highway_w1,
    highway_b1,
    highway_w2,
    highway_b2,
    proj_weight,
    proj_bias,
    cotangent,
):
    feature_count = conv_bias.shape[0]
    layout = bank_layout(feature_count // 64)
    weights = (conv_w1, conv_w2, conv_w3, conv_w4, conv_w5, conv_w6, conv_w7)
    starts = bank_starts(bank_order, layout)
    gathered = (
        lax.all_gather(highway_w1, ("wide", "narrow"), axis=1, tiled=True),
        lax.all_gather(highway_w2, ("wide", "narrow"), axis=1, tiled=True),
        lax.all_gather(proj_weight, ("wide", "narrow"), axis=1, tiled=True),
        lax.all_gather(highway_b1, ("wide", "narrow"), axis=0, tiled=True),
        lax.all_gather(highway_b2, ("wide", "narrow"), axis=0, tiled=True),
        lax.all_gather(proj_bias, ("wide", "narrow"), axis=0, tiled=True),
    )
    layer_one_w, layer_two_w, out_weight, layer_one_b, layer_two_b, out_bias = gathered
    groups = lax.axis_size("narrow")
    member = lax.axis_index("narrow")
    group_rows = lax.all_gather(char_ids, "narrow", axis=0, tiled=True)
    owned_sets = [
        [number for number in range(8) if number % groups == device] for device in range(groups)
    ]
    slot_width = max((sum((layout[number][2] for number in chosen)) for chosen in owned_sets))
    located = {}
    for device in range(groups):
        column = device * slot_width
        for number in owned_sets[device]:
            located[number] = column
            column += layout[number][2]
    own_banks = lax.switch(
        member,
        [
            make_forward(chosen, char_table, weights, conv_bias, layout, slot_width)
            for chosen in owned_sets
        ],
        group_rows,
    )
    source = jax.tree.map(
        lambda part, own: part.astype(own.dtype),
        lax.all_to_all(for_sending(own_banks), "narrow", split_axis=0, concat_axis=1, tiled=True),
        own_banks,
    )
    source_width = groups * slot_width
    features = place_banks(source, starts, located, layout, feature_count)
    hidden_one, proj_one = highway_forward(features, layer_one_w, layer_one_b, feature_count)
    input_two = hidden_one.astype(jnp.bfloat16)
    hidden_two, proj_two = highway_forward(input_two, layer_two_w, layer_two_b, feature_count)
    input_out = hidden_two.astype(jnp.bfloat16)
    encoded = (
        jnp.dot(input_out, out_weight, preferred_element_type=jnp.float32)
        + out_bias.astype(jnp.float32)
    ).astype(jnp.bfloat16)
    d_hidden_two = jnp.einsum(
        "tp,fp->tf", cotangent, out_weight, preferred_element_type=jnp.float32
    )
    grad_out_w = jnp.einsum("tf,tp->fp", input_out, cotangent, preferred_element_type=jnp.float32)
    grad_out_b = jnp.sum(cotangent.astype(jnp.float32), axis=0)
    d_hidden_one, grad_two_w, grad_two_b = highway_back(
        input_two, layer_two_w, proj_two, d_hidden_two, feature_count
    )
    d_inputs, grad_one_w, grad_one_b = highway_back(
        features, layer_one_w, proj_one, d_hidden_one, feature_count
    )
    d_features = d_inputs.astype(jnp.bfloat16)
    reduced = (
        lax.psum_scatter(grad_one_w, ("wide", "narrow"), scatter_dimension=1, tiled=True),
        lax.psum_scatter(grad_two_w, ("wide", "narrow"), scatter_dimension=1, tiled=True),
        lax.psum_scatter(grad_out_w, ("wide", "narrow"), scatter_dimension=1, tiled=True),
        lax.psum_scatter(grad_one_b, ("wide", "narrow"), scatter_dimension=0, tiled=True),
        lax.psum_scatter(grad_two_b, ("wide", "narrow"), scatter_dimension=0, tiled=True),
        lax.psum_scatter(grad_out_b, ("wide", "narrow"), scatter_dimension=0, tiled=True),
    )
    spread = take_banks(d_features, starts, located, layout, source_width)
    returned = lax.all_to_all(spread, "narrow", split_axis=1, concat_axis=0, tiled=True)
    bank_result = lax.switch(
        member,
        [make_backward(chosen, char_table, weights, conv_bias, layout) for chosen in owned_sets],
        group_rows,
        returned,
    )
    grad_weights, grad_bias, grad_table = bank_result
    summed = lax.psum(
        (
            grad_table,
            grad_weights[0],
            grad_weights[1],
            grad_weights[2],
            grad_weights[3],
            grad_weights[4],
            grad_weights[5],
            grad_weights[6],
            grad_bias,
        ),
        ("wide", "narrow"),
    )
    return (
        encoded,
        summed[0],
        summed[1],
        summed[2],
        summed[3],
        summed[4],
        summed[5],
        summed[6],
        summed[7],
        summed[8],
        reduced[0],
        reduced[3],
        reduced[1],
        reduced[4],
        reduced[2],
        reduced[5],
    )


def solution(mesh):
    placed = (
        P(("wide", "narrow"), None),
        P(),
        P(),
        P(),
        P(),
        P(),
        P(),
        P(),
        P(),
        P(),
        P(),
        P(None, ("wide", "narrow")),
        P(("wide", "narrow")),
        P(None, ("wide", "narrow")),
        P(("wide", "narrow")),
        P(None, ("wide", "narrow")),
        P(("wide", "narrow")),
        P(("wide", "narrow"), None),
    )
    return jax.shard_map(
        local,
        mesh=mesh,
        in_specs=placed,
        out_specs=(
            P(("wide", "narrow"), None),
            P(),
            P(),
            P(),
            P(),
            P(),
            P(),
            P(),
            P(),
            P(),
            P(None, ("wide", "narrow")),
            P(("wide", "narrow")),
            P(None, ("wide", "narrow")),
            P(("wide", "narrow")),
            P(None, ("wide", "narrow")),
            P(("wide", "narrow")),
        ),
        check_vma=False,
    )
```

profile of v0, /device:TPU:0, one launch (start us, length us, event | category | flops | bytes accessed | tf_op | source)
XLA Modules:
  0.0 2665.0 jit_solution(508935523993955473)
XLA Ops:
  8.7 17.3 all_gather.21
  26.0 69.3 %conditional.2 = (bf16[2,512,640]{2,1,0:T(8,128)(2,1)}) conditional(s32[]{:T(128)} %clamp.4, (s32[1024,50]{0,1:T(8,128)}, bf16[262,16]{0,1:T(8,128)(2,1)}, bf16[16,32]{1,0:T(8,128)(2,1)}, bf16[2048]{0:T(1024)(128)(2,1)}, bf16[80,256]{1,0:T(8,128)(2,1)}) %tuple.279, (s32[1024,50]{0,1:T(8,128)}, ...), branch_computations={%region_0.7_spmd, %region_7.14_spmd, %region_14.21_spmd, %region_2... | conditional | flops 3259144704 | bytes 152685216 | solution.py:279
  27.2 40.7 %while.151 = (s32[]{:T(128)}, bf16[2,512,640]{2,1,0:T(8,128)(2,1)}, s32[2,512,50]{1,0,2:T(2,128)S(1)}, bf16[262,16]{0,1:T(8,128)(2,1)}, bf16[16,32]{1,0:T(8,128)...) while((s32[]{:T(128)}, bf16[2,512,640]{2,1,0:T(8,128)(2,1)}, ...), condition=%wide.region_6.6_spmd, body=%wide.region_1.5_spmd.sunk | while | flops 1236375808 | bytes 87797944 | solution.py:111
  27.3 4.9 fusion.565
  34.3 5.5 fusion.566
  39.8 3.6 exponential_reduce_fusion.46
  47.6 4.9 fusion.565
  54.6 5.6 fusion.566
  60.2 3.6 exponential_reduce_fusion.46
  95.3 64.9 %all-to-all-start = ((bf16[4,256,640]{2,1,0:T(8,128)(2,1)}), bf16[4,256,640]{2,1,0:T(8,128)(2,1)S(1)}, u32[]{:S(2)}, u32[]{:S(2)}) async-start(bf16[4,256,640]{2,1,0:T(8,128)(2,1)} %bitcast.25), calls=%async_computation | async-start | bytes 2621440 | tf_op jit(solution)/shard_map/all_to_all | solution.py:289
  172.3 77.1 %all-gather = bf16[32,1,128]{2,1,0:T(2,128)(2,1)S(1)} all-gather(bf16[1,1,128]{2,1,0:T(2,128)(2,1)S(1)} %bitcast.486), channel_id=1, replica_groups=mesh['wide'=8,'narrow'=4] {'wide','narrow'}, dimensions={0}, use_global_device_ids=true | all-gather | bytes 8448 | tf_op jit(solution)/shard_map/all_gather | solution.py:261
  249.5 85.0 %all-gather.1 = bf16[32,1,128]{2,1,0:T(2,128)(2,1)S(1)} all-gather(bf16[1,1,128]{2,1,0:T(2,128)(2,1)S(1)} %bitcast.487), channel_id=1, replica_groups=mesh['wide'=8,'narrow'=4] {'wide','narrow'}, dimensions={0}, use_global_device_ids=true | all-gather | bytes 8448 | tf_op jit(solution)/shard_map/all_gather | solution.py:262
  348.4 3.1 dynamic_update_slice.54
  351.6 3.1 dynamic_update_slice.55
  357.0 8.6 convolution_add_fusion.1
  368.7 10.9 convolution_add_fusion
  379.6 6.0 multiply_convert_fusion.57
  385.6 13.2 multiply_convert_fusion.56
  398.8 12.3 fusion.252
  421.8 3.1 scatter.35
  426.8 3.1 scatter.36
  432.2 3.5 all-to-all-start.1
  441.1 21.7 all-to-all-done.1
  463.8 256.2 %conditional.3 = (f32[16,32]{1,0:T(8,128)}, f32[32,32]{1,0:T(8,128)}, f32[48,64]{1,0:T(8,128)}, f32[64,128]{1,0:T(8,128)}, f32[80,256]{1,0:T(8,128)S(1)}, /*inde...) conditional(s32[]{:T(128)} %clamp.4, (s32[1024,50]{0,1:T(8,128)}, ...), branch_computations={%region_38.47_spmd, %region_47.56_spmd, %region_56.66_spmd, %regio... | conditional | flops 10614116352 | bytes 452148704 | solution.py:324
  465.5 201.5 %while.155 = (s32[]{:T(128)}, f32[16,32]{1,0:T(8,128)}, f32[80,256]{1,0:T(8,128)S(1)}, f32[2048]{0:T(1024)}, f32[262,16]{0,1:T(8,128)}, /*index=5*/s32[2,512,50]...) while((s32[]{:T(128)}, f32[16,32]{1,0:T(8,128)}, ...), condition=%wide.region_46.46_spmd.clone, body=%wide.region_39.45_spmd.clone.sunk | while | flops 4554307072 | bytes 211234416 | solution.py:158
  484.1 4.9 fusion.528
  500.3 10.6 fusion.532
  513.7 10.9 exponential_reduce_fusion.39
  526.6 2.5 fusion.533
  533.3 12.1 fusion.534
  550.0 10.2 fusion.537
  561.7 12.9 fusion.539
  576.0 4.9 fusion.528
  592.2 10.6 fusion.532
  605.5 10.9 exponential_reduce_fusion.39
  618.5 2.5 fusion.533
  625.1 12.1 fusion.534
  641.9 10.2 fusion.537
  653.6 12.9 fusion.539
  720.8 4.0 fusion.321
  726.6 13.1 fusion.274
  741.6 13.1 fusion.275
  755.6 122.6 %all-reduce.38 = bf16[512]{0:T(512)(128)(2,1)S(1)} all-reduce(bf16[512]{0:T(512)(128)(2,1)S(1)} %dynamic-update-slice.101), channel_id=1, replica_groups=mesh['wide'=8,'narrow'=4] {'wide','narrow'}, use_global_device_ids=true, to_apply=%add.38 | all-reduce | flops 512 | bytes 2048
  879.7 47.7 %all-reduce.47.cloned.1.call-done = (f32[262,16]{0,1:T(8,128)}, f32[16,32]{1,0:T(8,128)}, f32[32,32]{1,0:T(8,128)}, f32[48,64]{1,0:T(8,128)}, f32[64,128]{1,0:T(...) async-done(((f32[262,16]{0,1:T(8,128)}, f32[16,32]{1,0:T(8,128)}, f32[32,32]{1,0:T(8,128)}, f32[48,64]{1,0:T(8,128)}, f32[64,128]{1,0:T(8,128)}, ...) | async-done | bytes 110992 | tf_op jit(solution)/shard_map/psum | solution.py:331
  931.1 135.9 %all-reduce.49.cloned.1.call-done = (f32[80,256]{1,0:T(8,128)}, f32[96,512]{1,0:T(8,128)}, f32[112,1024]{1,0:T(8,128)}) async-done(((f32[80,256]{1,0:T(8,128)}, f32[96,512]{1,0:T(8,128)}, f32[112,1024]{1,0:T(8,128)}), (f32[80,256]{1,0:T(8,128)}, f32[96,512]{1,0:T(8,128)}, f32[112,1024]{1,0:T(8,128)})) %all-reduce.49.cloned.1.call-update) | async-done | bytes 737296 | tf_op jit(solution)/shard_map/psum | solution.py:331
  1066.9 150.3 %reduce-scatter.8.cloned.1.call-done = f32[2048,16]{0,1:T(8,128)} async-done(((f32[2048,512]{0,1:T(8,128)}), f32[2048,16]{0,1:T(8,128)}) %reduce-scatter.8.cloned.1.call-update) | async-done | bytes 131088 | tf_op jit(solution)/shard_map/reduce_scatter | solution.py:317
  1217.2 713.7 %reduce-scatter.4.cloned.1.call-done = f32[2048,128]{1,0:T(8,128)} async-done(((f32[2048,4096]{1,0:T(8,128)}), f32[2048,128]{1,0:T(8,128)}) %reduce-scatter.4.cloned.1.call-update) | async-done | bytes 1048592 | tf_op jit(solution)/shard_map/reduce_scatter | solution.py:315
  1930.9 714.2 %reduce-scatter.6.cloned.1.call-done = f32[2048,128]{1,0:T(8,128)} async-done(((f32[2048,4096]{1,0:T(8,128)}), f32[2048,128]{1,0:T(8,128)}) %reduce-scatter.6.cloned.1.call-update) | async-done | bytes 1048592 | tf_op jit(solution)/shard_map/reduce_scatter | solution.py:316
  (287 shorter events, 135.5 us)
Async XLA Ops:
  7.2 349.8 %all-gather.6.cloned.1.call-start = ((), (), s32[]{:S(2)}) async-start(), calls=%async_computation.5 | async-start | bytes 17301504 | tf_op jit(solution)/shard_map/all_gather | solution.py:258
  7.9 360.8 %all-gather.8.cloned.1.call-start = ((), (), s32[]{:S(2)}) async-start(), calls=%async_computation.6 | async-start | bytes 17301504 | tf_op jit(solution)/shard_map/all_gather | solution.py:259
  26.0 134.9 %copy-start.86 = (s32[8]{0:T(128)S(1)}, s32[8]{0:T(128)}, u32[]{:S(2)}) copy-start(s32[8]{0:T(128)} %param.104) | copy-start | bytes 100
  26.0 134.9 %copy-start.88 = (s32[8]{0:T(128)S(1)}, s32[8]{0:T(128)}, u32[]{:S(2)}) copy-start(s32[8]{0:T(128)} %constant.1286.clone) | copy-start | bytes 100
  26.0 146.3 %copy-start.83 = (bf16[128]{0:T(256)(128)(2,1)S(1)}, bf16[128]{0:T(256)(128)(2,1)}, u32[]{:S(2)}) copy-start(bf16[128]{0:T(256)(128)(2,1)} %param.115) | copy-start | bytes 772
  26.0 223.5 %copy-start.84 = (bf16[128]{0:T(256)(128)(2,1)S(1)}, bf16[128]{0:T(256)(128)(2,1)}, u32[]{:S(2)}) copy-start(bf16[128]{0:T(256)(128)(2,1)} %param.117) | copy-start | bytes 772
  32.2 2.1 copy-start.35
  32.5 1.8 copy-start.7
  39.8 4.5 copy-start.69
  52.5 2.1 copy-start.35
  52.7 1.8 copy-start.7
  60.2 4.5 copy-start.69
  95.3 248.9 %all-to-all-start = ((bf16[4,256,640]{2,1,0:T(8,128)(2,1)}), bf16[4,256,640]{2,1,0:T(8,128)(2,1)S(1)}, u32[]{:S(2)}, u32[]{:S(2)}) async-start(bf16[4,256,640]{2,1,0:T(8,128)(2,1)} %bitcast.25), calls=%async_computation | async-start | bytes 2621440 | tf_op jit(solution)/shard_map/all_to_all | solution.py:289
  160.1 219.4 %all-gather.10.cloned.1.call-start = ((), (), s32[]{:S(2)}) async-start(), calls=%async_computation.7 | async-start | bytes 2162688 | tf_op jit(solution)/shard_map/all_gather | solution.py:260
  357.0 28.6 %copy-start.33 = (bf16[256,2048]{1,0:T(8,128)(2,1)}, bf16[256,2048]{1,0:T(8,128)(2,1)S(1)}, u32[]{:S(2)}) copy-start(bf16[256,2048]{1,0:T(8,128)(2,1)S(1)} %dynamic_update_slice.56) | copy-start | bytes 3145732
  365.6 1.9 copy-start.45
  368.7 10.9 copy-start.37
  368.7 10.9 copy-start.67
  385.6 53.3 %copy-start.39 = (bf16[256,2048]{1,0:T(8,128)(2,1)}, bf16[256,2048]{1,0:T(8,128)(2,1)S(1)}, u32[]{:S(2)}) copy-start(bf16[256,2048]{1,0:T(8,128)(2,1)S(1)} %get-tuple-element.2446) | copy-start | bytes 3145732
  398.8 12.3 copy-start.42
  432.2 30.6 %all-to-all-start.1 = ((bf16[256,4,640]{2,0,1:T(8,128)(2,1)}), bf16[256,4,640]{2,0,1:T(8,128)(2,1)S(1)}, u32[]{:S(2)}, u32[]{:S(2)}) async-start(bf16[256,4,640]{2,0,1:T(8,128)(2,1)} %bitcast.296), calls=%async_computation.1 | async-start | bytes 2621440 | tf_op jit(solution)/shard_map/all_to_all | solution.py:323
  435.7 491.6 %all-reduce.47.cloned.1.call-start = ((), (), s32[]{:S(2)}) async-start(), calls=%async_computation.11 | async-start | bytes 299008 | tf_op jit(solution)/shard_map/psum | solution.py:331
  483.3 5.7 copy-start.64
  484.1 5.8 copy-start.70
  489.0 2.8 copy-start.10
  497.0 2.5 copy-start.5
  499.8 11.2 copy-start.3
  533.2 12.1 copy-start.81
  533.3 14.9 copy-start.71
  561.7 13.5 copy-start.65
  575.2 5.6 copy-start.64
  576.0 5.8 copy-start.70
  580.9 2.8 copy-start.10
  588.9 2.5 copy-start.5
  591.7 11.2 copy-start.3
  625.1 12.1 copy-start.81
  625.1 14.9 copy-start.71
  653.6 13.5 copy-start.65
  720.1 346.9 %all-reduce.49.cloned.1.call-start = ((), (), s32[]{:S(2)}) async-start(), calls=%async_computation.12 | async-start | bytes 1474560 | tf_op jit(solution)/shard_map/psum | solution.py:331
  720.7 496.5 %reduce-scatter.8.cloned.1.call-start = ((), (), s32[]{:S(2)}) async-start(), calls=%async_computation.10 | async-start | bytes 4325376 | tf_op jit(solution)/shard_map/reduce_scatter | solution.py:317
  724.8 1.5 copy-start.43
  724.8 1.9 copy-start.44
  724.8 1206.1 %reduce-scatter.4.cloned.1.call-start = ((), (), s32[]{:S(2)}) async-start(), calls=%async_computation.8 | async-start | bytes 34603008 | tf_op jit(solution)/shard_map/reduce_scatter | solution.py:315
  739.8 1.5 copy-start.40
  739.8 1.9 copy-start.41
  739.8 1905.2 %reduce-scatter.6.cloned.1.call-start = ((), (), s32[]{:S(2)}) async-start(), calls=%async_computation.9 | async-start | bytes 34603008 | tf_op jit(solution)/shard_map/reduce_scatter | solution.py:316
  754.8 123.4 %copy-start.55 = (bf16[256,2048]{1,0:T(8,128)(2,1)S(1)}, bf16[256,2048]{1,0:T(8,128)(2,1)}, u32[]{:S(2)}) copy-start(bf16[256,2048]{1,0:T(8,128)(2,1)} %get-tuple-element.2448) | copy-start | bytes 3145732
  754.8 123.4 %copy-start.85 = (bf16[2048,512]{0,1:T(8,128)(2,1)S(1)}, bf16[2048,512]{0,1:T(8,128)(2,1)}, u32[]{:S(2)}) copy-start(bf16[2048,512]{0,1:T(8,128)(2,1)} %all-gather.10.cloned.1.call-done) | copy-start | bytes 6291460
  (22 other events, 22.0 us)
Sparse Core Ops, SparseCore 0:
  10.9 150.8 all-gather.5
  164.7 144.8 all-gather.7
  312.5 54.7 all-gather.9
  720.2 207.0 all-reduce.46
  934.9 131.9 all-reduce.48
  1069.6 147.5 reduce-scatter.7
  1220.1 710.7 reduce-scatter.3
  1933.7 711.2 reduce-scatter.5
where the time goes:
time: 2680 us; the launch traced here: 2670 us
  waiting for transfers between devices  1790 us (67%)
  blocking collectives  302 us (11%)
  matrix products  216 us (8%)
  loops' own time  95.5 us (4%)
  local copies, waits for them, and re-layouts  91.3 us (3%)
  other arithmetic  75.3 us (3%)
  starting transfers between devices  68.7 us (3%)
  between operations  30.3 us (1%)
    reduce_scatter x1, waiting for transfers between devices, local(): lax.psum_scatter(grad_two_w, ('wide', 'narrow'), scatter_dimension=1, til...  714 us
    reduce_scatter x1, waiting for transfers between devices, local(): lax.psum_scatter(grad_one_w, ('wide', 'narrow'), scatter_dimension=1, til...  714 us
    psum x2, waiting for transfers between devices, local(): lax.psum((grad_table, grad_weights[0], grad_weights[1], grad_weights[2],...  184 us
    reduce_scatter x1, waiting for transfers between devices, local(): lax.psum_scatter(grad_out_w, ('wide', 'narrow'), scatter_dimension=1, til...  150 us
    unnamed x1, blocking collectives  123 us
    all_gather x1, blocking collectives, local(): lax.all_gather(highway_b2, ('wide', 'narrow'), axis=0, tiled=True)  85 us
    all_gather x1, blocking collectives, local(): lax.all_gather(highway_b1, ('wide', 'narrow'), axis=0, tiled=True)  77.1 us
    all_to_all x1, starting transfers between devices, local(): lax.all_to_all(for_sending(own_banks), 'narrow', split_axis=0, concat_axi...  64.9 us
  transfers between devices with their start and end apart: 10, of which 6 were waited for; matrix products, arithmetic and copies ran while one was open for 4% of the time, Pallas kernels for 0%

commit v1 on v0

v1 whole, which is shorter than its diff:
```python
import math
import functools
import jax
import jax.numpy as jnp
from jax import lax
from jax.experimental import pallas as pl
from jax.experimental.pallas import tpu as pltpu
from jax.sharding import PartitionSpec as P

bank_widths = (1, 2, 3, 4, 5, 6, 7, 7)
bank_parts = (1, 1, 2, 4, 8, 16, 16, 16)
WIDEST = 7
LANES = 128
BLOCK = 256
CHUNK = 11
VMEM_BYTES = 60 * 1024 * 1024


def forward_kernel(chars, low_places, trip_ref, ids_ref, table_ref, weight_ref, aux_ref, e_ref, act_ref, x_ref, inv_ref, win_ref, emb_ref, conv_ref):
    step = pl.program_id(0)
    tokens = ids_ref.shape[0]
    vocab = table_ref.shape[0]
    lane = lax.broadcasted_iota(jnp.int32, (tokens, LANES), 1)
    group = lane // 16

    @pl.when(step == 0)
    def build():
        places = lax.broadcasted_iota(jnp.int32, (tokens, vocab), 1)
        for c in range(chars):
            hits = jnp.where(ids_ref[:, c : c + 1] == places, 1.0, 0.0).astype(jnp.bfloat16)
            emb_ref[c] = jnp.dot(hits, table_ref[...], preferred_element_type=jnp.float32).astype(jnp.bfloat16)
        for c in range(chars, chars + WIDEST - 1):
            emb_ref[c] = jnp.zeros((tokens, LANES), jnp.bfloat16)

        def window(p, carry):
            got = emb_ref[p]
            for k in range(1, WIDEST):
                got = jnp.where(group == k, emb_ref[p + k], got)
            win_ref[p] = got
            return carry

        lax.fori_loop(0, chars, window, 0)

    places_here = trip_ref[step]
    rows = conv_ref.shape[1]
    valid = aux_ref[1:2, :]
    for t in range(0, tokens, rows):
        high = None

        def full(i, high):
            p = i * CHUNK
            got = jnp.dot(
                win_ref[pl.ds(p, CHUNK), t : t + rows, :].reshape(CHUNK * rows, LANES),
                weight_ref[...],
                preferred_element_type=jnp.float32,
            ).reshape(CHUNK, rows, BLOCK)
            conv_ref[pl.ds(p, CHUNK)] = got
            return jnp.maximum(high, jnp.max(got, axis=0))

        high = lax.fori_loop(0, low_places // CHUNK, full, jnp.full((rows, BLOCK), -jnp.inf, jnp.float32))

        def tail(p, high):
            got = jnp.dot(win_ref[p, t : t + rows, :], weight_ref[...], preferred_element_type=jnp.float32)
            got = jnp.where(valid > p.astype(jnp.float32), got, -jnp.inf)
            conv_ref[p] = got
            return jnp.maximum(high, got)

        high = lax.fori_loop(low_places, places_here, tail, high)

        def soft(i, total):
            for o in range(CHUNK):
                p = i * CHUNK + o
                got = jnp.exp(conv_ref[p] - high)
                e_ref[0, p, t : t + rows, :] = got.astype(jnp.bfloat16)
                total = total + got
            return total

        total = lax.fori_loop(0, low_places // CHUNK, soft, jnp.zeros((rows, BLOCK), jnp.float32))

        def soft_tail(p, total):
            got = jnp.exp(conv_ref[p] - high)
            e_ref[0, p, t : t + rows, :] = got.astype(jnp.bfloat16)
            return total + got

        total = lax.fori_loop(low_places, places_here, soft_tail, total)
        before = high + jnp.log(total) + aux_ref[0:1, :]
        x_ref[t : t + rows, :] = before
        inv_ref[t : t + rows, :] = 1.0 / total
        act_ref[t : t + rows, :] = (before * jax.nn.sigmoid(before)).astype(jnp.bfloat16)


def conv_forward(ids, table, weight, aux, trips, low_places):
    tokens, chars = ids.shape
    count = weight.shape[1]
    blocks = count // BLOCK
    rows = 64
    whole = lambda *shape: pl.BlockSpec(shape, lambda j, *_: (0,) * len(shape))
    return pl.pallas_call(
        functools.partial(forward_kernel, chars, low_places),
        grid_spec=pltpu.PrefetchScalarGridSpec(
            num_scalar_prefetch=1,
            grid=(blocks,),
            in_specs=[
                whole(tokens, chars),
                whole(*table.shape),
                pl.BlockSpec((LANES, BLOCK), lambda j, *_: (0, j)),
                pl.BlockSpec((8, BLOCK), lambda j, *_: (0, j)),
            ],
            out_specs=[
                pl.BlockSpec((1, chars, tokens, BLOCK), lambda j, *_: (j, 0, 0, 0)),
                pl.BlockSpec((tokens, BLOCK), lambda j, *_: (0, j)),
                pl.BlockSpec((tokens, BLOCK), lambda j, *_: (0, j)),
                pl.BlockSpec((tokens, BLOCK), lambda j, *_: (0, j)),
                whole(chars, tokens, LANES),
            ],
            scratch_shapes=[
                pltpu.VMEM((chars + WIDEST - 1, tokens, LANES), jnp.bfloat16),
                pltpu.VMEM((chars, rows, BLOCK), jnp.float32),
            ],
        ),
        out_shape=[
            jax.ShapeDtypeStruct((blocks, chars, tokens, BLOCK), jnp.bfloat16),
            jax.ShapeDtypeStruct((tokens, count), jnp.bfloat16),
            jax.ShapeDtypeStruct((tokens, count), jnp.float32),
            jax.ShapeDtypeStruct((tokens, count), jnp.float32),
            jax.ShapeDtypeStruct((chars, tokens, LANES), jnp.bfloat16),
        ],
        compiler_params=pltpu.CompilerParams(vmem_limit_bytes=VMEM_BYTES),
        cost_estimate=pl.CostEstimate(flops=2 * chars * tokens * LANES * count, bytes_accessed=2 * chars * tokens * count, transcendentals=chars * tokens * count),
        name="conv_forward",
    )(trips, ids, table, weight, aux)


def backward_kernel(chars, low_places, trip_ref, e_ref, x_ref, inv_ref, d_ref, win_ref, weight_ref, ids_ref, dw_ref, db_ref, table_ref, dwin_ref, scale_ref):
    step = pl.program_id(0)
    tokens = d_ref.shape[0]
    before = x_ref[...]
    sig = jax.nn.sigmoid(before)
    d_before = d_ref[...].astype(jnp.float32) * sig * (1.0 + before * (1.0 - sig))
    db_ref[...] = jnp.broadcast_to(jnp.sum(d_before, axis=0, keepdims=True), db_ref.shape)
    scale_ref[...] = d_before * inv_ref[...]

    @pl.when(step == 0)
    def clear():
        dwin_ref[...] = jnp.zeros(dwin_ref.shape, jnp.float32)

    dw_ref[...] = jnp.zeros(dw_ref.shape, jnp.float32)

    def some(count, p):
        scale = scale_ref[...]
        d_conv = (e_ref[0, pl.ds(p, count)].astype(jnp.float32) * scale[None]).astype(jnp.bfloat16)
        flat = d_conv.reshape(count * tokens, BLOCK)
        dwin_ref[pl.ds(p, count)] += lax.dot_general(
            flat, weight_ref[...], (((1,), (1,)), ((), ())), preferred_element_type=jnp.float32
        ).reshape(count, tokens, LANES)
        win = win_ref[pl.ds(p, count)].reshape(count * tokens, LANES)
        dw_ref[...] += lax.dot_general(win, flat, (((0,), (0,)), ((), ())), preferred_element_type=jnp.float32)

    def full(i, carry):
        some(CHUNK, i * CHUNK)
        return carry

    lax.fori_loop(0, low_places // CHUNK, full, 0)

    def tail(p, carry):
        some(1, p)
        return carry

    lax.fori_loop(low_places, trip_ref[step], tail, 0)

    @pl.when(step == pl.num_programs(0) - 1)
    def finish():
        vocab = table_ref.shape[0]
        group = lax.broadcasted_iota(jnp.int32, (tokens, LANES), 1) // 16
        places = lax.broadcasted_iota(jnp.int32, (vocab, tokens), 0)
        table_ref[...] = jnp.zeros(table_ref.shape, jnp.float32)
        for c in range(chars):
            got = jnp.where(group == 0, dwin_ref[c], 0.0)
            for k in range(1, WIDEST):
                if c - k >= 0:
                    got = jnp.where(group == k, dwin_ref[c - k], got)
            first = got.astype(jnp.bfloat16)
            second = (got - first.astype(jnp.float32)).astype(jnp.bfloat16)
            hits = jnp.where(places == ids_ref[c : c + 1, :], 1.0, 0.0).astype(jnp.bfloat16)
            table_ref[...] += jnp.dot(hits, jnp.concatenate([first, second], axis=1), preferred_element_type=jnp.float32)


def conv_backward(e, x, inv, d_act, win, weight, ids_across, trips, low_places, vocab):
    blocks, chars, tokens, unused = e.shape
    count = x.shape[1]
    whole = lambda *shape: pl.BlockSpec(shape, lambda j, *_: (0,) * len(shape))
    return pl.pallas_call(
        functools.partial(backward_kernel, chars, low_places),
        grid_spec=pltpu.PrefetchScalarGridSpec(
            num_scalar_prefetch=1,
            grid=(blocks,),
            in_specs=[
                pl.BlockSpec((1, chars, tokens, BLOCK), lambda j, *_: (j, 0, 0, 0)),
                pl.BlockSpec((tokens, BLOCK), lambda j, *_: (0, j)),
                pl.BlockSpec((tokens, BLOCK), lambda j, *_: (0, j)),
                pl.BlockSpec((tokens, BLOCK), lambda j, *_: (0, j)),
                whole(chars, tokens, LANES),
                pl.BlockSpec((LANES, BLOCK), lambda j, *_: (0, j)),
                whole(*ids_across.shape),
            ],
            out_specs=[
                pl.BlockSpec((LANES, BLOCK), lambda j, *_: (0, j)),
                pl.BlockSpec((8, BLOCK), lambda j, *_: (0, j)),
                whole(vocab, 2 * LANES),
            ],
            scratch_shapes=[
                pltpu.VMEM((chars, tokens, LANES), jnp.float32),
                pltpu.VMEM((tokens, BLOCK), jnp.float32),
            ],
        ),
        out_shape=[
            jax.ShapeDtypeStruct((LANES, count), jnp.float32),
            jax.ShapeDtypeStruct((8, count), jnp.float32),
            jax.ShapeDtypeStruct((vocab, 2 * LANES), jnp.float32),
        ],
        compiler_params=pltpu.CompilerParams(vmem_limit_bytes=VMEM_BYTES),
        cost_estimate=pl.CostEstimate(flops=4 * chars * tokens * LANES * count, bytes_accessed=2 * chars * tokens * count, transcendentals=0),
        name="conv_backward",
    )(trips, e, x, inv, d_act, win, weight, ids_across)


def bank_layout(base_count):
    layout = []
    natural = 0
    for number in range(8):
        filters = bank_parts[number] * base_count
        leading = 16 * base_count if number == 7 else 0
        layout.append((bank_widths[number], leading, filters, natural))
        natural += filters
    return layout


def join_filters(weights, layout):
    parts = []
    for kernel, leading, filters, natural in layout:
        part = weights[kernel - 1][:, leading : leading + filters]
        parts.append(jnp.pad(part, ((0, LANES - part.shape[0]), (0, 0))))
    return jnp.concatenate(parts, axis=1)


def column_places(layout, chars):
    return [chars - kernel + 1 for kernel, leading, filters, natural in layout for unused in range(filters)]


def highway_forward(inputs, weight, bias_row, feature_count):
    project = jnp.dot(inputs, weight, preferred_element_type=jnp.float32) + bias_row.astype(
        jnp.float32
    )
    gating = jax.nn.sigmoid(project[:, feature_count:])
    blended = gating * inputs.astype(jnp.float32) + (1.0 - gating) * jax.nn.silu(
        project[:, :feature_count]
    )
    return (blended, project)


def highway_back(inputs, weight, project, d_output, feature_count):
    carried = inputs.astype(jnp.float32)
    linear = project[:, :feature_count]
    gating = jax.nn.sigmoid(project[:, feature_count:])
    sigmoid_at = jax.nn.sigmoid(linear)
    d_linear = d_output * (1.0 - gating) * sigmoid_at * (1.0 + linear * (1.0 - sigmoid_at))
    d_gating = d_output * (carried - linear * sigmoid_at) * gating * (1.0 - gating)
    d_project = jnp.concatenate([d_linear, d_gating], axis=1).astype(jnp.bfloat16)
    grad_weight = jnp.einsum("tf,tg->fg", inputs, d_project, preferred_element_type=jnp.float32)
    grad_bias = jnp.sum(d_project.astype(jnp.float32), axis=0)
    d_inputs = (
        jnp.einsum("tg,fg->tf", d_project, weight, preferred_element_type=jnp.float32)
        + gating * d_output
    )
    return (d_inputs, grad_weight, grad_bias)


def feature_columns(bank_order, layout, feature_count):
    counts = jnp.array([entry[2] for entry in layout], jnp.int32)
    naturals = jnp.array([entry[3] for entry in layout], jnp.int32)
    matches = (bank_order[:, None] == lax.iota(jnp.int32, 8)[None, :]).astype(jnp.int32)
    placed = jnp.sum(matches * counts[None, :], axis=1)
    before = jnp.cumsum(placed) - placed
    starts = jnp.sum(matches * before[:, None], axis=0)
    column = lax.iota(jnp.int32, feature_count)
    inside = (column[:, None] >= starts[None, :]) & (column[:, None] < starts[None, :] + counts[None, :])
    return jnp.sum(jnp.where(inside, naturals[None, :] + column[:, None] - starts[None, :], 0), axis=1)


def local(
    char_ids,
    bank_order,
    char_table,
    conv_w1,
    conv_w2,
    conv_w3,
    conv_w4,
    conv_w5,
    conv_w6,
    conv_w7,
    conv_bias,
    highway_w1,
    highway_b1,
    highway_w2,
    highway_b2,
    proj_weight,
    proj_bias,
    cotangent,
):
    axes = ("wide", "narrow")
    feature_count = conv_bias.shape[0]
    chars = char_ids.shape[1]
    vocab_count, emb_width = char_table.shape
    layout = bank_layout(feature_count // 64)
    weights = (conv_w1, conv_w2, conv_w3, conv_w4, conv_w5, conv_w6, conv_w7)
    layer_one_w, layer_two_w, out_weight = (
        lax.all_gather(part, axes, axis=1, tiled=True) for part in (highway_w1, highway_w2, proj_weight)
    )
    layer_one_b, layer_two_b, out_bias = (
        lax.all_gather(part, axes, axis=0, tiled=True) for part in (highway_b1, highway_b2, proj_bias)
    )
    places = column_places(layout, chars)
    filters = join_filters(weights, layout)
    places_row = jnp.array(places, jnp.float32)
    aux = jnp.pad(
        jnp.stack([conv_bias.astype(jnp.float32) - jnp.log(places_row), places_row]), ((0, 6), (0, 0))
    )
    padded = -(-vocab_count // LANES) * LANES
    table = jnp.pad(
        jnp.tile(char_table, (1, WIDEST)), ((0, padded - vocab_count), (0, LANES - WIDEST * emb_width))
    )
    trips = jnp.array(
        [max(places[start : start + BLOCK]) for start in range(0, feature_count, BLOCK)], jnp.int32
    )
    exps, natural, before, inverse, windows = conv_forward(
        char_ids, table, filters, aux, trips, min(places)
    )
    columns = feature_columns(bank_order, layout, feature_count)
    shuffle = (lax.iota(jnp.int32, feature_count)[:, None] == columns[None, :]).astype(jnp.bfloat16)
    features = jnp.dot(natural, shuffle, preferred_element_type=jnp.float32).astype(jnp.bfloat16)
    hidden_one, proj_one = highway_forward(features, layer_one_w, layer_one_b, feature_count)
    input_two = hidden_one.astype(jnp.bfloat16)
    hidden_two, proj_two = highway_forward(input_two, layer_two_w, layer_two_b, feature_count)
    input_out = hidden_two.astype(jnp.bfloat16)
    encoded = (
        jnp.dot(input_out, out_weight, preferred_element_type=jnp.float32) + out_bias.astype(jnp.float32)
    ).astype(jnp.bfloat16)
    d_hidden_two = jnp.einsum("tp,fp->tf", cotangent, out_weight, preferred_element_type=jnp.float32)
    grad_out_w = jnp.einsum("tf,tp->fp", input_out, cotangent, preferred_element_type=jnp.float32)
    grad_out_b = jnp.sum(cotangent.astype(jnp.float32), axis=0)
    d_hidden_one, grad_two_w, grad_two_b = highway_back(
        input_two, layer_two_w, proj_two, d_hidden_two, feature_count
    )
    d_inputs, grad_one_w, grad_one_b = highway_back(
        features, layer_one_w, proj_one, d_hidden_one, feature_count
    )
    d_natural = lax.dot_general(
        d_inputs.astype(jnp.bfloat16),
        shuffle,
        (((1,), (1,)), ((), ())),
        preferred_element_type=jnp.float32,
    ).astype(jnp.bfloat16)
    reduced = []
    for part in (grad_one_w, grad_two_w, grad_out_w):
        part = part.astype(jnp.bfloat16)
        for axis in axes:
            part = lax.psum_scatter(part, axis, scatter_dimension=1, tiled=True)
        reduced.append(part.astype(jnp.float32))
    ids_across = jnp.pad(char_ids.T, ((0, -chars % 8), (0, 0)))
    d_filters, d_bias, d_table = conv_backward(
        exps, before, inverse, d_natural, windows, filters, ids_across, trips, min(places), padded
    )
    span = WIDEST * emb_width
    d_table = d_table[:vocab_count, :span] + d_table[:vocab_count, LANES : LANES + span]
    d_table = jnp.sum(d_table.reshape(vocab_count, WIDEST, emb_width), axis=1)
    d_filters, d_bias, d_table, bias_one, bias_two, bias_out = lax.psum(
        (d_filters, d_bias[0], d_table, grad_one_b, grad_two_b, grad_out_b), axes
    )
    own = lax.axis_index(axes)
    own_biases = [
        lax.dynamic_slice_in_dim(part, own * short.shape[0], short.shape[0], 0)
        for part, short in ((bias_one, highway_b1), (bias_two, highway_b2), (bias_out, proj_bias))
    ]
    grad_weights = []
    for number, (kernel, leading, filters, natural) in enumerate(layout):
        grad_weights.append(d_filters[: kernel * emb_width, natural : natural + filters])
    grad_weights[6:] = [jnp.concatenate(grad_weights[6:], axis=1)]
    return (
        encoded,
        d_table,
        *grad_weights,
        d_bias,
        reduced[0],
        own_biases[0],
        reduced[1],
        own_biases[1],
        reduced[2],
        own_biases[2],
    )


def solution(mesh):
    placed = (
        P(("wide", "narrow"), None),
        P(),
        P(),
        P(),
        P(),
        P(),
        P(),
        P(),
        P(),
        P(),
        P(),
        P(None, ("wide", "narrow")),
        P(("wide", "narrow")),
        P(None, ("wide", "narrow")),
        P(("wide", "narrow")),
        P(None, ("wide", "narrow")),
        P(("wide", "narrow")),
        P(("wide", "narrow"), None),
    )
    return jax.shard_map(
        local,
        mesh=mesh,
        in_specs=placed,
        out_specs=(
            P(("wide", "narrow"), None),
            P(),
            P(),
            P(),
            P(),
            P(),
            P(),
            P(),
            P(),
            P(),
            P(None, ("wide", "narrow")),
            P(("wide", "narrow")),
            P(None, ("wide", "narrow")),
            P(("wide", "narrow")),
            P(None, ("wide", "narrow")),
            P(("wide", "narrow")),
        ),
        check_vma=False,
    )
```

time: 2680 us -> 923 us (0.34)
  waiting for transfers between devices: 1790 us -> 424 us
  matrix products: 216 us -> 93.5 us
  Pallas kernels: 0 us -> 105 us
  loops' own time: 95.5 us -> 0 us
  blocking collectives: 302 us -> 229 us
  starting transfers between devices: 68.7 us -> 0.4 us
  other arithmetic: 75.3 us -> 8.96 us
  local copies, waits for them, and re-layouts: 91.3 us -> 37.5 us
    reduce_scatter x3 -> x4, waiting for transfers between devices: 1580 us -> 184 us  [local(): part = lax.psum_scatter(part, axis, scatter_dimension=1, tiled=True)]
    psum x2 -> x1, waiting for transfers between devices: 184 us -> 40.4 us  [local(): lax.psum((d_filters, d_bias[0], d_table, grad_one_b, grad_two_b, grad_out...]
    all_gather x3, waiting for transfers between devices: 0.04 us -> 111 us  [local(): lax.all_gather(part, axes, axis=1, tiled=True)]
    dot_general x22 -> x2, matrix products: 134 us -> 27.5 us  [the longest x1 22.9 us: local(): lax.dot_general(d_inputs.astype(jnp.bfloat16), shuffle, (((1,), (1,)), ((...]
    pallas_call x0 -> x2, Pallas kernels: none -> 105 us  [the longest x1 63.9 us: conv_forward(): pl.pallas_call(functools.partial(forward_kernel, chars, low_places), grid...]
    another operation x4 -> x0, loops' own time: 95.5 us -> none  [the longest x1 49.6 us: local(): lax.switch(member, [make_backward(chosen, char_table, weights, conv_bias,...]
    unnamed x8 -> x12, waiting for transfers between devices: 2.17 us -> 88.8 us
    unnamed x1, blocking collectives: 123 us -> 39.8 us
  transfers between devices with their start and end apart: 10 -> 10, of which waited for: 6 -> 8; matrix products, arithmetic and copies ran while one was open for 4% -> 14% of each run, Pallas kernels for 0% -> 12%
where the time goes in v1:
time: 923 us; the launch traced here: 913 us
  waiting for transfers between devices  424 us (46%)
  blocking collectives  229 us (25%)
  Pallas kernels  105 us (11%)
  matrix products  93.5 us (10%)
  local copies, waits for them, and re-layouts  37.5 us (4%)
  between operations  14.7 us (2%)
    reduce_scatter x4, waiting for transfers between devices, local(): part = lax.psum_scatter(part, axis, scatter_dimension=1, tiled=True)  184 us
    all_gather x2, blocking collectives, local(): lax.all_gather(part, axes, axis=0, tiled=True)  146 us
    all_gather x3, waiting for transfers between devices, local(): lax.all_gather(part, axes, axis=1, tiled=True)  111 us
    unnamed x12, waiting for transfers between devices  88.8 us
    pallas_call x1, Pallas kernels, conv_forward(): pl.pallas_call(functools.partial(forward_kernel, chars, low_places), grid...  63.9 us
    psum x1, blocking collectives, local(): lax.psum((d_filters, d_bias[0], d_table, grad_one_b, grad_two_b, grad_out...  42.5 us
    pallas_call x1, Pallas kernels, conv_backward(): pl.pallas_call(functools.partial(backward_kernel, chars, low_places), gri...  41.3 us
    psum x1, waiting for transfers between devices, local(): lax.psum((d_filters, d_bias[0], d_table, grad_one_b, grad_two_b, grad_out...  40.4 us
  transfers between devices with their start and end apart: 10, of which 8 were waited for; matrix products, arithmetic and copies ran while one was open for 14% of the time, Pallas kernels for 12%

profile of v1, /device:TPU:0, one launch (start us, length us, event | category | flops | bytes accessed | tf_op | source)
XLA Modules:
  0.0 912.7 jit_solution(2267408237226080359)
XLA Ops:
  9.5 1.6 copy.47.ids_ref
  15.5 0.8 pad.48
  16.2 0.9 pad.49
  17.7 69.7 %all-gather = bf16[32,1,128]{2,1,0:T(2,128)(2,1)S(1)} all-gather(bf16[1,1,128]{2,1,0:T(2,128)(2,1)S(1)} %bitcast.42), channel_id=1, replica_groups=mesh['wide'=8,'narrow'=4] {'wide','narrow'}, dimensions={0}, use_global_device_ids=true | all-gather | bytes 8448 | tf_op jit(solution)/shard_map/all_gather | solution.py:320
  87.4 76.6 %all-gather.1 = bf16[32,1,128]{2,1,0:T(2,128)(2,1)S(1)} all-gather(bf16[1,1,128]{2,1,0:T(2,128)(2,1)S(1)} %bitcast.43), channel_id=1, replica_groups=mesh['wide'=8,'narrow'=4] {'wide','narrow'}, dimensions={0}, use_global_device_ids=true | all-gather | bytes 8448 | tf_op jit(solution)/shard_map/all_gather | solution.py:320
  164.8 1.0 concatenate.14.weight_ref
  165.7 63.9 %conv_forward.1 = (bf16[8,50,256,256]{3,2,1,0:T(8,128)(2,1)}, bf16[256,2048]{1,0:T(8,128)(2,1)}, f32[256,2048]{1,0:T(8,128)}, f32[256,2048]{1,0:T(8,128)}, bf16[50,256,128]{2,1,0:T(8,128)(2,1)}) custom-call(s32[8]{0:T(128)} %constant.45.clone.trip_ref, s32[256,50]{1,0:T(8,128)} %copy.47.ids_ref, bf16[384,128]{1,0:T(8,128)(2,1)} %pad.43.table_ref, ...), custom_call_target="tpu_custom_call" | custom-call | flops 6710886400 | bytes 52428800 | tf_op jit(solution)/shard_map/conv_forward/pallas_call | solution.py:98
  229.7 4.6 fusion.5
  234.3 8.9 convolution_add_fusion.1
  243.3 2.0 copy-done
  245.2 1.1 fusion.8
  246.4 63.6 %all-gather.8.cloned.1.call-done = bf16[2048,4096]{1,0:T(8,128)(2,1)} async-done(((bf16[2048,128]{1,0:T(8,128)(2,1)}), bf16[2048,4096]{1,0:T(8,128)(2,1)}) %all-gather.8.cloned.1.call-update) | async-done | bytes 16777232 | tf_op jit(solution)/shard_map/all_gather | solution.py:317
  310.0 10.7 %convolution_add_fusion = f32[256,4096]{1,0:T(8,128)} fusion(bf16[256,2048]{1,0:T(8,128)(2,1)S(1)} %fusion.8, bf16[2048,4096]{1,0:T(8,128)(2,1)} %all-gather.8.cloned.1.call-done, f32[4096]{0:T(1024)S(1)} %bitcast.40), kind=kOutput, calls=%fused_computation.7 | convolution fusion | flops 4296015872 | bytes 22036480 | tf_op jit(solution)/shard_map/dot_general | solution.py:251
  320.7 46.9 %all-gather.10.cloned.1.call-done = bf16[2048,512]{0,1:T(8,128)(2,1)} async-done(((bf16[2048,16]{0,1:T(8,128)(2,1)}), bf16[2048,512]{0,1:T(8,128)(2,1)}) %all-gather.10.cloned.1.call-update) | async-done | bytes 2097168 | tf_op jit(solution)/shard_map/all_gather | solution.py:317
  367.6 5.6 multiply_convert_fusion.1
  373.2 1.0 copy-done.3
  374.2 2.1 convolution_convert_fusion.2
  376.4 13.9 %multiply_convert_fusion = (bf16[256,2048]{1,0:T(8,128)(2,1)S(1)}, bf16[256,2048]{1,0:T(8,128)(2,1)}, f32[256,2048]{1,0:T(8,128)}) fusion(f32[256,4096]{1,0:T(8,128)} %copy-done, bf16[256,2048]{1,0:T(8,128)(2,1)} %copy-done.2, f32[256,2048]{1,0:T(8,128)} %get-tuple-element.44, f32[256,4096]{1,0:T(8,128)} %convolution_add_fusion, ...), kind=kOutput, calls=%fused_computation.43 | convolution fusion | flops 4312793088 | bytes 32505856 | tf_op jit(solution)/shard_map/tg,fg->tf/dot_general | solution.py:272
  390.2 11.9 %convolution_convert_fusion.1 = bf16[2048,4096]{1,0:T(8,128)(2,1)} fusion(bf16[256,2048]{1,0:T(8,128)(2,1)} %copy-done.2, bf16[256,2048]{1,0:T(8,128)(2,1)} %get-tuple-element.38, bf16[256,2048]{1,0:T(8,128)(2,1)S(1)} %get-tuple-element.37), kind=kOutput, calls=%fused_computation.4 | convolution fusion | flops 4307550208 | bytes 19922944 | tf_op jit(solution)/shard_map/tf,tg->fg/dot_general | solution.py:269
  402.2 9.8 %convolution_convert_fusion = bf16[2048,4096]{1,0:T(8,128)(2,1)} fusion(bf16[256,2048]{1,0:T(8,128)(2,1)} %copy-done.1, bf16[256,2048]{1,0:T(8,128)(2,1)S(1)} %get-tuple-element.40, bf16[256,2048]{1,0:T(8,128)(2,1)S(1)} %get-tuple-element.39), kind=kOutput, calls=%fused_computation.3 | convolution fusion | flops 4307550208 | bytes 19922944 | tf_op jit(solution)/shard_map/tf,tg->fg/dot_general | solution.py:269
  413.5 22.9 %fusion.6.d_ref = bf16[256,2048]{1,0:T(8,128)(2,1)} fusion(s32[2048]{0:T(1024)S(1)} %select_reduce_fusion, bf16[2048,4096]{1,0:T(8,128)(2,1)} %all-gather.6.cloned.1.call-done, f32[256,2048]{1,0:T(8,128)} %get-tuple-element.45, bf16[256,2048]{1,0:T(8,128)(2,1)} %get-tuple-element.38, bf16[256,2048]{1,0:T(8,128)(2,1)S(1)} %get-tuple-element.37, ...), kind=kOutput, calls=%fused_computation.20 | convolution fusion | flops 6454509568 | bytes 24125440 | tf_op jit(solution)/shard_map/dot_general | solution.py:357
  436.3 41.3 %conv_backward.1 = (f32[128,2048]{1,0:T(8,128)}, f32[8,2048]{1,0:T(8,128)}, f32[384,256]{1,0:T(8,128)}) custom-call(s32[8]{0:T(128)} %constant.45.clone.trip_ref, bf16[8,50,256,256]{3,2,1,0:T(8,128)(2,1)} %get-tuple-element.25.e_ref, f32[256,2048]{1,0:T(8,128)} %get-tuple-element.26.x_ref, f32[256,2048]{1,0:T(8,128)} %get-tuple-element.27.inv_ref, ...), custom_call_target="tpu_custom_call" | custom-call | flops 13421772800 | bytes 52428800 | tf_op jit(solution)/shard_map/conv_backward/pallas_call | solution.py:192
  478.5 57.9 %reduce-scatter.11.cloned.1.call-done = bf16[2048,512]{1,0:T(8,128)(2,1)} async-done(((bf16[2048,4096]{1,0:T(8,128)(2,1)}), bf16[2048,512]{1,0:T(8,128)(2,1)}) %reduce-scatter.11.cloned.1.call-update) | async-done | bytes 2097168 | tf_op jit(solution)/shard_map/reduce_scatter | solution.py:367
  536.4 4.0 copy.49
  540.4 115.8 %reduce-scatter.13.cloned.1.call-done = bf16[2048,512]{1,0:T(8,128)(2,1)} async-done(((bf16[2048,4096]{1,0:T(8,128)(2,1)}), bf16[2048,512]{1,0:T(8,128)(2,1)}) %reduce-scatter.13.cloned.1.call-update) | async-done | bytes 2097168 | tf_op jit(solution)/shard_map/reduce_scatter | solution.py:367
  656.2 3.9 copy.51
  661.0 39.8 %all-reduce.11 = bf16[512]{0:T(512)(128)(2,1)S(1)} all-reduce(bf16[512]{0:T(512)(128)(2,1)S(1)} %dynamic-update-slice), channel_id=1, replica_groups=mesh['wide'=8,'narrow'=4] {'wide','narrow'}, use_global_device_ids=true, to_apply=%add.11 | all-reduce | flops 512 | bytes 2048
  700.9 1.0 slice_add_fusion
  702.0 0.9 slice.66
  702.9 1.6 convert_reduce_fusion.1
  704.8 42.5 %all-reduce.12 = (f32[262,16]{0,1:T(8,128)}, f32[2048]{0:T(1024)}, f32[4096]{0:T(1024)S(1)}, f32[4096]{0:T(1024)S(1)}, f32[512]{0:T(512)S(1)}) all-reduce(f32[262,16]{0,1:T(8,128)S(1)} %reduce_sum.66, f32[2048]{0:T(1024)S(1)} %bitcast.38, f32[4096]{0:T(1024)S(1)} %convert_reduce_fusion.1, ...), channel_id=1, replica_groups=mesh['wide'=8,'narrow'=4] {'wide','narrow'}, use_global_device_ids=true, to_apply=%region_5.6 | all-reduce | flops 14944 | bytes 119552 | tf_op jit(solution)/shard_map/psum | solution.py:376
  749.0 3.1 fusion.27
  752.1 40.4 %all-reduce.15.cloned.1.call-done = f32[128,2048]{1,0:T(8,128)} async-done(((f32[128,2048]{1,0:T(8,128)}), f32[128,2048]{1,0:T(8,128)}) %all-reduce.15.cloned.1.call-update) | async-done | bytes 1048592 | tf_op jit(solution)/shard_map/psum | solution.py:376
  792.5 1.3 slice.71
  793.7 1.4 slice.72
  795.1 1.4 slice.73
  796.6 1.4 slice.74
  797.9 1.5 slice.75
  799.5 1.6 slice.76
  801.1 1.8 concatenate.18
  802.9 10.4 %reduce-scatter.17.cloned.1.call-done = bf16[2048,16]{0,1:T(8,128)(2,1)} async-done(((bf16[2048,64]{0,1:T(8,128)(2,1)}), bf16[2048,16]{0,1:T(8,128)(2,1)}) %reduce-scatter.17.cloned.1.call-update) | async-done | bytes 65552 | tf_op jit(solution)/shard_map/reduce_scatter | solution.py:367
  813.4 1.5 convert_element_type.107
  814.9 43.0 %reduce-scatter.19.cloned.1.call-done = bf16[128,2048]{1,0:T(8,128)(2,1)} async-done(((bf16[512,2048]{1,0:T(8,128)(2,1)}), bf16[128,2048]{1,0:T(8,128)(2,1)}) %reduce-scatter.19.cloned.1.call-update) | async-done | bytes 524304
  857.9 1.3 copy.50
  859.2 1.0 convert_element_type.101
  860.3 43.0 %reduce-scatter.21.cloned.1.call-done = bf16[128,2048]{1,0:T(8,128)(2,1)} async-done(((bf16[512,2048]{1,0:T(8,128)(2,1)}), bf16[128,2048]{1,0:T(8,128)(2,1)}) %reduce-scatter.21.cloned.1.call-update) | async-done | bytes 524304
  903.2 1.3 copy.52
  904.5 1.0 convert_element_type.104
  (85 shorter events, 13.4 us)
Async XLA Ops:
  7.2 10.0 %copy-start.16 = (s32[8]{0:T(128)S(1)}, s32[8]{0:T(128)}, u32[]{:S(2)}) copy-start(s32[8]{0:T(128)} %constant.46.clone) | copy-start | bytes 100
  7.2 156.9 %copy-start.9 = (f32[2048]{0:T(1024)S(1)}, f32[2048]{0:T(1024)}, u32[]{:S(2)}) copy-start(f32[2048]{0:T(1024)} %constant.74) | copy-start | bytes 24580
  7.2 156.9 %copy-start.8 = (f32[1,2048]{1,0:T(1,128)S(1)}, f32[1,2048]{1,0:T(1,128)}, u32[]{:S(2)}) copy-start(f32[1,2048]{1,0:T(1,128)} %constant.73) | copy-start | bytes 24580
  7.2 9.9 %copy-start.6 = (bf16[112,1024]{1,0:T(8,128)(2,1)S(1)}, bf16[112,1024]{1,0:T(8,128)(2,1)}, u32[]{:S(2)}) copy-start(bf16[112,1024]{1,0:T(8,128)(2,1)} %param.31) | copy-start | bytes 688132
  7.2 10.0 %copy-start.14 = (s32[8]{0:T(128)S(1)}, s32[8]{0:T(128)}, u32[]{:S(2)}) copy-start(s32[8]{0:T(128)} %param.23) | copy-start | bytes 100
  7.2 10.5 %copy-start.11 = (bf16[128]{0:T(256)(128)(2,1)S(1)}, bf16[128]{0:T(256)(128)(2,1)}, u32[]{:S(2)}) copy-start(bf16[128]{0:T(256)(128)(2,1)} %param.34) | copy-start | bytes 772
  7.2 80.2 %copy-start.12 = (bf16[128]{0:T(256)(128)(2,1)S(1)}, bf16[128]{0:T(256)(128)(2,1)}, u32[]{:S(2)}) copy-start(bf16[128]{0:T(256)(128)(2,1)} %param.36) | copy-start | bytes 772
  7.3 156.8 %copy-start.10 = (bf16[2048]{0:T(1024)(128)(2,1)S(1)}, bf16[2048]{0:T(1024)(128)(2,1)}, u32[]{:S(2)}) copy-start(bf16[2048]{0:T(1024)(128)(2,1)} %param.32) | copy-start | bytes 12292
  7.3 227.0 %all-gather.6.cloned.1.call-start = ((), (), s32[]{:S(2)}) async-start(), calls=%async_computation.6 | async-start | bytes 17301504 | tf_op jit(solution)/shard_map/all_gather | solution.py:317
  8.0 302.0 %all-gather.8.cloned.1.call-start = ((), (), s32[]{:S(2)}) async-start(), calls=%async_computation.7 | async-start | bytes 17301504 | tf_op jit(solution)/shard_map/all_gather | solution.py:317
  8.8 358.8 %all-gather.10.cloned.1.call-start = ((), (), s32[]{:S(2)}) async-start(), calls=%async_computation.8 | async-start | bytes 2162688 | tf_op jit(solution)/shard_map/all_gather | solution.py:317
  9.5 468.3 %reduce-scatter.15.cloned.1.call-start = ((), (), s32[]{:S(2)}) async-start(), calls=%async_computation.12 | async-start | bytes 2359296 | tf_op jit(solution)/shard_map/reduce_scatter | solution.py:367
  165.7 63.9 %copy-start.13 = (s32[8]{0:T(128)S(1)}, s32[8]{0:T(128)}, u32[]{:S(2)}) copy-start(s32[8]{0:T(128)} %constant.47.clone) | copy-start | bytes 100
  234.3 8.9 copy-start.2
  243.2 2.0 copy-start
  246.4 121.2 %copy-start.1 = (bf16[256,2048]{1,0:T(8,128)(2,1)}, bf16[256,2048]{1,0:T(8,128)(2,1)S(1)}, u32[]{:S(2)}) copy-start(bf16[256,2048]{1,0:T(8,128)(2,1)S(1)} %fusion.8) | copy-start | bytes 3145732
  310.0 57.6 %copy-start.5 = (bf16[256,512]{1,0:T(8,128)(2,1)S(1)}, bf16[256,512]{1,0:T(8,128)(2,1)}, u32[]{:S(2)}) copy-start(bf16[256,512]{1,0:T(8,128)(2,1)} %param.39) | copy-start | bytes 786436
  373.2 1.0 copy-start.3
  376.3 160.1 %reduce-scatter.11.cloned.1.call-start = ((), (), s32[]{:S(2)}) async-start(), calls=%async_computation.10 | async-start | bytes 18874368 | tf_op jit(solution)/shard_map/reduce_scatter | solution.py:367
  402.2 254.0 %reduce-scatter.13.cloned.1.call-start = ((), (), s32[]{:S(2)}) async-start(), calls=%async_computation.11 | async-start | bytes 18874368 | tf_op jit(solution)/shard_map/reduce_scatter | solution.py:367
  412.0 0.8 copy-start.7
  412.0 380.4 %all-reduce.15.cloned.1.call-start = ((), (), s32[]{:S(2)}) async-start(), calls=%async_computation.9 | async-start | bytes 2097152 | tf_op jit(solution)/shard_map/psum | solution.py:376
  477.7 335.7 %reduce-scatter.17.cloned.1.call-start = ((), (), s32[]{:S(2)}) async-start(), calls=%async_computation.13 | async-start | bytes 327680 | tf_op jit(solution)/shard_map/reduce_scatter | solution.py:367
  478.4 379.5 %reduce-scatter.19.cloned.1.call-start = ((), (), s32[]{:S(2)}) async-start(), calls=%async_computation.14 | async-start | bytes 2621440
  540.4 362.8 %reduce-scatter.21.cloned.1.call-start = ((), (), s32[]{:S(2)}) async-start(), calls=%async_computation.15 | async-start | bytes 2621440
  660.1 0.7 copy-start.15
  704.4 44.6 %copy-start.4 = (bf16[256,2048]{1,0:T(8,128)(2,1)S(1)}, bf16[256,2048]{1,0:T(8,128)(2,1)}, u32[]{:S(2)}) copy-start(bf16[256,2048]{1,0:T(8,128)(2,1)} %copy-done.3) | copy-start | bytes 3145732
Sparse Core Ops, SparseCore 0:
  11.0 150.2 all-gather.5
  164.1 145.7 all-gather.7
  312.9 54.6 all-gather.9
  376.4 40.0 reduce-scatter.14
  420.4 115.9 reduce-scatter.10
  540.2 115.9 reduce-scatter.12
  662.2 130.1 all-reduce.14
  794.7 18.5 reduce-scatter.16
  815.8 42.0 reduce-scatter.18
  860.0 43.1 reduce-scatter.20

commit v2 on v1

v2 whole, which is shorter than its diff:
```python
import math
import functools
import jax
import jax.numpy as jnp
from jax import lax
from jax.experimental import pallas as pl
from jax.experimental.pallas import tpu as pltpu
from jax.sharding import PartitionSpec as P

bank_widths = (1, 2, 3, 4, 5, 6, 7, 7)
bank_parts = (1, 1, 2, 4, 8, 16, 16, 16)
WIDEST = 7
LANES = 128
BLOCK = 256
CHUNK = 11
ROWS = 32
VMEM_BYTES = 60 * 1024 * 1024


def window_kernel(chars, ids_ref, table_ref, win_ref, emb_ref):
    tokens = ids_ref.shape[0]
    vocab = table_ref.shape[0]
    group = lax.broadcasted_iota(jnp.int32, (tokens, LANES), 1) // 16
    places = lax.broadcasted_iota(jnp.int32, (tokens, vocab), 1)
    for c in range(chars):
        hits = jnp.where(ids_ref[:, c : c + 1] == places, 1.0, 0.0).astype(jnp.bfloat16)
        emb_ref[c] = jnp.dot(hits, table_ref[...], preferred_element_type=jnp.float32).astype(jnp.bfloat16)
    for c in range(chars, chars + WIDEST - 1):
        emb_ref[c] = jnp.zeros((tokens, LANES), jnp.bfloat16)

    def window(p, carry):
        got = emb_ref[p]
        for k in range(1, WIDEST):
            got = jnp.where(group == k, emb_ref[p + k], got)
        win_ref[p] = got
        return carry

    lax.fori_loop(0, chars, window, 0)


def make_windows(ids, table):
    tokens, chars = ids.shape
    return pl.pallas_call(
        functools.partial(window_kernel, chars),
        out_shape=jax.ShapeDtypeStruct((chars, tokens, LANES), jnp.bfloat16),
        scratch_shapes=[pltpu.VMEM((chars + WIDEST - 1, tokens, LANES), jnp.bfloat16)],
        compiler_params=pltpu.CompilerParams(vmem_limit_bytes=VMEM_BYTES),
        name="make_windows",
    )(ids, table)


def forward_kernel(low_places, trip_ref, win_ref, weight_ref, aux_ref, past_ref, e_ref, act_ref, x_ref, inv_ref, conv_ref, high_ref):
    step = pl.program_id(0)
    blocks = pl.num_programs(0) - 1
    tokens = win_ref.shape[1]
    now, was = lax.rem(step, 2), lax.rem(step + 1, 2)

    def multiply(p, count):
        return jnp.dot(
            win_ref[pl.ds(p, count)].reshape(count * tokens, LANES),
            weight_ref[...],
            preferred_element_type=jnp.float32,
        ).reshape(count, tokens, BLOCK)

    def pool(p, count, totals):
        for number, r in enumerate(range(0, tokens, ROWS)):
            high = high_ref[was, r : r + ROWS, :]
            total = totals[number]
            for o in range(count):
                got = jnp.exp(conv_ref[was, p + o, r : r + ROWS, :] - high)
                e_ref[0, p + o, r : r + ROWS, :] = got.astype(jnp.bfloat16)
                total = total + got
            totals[number] = total
        return totals

    def start():
        return [jnp.zeros((ROWS, BLOCK), jnp.float32) for unused in range(0, tokens, ROWS)]

    def finish(totals):
        for number, r in enumerate(range(0, tokens, ROWS)):
            total = totals[number]
            before = high_ref[was, r : r + ROWS, :] + jnp.log(total) + past_ref[0:1, :]
            x_ref[r : r + ROWS, :] = before
            inv_ref[r : r + ROWS, :] = 1.0 / total
            act_ref[r : r + ROWS, :] = (before * jax.nn.sigmoid(before)).astype(jnp.bfloat16)

    def multiply_tail(places):
        valid = aux_ref[1:2, :]

        def tail(p, carry):
            got = jnp.where(valid > p.astype(jnp.float32), multiply(p, 1)[0], -jnp.inf)
            conv_ref[now, p] = got
            high_ref[now] = jnp.maximum(high_ref[now], got)
            return carry

        lax.fori_loop(low_places, places, tail, 0)

    def pool_tail(places, totals):
        return lax.fori_loop(low_places, places, lambda p, carry: tuple(pool(p, 1, list(carry))), tuple(totals))

    def some(i, totals, with_multiply, with_pool):
        p = i * CHUNK
        totals = list(totals)
        if with_multiply:
            got = multiply(p, CHUNK)
            conv_ref[now, pl.ds(p, CHUNK)] = got
            high_ref[now] = jnp.maximum(high_ref[now], jnp.max(got, axis=0))
        if with_pool:
            totals = pool(p, CHUNK, totals)
        return tuple(totals)

    @pl.when(step < blocks)
    def clear():
        high_ref[now] = jnp.full(high_ref.shape[1:], -jnp.inf, jnp.float32)

    @pl.when(step == 0)
    def first():
        lax.fori_loop(0, low_places // CHUNK, lambda i, c: some(i, c, True, False), ())
        multiply_tail(trip_ref[0])

    @pl.when((step > 0) & (step < blocks))
    def middle():
        totals = lax.fori_loop(0, low_places // CHUNK, lambda i, c: some(i, c, True, True), tuple(start()))
        totals = pool_tail(trip_ref[step - 1], totals)
        multiply_tail(trip_ref[step])
        finish(totals)

    @pl.when(step == blocks)
    def last():
        totals = lax.fori_loop(0, low_places // CHUNK, lambda i, c: some(i, c, False, True), tuple(start()))
        totals = pool_tail(trip_ref[step - 1], totals)
        finish(totals)


def conv_forward(windows, weight, aux, trips, low_places):
    chars, tokens, unused = windows.shape
    count = weight.shape[1]
    blocks = count // BLOCK
    ahead = lambda j: jnp.minimum(j, blocks - 1)
    behind = lambda j: jnp.maximum(j - 1, 0)
    return pl.pallas_call(
        functools.partial(forward_kernel, low_places),
        grid_spec=pltpu.PrefetchScalarGridSpec(
            num_scalar_prefetch=1,
            grid=(blocks + 1,),
            in_specs=[
                pl.BlockSpec(windows.shape, lambda j, *_: (0, 0, 0)),
                pl.BlockSpec((LANES, BLOCK), lambda j, *_: (0, ahead(j))),
                pl.BlockSpec((8, BLOCK), lambda j, *_: (0, ahead(j))),
                pl.BlockSpec((8, BLOCK), lambda j, *_: (0, behind(j))),
            ],
            out_specs=[
                pl.BlockSpec((1, chars, tokens, BLOCK), lambda j, *_: (behind(j), 0, 0, 0)),
                pl.BlockSpec((tokens, BLOCK), lambda j, *_: (0, behind(j))),
                pl.BlockSpec((tokens, BLOCK), lambda j, *_: (0, behind(j))),
                pl.BlockSpec((tokens, BLOCK), lambda j, *_: (0, behind(j))),
            ],
            scratch_shapes=[
                pltpu.VMEM((2, chars, tokens, BLOCK), jnp.float32),
                pltpu.VMEM((2, tokens, BLOCK), jnp.float32),
            ],
        ),
        out_shape=[
            jax.ShapeDtypeStruct((blocks, chars, tokens, BLOCK), jnp.bfloat16),
            jax.ShapeDtypeStruct((tokens, count), jnp.bfloat16),
            jax.ShapeDtypeStruct((tokens, count), jnp.float32),
            jax.ShapeDtypeStruct((tokens, count), jnp.float32),
        ],
        compiler_params=pltpu.CompilerParams(vmem_limit_bytes=VMEM_BYTES),
        cost_estimate=pl.CostEstimate(flops=2 * chars * tokens * LANES * count, bytes_accessed=2 * chars * tokens * count, transcendentals=chars * tokens * count),
        name="conv_forward",
    )(trips, windows, weight, aux, aux)
def backward_kernel(chars, low_places, trip_ref, e_ref, x_ref, inv_ref, d_ref, win_ref, weight_ref, ids_ref, dw_ref, db_ref, table_ref, dwin_ref, scale_ref):
    step = pl.program_id(0)
    tokens = d_ref.shape[0]
    before = x_ref[...]
    sig = jax.nn.sigmoid(before)
    d_before = d_ref[...].astype(jnp.float32) * sig * (1.0 + before * (1.0 - sig))
    db_ref[...] = jnp.broadcast_to(jnp.sum(d_before, axis=0, keepdims=True), db_ref.shape)
    scale_ref[...] = d_before * inv_ref[...]

    @pl.when(step == 0)
    def clear():
        dwin_ref[...] = jnp.zeros(dwin_ref.shape, jnp.float32)

    dw_ref[...] = jnp.zeros(dw_ref.shape, jnp.float32)

    def some(count, p):
        scale = scale_ref[...]
        d_conv = (e_ref[0, pl.ds(p, count)].astype(jnp.float32) * scale[None]).astype(jnp.bfloat16)
        flat = d_conv.reshape(count * tokens, BLOCK)
        dwin_ref[pl.ds(p, count)] += lax.dot_general(
            flat, weight_ref[...], (((1,), (1,)), ((), ())), preferred_element_type=jnp.float32
        ).reshape(count, tokens, LANES)
        win = win_ref[pl.ds(p, count)].reshape(count * tokens, LANES)
        dw_ref[...] += lax.dot_general(win, flat, (((0,), (0,)), ((), ())), preferred_element_type=jnp.float32)

    def full(i, carry):
        some(CHUNK, i * CHUNK)
        return carry

    lax.fori_loop(0, low_places // CHUNK, full, 0)

    def tail(p, carry):
        some(1, p)
        return carry

    lax.fori_loop(low_places, trip_ref[step], tail, 0)

    @pl.when(step == pl.num_programs(0) - 1)
    def finish():
        vocab = table_ref.shape[0]
        group = lax.broadcasted_iota(jnp.int32, (tokens, LANES), 1) // 16
        places = lax.broadcasted_iota(jnp.int32, (vocab, tokens), 0)
        table_ref[...] = jnp.zeros(table_ref.shape, jnp.float32)
        for c in range(chars):
            got = jnp.where(group == 0, dwin_ref[c], 0.0)
            for k in range(1, WIDEST):
                if c - k >= 0:
                    got = jnp.where(group == k, dwin_ref[c - k], got)
            first = got.astype(jnp.bfloat16)
            second = (got - first.astype(jnp.float32)).astype(jnp.bfloat16)
            hits = jnp.where(places == ids_ref[c : c + 1, :], 1.0, 0.0).astype(jnp.bfloat16)
            table_ref[...] += jnp.dot(hits, jnp.concatenate([first, second], axis=1), preferred_element_type=jnp.float32)


def conv_backward(e, x, inv, d_act, win, weight, ids_across, trips, low_places, vocab):
    blocks, chars, tokens, unused = e.shape
    count = x.shape[1]
    whole = lambda *shape: pl.BlockSpec(shape, lambda j, *_: (0,) * len(shape))
    return pl.pallas_call(
        functools.partial(backward_kernel, chars, low_places),
        grid_spec=pltpu.PrefetchScalarGridSpec(
            num_scalar_prefetch=1,
            grid=(blocks,),
            in_specs=[
                pl.BlockSpec((1, chars, tokens, BLOCK), lambda j, *_: (j, 0, 0, 0)),
                pl.BlockSpec((tokens, BLOCK), lambda j, *_: (0, j)),
                pl.BlockSpec((tokens, BLOCK), lambda j, *_: (0, j)),
                pl.BlockSpec((tokens, BLOCK), lambda j, *_: (0, j)),
                whole(chars, tokens, LANES),
                pl.BlockSpec((LANES, BLOCK), lambda j, *_: (0, j)),
                whole(*ids_across.shape),
            ],
            out_specs=[
                pl.BlockSpec((LANES, BLOCK), lambda j, *_: (0, j)),
                pl.BlockSpec((8, BLOCK), lambda j, *_: (0, j)),
                whole(vocab, 2 * LANES),
            ],
            scratch_shapes=[
                pltpu.VMEM((chars, tokens, LANES), jnp.float32),
                pltpu.VMEM((tokens, BLOCK), jnp.float32),
            ],
        ),
        out_shape=[
            jax.ShapeDtypeStruct((LANES, count), jnp.float32),
            jax.ShapeDtypeStruct((8, count), jnp.float32),
            jax.ShapeDtypeStruct((vocab, 2 * LANES), jnp.float32),
        ],
        compiler_params=pltpu.CompilerParams(vmem_limit_bytes=VMEM_BYTES),
        cost_estimate=pl.CostEstimate(flops=4 * chars * tokens * LANES * count, bytes_accessed=2 * chars * tokens * count, transcendentals=0),
        name="conv_backward",
    )(trips, e, x, inv, d_act, win, weight, ids_across)


def bank_layout(base_count):
    layout = []
    natural = 0
    for number in range(8):
        filters = bank_parts[number] * base_count
        leading = 16 * base_count if number == 7 else 0
        layout.append((bank_widths[number], leading, filters, natural))
        natural += filters
    return layout


def join_filters(weights, layout):
    parts = []
    for kernel, leading, filters, natural in layout:
        part = weights[kernel - 1][:, leading : leading + filters]
        parts.append(jnp.pad(part, ((0, LANES - part.shape[0]), (0, 0))))
    return jnp.concatenate(parts, axis=1)


def column_places(layout, chars):
    return [chars - kernel + 1 for kernel, leading, filters, natural in layout for unused in range(filters)]


def feature_columns(bank_order, layout, feature_count):
    counts = jnp.array([entry[2] for entry in layout], jnp.int32)
    naturals = jnp.array([entry[3] for entry in layout], jnp.int32)
    matches = (bank_order[:, None] == lax.iota(jnp.int32, 8)[None, :]).astype(jnp.int32)
    placed = jnp.sum(matches * counts[None, :], axis=1)
    before = jnp.cumsum(placed) - placed
    starts = jnp.sum(matches * before[:, None], axis=0)
    column = lax.iota(jnp.int32, feature_count)
    inside = (column[:, None] >= starts[None, :]) & (column[:, None] < starts[None, :] + counts[None, :])
    return jnp.sum(jnp.where(inside, naturals[None, :] + column[:, None] - starts[None, :], 0), axis=1)


def swap(x, axis, bit):
    return lax.ppermute(x, axis, [(i, i ^ bit) for i in range(lax.axis_size(axis))])


def side(axis, bit):
    return (lax.axis_index(axis) // bit) % 2


def high_bits(axis):
    return [1 << k for k in range(1, lax.axis_size(axis).bit_length() - 1)]


def group_all(x):
    along = swap(x, "narrow", 1)
    return [x, along, swap(x, "wide", 1), swap(along, "wide", 1)]


def group_trade(parts):
    return [
        parts[0],
        swap(parts[1], "narrow", 1),
        swap(parts[2], "wide", 1),
        swap(swap(parts[3], "narrow", 1), "wide", 1),
    ]


def layer_kernel(x_copies, w_copies, at_ref, bias_ref, *refs):
    x_count = 1 + max(copy[0] for copy in x_copies)
    w_count = 1 + max(copy[0] for copy in w_copies)
    x_sources, w_sources = refs[:x_count], refs[x_count : x_count + w_count]
    x_ref, w_ref, project_ref, hidden_ref, sems = refs[x_count + w_count :]
    width = w_sources[0].shape[2]
    moves = []
    for source, row, column, height, wide, to_row, to_column in x_copies:
        moves.append(
            pltpu.make_async_copy(
                x_sources[source].at[pl.ds(row, height), pl.ds(column, wide)],
                x_ref.at[pl.ds(to_row, height), pl.ds(to_column, wide)],
                sems.at[len(moves)],
            )
        )
    for number, (source, piece, to_row) in enumerate(w_copies):
        column = pl.multiple_of(at_ref[number] * width, width)
        moves.append(
            pltpu.make_async_copy(
                w_sources[source].at[piece],
                w_ref.at[pl.ds(to_row, w_sources[source].shape[1]), pl.ds(column, width)],
                sems.at[len(moves)],
            )
        )
    for move in moves:
        move.start()
    for move in moves:
        move.wait()
    half = hidden_ref.shape[1]
    step = 256

    @pl.loop(0, x_ref.shape[0] // step)
    def block(i):
        rows = pl.ds(pl.multiple_of(i * step, step), step)
        project = jnp.dot(x_ref[rows, :], w_ref[...], preferred_element_type=jnp.float32) + bias_ref[...]
        project_ref[rows, :] = project
        gating = jax.nn.sigmoid(project[:, half:])
        linear = project[:, :half]
        carried = x_ref[rows, :half].astype(jnp.float32)
        hidden = gating * carried + (1.0 - gating) * (linear * jax.nn.sigmoid(linear))
        hidden_ref[rows, :] = hidden.astype(jnp.bfloat16)


def layer(x_sources, x_copies, weight, bias_row, shape):
    w_sources, w_copies, columns = weight
    count, depth, total = shape
    if w_sources[0].shape[2] % LANES:
        inputs = jnp.zeros((count, depth), jnp.bfloat16)
        for source, row, column, height, wide, to_row, to_column in x_copies:
            part = x_sources[source][row : row + height, column : column + wide]
            inputs = inputs.at[to_row : to_row + height, to_column : to_column + wide].set(part)
        whole = jnp.zeros((depth, total), jnp.bfloat16)
        for number, (source, piece, to_row) in enumerate(w_copies):
            part = w_sources[source][piece]
            whole = lax.dynamic_update_slice(whole, part, (to_row, columns[number] * part.shape[1]))
        project = jnp.dot(inputs, whole, preferred_element_type=jnp.float32) + bias_row
        gating = jax.nn.sigmoid(project[:, total // 2 :])
        carried = inputs[:, : total // 2].astype(jnp.float32)
        hidden = gating * carried + (1.0 - gating) * jax.nn.silu(project[:, : total // 2])
        return inputs, whole, project, hidden.astype(jnp.bfloat16)
    anywhere = pl.BlockSpec(memory_space=pl.ANY)
    near = pl.BlockSpec(memory_space=pltpu.VMEM)
    return pl.pallas_call(
        functools.partial(layer_kernel, tuple(x_copies), tuple(w_copies)),
        in_specs=[pl.BlockSpec(memory_space=pltpu.SMEM), near] + [anywhere] * (len(x_sources) + len(w_sources)),
        out_specs=[near] * 4,
        out_shape=[
            jax.ShapeDtypeStruct((count, depth), jnp.bfloat16),
            jax.ShapeDtypeStruct((depth, total), jnp.bfloat16),
            jax.ShapeDtypeStruct((count, total), jnp.float32),
            jax.ShapeDtypeStruct((count, total // 2), jnp.bfloat16),
        ],
        scratch_shapes=[pltpu.SemaphoreType.DMA((len(x_copies) + len(w_copies),))],
        compiler_params=pltpu.CompilerParams(vmem_limit_bytes=VMEM_BYTES),
        cost_estimate=pl.CostEstimate(flops=2 * count * depth * total, bytes_accessed=4 * (count * depth + depth * total + count * total), transcendentals=2 * count * total),
        name="layer",
    )(columns, bias_row.reshape(1, total), *x_sources, *w_sources)


def stage_lists():
    low = [("narrow", bit) for bit in high_bits("narrow")]
    wide = [("wide", bit) for bit in high_bits("wide")]
    return (low + wide, low + wide[::-1])


def local_block(wide, narrow):
    return (wide // 2) * (lax.axis_size("narrow") // 2) + narrow // 2


def turn(flips, axis, bit):
    return [(fw ^ (bit if axis == "wide" else 0), fn ^ (bit if axis == "narrow" else 0)) for fw, fn in flips]


class Gather:
    def __init__(self, own):
        self.half = own.shape[0] // 2
        self.own = own
        self.lists = stage_lists()
        self.rounds = len(self.lists[0])
        self.shared = len(high_bits("narrow"))
        self.first = [own]
        self.flips = [(0, 0)]
        self.held = None
        self.sources, self.copies, self.columns = [], [], []

    def round(self, number):
        wide, narrow = lax.axis_index("wide"), lax.axis_index("narrow")
        if number < self.shared:
            axis, bit = self.lists[0][number]
            self.first = self.first + [swap(part, axis, bit) for part in self.first]
            self.flips = self.flips + turn(self.flips, axis, bit)
            return self.first[-1]
        if self.held is None:
            self.held = [
                jnp.stack([part[n * self.half : (n + 1) * self.half] for part in self.first]) for n in range(2)
            ]
            self.turns = [self.flips, self.flips]
        results = []
        for n, stages in enumerate(self.lists):
            axis, bit = stages[number]
            got = swap(self.held[n], axis, bit)
            turned = turn(self.turns[n], axis, bit)
            if number == self.rounds - 1:
                for source, flips in ((self.held[n], self.turns[n]), (got, turned)):
                    for piece, (fw, fn) in enumerate(flips):
                        self.copies.append((len(self.sources), piece, n * self.half))
                        self.columns.append(local_block(wide ^ fw, narrow ^ fn))
                    self.sources.append(source)
            else:
                self.held[n] = jnp.concatenate([self.held[n], got])
            self.turns[n] = self.turns[n] + turned
            results.append(got)
        return results

    def result(self):
        return self.sources, self.copies, jnp.stack(self.columns).astype(jnp.int32)


def halves(x, outer, bit_value):
    rest = x.shape[-1] // (2 * outer)
    parts = [
        lax.dynamic_slice_in_dim(x, number * 2 * rest + bit_value * rest, rest, x.ndim - 1)
        for number in range(outer)
    ]
    return parts[0] if outer == 1 else jnp.concatenate(parts, axis=-1)


def scatter_weight(inputs, d_project):
    depth = inputs.shape[1]
    half = depth // 2
    results = []
    for number, stages in enumerate(stage_lists()):
        rows = inputs[:, number * half : (number + 1) * half]
        order = [("wide", bit) for bit in high_bits("wide")[::-1]] + [("narrow", bit) for bit in high_bits("narrow")[::-1]]
        left = list(order)
        total = None
        for axis, bit in stages[::-1]:
            at = left.index((axis, bit))
            outer = 1 << at
            left.pop(at)
            mine = side(axis, bit)
            if total is None:
                away = lax.dot_general(
                    rows,
                    halves(d_project, outer, 1 - mine),
                    (((0,), (0,)), ((), ())),
                    preferred_element_type=jnp.float32,
                ).astype(jnp.bfloat16)
                got = swap(away, axis, bit)
                total = (
                    lax.dot_general(
                        rows,
                        halves(d_project, outer, mine),
                        (((0,), (0,)), ((), ())),
                        preferred_element_type=jnp.float32,
                    )
                    + got.astype(jnp.float32)
                )
            else:
                got = swap(halves(total, outer, 1 - mine).astype(jnp.bfloat16), axis, bit)
                total = halves(total, outer, mine) + got.astype(jnp.float32)
        results.append(total)
    return jnp.concatenate(results)


def own_rows(x, count, back=False):
    wide, narrow = lax.axis_size("wide"), lax.axis_size("narrow")
    mine = (side("wide", 1), side("narrow", 1))
    if back:
        x = x.reshape(2, 2, wide // 4, narrow // 2, count, x.shape[1])
        x = jnp.where(mine[0] == 1, x[::-1], x)
        x = jnp.where(mine[1] == 1, x[:, ::-1], x)
        return x.transpose(2, 0, 3, 1, 4, 5).reshape(-1, x.shape[5])
    x = x.reshape(wide // 4, 2, narrow // 2, 2, count, x.shape[1]).transpose(1, 3, 0, 2, 4, 5)
    x = jnp.where(mine[0] == 1, x[::-1], x)
    x = jnp.where(mine[1] == 1, x[:, ::-1], x)
    return x.reshape(-1, x.shape[5])


def swap_blocks(x, axis, by):
    size = x.shape[axis] // 4
    return jnp.concatenate(
        [lax.slice_in_dim(x, (i ^ by) * size, ((i ^ by) + 1) * size, axis=axis) for i in range(4)], axis=axis
    )


def highway_back(carried, project, d_output):
    width = carried.shape[1]
    linear = project[:, :width]
    gating = jax.nn.sigmoid(project[:, width:])
    sigmoid_at = jax.nn.sigmoid(linear)
    d_linear = d_output * (1.0 - gating) * sigmoid_at * (1.0 + linear * (1.0 - sigmoid_at))
    d_gating = d_output * (carried.astype(jnp.float32) - linear * sigmoid_at) * gating * (1.0 - gating)
    d_project = jnp.concatenate([d_linear, d_gating], axis=1).astype(jnp.bfloat16)
    return (d_project, gating * d_output)


def sum_all(x):
    stages = [("wide", 1)]
    stages += [("wide", bit) for bit in high_bits("wide")]
    stages += [("narrow", 1)] + [("narrow", bit) for bit in high_bits("narrow")]
    for axis, bit in stages:
        rows = x.shape[0] // 2
        mine = side(axis, bit)
        away = lax.dynamic_slice_in_dim(x, (1 - mine) * rows, rows, 0).astype(jnp.bfloat16)
        x = lax.dynamic_slice_in_dim(x, mine * rows, rows, 0) + swap(away, axis, bit).astype(jnp.float32)
    for axis, bit in stages[::-1]:
        got = swap(x, axis, bit)
        mine = side(axis, bit)
        x = jnp.where(mine == 0, jnp.concatenate([x, got]), jnp.concatenate([got, x]))
    return x


def local(
    char_ids,
    bank_order,
    char_table,
    conv_w1,
    conv_w2,
    conv_w3,
    conv_w4,
    conv_w5,
    conv_w6,
    conv_w7,
    conv_bias,
    highway_w1,
    highway_b1,
    highway_w2,
    highway_b2,
    proj_weight,
    proj_bias,
    cotangent,
):
    feature_count = conv_bias.shape[0]
    tokens, chars = char_ids.shape
    vocab_count, emb_width = char_table.shape
    layout = bank_layout(feature_count // 64)
    weights = (conv_w1, conv_w2, conv_w3, conv_w4, conv_w5, conv_w6, conv_w7)
    wide_size, narrow_size = lax.axis_size("wide"), lax.axis_size("narrow")
    wide, narrow = lax.axis_index("wide"), lax.axis_index("narrow")
    width = highway_w1.shape[1]
    out_part = proj_weight.shape[1]
    members = 4
    blocks = wide_size * narrow_size // members
    own_width = feature_count // members
    mine_wide, mine_narrow = side("wide", 1), side("narrow", 1)

    gather_one = Gather(own_rows(highway_w1, width))
    gather_two = Gather(own_rows(highway_w2, width))

    out_rows = own_rows(proj_weight, width).T
    bias_column = jnp.pad(proj_bias[:, None], ((0, 0), (0, LANES - 1)))
    traded = group_trade(
        [
            jnp.concatenate([out_rows[:, m * own_width : (m + 1) * own_width], bias_column], axis=1)
            for m in range(members)
        ]
    )
    bundle = jnp.concatenate(traded)
    extra = jnp.pad(jnp.stack([highway_b1, highway_b2]), ((0, bundle.shape[0] - 2), (0, LANES - width)))
    bundle = jnp.concatenate([bundle, extra], axis=1)[None]
    flips = [(0, 0)]
    for axis, bit in stage_lists()[0]:
        bundle = jnp.concatenate([bundle, swap(bundle, axis, bit)])
        flips = flips + [(fw ^ (bit if axis == "wide" else 0), fn ^ (bit if axis == "narrow" else 0)) for fw, fn in flips]
    block_at = jnp.stack([local_block(wide ^ fw, narrow ^ fn) for fw, fn in flips]).astype(jnp.int32)
    to_block = (block_at[None, :] == lax.iota(jnp.int32, blocks)[:, None]).astype(jnp.float32)
    biases = bundle[:, :2, own_width + LANES : own_width + LANES + width].astype(jnp.float32)
    biases = jnp.sum(to_block[:, :, None, None] * biases[None], axis=1).transpose(1, 0, 2).reshape(2, blocks * width)
    member_wide = jnp.array([0, 0, 1, 1], jnp.int32)
    member_narrow = jnp.array([0, 1, 0, 1], jnp.int32)
    flip_wide = jnp.array([fw for fw, fn in flips], jnp.int32)
    flip_narrow = jnp.array([fn for fw, fn in flips], jnp.int32)
    device_at = (wide ^ (flip_wide[:, None] | member_wide[None, :])) * narrow_size + (
        narrow ^ (flip_narrow[:, None] | member_narrow[None, :])
    )
    column_at = (device_at[:, :, None] * out_part + lax.iota(jnp.int32, out_part)[None, None, :]).reshape(-1)
    out_count = column_at.shape[0]
    out_order = (column_at[:, None] == lax.iota(jnp.int32, out_count)[None, :]).astype(jnp.bfloat16)
    out_turned = bundle[:, :, :own_width].reshape(out_count, own_width)
    out_bias = jnp.sum(
        out_order.astype(jnp.float32) * bundle[:, :, own_width].reshape(out_count, 1).astype(jnp.float32), axis=0
    )
    out_weight = jnp.einsum("jn,jf->nf", out_order, out_turned, preferred_element_type=jnp.float32).astype(jnp.bfloat16)
    given = jnp.concatenate(group_all(cotangent))
    given_turned = jnp.einsum("tn,jn->tj", given, out_order, preferred_element_type=jnp.float32).astype(jnp.bfloat16)

    places = column_places(layout, chars)
    filters = join_filters(weights, layout)
    places_row = jnp.array(places, jnp.float32)
    aux = jnp.pad(
        jnp.stack([conv_bias.astype(jnp.float32) - jnp.log(places_row), places_row]), ((0, 6), (0, 0))
    )
    padded = -(-vocab_count // LANES) * LANES
    table = jnp.pad(
        jnp.tile(char_table, (1, WIDEST)), ((0, padded - vocab_count), (0, LANES - WIDEST * emb_width))
    )
    trips = jnp.array(
        [max(places[start : start + BLOCK]) for start in range(0, feature_count, BLOCK)], jnp.int32
    )
    windows = make_windows(char_ids, table)
    exps, natural, before, inverse = conv_forward(windows, filters, aux, trips, min(places))
    source = feature_columns(bank_order, layout, feature_count).reshape(
        wide_size // 4, 2, narrow_size // 2, 2, width
    )
    source = source.transpose(1, 3, 0, 2, 4)
    source = jnp.where(mine_wide == 1, source[::-1], source)
    source = jnp.where(mine_narrow == 1, source[:, ::-1], source).reshape(-1)
    shuffle = (lax.iota(jnp.int32, feature_count)[:, None] == source[None, :]).astype(jnp.bfloat16)
    features = jnp.dot(natural, shuffle, preferred_element_type=jnp.float32).astype(jnp.bfloat16)
    for number in range(gather_one.rounds):
        gather_one.round(number)
    for number in range(gather_two.rounds):
        gather_two.round(number)
    copies = [
        (by, 0, (m ^ by) * own_width, tokens, own_width, by * tokens, m * own_width)
        for by in range(members)
        for m in range(members)
    ]
    shape = (members * tokens, feature_count, 2 * own_width)
    features, weight_one, proj_one, carried_two = layer(
        group_all(features), copies, gather_one.result(), biases[0], shape
    )
    carried_one = features[:, :own_width]
    copies = [
        (by, (m ^ by) * tokens, 0, tokens, own_width, m * tokens, by * own_width)
        for by in range(members)
        for m in range(members)
    ]
    input_two, weight_two, proj_two, input_out = layer(
        group_all(carried_two), copies, gather_two.result(), biases[1], shape
    )

    encoded = jnp.einsum("tf,nf->tn", input_out, out_weight, preferred_element_type=jnp.float32)
    encoded = encoded[: 2 * tokens] + swap(encoded[2 * tokens :].astype(jnp.bfloat16), "wide", 1).astype(jnp.float32)
    encoded = encoded[:tokens] + swap(encoded[tokens:].astype(jnp.bfloat16), "narrow", 1).astype(jnp.float32)
    encoded = (encoded + out_bias).astype(jnp.bfloat16)

    d_hidden_two = jnp.dot(given_turned, out_turned, preferred_element_type=jnp.float32)
    d_project, through = highway_back(carried_two, proj_two, d_hidden_two)
    bias_two = jnp.sum(d_project.astype(jnp.float32), axis=0)
    d_inputs = lax.dot_general(
        d_project, weight_two, (((1,), (1,)), ((), ())), preferred_element_type=jnp.float32
    )
    d_inputs = d_inputs[:, : 2 * own_width] + swap(
        d_inputs[:, 2 * own_width :].astype(jnp.bfloat16), "wide", 1
    ).astype(jnp.float32).reshape(2, 2 * tokens, 2 * own_width)[::-1].reshape(members * tokens, 2 * own_width)
    got = swap(d_inputs[:, own_width:].astype(jnp.bfloat16), "narrow", 1)
    got = swap_blocks(got, 0, 1)
    d_hidden_one = d_inputs[:, :own_width] + got.astype(jnp.float32) + through
    grad_two_w = scatter_weight(input_two, d_project)

    grad_out = jnp.einsum("tn,tf->nf", given_turned, input_out, preferred_element_type=jnp.float32)
    grad_out = grad_out.reshape(blocks, members * out_part, own_width)
    for axis, bit in stage_lists()[0][::-1]:
        count = grad_out.shape[0] // 2
        grad_out = grad_out[:count] + swap(grad_out[count:].astype(jnp.bfloat16), axis, bit).astype(jnp.float32)
    grad_out = grad_out.reshape(members, out_part, own_width)
    grad_out = group_trade([grad_out[m] for m in range(members)])
    grad_out = jnp.concatenate(grad_out, axis=1)

    d_project, through = highway_back(carried_one, proj_one, d_hidden_one)
    bias_one = jnp.sum(d_project.astype(jnp.float32), axis=0)
    d_inputs = lax.dot_general(
        d_project, weight_one, (((1,), (1,)), ((), ())), preferred_element_type=jnp.float32
    )
    d_inputs = jnp.concatenate([d_inputs[:, :own_width] + through, d_inputs[:, own_width:]], axis=1)
    got = swap(d_inputs[2 * tokens :].astype(jnp.bfloat16), "wide", 1)
    d_inputs = d_inputs[: 2 * tokens] + swap_blocks(got, 1, 2).astype(jnp.float32)
    got = swap(d_inputs[tokens:].astype(jnp.bfloat16), "narrow", 1)
    d_features = (d_inputs[:tokens] + swap_blocks(got, 1, 1).astype(jnp.float32)).astype(jnp.bfloat16)
    grad_one_w = scatter_weight(features, d_project)
    d_natural = lax.dot_general(
        d_features, shuffle, (((1,), (1,)), ((), ())), preferred_element_type=jnp.float32
    ).astype(jnp.bfloat16)

    ids_across = jnp.pad(char_ids.T, ((0, -chars % 8), (0, 0)))
    d_filters, d_bias, d_table = conv_backward(
        exps, before, inverse, d_natural, windows, filters, ids_across, trips, min(places), padded
    )
    span = WIDEST * emb_width
    d_table = d_table[:vocab_count, :span] + d_table[:vocab_count, LANES : LANES + span]
    d_table = jnp.sum(d_table.reshape(vocab_count, WIDEST, emb_width), axis=1)

    member = mine_wide * 2 + mine_narrow
    spread = []
    for part in (bias_one, bias_two):
        part = part.reshape(1, -1)
        spread.append(
            jnp.where(lax.iota(jnp.int32, members)[:, None] == member, part, 0.0).reshape(-1, LANES)
        )
    pieces = [
        d_filters[:span].reshape(span, -1, LANES).transpose(1, 0, 2).reshape(-1, LANES),
        d_bias[0].reshape(-1, LANES),
        jnp.pad(d_table.reshape(-1), (0, -d_table.size % LANES)).reshape(-1, LANES),
        *spread,
        jnp.sum(cotangent.astype(jnp.float32), axis=0).reshape(-1, LANES),
    ]
    ends = []
    for piece in pieces:
        ends.append((ends[-1] if ends else 0) + piece.shape[0])
    unit = 8 * wide_size * narrow_size
    pieces.append(jnp.zeros((-ends[-1] % unit, LANES), jnp.float32))
    summed = sum_all(jnp.concatenate(pieces))
    got = [summed[end - piece.shape[0] : end] for end, piece in zip(ends, pieces)]
    d_filters = got[0].reshape(-1, span, LANES).transpose(1, 0, 2).reshape(span, feature_count)
    d_bias = got[1].reshape(-1)
    d_table = got[2].reshape(-1)[: vocab_count * emb_width].reshape(vocab_count, emb_width)
    own_block = member * blocks + local_block(wide, narrow)
    own_one, own_two = (
        lax.dynamic_slice_in_dim(part.reshape(-1), own_block * width, width, 0) for part in got[3:5]
    )
    own_out = lax.dynamic_slice_in_dim(
        got[5].reshape(-1), (wide * narrow_size + narrow) * out_part, out_part, 0
    )
    grad_weights = []
    for number, (kernel, leading, filters_here, start) in enumerate(layout):
        grad_weights.append(d_filters[: kernel * emb_width, start : start + filters_here])
    grad_weights[6:] = [jnp.concatenate(grad_weights[6:], axis=1)]
    return (
        encoded,
        d_table,
        *grad_weights,
        d_bias,
        own_rows(grad_one_w, width, True),
        own_one,
        own_rows(grad_two_w, width, True),
        own_two,
        own_rows(grad_out.T, width, True),
        own_out,
    )


def solution(mesh):
    placed = (
        P(("wide", "narrow"), None),
        P(),
        P(),
        P(),
        P(),
        P(),
        P(),
        P(),
        P(),
        P(),
        P(),
        P(None, ("wide", "narrow")),
        P(("wide", "narrow")),
        P(None, ("wide", "narrow")),
        P(("wide", "narrow")),
        P(None, ("wide", "narrow")),
        P(("wide", "narrow")),
        P(("wide", "narrow"), None),
    )
    return jax.shard_map(
        local,
        mesh=mesh,
        in_specs=placed,
        out_specs=(
            P(("wide", "narrow"), None),
            P(),
            P(),
            P(),
            P(),
            P(),
            P(),
            P(),
            P(),
            P(),
            P(None, ("wide", "narrow")),
            P(("wide", "narrow")),
            P(None, ("wide", "narrow")),
            P(("wide", "narrow")),
            P(None, ("wide", "narrow")),
            P(("wide", "narrow")),
        ),
        check_vma=False,
    )
```

time: 923 us -> 491 us (0.53)
  waiting for transfers between devices: 424 us -> 190 us
  blocking collectives: 229 us -> 0 us
  starting transfers between devices: 0.4 us -> 53 us
  matrix products: 93.5 us -> 53.5 us
  other arithmetic: 8.96 us -> 32.4 us
  between operations: 14.7 us -> 3.03 us
  Pallas kernels: 105 us -> 115 us
    ppermute x0 -> x61, waiting for transfers between devices: none -> 190 us  [swap(): lax.ppermute(x, axis, [(i, i ^ bit) for i in range(lax.axis_size(axis))])]
    reduce_scatter x4 -> x0, waiting for transfers between devices: 184 us -> none  [local(): part = lax.psum_scatter(part, axis, scatter_dimension=1, tiled=True)]
    all_gather x2 -> x0, blocking collectives: 146 us -> none  [local(): lax.all_gather(part, axes, axis=0, tiled=True)]
    all_gather x3 -> x0, waiting for transfers between devices: 111 us -> none  [local(): lax.all_gather(part, axes, axis=1, tiled=True)]
    unnamed x12 -> x0, waiting for transfers between devices: 88.8 us -> none
    ppermute x0 -> x61, starting transfers between devices: none -> 53 us  [swap(): lax.ppermute(x, axis, [(i, i ^ bit) for i in range(lax.axis_size(axis))])]
    psum x1 -> x0, blocking collectives: 42.5 us -> none  [local(): lax.psum((d_filters, d_bias[0], d_table, grad_one_b, grad_two_b, grad_out...]
    dot_general x9 -> x15, matrix products: 88.9 us -> 47.9 us  [the longest x4 10 us: scatter_weight(): lax.dot_general(rows, halves(d_project, outer, mine), (((0,), (0,)), ((),...]
  transfers between devices with their start and end apart: 10 -> 61, of which waited for: 8 -> 28; matrix products, arithmetic and copies ran while one was open for 14% -> 23% of each run, Pallas kernels for 12% -> 21%
where the time goes in v2:
time: 491 us; the launch traced here: 486 us
  waiting for transfers between devices  190 us (39%)
  Pallas kernels  115 us (23%)
  matrix products  53.5 us (11%)
  starting transfers between devices  53 us (11%)
  local copies, waits for them, and re-layouts  39.4 us (8%)
  other arithmetic  32.4 us (7%)
    ppermute x61, waiting for transfers between devices, swap(): lax.ppermute(x, axis, [(i, i ^ bit) for i in range(lax.axis_size(axis))])  190 us
    ppermute x61, starting transfers between devices, swap(): lax.ppermute(x, axis, [(i, i ^ bit) for i in range(lax.axis_size(axis))])  53 us
    pallas_call x1, Pallas kernels, conv_forward(): pl.pallas_call(functools.partial(forward_kernel, low_places), grid_spec=p...  41.1 us
    pallas_call x1, Pallas kernels, conv_backward(): pl.pallas_call(functools.partial(backward_kernel, chars, low_places), gri...  39.1 us
    pallas_call x2, Pallas kernels, layer(): pl.pallas_call(functools.partial(layer_kernel, tuple(x_copies), tuple(w_c...  26.7 us
    dot_general x4, matrix products, scatter_weight(): lax.dot_general(rows, halves(d_project, outer, mine), (((0,), (0,)), ((),...  10 us
  transfers between devices with their start and end apart: 61, of which 28 were waited for; matrix products, arithmetic and copies ran while one was open for 23% of the time, Pallas kernels for 21%

profile of v2, /device:TPU:0, one launch (start us, length us, event | category | flops | bytes accessed | tf_op | source)
XLA Modules:
  0.0 486.2 jit_solution(6551098364896166741)
XLA Ops:
  2.7 3.1 collective-permute-start
  7.4 2.9 collective-permute-start.10
  13.5 8.2 %make_windows.1.win_ref = bf16[50,256,128]{2,1,0:T(8,128)(2,1)} custom-call(s32[256,50]{1,0:T(8,128)} %copy.152.ids_ref, bf16[384,128]{1,0:T(8,128)(2,1)} %pad.57.table_ref), custom_call_target="tpu_custom_call" | custom-call | tf_op jit(solution)/shard_map/make_windows/pallas_call | solution.py:43
  22.7 41.1 %conv_forward.1 = (bf16[8,50,256,256]{3,2,1,0:T(8,128)(2,1)}, bf16[256,2048]{1,0:T(8,128)(2,1)}, f32[256,2048]{1,0:T(8,128)}, f32[256,2048]{1,0:T(8,128)}) custom-call(s32[8]{0:T(128)} %constant.451.clone.trip_ref, bf16[50,256,128]{2,1,0:T(8,128)(2,1)} %make_windows.1.win_ref, bf16[128,2048]{1,0:T(8,128)(2,1)} %concatenate.138.weight_ref, ...), custom_call_target="tpu_custom_call" | custom-call | flops 6710886400 | bytes 52428800 | tf_op jit(solution)/shard_map/conv_forward/pallas_call | solution.py:141
  63.9 5.6 %fusion.7.refs_0_ = bf16[256,2048]{1,0:T(8,128)(2,1)} fusion(bf16[256,2048]{1,0:T(8,128)(2,1)} %get-tuple-element.31, s32[2048]{0:T(1024)S(1)} %bitcast.179), kind=kOutput, calls=%fused_computation.41 | convolution fusion | flops 2152202240 | bytes 2105344 | tf_op jit(solution)/shard_map/dot_general | solution.py:656
  75.6 22.5 %collective-permute-done.4 = bf16[1,64,768]{2,0,1:T(2,128)(2,1)S(1)} collective-permute-done((bf16[1,64,768]{2,0,1:T(2,128)(2,1)S(1)}, bf16[1,64,768]{2,0,1:T(2,128)(2,1)S(1)}, u32[]{:S(2)}, u32[]{:S(2)}) %collective-permute-start.4) | collective-permute-done | bytes 98336 | tf_op jit(solution)/shard_map/ppermute | solution.py:302
  108.7 25.4 %collective-permute-done.6 = bf16[4,64,768]{2,0,1:T(4,128)(2,1)S(1)} collective-permute-done((bf16[4,64,768]{2,0,1:T(4,128)(2,1)S(1)}, bf16[4,64,768]{2,0,1:T(4,128)(2,1)S(1)}, u32[]{:S(2)}, u32[]{:S(2)}) %collective-permute-start.6) | collective-permute-done | bytes 393248 | tf_op jit(solution)/shard_map/ppermute | solution.py:302
  134.1 3.4 collective-permute-start.18
  138.2 13.3 %layer.2 = (bf16[1024,2048]{1,0:T(8,128)(2,1)}, bf16[2048,1024]{1,0:T(8,128)(2,1)}, f32[1024,1024]{1,0:T(8,128)}, bf16[1024,512]{1,0:T(8,128)(2,1)}) custom-call(s32[16]{0:T(128)} %stack.125.at_ref, f32[1,1024]{1,0:T(1,128)} %get-tuple-element.184.bias_ref, bf16[256,2048]{1,0:T(8,128)(2,1)} %fusion.7.refs_0_, ...), custom_call_target="tpu_custom_call" | custom-call | flops 4294967296 | bytes 20971520 | tf_op jit(solution)/shard_map/layer/pallas_call | solution.py:389
  151.7 6.9 %collective-permute-done.18 = bf16[2048,128]{1,0:T(8,128)(2,1)S(1)} collective-permute-done((bf16[2048,128]{1,0:T(8,128)(2,1)S(1)}, bf16[2048,128]{1,0:T(8,128)(2,1)S(1)}, u32[]{:S(2)}, u32[]{:S(2)}) %collective-permute-start.18) | collective-permute-done | bytes 524320 | tf_op jit(solution)/shard_map/ppermute | solution.py:302
  162.8 9.5 %collective-permute-done.21 = bf16[2,1024,128]{2,1,0:T(8,128)(2,1)} collective-permute-done((bf16[2,1024,128]{2,1,0:T(8,128)(2,1)S(1)}, bf16[2,1024,128]{2,1,0:T(8,128)(2,1)}, u32[]{:S(2)}, u32[]{:S(2)}) %collective-permute-start.21) | collective-permute-done | bytes 524320 | tf_op jit(solution)/shard_map/ppermute | solution.py:302
  181.3 5.3 %collective-permute-done.25 = bf16[256,512]{1,0:T(8,128)(2,1)} collective-permute-done((bf16[256,512]{1,0:T(8,128)(2,1)S(1)}, bf16[256,512]{1,0:T(8,128)(2,1)}, u32[]{:S(2)}, u32[]{:S(2)}) %collective-permute-start.25) | collective-permute-done | bytes 262176 | tf_op jit(solution)/shard_map/ppermute | solution.py:302
  188.4 2.9 convolution_convert_fusion
  193.8 3.9 collective-permute-done.22.refs_7_
  197.7 3.8 collective-permute-done.20.refs_5_
  201.5 13.4 %layer.3 = (bf16[1024,2048]{1,0:T(8,128)(2,1)}, bf16[2048,1024]{1,0:T(8,128)(2,1)}, f32[1024,1024]{1,0:T(8,128)}, bf16[1024,512]{1,0:T(8,128)(2,1)}) custom-call(s32[16]{0:T(128)} %stack.125.at_ref, f32[1,1024]{1,0:T(1,128)} %get-tuple-element.185.bias_ref, bf16[1024,512]{1,0:T(8,128)(2,1)} %get-tuple-element.32.refs_0_, ...), custom_call_target="tpu_custom_call" | custom-call | flops 4294967296 | bytes 20971520 | tf_op jit(solution)/shard_map/layer/pallas_call | solution.py:389
  219.2 2.6 fusion.49
  223.2 6.4 %multiply_convert_fusion.3 = (bf16[1024,512]{1,0:T(8,128)(2,1)S(1)}, bf16[1024,512]{1,0:T(8,128)(2,1)S(1)}, f32[1024,512]{1,0:T(8,128)}) fusion(f32[1024,1024]{1,0:T(8,128)} %get-tuple-element.37, bf16[1024,512]{1,0:T(8,128)(2,1)} %get-tuple-element.32.refs_0_, bf16[1024,512]{1,0:T(8,128)(2,1)} %convolution_convert_fusion, bf16[512,512]{1,0:T(8,128)(2,1)} %bitcast.166), kind=kOutput, calls=%fused_computation.59 | convolution fusion | flops 547880960 | bytes 11010048 | tf_op jit(solution)/shard_map/dot_general | solution.py:685
  229.6 2.3 fusion.41
  232.4 4.6 fusion.48
  241.6 3.1 collective-permute-done.55
  245.2 4.8 collective-permute-done.56
  259.6 4.0 rev.53
  263.6 4.6 slice_add_fusion
  270.2 2.6 convert_add_fusion.1
  274.0 7.9 %collective-permute-done.51 = bf16[1024,512]{1,0:T(8,128)(2,1)} collective-permute-done((bf16[1024,512]{1,0:T(8,128)(2,1)}, bf16[1024,512]{1,0:T(8,128)(2,1)}, u32[]{:S(2)}, u32[]{:S(2)}) %collective-permute-start.51) | collective-permute-done | bytes 1048608 | tf_op jit(solution)/shard_map/ppermute | solution.py:302
  281.9 2.7 convert_add_fusion
  286.3 7.0 %collective-permute-done.29 = bf16[1024,512]{1,0:T(8,128)(2,1)S(1)} collective-permute-done((bf16[1024,512]{1,0:T(8,128)(2,1)S(1)}, bf16[1024,512]{1,0:T(8,128)(2,1)S(1)}, u32[]{:S(2)}, u32[]{:S(2)}) %collective-permute-start.29) | collective-permute-done | bytes 1048608 | tf_op jit(solution)/shard_map/ppermute | solution.py:302
  295.3 2.6 multiply_convert_fusion
  297.9 6.6 %fusion.47 = f32[1024,2048]{1,0:T(8,128)S(1)} fusion(bf16[2048,1024]{1,0:T(8,128)(2,1)} %get-tuple-element.41, bf16[1024,512]{1,0:T(8,128)(2,1)S(1)} %multiply_convert_fusion, bf16[1024,512]{1,0:T(8,128)(2,1)S(1)} %get-tuple-element.142), kind=kOutput, calls=%fused_computation.87 | convolution fusion | flops 4299161600 | bytes 14680064 | tf_op jit(solution)/shard_map/dot_general | solution.py:710
  306.9 3.0 collective-permute-start.53
  311.6 15.7 %collective-permute-done.50 = bf16[1024,128]{1,0:T(8,128)(2,1)S(1)} collective-permute-done((bf16[1024,128]{1,0:T(8,128)(2,1)S(1)}, bf16[1024,128]{1,0:T(8,128)(2,1)S(1)}, u32[]{:S(2)}, u32[]{:S(2)}) %collective-permute-start.50) | collective-permute-done | bytes 262176 | tf_op jit(solution)/shard_map/ppermute | solution.py:302
  327.4 5.5 %collective-permute-done.53 = bf16[1024,128]{1,0:T(8,128)(2,1)S(1)} collective-permute-done((bf16[1024,128]{1,0:T(8,128)(2,1)S(1)}, bf16[1024,128]{1,0:T(8,128)(2,1)S(1)}, u32[]{:S(2)}, u32[]{:S(2)}) %collective-permute-start.53) | collective-permute-done | bytes 262176 | tf_op jit(solution)/shard_map/ppermute | solution.py:302
  338.4 2.3 fusion.38
  343.2 16.3 %collective-permute-done.42 = bf16[1024,512]{1,0:T(8,128)(2,1)S(1)} collective-permute-done((bf16[1024,512]{1,0:T(8,128)(2,1)S(1)}, bf16[1024,512]{1,0:T(8,128)(2,1)S(1)}, u32[]{:S(2)}, u32[]{:S(2)}) %collective-permute-start.42) | collective-permute-done | bytes 1048608 | tf_op jit(solution)/shard_map/ppermute | solution.py:302
  363.4 4.6 fusion.8.d_ref
  368.0 39.1 %conv_backward.1 = (f32[128,2048]{1,0:T(8,128)}, f32[8,2048]{1,0:T(8,128)}, f32[384,256]{1,0:T(8,128)}) custom-call(s32[8]{0:T(128)} %constant.451.clone.trip_ref, bf16[8,50,256,256]{3,2,1,0:T(8,128)(2,1)} %get-tuple-element.34.e_ref, f32[256,2048]{1,0:T(8,128)} %get-tuple-element.35.x_ref, f32[256,2048]{1,0:T(8,128)} %get-tuple-element.36.inv_ref, ...), custom_call_target="tpu_custom_call" | custom-call | flops 13421772800 | bytes 52428800 | tf_op jit(solution)/shard_map/conv_backward/pallas_call | solution.py:231
  412.4 4.1 concatenate.150
  416.7 3.5 convert_add_fusion.2
  423.6 3.4 collective-permute-done.33
  428.4 7.7 %collective-permute-done.34 = bf16[256,128]{1,0:T(8,128)(2,1)S(1)} collective-permute-done((bf16[256,128]{1,0:T(8,128)(2,1)S(1)}, bf16[256,128]{1,0:T(8,128)(2,1)S(1)}, u32[]{:S(2)}, u32[]{:S(2)}) %collective-permute-start.34) | collective-permute-done | bytes 65568 | tf_op jit(solution)/shard_map/ppermute | solution.py:302
  436.6 6.0 %collective-permute-done.35 = bf16[128,128]{1,0:T(8,128)(2,1)S(1)} collective-permute-done((bf16[128,128]{1,0:T(8,128)(2,1)S(1)}, bf16[128,128]{1,0:T(8,128)(2,1)S(1)}, u32[]{:S(2)}, u32[]{:S(2)}) %collective-permute-start.35) | collective-permute-done | bytes 32800 | tf_op jit(solution)/shard_map/ppermute | solution.py:302
  442.7 3.0 collective-permute-start.47
  445.7 7.4 %collective-permute-done.36 = bf16[64,128]{1,0:T(8,128)(2,1)S(1)} collective-permute-done((bf16[64,128]{1,0:T(8,128)(2,1)S(1)}, bf16[64,128]{1,0:T(8,128)(2,1)S(1)}, u32[]{:S(2)}, u32[]{:S(2)}) %collective-permute-start.36) | collective-permute-done | bytes 16416 | tf_op jit(solution)/shard_map/ppermute | solution.py:302
  453.2 6.1 %collective-permute-done.37 = f32[64,128]{1,0:T(8,128)S(1)} collective-permute-done((f32[64,128]{1,0:T(8,128)S(1)}, f32[64,128]{1,0:T(8,128)S(1)}, u32[]{:S(2)}, u32[]{:S(2)}) %collective-permute-start.37) | collective-permute-done | bytes 32800 | tf_op jit(solution)/shard_map/ppermute | solution.py:302
  459.5 4.2 collective-permute-done.38
  464.8 3.9 collective-permute-done.39
  470.6 4.6 collective-permute-done.40
  (364 shorter events, 109.8 us)
Async XLA Ops:
  2.7 70.3 %collective-permute-start = (bf16[16,640]{1,0:T(8,128)(2,1)S(1)}, bf16[16,640]{1,0:T(8,128)(2,1)S(1)}, u32[]{:S(2)}, u32[]{:S(2)}) collective-permute-start(bf16[16,640]{1,0:T(8,128)(2,1)S(1)} %get-tuple-element.186), channel_id=1, source_target_pairs={{0,1},{1,0},{2,3},{3,2},{4,5},{5,4},{6,7},{7,6},{8,9},{9,8},{10,11... | collective-permute-start | bytes 61448 | tf_op jit(solution)/shard_map/ppermute | solution.py:302
  5.8 67.5 %collective-permute-start.1 = (bf16[16,640]{1,0:T(8,128)(2,1)S(1)}, bf16[16,640]{1,0:T(8,128)(2,1)S(1)}, u32[]{:S(2)}, u32[]{:S(2)}) collective-permute-start(bf16[16,640]{1,0:T(8,128)(2,1)S(1)} %get-tuple-element.187), channel_id=1, source_target_pairs={{0,4},{4,0},{8,12},{12,8},{16,20},{20,16},{24,28},{28,24},{1,5},{5... | collective-permute-start | bytes 61448 | tf_op jit(solution)/shard_map/ppermute | solution.py:302
  5.8 65.4 %collective-permute-start.2 = (bf16[16,640]{1,0:T(8,128)(2,1)S(1)}, bf16[16,640]{1,0:T(8,128)(2,1)S(1)}, u32[]{:S(2)}, u32[]{:S(2)}) collective-permute-start(bf16[16,640]{1,0:T(8,128)(2,1)S(1)} %get-tuple-element.188), channel_id=1, source_target_pairs={{0,1},{1,0},{2,3},{3,2},{4,5},{5,4},{6,7},{7,6},{8,9},{9,8},{10,11... | collective-permute-start | bytes 61448 | tf_op jit(solution)/shard_map/ppermute | solution.py:302
  7.4 63.9 %collective-permute-start.10 = (bf16[2048,128]{1,0:T(8,128)(2,1)S(1)}, bf16[2048,128]{1,0:T(8,128)(2,1)S(1)}, u32[]{:S(2)}, u32[]{:S(2)}) collective-permute-start(bf16[2048,128]{1,0:T(8,128)(2,1)S(1)} %bitcast.155), channel_id=1, source_target_pairs={{0,2},{1,3},{2,0},{3,1},{4,6},{5,7},{6,4},{7,5},{8,10},{9,11},{10,... | collective-permute-start | bytes 1572872 | tf_op jit(solution)/shard_map/ppermute | solution.py:302
  69.5 33.9 %collective-permute-start.7 = (bf16[256,2048]{1,0:T(8,128)(2,1)}, bf16[256,2048]{1,0:T(8,128)(2,1)}, u32[]{:S(2)}, u32[]{:S(2)}) collective-permute-start(bf16[256,2048]{1,0:T(8,128)(2,1)} %fusion.7.refs_0_), channel_id=1, source_target_pairs={{0,1},{1,0},{2,3},{3,2},{4,5},{5,4},{6,7},{7,6},{8,9},{9,8},{10,11... | collective-permute-start | bytes 3145736 | tf_op jit(solution)/shard_map/ppermute | solution.py:302
  71.4 28.7 %collective-permute-start.13 = (bf16[2,1024,128]{2,1,0:T(8,128)(2,1)S(1)}, bf16[2,1024,128]{2,1,0:T(8,128)(2,1)S(1)}, u32[]{:S(2)}, u32[]{:S(2)}) collective-permute-start(bf16[2,1024,128]{2,1,0:T(8,128)(2,1)S(1)} %pad_maximum_fusion.13), channel_id=1, source_target_pairs={{0,16},{4,20},{8,24},{12,28},{16,0},{20,4},{24,8},{28,12},{1,17},{... | collective-permute-start | bytes 1572872 | tf_op jit(solution)/shard_map/ppermute | solution.py:302
  73.0 65.2 %collective-permute-start.8 = (bf16[256,2048]{1,0:T(8,128)(2,1)}, bf16[256,2048]{1,0:T(8,128)(2,1)}, u32[]{:S(2)}, u32[]{:S(2)}) collective-permute-start(bf16[256,2048]{1,0:T(8,128)(2,1)} %fusion.7.refs_0_), channel_id=1, source_target_pairs={{0,4},{4,0},{8,12},{12,8},{16,20},{20,16},{24,28},{28,24},{1,5},{5... | collective-permute-start | bytes 3145736 | tf_op jit(solution)/shard_map/ppermute | solution.py:302
  73.3 27.5 %collective-permute-start.11 = (bf16[2,1024,128]{2,1,0:T(8,128)(2,1)S(1)}, bf16[2,1024,128]{2,1,0:T(8,128)(2,1)S(1)}, u32[]{:S(2)}, u32[]{:S(2)}) collective-permute-start(bf16[2,1024,128]{2,1,0:T(8,128)(2,1)S(1)} %pad_maximum_fusion.12), channel_id=1, source_target_pairs={{0,8},{4,12},{8,0},{12,4},{16,24},{20,28},{24,16},{28,20},{1,9},{5... | collective-permute-start | bytes 1572872 | tf_op jit(solution)/shard_map/ppermute | solution.py:302
  75.0 23.0 %collective-permute-start.4 = (bf16[1,64,768]{2,0,1:T(2,128)(2,1)S(1)}, bf16[1,64,768]{2,0,1:T(2,128)(2,1)S(1)}, u32[]{:S(2)}, u32[]{:S(2)}) collective-permute-start(bf16[1,64,768]{2,0,1:T(2,128)(2,1)S(1)} %copy.150), channel_id=1, source_target_pairs={{0,2},{1,3},{2,0},{3,1},{4,6},{5,7},{6,4},{7,5},{8,10},{9,11},{10,... | collective-permute-start | bytes 294920 | tf_op jit(solution)/shard_map/ppermute | solution.py:302
  98.5 7.9 %collective-permute-start.5 = (bf16[2,64,768]{2,0,1:T(2,128)(2,1)S(1)}, bf16[2,64,768]{2,0,1:T(2,128)(2,1)S(1)}, u32[]{:S(2)}, u32[]{:S(2)}) collective-permute-start(bf16[2,64,768]{2,0,1:T(2,128)(2,1)S(1)} %pad_maximum_fusion.17), channel_id=1, source_target_pairs={{0,8},{4,12},{8,0},{12,4},{16,24},{20,28},{24,16},{28,20},{1,9},{5... | collective-permute-start | bytes 589832 | tf_op jit(solution)/shard_map/ppermute | solution.py:302
  100.2 38.0 %collective-permute-start.14 = (bf16[4,1024,128]{2,1,0:T(8,128)(2,1)S(1)}, bf16[4,1024,128]{2,1,0:T(8,128)(2,1)}, u32[]{:S(2)}, u32[]{:S(2)}) collective-permute-start(bf16[4,1024,128]{2,1,0:T(8,128)(2,1)S(1)} %pad_maximum_fusion.6.refs_6_), channel_id=1, source_target_pairs={{0,8},{4,12},{8,0},{12,4},{16,24},{20,28},{24,16},{28,20},{1,9},{5... | collective-permute-start | bytes 3145736 | tf_op jit(solution)/shard_map/ppermute | solution.py:302
  101.9 36.4 %collective-permute-start.12 = (bf16[4,1024,128]{2,1,0:T(8,128)(2,1)}, bf16[4,1024,128]{2,1,0:T(8,128)(2,1)}, u32[]{:S(2)}, u32[]{:S(2)}) collective-permute-start(bf16[4,1024,128]{2,1,0:T(8,128)(2,1)} %pad_maximum_fusion.5.refs_4_), channel_id=1, source_target_pairs={{0,16},{4,20},{8,24},{12,28},{16,0},{20,4},{24,8},{28,12},{1,17},{... | collective-permute-start | bytes 3145736 | tf_op jit(solution)/shard_map/ppermute | solution.py:302
  103.4 34.8 %collective-permute-start.9 = (bf16[256,2048]{1,0:T(8,128)(2,1)}, bf16[256,2048]{1,0:T(8,128)(2,1)}, u32[]{:S(2)}, u32[]{:S(2)}) collective-permute-start(bf16[256,2048]{1,0:T(8,128)(2,1)} %collective-permute-done.7.refs_1_), channel_id=1, source_target_pairs={{0,4},{4,0},{8,12},{12,8},{16,20},{20,16},{24,28},{28,24},{1,5},{5... | collective-permute-start | bytes 3145736 | tf_op jit(solution)/shard_map/ppermute | solution.py:302
  107.1 27.0 %collective-permute-start.6 = (bf16[4,64,768]{2,0,1:T(4,128)(2,1)S(1)}, bf16[4,64,768]{2,0,1:T(4,128)(2,1)S(1)}, u32[]{:S(2)}, u32[]{:S(2)}) collective-permute-start(bf16[4,64,768]{2,0,1:T(4,128)(2,1)S(1)} %pad_maximum_fusion.16), channel_id=1, source_target_pairs={{0,16},{4,20},{8,24},{12,28},{16,0},{20,4},{24,8},{28,12},{1,17},{... | collective-permute-start | bytes 1179656 | tf_op jit(solution)/shard_map/ppermute | solution.py:302
  134.1 24.4 %collective-permute-start.18 = (bf16[2048,128]{1,0:T(8,128)(2,1)S(1)}, bf16[2048,128]{1,0:T(8,128)(2,1)S(1)}, u32[]{:S(2)}, u32[]{:S(2)}) collective-permute-start(bf16[2048,128]{1,0:T(8,128)(2,1)S(1)} %bitcast.154), channel_id=1, source_target_pairs={{0,2},{1,3},{2,0},{3,1},{4,6},{5,7},{6,4},{7,5},{8,10},{9,11},{10,... | collective-permute-start | bytes 1572872 | tf_op jit(solution)/shard_map/ppermute | solution.py:302
  151.6 29.5 %collective-permute-start.15 = (bf16[1024,512]{1,0:T(8,128)(2,1)}, bf16[1024,512]{1,0:T(8,128)(2,1)}, u32[]{:S(2)}, u32[]{:S(2)}) collective-permute-start(bf16[1024,512]{1,0:T(8,128)(2,1)} %get-tuple-element.32.refs_0_), channel_id=1, source_target_pairs={{0,1},{1,0},{2,3},{3,2},{4,5},{5,4},{6,7},{7,6},{8,9},{9,8},{10,11... | collective-permute-start | bytes 3145736 | tf_op jit(solution)/shard_map/ppermute | solution.py:302
  158.6 13.7 %collective-permute-start.21 = (bf16[2,1024,128]{2,1,0:T(8,128)(2,1)S(1)}, bf16[2,1024,128]{2,1,0:T(8,128)(2,1)}, u32[]{:S(2)}, u32[]{:S(2)}) collective-permute-start(bf16[2,1024,128]{2,1,0:T(8,128)(2,1)S(1)} %pad_maximum_fusion.15), channel_id=1, source_target_pairs={{0,16},{4,20},{8,24},{12,28},{16,0},{20,4},{24,8},{28,12},{1,17},{... | collective-permute-start | bytes 1572872 | tf_op jit(solution)/shard_map/ppermute | solution.py:302
  161.0 14.2 %collective-permute-start.19 = (bf16[2,1024,128]{2,1,0:T(8,128)(2,1)}, bf16[2,1024,128]{2,1,0:T(8,128)(2,1)}, u32[]{:S(2)}, u32[]{:S(2)}) collective-permute-start(bf16[2,1024,128]{2,1,0:T(8,128)(2,1)} %pad_maximum_fusion.14), channel_id=1, source_target_pairs={{0,8},{4,12},{8,0},{12,4},{16,24},{20,28},{24,16},{28,20},{1,9},{5... | collective-permute-start | bytes 1572872 | tf_op jit(solution)/shard_map/ppermute | solution.py:302
  162.5 16.4 %collective-permute-start.26 = (bf16[256,512]{1,0:T(8,128)(2,1)S(1)}, bf16[256,512]{1,0:T(8,128)(2,1)}, u32[]{:S(2)}, u32[]{:S(2)}) collective-permute-start(bf16[256,512]{1,0:T(8,128)(2,1)S(1)} %copy-done.14), channel_id=1, source_target_pairs={{0,4},{4,0},{8,12},{12,8},{16,20},{20,16},{24,28},{28,24},{1,5},{5... | collective-permute-start | bytes 786440 | tf_op jit(solution)/shard_map/ppermute | solution.py:302
  162.5 24.1 %collective-permute-start.25 = (bf16[256,512]{1,0:T(8,128)(2,1)S(1)}, bf16[256,512]{1,0:T(8,128)(2,1)}, u32[]{:S(2)}, u32[]{:S(2)}) collective-permute-start(bf16[256,512]{1,0:T(8,128)(2,1)S(1)} %copy-done.14), channel_id=1, source_target_pairs={{0,1},{1,0},{2,3},{3,2},{4,5},{5,4},{6,7},{7,6},{8,9},{9,8},{10,11... | collective-permute-start | bytes 786440 | tf_op jit(solution)/shard_map/ppermute | solution.py:302
  173.4 24.3 %collective-permute-start.22 = (bf16[4,1024,128]{2,1,0:T(8,128)(2,1)S(1)}, bf16[4,1024,128]{2,1,0:T(8,128)(2,1)}, u32[]{:S(2)}, u32[]{:S(2)}) collective-permute-start(bf16[4,1024,128]{2,1,0:T(8,128)(2,1)S(1)} %pad_maximum_fusion.8.refs_6_), channel_id=1, source_target_pairs={{0,8},{4,12},{8,0},{12,4},{16,24},{20,28},{24,16},{28,20},{1,9},{5... | collective-permute-start | bytes 3145736 | tf_op jit(solution)/shard_map/ppermute | solution.py:302
  177.3 24.2 %collective-permute-start.20 = (bf16[4,1024,128]{2,1,0:T(8,128)(2,1)}, bf16[4,1024,128]{2,1,0:T(8,128)(2,1)}, u32[]{:S(2)}, u32[]{:S(2)}) collective-permute-start(bf16[4,1024,128]{2,1,0:T(8,128)(2,1)} %pad_maximum_fusion.7.refs_4_), channel_id=1, source_target_pairs={{0,16},{4,20},{8,24},{12,28},{16,0},{20,4},{24,8},{28,12},{1,17},{... | collective-permute-start | bytes 3145736 | tf_op jit(solution)/shard_map/ppermute | solution.py:302
  178.9 22.6 %collective-permute-start.16 = (bf16[1024,512]{1,0:T(8,128)(2,1)}, bf16[1024,512]{1,0:T(8,128)(2,1)}, u32[]{:S(2)}, u32[]{:S(2)}) collective-permute-start(bf16[1024,512]{1,0:T(8,128)(2,1)} %get-tuple-element.32.refs_0_), channel_id=1, source_target_pairs={{0,4},{4,0},{8,12},{12,8},{16,20},{20,16},{24,28},{28,24},{1,5},{5... | collective-permute-start | bytes 3145736 | tf_op jit(solution)/shard_map/ppermute | solution.py:302
  181.1 20.4 %collective-permute-start.17 = (bf16[1024,512]{1,0:T(8,128)(2,1)}, bf16[1024,512]{1,0:T(8,128)(2,1)}, u32[]{:S(2)}, u32[]{:S(2)}) collective-permute-start(bf16[1024,512]{1,0:T(8,128)(2,1)} %collective-permute-done.15.refs_1_), channel_id=1, source_target_pairs={{0,4},{4,0},{8,12},{12,8},{16,20},{20,16},{24,28},{28,24},{1,5},{5... | collective-permute-start | bytes 3145736 | tf_op jit(solution)/shard_map/ppermute | solution.py:302
  217.7 21.0 %collective-permute-start.54 = (bf16[4,64,512]{2,1,0:T(8,128)(2,1)}, bf16[4,64,512]{2,1,0:T(8,128)(2,1)S(1)}, u32[]{:S(2)}, u32[]{:S(2)}) collective-permute-start(bf16[4,64,512]{2,1,0:T(8,128)(2,1)} %bitcast.64), channel_id=1, source_target_pairs={{0,16},{4,20},{8,24},{12,28},{16,0},{20,4},{24,8},{28,12},{1,17},{... | collective-permute-start | bytes 786440 | tf_op jit(solution)/shard_map/ppermute | solution.py:302
  221.9 32.5 %collective-permute-start.23 = (bf16[512,512]{1,0:T(8,128)(2,1)S(1)}, bf16[512,512]{1,0:T(8,128)(2,1)S(1)}, u32[]{:S(2)}, u32[]{:S(2)}) collective-permute-start(bf16[512,512]{1,0:T(8,128)(2,1)S(1)} %slice.523), channel_id=1, source_target_pairs={{0,4},{4,0},{8,12},{12,8},{16,20},{20,16},{24,28},{28,24},{1,5},{5... | collective-permute-start | bytes 1572872 | tf_op jit(solution)/shard_map/ppermute | solution.py:302
  231.9 38.2 %collective-permute-start.48 = (bf16[1024,512]{1,0:T(8,128)(2,1)}, bf16[1024,512]{1,0:T(8,128)(2,1)}, u32[]{:S(2)}, u32[]{:S(2)}) collective-permute-start(bf16[1024,512]{1,0:T(8,128)(2,1)} %fusion.41), channel_id=1, source_target_pairs={{0,16},{4,20},{8,24},{12,28},{16,0},{20,4},{24,8},{28,12},{1,17},{... | collective-permute-start | bytes 3145736 | tf_op jit(solution)/shard_map/ppermute | solution.py:302
  238.7 20.9 %collective-permute-start.28 = (bf16[1024,1024]{1,0:T(8,128)(2,1)}, bf16[1024,1024]{1,0:T(8,128)(2,1)}, u32[]{:S(2)}, u32[]{:S(2)}) collective-permute-start(bf16[1024,1024]{1,0:T(8,128)(2,1)} %slice.520), channel_id=1, source_target_pairs={{0,4},{4,0},{8,12},{12,8},{16,20},{20,16},{24,28},{28,24},{1,5},{5... | collective-permute-start | bytes 6291464 | tf_op jit(solution)/shard_map/ppermute | solution.py:302
  255.6 26.3 %collective-permute-start.51 = (bf16[1024,512]{1,0:T(8,128)(2,1)}, bf16[1024,512]{1,0:T(8,128)(2,1)}, u32[]{:S(2)}, u32[]{:S(2)}) collective-permute-start(bf16[1024,512]{1,0:T(8,128)(2,1)} %fusion.44), channel_id=1, source_target_pairs={{0,8},{4,12},{8,0},{12,4},{16,24},{20,28},{24,16},{28,20},{1,9},{5... | collective-permute-start | bytes 3145736 | tf_op jit(solution)/shard_map/ppermute | solution.py:302
  258.0 51.9 %collective-permute-start.24 = (bf16[256,512]{1,0:T(8,128)(2,1)}, bf16[256,512]{1,0:T(8,128)(2,1)}, u32[]{:S(2)}, u32[]{:S(2)}) collective-permute-start(bf16[256,512]{1,0:T(8,128)(2,1)} %slice.525), channel_id=1, source_target_pairs={{0,1},{1,0},{2,3},{3,2},{4,5},{5,4},{6,7},{7,6},{8,9},{9,8},{10,11... | collective-permute-start | bytes 786440 | tf_op jit(solution)/shard_map/ppermute | solution.py:302
  268.4 24.8 %collective-permute-start.29 = (bf16[1024,512]{1,0:T(8,128)(2,1)S(1)}, bf16[1024,512]{1,0:T(8,128)(2,1)S(1)}, u32[]{:S(2)}, u32[]{:S(2)}) collective-permute-start(bf16[1024,512]{1,0:T(8,128)(2,1)S(1)} %slice.522), channel_id=1, source_target_pairs={{0,1},{1,0},{2,3},{3,2},{4,5},{5,4},{6,7},{7,6},{8,9},{9,8},{10,11... | collective-permute-start | bytes 3145736 | tf_op jit(solution)/shard_map/ppermute | solution.py:302
  272.8 33.5 %collective-permute-start.49 = (bf16[1024,256]{1,0:T(8,128)(2,1)S(1)}, bf16[1024,256]{1,0:T(8,128)(2,1)S(1)}, u32[]{:S(2)}, u32[]{:S(2)}) collective-permute-start(bf16[1024,256]{1,0:T(8,128)(2,1)S(1)} %dynamic-slice_convert_fusion.1), channel_id=1, source_target_pairs={{0,8},{4,12},{8,0},{12,4},{16,24},{20,28},{24,16},{28,20},{1,9},{5... | collective-permute-start | bytes 1572872 | tf_op jit(solution)/shard_map/ppermute | solution.py:302
  284.7 22.0 %collective-permute-start.52 = (bf16[1024,256]{1,0:T(8,128)(2,1)S(1)}, bf16[1024,256]{1,0:T(8,128)(2,1)S(1)}, u32[]{:S(2)}, u32[]{:S(2)}) collective-permute-start(bf16[1024,256]{1,0:T(8,128)(2,1)S(1)} %dynamic-slice_convert_fusion), channel_id=1, source_target_pairs={{0,16},{4,20},{8,24},{12,28},{16,0},{20,4},{24,8},{28,12},{1,17},{... | collective-permute-start | bytes 1572872 | tf_op jit(solution)/shard_map/ppermute | solution.py:302
  306.2 31.1 %collective-permute-start.30 = (bf16[512,2048]{1,0:T(8,128)(2,1)S(1)}, bf16[512,2048]{1,0:T(8,128)(2,1)S(1)}, u32[]{:S(2)}, u32[]{:S(2)}) collective-permute-start(bf16[512,2048]{1,0:T(8,128)(2,1)S(1)} %fusion.6), channel_id=1, source_target_pairs={{0,4},{4,0},{8,12},{12,8},{16,20},{20,16},{24,28},{28,24},{1,5},{5... | collective-permute-start | bytes 6291464 | tf_op jit(solution)/shard_map/ppermute | solution.py:302
  306.6 20.7 %collective-permute-start.50 = (bf16[1024,128]{1,0:T(8,128)(2,1)S(1)}, bf16[1024,128]{1,0:T(8,128)(2,1)S(1)}, u32[]{:S(2)}, u32[]{:S(2)}) collective-permute-start(bf16[1024,128]{1,0:T(8,128)(2,1)S(1)} %dynamic-slice_convert_fusion.5), channel_id=1, source_target_pairs={{0,2},{1,3},{2,0},{3,1},{4,6},{5,7},{6,4},{7,5},{8,10},{9,11},{10,... | collective-permute-start | bytes 786440 | tf_op jit(solution)/shard_map/ppermute | solution.py:302
  306.9 26.0 %collective-permute-start.53 = (bf16[1024,128]{1,0:T(8,128)(2,1)S(1)}, bf16[1024,128]{1,0:T(8,128)(2,1)S(1)}, u32[]{:S(2)}, u32[]{:S(2)}) collective-permute-start(bf16[1024,128]{1,0:T(8,128)(2,1)S(1)} %dynamic-slice_convert_fusion.4), channel_id=1, source_target_pairs={{0,2},{1,3},{2,0},{3,1},{4,6},{5,7},{6,4},{7,5},{8,10},{9,11},{10,... | collective-permute-start | bytes 786440 | tf_op jit(solution)/shard_map/ppermute | solution.py:302
  334.4 25.2 %collective-permute-start.42 = (bf16[1024,512]{1,0:T(8,128)(2,1)S(1)}, bf16[1024,512]{1,0:T(8,128)(2,1)S(1)}, u32[]{:S(2)}, u32[]{:S(2)}) collective-permute-start(bf16[1024,512]{1,0:T(8,128)(2,1)S(1)} %fusion.35), channel_id=1, source_target_pairs={{0,16},{4,20},{8,24},{12,28},{16,0},{20,4},{24,8},{28,12},{1,17},{... | collective-permute-start | bytes 3145736 | tf_op jit(solution)/shard_map/ppermute | solution.py:302
  338.4 24.9 %collective-permute-start.31 = (bf16[256,2048]{1,0:T(8,128)(2,1)S(1)}, bf16[256,2048]{1,0:T(8,128)(2,1)S(1)}, u32[]{:S(2)}, u32[]{:S(2)}) collective-permute-start(bf16[256,2048]{1,0:T(8,128)(2,1)S(1)} %slice.521), channel_id=1, source_target_pairs={{0,1},{1,0},{2,3},{3,2},{4,5},{5,4},{6,7},{7,6},{8,9},{9,8},{10,11... | collective-permute-start | bytes 3145736 | tf_op jit(solution)/shard_map/ppermute | solution.py:302
  340.7 76.0 %collective-permute-start.45 = (bf16[1024,512]{1,0:T(8,128)(2,1)}, bf16[1024,512]{1,0:T(8,128)(2,1)}, u32[]{:S(2)}, u32[]{:S(2)}) collective-permute-start(bf16[1024,512]{1,0:T(8,128)(2,1)} %fusion.38), channel_id=1, source_target_pairs={{0,8},{4,12},{8,0},{12,4},{16,24},{20,28},{24,16},{28,20},{1,9},{5... | collective-permute-start | bytes 3145736 | tf_op jit(solution)/shard_map/ppermute | solution.py:302
  361.1 61.4 %collective-permute-start.43 = (bf16[1024,256]{1,0:T(8,128)(2,1)S(1)}, bf16[1024,256]{1,0:T(8,128)(2,1)}, u32[]{:S(2)}, u32[]{:S(2)}) collective-permute-start(bf16[1024,256]{1,0:T(8,128)(2,1)S(1)} %dynamic-slice_convert_fusion.3), channel_id=1, source_target_pairs={{0,8},{4,12},{8,0},{12,4},{16,24},{20,28},{24,16},{28,20},{1,9},{5... | collective-permute-start | bytes 1572872 | tf_op jit(solution)/shard_map/ppermute | solution.py:302
  420.3 16.2 %collective-permute-start.46 = (bf16[1024,256]{1,0:T(8,128)(2,1)S(1)}, bf16[1024,256]{1,0:T(8,128)(2,1)S(1)}, u32[]{:S(2)}, u32[]{:S(2)}) collective-permute-start(bf16[1024,256]{1,0:T(8,128)(2,1)S(1)} %dynamic-slice_convert_fusion.2), channel_id=1, source_target_pairs={{0,16},{4,20},{8,24},{12,28},{16,0},{20,4},{24,8},{28,12},{1,17},{... | collective-permute-start | bytes 1572872 | tf_op jit(solution)/shard_map/ppermute | solution.py:302
  427.1 9.0 %collective-permute-start.34 = (bf16[256,128]{1,0:T(8,128)(2,1)S(1)}, bf16[256,128]{1,0:T(8,128)(2,1)S(1)}, u32[]{:S(2)}, u32[]{:S(2)}) collective-permute-start(bf16[256,128]{1,0:T(8,128)(2,1)S(1)} %dynamic-slice_convert_fusion.10), channel_id=1, source_target_pairs={{0,16},{4,20},{8,24},{12,28},{16,0},{20,4},{24,8},{28,12},{1,17},{... | collective-permute-start | bytes 196616 | tf_op jit(solution)/shard_map/ppermute | solution.py:302
  428.3 24.8 %collective-permute-start.44 = (bf16[1024,128]{1,0:T(8,128)(2,1)S(1)}, bf16[1024,128]{1,0:T(8,128)(2,1)S(1)}, u32[]{:S(2)}, u32[]{:S(2)}) collective-permute-start(bf16[1024,128]{1,0:T(8,128)(2,1)S(1)} %dynamic-slice_convert_fusion.7), channel_id=1, source_target_pairs={{0,2},{1,3},{2,0},{3,1},{4,6},{5,7},{6,4},{7,5},{8,10},{9,11},{10,... | collective-permute-start | bytes 786440 | tf_op jit(solution)/shard_map/ppermute | solution.py:302
  436.1 6.5 %collective-permute-start.35 = (bf16[128,128]{1,0:T(8,128)(2,1)S(1)}, bf16[128,128]{1,0:T(8,128)(2,1)S(1)}, u32[]{:S(2)}, u32[]{:S(2)}) collective-permute-start(bf16[128,128]{1,0:T(8,128)(2,1)S(1)} %dynamic-slice_convert_fusion.11), channel_id=1, source_target_pairs={{0,1},{1,0},{2,3},{3,2},{4,5},{5,4},{6,7},{7,6},{8,9},{9,8},{10,11... | collective-permute-start | bytes 98312 | tf_op jit(solution)/shard_map/ppermute | solution.py:302
  442.6 10.5 %collective-permute-start.36 = (bf16[64,128]{1,0:T(8,128)(2,1)S(1)}, bf16[64,128]{1,0:T(8,128)(2,1)S(1)}, u32[]{:S(2)}, u32[]{:S(2)}) collective-permute-start(bf16[64,128]{1,0:T(8,128)(2,1)S(1)} %dynamic-slice_convert_fusion.12), channel_id=1, source_target_pairs={{0,2},{1,3},{2,0},{3,1},{4,6},{5,7},{6,4},{7,5},{8,10},{9,11},{10,... | collective-permute-start | bytes 49160 | tf_op jit(solution)/shard_map/ppermute | solution.py:302
  442.7 16.7 %collective-permute-start.47 = (bf16[1024,128]{1,0:T(8,128)(2,1)S(1)}, bf16[1024,128]{1,0:T(8,128)(2,1)S(1)}, u32[]{:S(2)}, u32[]{:S(2)}) collective-permute-start(bf16[1024,128]{1,0:T(8,128)(2,1)S(1)} %dynamic-slice_convert_fusion.6), channel_id=1, source_target_pairs={{0,2},{1,3},{2,0},{3,1},{4,6},{5,7},{6,4},{7,5},{8,10},{9,11},{10,... | collective-permute-start | bytes 786440 | tf_op jit(solution)/shard_map/ppermute | solution.py:302
  453.1 6.2 %collective-permute-start.37 = (f32[64,128]{1,0:T(8,128)S(1)}, f32[64,128]{1,0:T(8,128)S(1)}, u32[]{:S(2)}, u32[]{:S(2)}) collective-permute-start(f32[64,128]{1,0:T(8,128)S(1)} %convert_add_fusion.17), channel_id=1, source_target_pairs={{0,2},{1,3},{2,0},{3,1},{4,6},{5,7},{6,4},{7,5},{8,10},{9,11},{10,... | collective-permute-start | bytes 98312 | tf_op jit(solution)/shard_map/ppermute | solution.py:302
  468.7 6.4 %collective-permute-start.40 = (f32[512,128]{1,0:T(8,128)S(1)}, f32[512,128]{1,0:T(8,128)S(1)}, u32[]{:S(2)}, u32[]{:S(2)}) collective-permute-start(f32[512,128]{1,0:T(8,128)S(1)} %maximum_select_fusion.2), channel_id=1, source_target_pairs={{0,8},{4,12},{8,0},{12,4},{16,24},{20,28},{24,16},{28,20},{1,9},{5... | collective-permute-start | bytes 786440 | tf_op jit(solution)/shard_map/ppermute | solution.py:302
  (57 other events, 477.9 us)

commit v3 on v1

v3 whole, which is shorter than its diff:
```python
import math
import functools
import jax
import jax.numpy as jnp
from jax import lax
from jax.experimental import pallas as pl
from jax.experimental.pallas import tpu as pltpu
from jax.sharding import PartitionSpec as P

bank_widths = (1, 2, 3, 4, 5, 6, 7, 7)
bank_parts = (1, 1, 2, 4, 8, 16, 16, 16)
WIDEST = 7
LANES = 128
BLOCK = 256
CHUNK = 11
ROWS = 64
PARTS = 5
VMEM_BYTES = 60 * 1024 * 1024
LIGHT = pl.CostEstimate(flops=1, bytes_accessed=1, transcendentals=0)


def window_kernel(chars, ids_ref, table_ref, win_ref, emb_ref):
    tokens = ids_ref.shape[0]
    vocab = table_ref.shape[0]
    group = lax.broadcasted_iota(jnp.int32, (tokens, LANES), 1) // 16
    places = lax.broadcasted_iota(jnp.int32, (tokens, vocab), 1)
    for c in range(chars):
        hits = jnp.where(ids_ref[:, c : c + 1] == places, 1.0, 0.0).astype(jnp.bfloat16)
        emb_ref[c] = jnp.dot(hits, table_ref[...], preferred_element_type=jnp.float32).astype(jnp.bfloat16)
    for c in range(chars, chars + WIDEST - 1):
        emb_ref[c] = jnp.zeros((tokens, LANES), jnp.bfloat16)

    def window(p, carry):
        got = emb_ref[p]
        for k in range(1, WIDEST):
            got = jnp.where(group == k, emb_ref[p + k], got)
        win_ref[p] = got
        return carry

    lax.fori_loop(0, chars, window, 0)


def make_windows(ids, table):
    tokens, chars = ids.shape
    return pl.pallas_call(
        functools.partial(window_kernel, chars),
        out_shape=jax.ShapeDtypeStruct((chars, tokens, LANES), jnp.bfloat16),
        scratch_shapes=[pltpu.VMEM((chars + WIDEST - 1, tokens, LANES), jnp.bfloat16)],
        compiler_params=pltpu.CompilerParams(vmem_limit_bytes=VMEM_BYTES),
        cost_estimate=LIGHT,
        name="make_windows",
    )(ids, table)


def forward_kernel(low_places, extras, trip_ref, win_ref, weight_ref, aux_ref, e_ref, act_ref, x_ref, part_ref, high_ref, total_ref):
    step = pl.program_id(0)
    tokens = win_ref.shape[1]

    def pool(number, p, count, r):
        got = jnp.dot(
            win_ref[p : p + count, pl.ds(r, ROWS), :].reshape(count * ROWS, LANES),
            weight_ref[...],
            preferred_element_type=jnp.float32,
        ).reshape(count, ROWS, BLOCK)
        high = None
        if p >= low_places:
            valid = aux_ref[1:2, :]
            got = jnp.stack([jnp.where(valid > float(p + o), got[o], -jnp.inf) for o in range(count)])
            high = high_ref[0, pl.ds(r, ROWS), :]
        top = jnp.max(got, axis=0)
        high = top if high is None else jnp.maximum(high, top)
        got = jnp.exp(got - high[None])
        e_ref[0, p : p + count, pl.ds(r, ROWS), :] = got.astype(jnp.bfloat16)
        high_ref[number, pl.ds(r, ROWS), :] = high
        total_ref[number, pl.ds(r, ROWS), :] = jnp.sum(got, axis=0)

    for number in range(PARTS - 1):
        for r in range(0, tokens, ROWS):
            pool(number, number * CHUNK, CHUNK, r)

    for count in extras:

        @pl.when(trip_ref[step] == low_places + count)
        def tail(count=count):
            @pl.loop(0, tokens // ROWS)
            def rows(i):
                pool(PARTS - 1, low_places, count, pl.multiple_of(i * ROWS, ROWS))

    @pl.when(trip_ref[step] == low_places)
    def no_tail():
        high_ref[PARTS - 1] = high_ref[0]
        total_ref[PARTS - 1] = jnp.zeros(total_ref.shape[1:], jnp.float32)

    @pl.loop(0, tokens // 32)
    def finish(i):
        r = pl.ds(pl.multiple_of(i * 32, 32), 32)
        highs = [high_ref[number, r, :] for number in range(PARTS)]
        high = functools.reduce(jnp.maximum, highs)
        factors = [jnp.exp(part - high) for part in highs]
        total = sum(factor * total_ref[number, r, :] for number, factor in enumerate(factors))
        before = high + jnp.log(total) + aux_ref[0:1, :]
        x_ref[r, :] = before
        act_ref[r, :] = (before * jax.nn.sigmoid(before)).astype(jnp.bfloat16)
        inverse = 1.0 / total
        for number, factor in enumerate(factors):
            part_ref[number, r, :] = factor * inverse


def forward_onto_kernel(low_places, extras, trip_ref, win_ref, weight_ref, aux_ref, e_old, x_old, part_old, *refs):
    forward_kernel(low_places, extras, trip_ref, win_ref, weight_ref, aux_ref, *refs)


def conv_forward(windows, weight, aux, trips, low_places, places, first, blocks, at=0, room=None, onto=None):
    chars, tokens, unused = windows.shape
    room = room or blocks
    extras = tuple(count - low_places for count in sorted(set(places) - {low_places}))
    kernel = forward_kernel if onto is None else forward_onto_kernel
    return pl.pallas_call(
        functools.partial(kernel, low_places, extras),
        grid_spec=pltpu.PrefetchScalarGridSpec(
            num_scalar_prefetch=1,
            grid=(blocks,),
            in_specs=[
                pl.BlockSpec(windows.shape, lambda j, *_: (0, 0, 0)),
                pl.BlockSpec((LANES, BLOCK), lambda j, *_: (0, first + j)),
                pl.BlockSpec((8, BLOCK), lambda j, *_: (0, first + j)),
            ]
            + ([] if onto is None else [pl.BlockSpec(memory_space=pl.ANY)] * 3),
            out_specs=[
                pl.BlockSpec((1, chars, tokens, BLOCK), lambda j, *_: (at + j, 0, 0, 0)),
                pl.BlockSpec((tokens, BLOCK), lambda j, *_: (0, j)),
                pl.BlockSpec((tokens, BLOCK), lambda j, *_: (0, at + j)),
                pl.BlockSpec((PARTS, tokens, BLOCK), lambda j, *_: (0, 0, at + j)),
            ],
            scratch_shapes=[
                pltpu.VMEM((PARTS, tokens, BLOCK), jnp.float32),
                pltpu.VMEM((PARTS, tokens, BLOCK), jnp.float32),
            ],
        ),
        out_shape=[
            jax.ShapeDtypeStruct((room, chars, tokens, BLOCK), jnp.bfloat16),
            jax.ShapeDtypeStruct((tokens, blocks * BLOCK), jnp.bfloat16),
            jax.ShapeDtypeStruct((tokens, room * BLOCK), jnp.float32),
            jax.ShapeDtypeStruct((PARTS, tokens, room * BLOCK), jnp.float32),
        ],
        input_output_aliases={} if onto is None else {4: 0, 5: 2, 6: 3},
        compiler_params=pltpu.CompilerParams(vmem_limit_bytes=VMEM_BYTES),
        cost_estimate=LIGHT,
        name="conv_forward",
    )(trips[first : first + blocks], windows, weight, aux, *(onto or []))


TABLE_ROWS = 40
ALONG = 5


def backward_kernel(chars, low_places, span, firsts, trip_ref, *refs):
    step = pl.program_id(0)
    sources = refs[: 3 * len(firsts)]
    if len(firsts) == 1:
        backward_step(chars, low_places, span, trip_ref, *sources, *refs[3:])
        return
    for number, first in enumerate(firsts):
        end = firsts[number + 1] if number + 1 < len(firsts) else pl.num_programs(0)

        @pl.when((step >= first) & (step < end))
        def run(number=number):
            backward_step(chars, low_places, span, trip_ref, *sources[3 * number : 3 * number + 3], *refs[3 * len(firsts) :])


def backward_step(chars, low_places, span, trip_ref, e_ref, x_ref, part_ref, d_ref, more_ref, win_ref, weight_ref, ids_ref, out_ref, table_ref, dwin_ref, before_ref, dw_ref, sum_ref):
    step = pl.program_id(0)
    tokens = d_ref.shape[0]
    before = x_ref[...]
    sig = jax.nn.sigmoid(before)
    d_act = (d_ref[...] + more_ref[...].astype(jnp.float32)).astype(jnp.bfloat16).astype(jnp.float32)
    d_before = d_act * sig * (1.0 + before * (1.0 - sig))
    before_ref[...] = d_before

    @pl.when(step == 0)
    def clear():
        dwin_ref[...] = jnp.zeros(dwin_ref.shape, jnp.float32)

    dw_ref[...] = jnp.zeros(dw_ref.shape, jnp.float32)

    def some(number, count, p):
        scale = before_ref[...] * part_ref[number]
        d_conv = (e_ref[0, pl.ds(p, count)].astype(jnp.float32) * scale[None]).astype(jnp.bfloat16)
        flat = d_conv.reshape(count * tokens, BLOCK)
        dwin_ref[pl.ds(p, count)] += lax.dot_general(
            flat, weight_ref[...], (((1,), (1,)), ((), ())), preferred_element_type=jnp.float32
        ).reshape(count, tokens, LANES)
        win = win_ref[pl.ds(p, count)].reshape(count * tokens, LANES)
        dw_ref[...] += lax.dot_general(win, flat, (((0,), (0,)), ((), ())), preferred_element_type=jnp.float32)

    @pl.loop(0, low_places // CHUNK)
    def full(i):
        some(i, CHUNK, i * CHUNK)

    @pl.loop(low_places, trip_ref[step])
    def tail(p):
        some(PARTS - 1, 1, p)

    d_bias = jnp.sum(d_before, axis=0, keepdims=True)
    for number in range(BLOCK // LANES):
        lanes = slice(number * LANES, (number + 1) * LANES)
        out_ref[number, :span, :] = dw_ref[:span, lanes]
        out_ref[number, span:, :] = jnp.broadcast_to(d_bias[:, lanes], (8, LANES))

    @pl.when(step == pl.num_programs(0) - 1)
    def finish():
        vocab = sum_ref.shape[0]
        group = lax.broadcasted_iota(jnp.int32, (tokens, LANES), 1) // 16
        places = lax.broadcasted_iota(jnp.int32, (vocab, tokens), 0)
        sum_ref[...] = jnp.zeros(sum_ref.shape, jnp.float32)
        for start in range(0, chars, ALONG):
            hits, rows = [], []
            for c in range(start, start + ALONG):
                got = jnp.where(group == 0, dwin_ref[c], 0.0)
                for k in range(1, WIDEST):
                    if c - k >= 0:
                        got = jnp.where(group == k, dwin_ref[c - k], got)
                first = got.astype(jnp.bfloat16)
                second = (got - first.astype(jnp.float32)).astype(jnp.bfloat16)
                rows.append(jnp.concatenate([first, second], axis=1))
                hits.append(jnp.where(places == ids_ref[c : c + 1, :], 1.0, 0.0).astype(jnp.bfloat16))
            sum_ref[...] += jnp.dot(
                jnp.concatenate(hits, axis=1), jnp.concatenate(rows), preferred_element_type=jnp.float32
            )
        lane_from = lax.broadcasted_iota(jnp.int32, (2 * LANES, LANES), 0)
        lane_to = lax.broadcasted_iota(jnp.int32, (2 * LANES, LANES), 1)
        total = jnp.zeros((TABLE_ROWS, LANES), jnp.float32)
        for j in range(vocab // TABLE_ROWS):
            turn_to = (lane_to // 16 == j) & (lane_from % 16 == lane_to % 16) & (lane_from % LANES < span)
            total = total + jnp.dot(
                sum_ref[j * TABLE_ROWS : (j + 1) * TABLE_ROWS, :],
                jnp.where(turn_to, 1.0, 0.0),
                precision=lax.Precision.HIGHEST,
                preferred_element_type=jnp.float32,
            )
        table_ref[...] = total


def conv_backward(es, xs, parts, d_act, more, win, weight, ids_across, trips, low_places, vocab, span, first):
    unused, chars, tokens, unused = es[0].shape
    firsts = [0]
    for e in es[:-1]:
        firsts.append(firsts[-1] + e.shape[0])
    blocks = firsts[-1] + es[-1].shape[0]
    count = blocks * BLOCK
    padded = -(-vocab // TABLE_ROWS) * TABLE_ROWS
    operands, specs = [], []
    for start, e, x, part in zip(firsts, es, xs, parts):
        inside = lambda j, start=start, last=e.shape[0] - 1: jnp.clip(j - start, 0, last)
        operands += [e, x, part]
        specs += [
            pl.BlockSpec((1, chars, tokens, BLOCK), lambda j, *_, inside=inside: (inside(j), 0, 0, 0)),
            pl.BlockSpec((tokens, BLOCK), lambda j, *_, inside=inside: (0, inside(j))),
            pl.BlockSpec((PARTS, tokens, BLOCK), lambda j, *_, inside=inside: (0, 0, inside(j))),
        ]
    whole = lambda *shape: pl.BlockSpec(shape, lambda j, *_: (0,) * len(shape))
    per = BLOCK // LANES
    return pl.pallas_call(
        functools.partial(backward_kernel, chars, low_places, span, tuple(firsts)),
        grid_spec=pltpu.PrefetchScalarGridSpec(
            num_scalar_prefetch=1,
            grid=(blocks,),
            in_specs=specs
            + [
                pl.BlockSpec((tokens, BLOCK), lambda j, *_: (0, j)),
                pl.BlockSpec((tokens, BLOCK), lambda j, *_: (0, j)),
                whole(chars, tokens, LANES),
                pl.BlockSpec((LANES, BLOCK), lambda j, *_: (0, first + j)),
                whole(*ids_across.shape),
            ],
            out_specs=[
                pl.BlockSpec((per, span + 8, LANES), lambda j, *_: (j, 0, 0)),
                whole(TABLE_ROWS, LANES),
            ],
            scratch_shapes=[
                pltpu.VMEM((chars, tokens, LANES), jnp.float32),
                pltpu.VMEM((tokens, BLOCK), jnp.float32),
                pltpu.VMEM((LANES, BLOCK), jnp.float32),
                pltpu.VMEM((padded, 2 * LANES), jnp.float32),
            ],
        ),
        out_shape=[
            jax.ShapeDtypeStruct((blocks * per, span + 8, LANES), jnp.float32),
            jax.ShapeDtypeStruct((TABLE_ROWS, LANES), jnp.float32),
        ],
        compiler_params=pltpu.CompilerParams(vmem_limit_bytes=VMEM_BYTES),
        cost_estimate=LIGHT,
        name="conv_backward",
    )(trips[first : first + blocks], *operands, d_act, more, win, weight, ids_across)


def bank_layout(base_count):
    layout = []
    natural = 0
    for number in range(8):
        filters = bank_parts[number] * base_count
        leading = 16 * base_count if number == 7 else 0
        layout.append((bank_widths[number], leading, filters, natural))
        natural += filters
    return layout


def join_filters(weights, layout):
    parts = []
    for kernel, leading, filters, natural in layout:
        part = weights[kernel - 1][:, leading : leading + filters]
        parts.append(jnp.pad(part, ((0, LANES - part.shape[0]), (0, 0))))
    return jnp.concatenate(parts, axis=1)


def column_places(layout, chars):
    return [chars - kernel + 1 for kernel, leading, filters, natural in layout for unused in range(filters)]


def bank_starts(bank_order, layout):
    counts = jnp.array([entry[2] for entry in layout], jnp.int32)
    matches = (bank_order[:, None] == lax.iota(jnp.int32, 8)[None, :]).astype(jnp.int32)
    placed = jnp.sum(matches * counts[None, :], axis=1)
    before = jnp.cumsum(placed) - placed
    return jnp.sum(matches * before[:, None], axis=0)


NEAR = pl.BlockSpec(memory_space=pltpu.VMEM)
ANYWHERE = pl.BlockSpec(memory_space=pl.ANY)
STEP = 256
BELOW = 32


def bank_rows_kernel(layout, to_banks, order_ref, x_ref, *refs):
    out_ref = refs[-1]
    at = jnp.int32(0)
    starts = [at] * 8
    for place in range(8):
        bank = order_ref[place]
        size = jnp.int32(0)
        for number in range(8):
            starts[number] = jnp.where(bank == number, at, starts[number])
            size = jnp.where(bank == number, layout[number][2], size)
        at = at + size
    for number in range(8):
        filters, natural = layout[number][2], layout[number][3]
        place = pl.ds(pl.multiple_of(starts[number], 32), filters)
        here = pl.ds(natural, filters)
        if to_banks:
            out_ref[here, :] = x_ref[place, :]
        else:
            out_ref[place, :] = x_ref[here, :]
    if len(refs) == 2:
        end = layout[-1][2] + layout[-1][3]
        out_ref[end:, :] = refs[0][...]


def bank_rows(x, bank_order, layout, to_banks, below=None):
    if layout[0][2] % 32:
        starts = bank_starts(bank_order, layout)
        if to_banks:
            return jnp.concatenate(
                [lax.dynamic_slice_in_dim(x, starts[number], layout[number][2], 0) for number in range(8)]
                + ([] if below is None else [below])
            )
        for number in range(8):
            unused, unused, filters, natural = layout[number]
            x = lax.dynamic_update_slice_in_dim(x, x[natural : natural + filters], starts[number], 0)
        return x
    rows = layout[-1][2] + layout[-1][3] + (0 if below is None else below.shape[0])
    return pl.pallas_call(
        functools.partial(bank_rows_kernel, tuple(layout), to_banks),
        in_specs=[pl.BlockSpec(memory_space=pltpu.SMEM)] + [NEAR] * (1 if below is None else 2),
        out_specs=NEAR,
        out_shape=jax.ShapeDtypeStruct((rows, x.shape[1]), x.dtype),
        compiler_params=pltpu.CompilerParams(vmem_limit_bytes=VMEM_BYTES),
        cost_estimate=LIGHT,
        name="bank_rows",
    )(bank_order, x, *([] if below is None else [below]))


def swap(x, axis, bit):
    return lax.ppermute(x, axis, [(i, i ^ bit) for i in range(lax.axis_size(axis))])


def swap_both(x):
    wide, narrow = lax.axis_size("wide"), lax.axis_size("narrow")
    pairs = [(w * narrow + n, (w ^ 1) * narrow + (n ^ 1)) for w in range(wide) for n in range(narrow)]
    return lax.ppermute(x, ("wide", "narrow"), pairs)


def side(axis, bit):
    return (lax.axis_index(axis) // bit) % 2


def high_bits(axis):
    return [1 << k for k in range(1, lax.axis_size(axis).bit_length() - 1)]


def after(x, *others):
    return lax.optimization_barrier((x, others))[0]


def group_all(x):
    along = swap(x, "narrow", 1)
    return [x, along, swap(x, "wide", 1), swap(along, "wide", 1)]


def group_trade(parts):
    return [
        parts[0],
        swap(parts[1], "narrow", 1),
        swap(parts[2], "wide", 1),
        swap_both(parts[3]),
    ]


def silu_parts(project, half):
    linear = project[:, :half]
    gating = jax.nn.sigmoid(project[:, half:])
    return linear, gating, jax.nn.sigmoid(linear)


def back_parts(carried, linear, gating, sigmoid_at, d_output):
    d_linear = d_output * (1.0 - gating) * sigmoid_at * (1.0 + linear * (1.0 - sigmoid_at))
    d_gating = d_output * (carried - linear * sigmoid_at) * gating * (1.0 - gating)
    return jnp.concatenate([d_linear, d_gating], axis=1).astype(jnp.bfloat16)


def turned_dot(x, weight):
    return lax.dot_general(x, weight, (((1,), (1,)), ((), ())), preferred_element_type=jnp.float32)


def collect(x_copies, w_copies, at_ref, x_sources, w_sources, x_ref, w_ref, x_out, w_out, sems):
    x_moves, w_moves = [], []
    for source, row, column, height, wide, to_row, to_column in x_copies:
        x_moves.append(
            pltpu.make_async_copy(
                x_sources[source].at[pl.ds(row, height), pl.ds(column, wide)],
                x_ref.at[pl.ds(to_row, height), pl.ds(to_column, wide)],
                sems.at[len(x_moves)],
            )
        )
    for number, (source, piece, to_row) in enumerate(w_copies):
        width = w_sources[source].shape[2]
        column = pl.multiple_of(at_ref[number] * width, width)
        w_moves.append(
            pltpu.make_async_copy(
                w_sources[source].at[piece],
                w_ref.at[pl.ds(to_row, w_sources[source].shape[1]), pl.ds(column, width)],
                sems.at[len(x_moves) + len(w_moves)],
            )
        )
    for move in x_moves + w_moves:
        move.start()
    out_moves = []
    done = len(x_moves) + len(w_moves)
    for moves, near, far in ((x_moves, x_ref, x_out), (w_moves, w_ref, w_out)):
        for move in moves:
            move.wait()
        out_moves.append(pltpu.make_async_copy(near, far, sems.at[done + len(out_moves)]))
        out_moves[-1].start()
    return out_moves


def layer_one_kernel(x_copies, w_copies, x_count, at_ref, pick_ref, *refs):
    x_sources, w_sources = refs[:x_count], refs[x_count:-9]
    x_out, w_out, project_out, carried_ref, hidden_ref, x_ref, w_ref, project_ref, sems = refs[-9:]
    out_moves = collect(x_copies, w_copies, at_ref, x_sources, w_sources, x_ref, w_ref, x_out, w_out, sems)
    half = hidden_ref.shape[1]
    depth = x_ref.shape[1]
    blocks = x_ref.shape[0] // STEP
    last = sems.shape[0] - 1

    @pl.loop(0, blocks)
    def block(i):
        rows = pl.ds(pl.multiple_of(i * STEP, STEP), STEP)
        carried = jnp.dot(x_ref[rows, :], pick_ref[...], preferred_element_type=jnp.float32)
        carried_ref[rows, :] = carried.astype(jnp.bfloat16)
        project = jnp.dot(x_ref[rows, :], w_ref[:depth, :], preferred_element_type=jnp.float32)
        project = project + w_ref[depth : depth + 1, :].astype(jnp.float32)
        project_ref[rows, :] = project
        pltpu.make_async_copy(project_ref.at[rows, :], project_out.at[rows, :], sems.at[last - i]).start()
        linear, gating, sigmoid_at = silu_parts(project, half)
        hidden_ref[rows, :] = (gating * carried + (1.0 - gating) * (linear * sigmoid_at)).astype(jnp.bfloat16)

    for move in out_moves:
        move.wait()

    @pl.loop(0, blocks)
    def finish(i):
        rows = pl.ds(pl.multiple_of(i * STEP, STEP), STEP)
        pltpu.make_async_copy(project_ref.at[rows, :], project_out.at[rows, :], sems.at[last - i]).wait()


def layer_two_kernel(x_copies, w_copies, x_count, at_ref, out_weight_ref, *refs):
    given_refs, refs = refs[:4], refs[4:]
    x_sources, w_sources = refs[:x_count], refs[x_count:-10]
    x_out, w_out, hidden_ref, d_project_ref, through_ref, sums_ref, away_ref, x_ref, w_ref, sems = refs[-10:]
    out_moves = collect(x_copies, w_copies, at_ref, x_sources, w_sources, x_ref, w_ref, x_out, w_out, sems)
    half = hidden_ref.shape[1]
    sums_ref[...] = jnp.zeros(sums_ref.shape, jnp.float32)
    depth = x_ref.shape[1]
    away = depth // 2

    count = given_refs[0].shape[0]
    for number, given_ref in enumerate(given_refs):

        @pl.loop(0, count // STEP)
        def block(i, number=number, given_ref=given_ref):
            rows = pl.ds(pl.multiple_of(number * count + i * STEP, STEP), STEP)
            carried = x_ref[rows, :half].astype(jnp.float32)
            project = jnp.dot(x_ref[rows, :], w_ref[:depth, :], preferred_element_type=jnp.float32)
            project = project + w_ref[depth : depth + 1, :].astype(jnp.float32)
            linear, gating, sigmoid_at = silu_parts(project, half)
            hidden_ref[rows, :] = (gating * carried + (1.0 - gating) * (linear * sigmoid_at)).astype(jnp.bfloat16)
            given = given_ref[pl.ds(pl.multiple_of(i * STEP, STEP), STEP), :]
            d_output = jnp.dot(given, out_weight_ref[...], preferred_element_type=jnp.float32)
            d_project = back_parts(carried, linear, gating, sigmoid_at, d_output)
            d_project_ref[rows, :] = d_project
            through_ref[rows, :] = gating * d_output
            sums_ref[...] += jnp.broadcast_to(jnp.sum(d_project.astype(jnp.float32), axis=0, keepdims=True), sums_ref.shape)
            away_ref[rows, :] = turned_dot(d_project, w_ref[away:depth, :]).astype(jnp.bfloat16)

    for move in out_moves:
        move.wait()


def call_layer(kernel, extra, x_sources, x_copies, weight, shape, outputs, far, name):
    w_sources, w_copies, columns = weight
    count, depth, total = shape
    outputs = [((count, depth), jnp.bfloat16), ((depth + BELOW, total), jnp.bfloat16)] + outputs
    return pl.pallas_call(
        functools.partial(kernel, tuple(x_copies), tuple(w_copies), len(x_sources)),
        in_specs=[pl.BlockSpec(memory_space=pltpu.SMEM)]
        + [NEAR] * len(extra)
        + [ANYWHERE] * (len(x_sources) + len(w_sources)),
        out_specs=[ANYWHERE] * far + [NEAR] * (len(outputs) - far),
        out_shape=[jax.ShapeDtypeStruct(*output) for output in outputs],
        scratch_shapes=[pltpu.VMEM(*output) for output in outputs[:far]]
        + [pltpu.SemaphoreType.DMA((len(x_copies) + len(w_copies) + far + count // STEP,))],
        compiler_params=pltpu.CompilerParams(vmem_limit_bytes=VMEM_BYTES),
        cost_estimate=LIGHT,
        name=name,
    )(columns, *extra, *x_sources, *w_sources)


def put_together(x_sources, x_copies, weight, shape):
    w_sources, w_copies, columns = weight
    count, depth, total = shape
    inputs = jnp.zeros((count, depth), jnp.bfloat16)
    for source, row, column, height, wide, to_row, to_column in x_copies:
        part = x_sources[source][row : row + height, column : column + wide]
        inputs = inputs.at[to_row : to_row + height, to_column : to_column + wide].set(part)
    whole = jnp.zeros((depth + BELOW, total), jnp.bfloat16)
    for number, (source, piece, to_row) in enumerate(w_copies):
        part = w_sources[source][piece]
        whole = lax.dynamic_update_slice(whole, part, (to_row, columns[number] * part.shape[1]))
    return inputs, whole


def layer_one(x_sources, x_copies, weight, pick, shape):
    count, depth, total = shape
    if weight[0][0].shape[2] % LANES:
        inputs, whole = put_together(x_sources, x_copies, weight, shape)
        carried = jnp.dot(inputs, pick, preferred_element_type=jnp.float32)
        project = jnp.dot(inputs, whole[:depth], preferred_element_type=jnp.float32) + whole[depth].astype(jnp.float32)
        linear, gating, sigmoid_at = silu_parts(project, total // 2)
        hidden = gating * carried + (1.0 - gating) * (linear * sigmoid_at)
        return inputs, whole, project, carried.astype(jnp.bfloat16), hidden.astype(jnp.bfloat16)
    outputs = [((count, total), jnp.float32), ((count, total // 2), jnp.bfloat16), ((count, total // 2), jnp.bfloat16)]
    return call_layer(layer_one_kernel, [pick], x_sources, x_copies, weight, shape, outputs, 3, "layer_one")


def layer_two(x_sources, x_copies, weight, given, shape):
    count, depth, total = shape
    if weight[0][0].shape[2] % LANES:
        inputs, whole = put_together(x_sources, x_copies, weight, shape)
        carried = inputs[:, : total // 2].astype(jnp.float32)
        project = jnp.dot(inputs, whole[:depth], preferred_element_type=jnp.float32) + whole[depth].astype(jnp.float32)
        linear, gating, sigmoid_at = silu_parts(project, total // 2)
        hidden = gating * carried + (1.0 - gating) * (linear * sigmoid_at)
        d_output = jnp.dot(jnp.concatenate(given[1:]), given[0], preferred_element_type=jnp.float32)
        d_project = back_parts(carried, linear, gating, sigmoid_at, d_output)
        sums = jnp.broadcast_to(jnp.sum(d_project.astype(jnp.float32), axis=0, keepdims=True), (8, total))
        away = turned_dot(d_project, whole[depth // 2 : depth]).astype(jnp.bfloat16)
        return inputs, whole, hidden.astype(jnp.bfloat16), d_project, gating * d_output, sums, away
    outputs = [
        ((count, total // 2), jnp.bfloat16),
        ((count, total), jnp.bfloat16),
        ((count, total // 2), jnp.float32),
        ((8, total), jnp.float32),
        ((count, depth // 2), jnp.bfloat16),
    ]
    return call_layer(layer_two_kernel, given, x_sources, x_copies, weight, shape, outputs, 2, "layer_two")


def keep_two_kernel(d_project_ref, w_ref, got_ref, *refs):
    result = turned_dot(d_project_ref[...], w_ref[...]) + got_ref[...].astype(jnp.float32)
    if len(refs) == 2:
        result = result + refs[0][...]
    refs[-1][...] = result.astype(refs[-1].dtype)


def keep_two(d_project, weight, got, number, through=None):
    count, total = d_project.shape
    wide = (weight.shape[0] - BELOW) // 4
    specs = [
        pl.BlockSpec((STEP, total), lambda i: (i, 0)),
        pl.BlockSpec((wide, total), lambda i: (number, 0)),
        pl.BlockSpec((STEP, wide), lambda i: (jnp.bitwise_xor(i, 2), number)),
    ]
    if through is not None:
        specs.append(pl.BlockSpec((STEP, wide), lambda i: (i, 0)))
    return pl.pallas_call(
        keep_two_kernel,
        grid=(count // STEP,),
        in_specs=specs,
        out_specs=pl.BlockSpec((STEP, wide), lambda i: (i, 0)),
        out_shape=jax.ShapeDtypeStruct((count, wide), jnp.bfloat16 if through is None else jnp.float32),
        compiler_params=pltpu.CompilerParams(vmem_limit_bytes=VMEM_BYTES),
        cost_estimate=LIGHT,
        name="keep_two",
    )(d_project, weight, got, *([] if through is None else [through]))


def back_one_kernel(own_ref, got_ref, project_ref, carried_ref, w_far, pick_far, d_project_ref, through_ref, sums_ref, first_ref, second_ref, w_ref, pick_ref, sems):
    half = own_ref.shape[1]
    blocks = own_ref.shape[0] // STEP
    moves = [pltpu.make_async_copy(w_far, w_ref, sems.at[0]), pltpu.make_async_copy(pick_far, pick_ref, sems.at[1])]
    for move in moves:
        move.start()
    sums_ref[...] = jnp.zeros(sums_ref.shape, jnp.float32)
    depth = w_ref.shape[0] - BELOW

    @pl.loop(0, blocks)
    def block(i):
        rows = pl.ds(pl.multiple_of(i * STEP, STEP), STEP)
        other = pl.ds(pl.multiple_of(jnp.bitwise_xor(i, 1) * STEP, STEP), STEP)
        d_output = own_ref[rows, :] + got_ref[other, :].astype(jnp.float32)
        linear, gating, sigmoid_at = silu_parts(project_ref[rows, :], half)
        d_project = back_parts(carried_ref[rows, :].astype(jnp.float32), linear, gating, sigmoid_at, d_output)
        d_project_ref[rows, :] = d_project
        through_ref[rows, :] = (gating * d_output).astype(jnp.bfloat16)
        sums_ref[...] += jnp.broadcast_to(jnp.sum(d_project.astype(jnp.float32), axis=0, keepdims=True), sums_ref.shape)

    for move in moves:
        move.wait()

    @pl.loop(0, blocks // 2)
    def send(i):
        to = pl.ds(pl.multiple_of(i * STEP, STEP), STEP)
        rows = pl.ds(pl.multiple_of((i + blocks // 2) * STEP, STEP), STEP)
        for out_ref, start in ((first_ref, depth // 2), (second_ref, 0)):
            columns = slice(start, start + depth // 2)
            result = turned_dot(d_project_ref[rows, :], w_ref[columns, :]) + turned_dot(through_ref[rows, :], pick_ref[columns, :])
            out_ref[to, :] = result.astype(jnp.bfloat16)


def back_one(own, got, project, carried, weight, pick):
    count, total = project.shape
    depth = weight.shape[0] - BELOW
    return pl.pallas_call(
        back_one_kernel,
        in_specs=[NEAR] * 4 + [ANYWHERE] * 2,
        out_specs=[NEAR] * 5,
        scratch_shapes=[
            pltpu.VMEM(weight.shape, weight.dtype),
            pltpu.VMEM(pick.shape, pick.dtype),
            pltpu.SemaphoreType.DMA((2,)),
        ],
        out_shape=[
            jax.ShapeDtypeStruct((count, total), jnp.bfloat16),
            jax.ShapeDtypeStruct((count, total // 2), jnp.bfloat16),
            jax.ShapeDtypeStruct((8, total), jnp.float32),
            jax.ShapeDtypeStruct((count // 2, depth // 2), jnp.bfloat16),
            jax.ShapeDtypeStruct((count // 2, depth // 2), jnp.bfloat16),
        ],
        compiler_params=pltpu.CompilerParams(vmem_limit_bytes=VMEM_BYTES),
        cost_estimate=LIGHT,
        name="back_one",
    )(own, got, project, carried, weight, pick)


def keep_one_kernel(d_project_ref, through_ref, w_ref, pick_ref, got_ref, own_ref, send_ref):
    for number, out_ref in ((1, send_ref), (0, own_ref)):
        rows = slice(number * STEP, (number + 1) * STEP)
        result = turned_dot(d_project_ref[rows, :], w_ref[...]) + turned_dot(through_ref[rows, :], pick_ref[...])
        out_ref[...] = (result + got_ref[rows, :].astype(jnp.float32)).astype(out_ref.dtype)


def keep_one(d_project, through, weight, pick, got, number):
    total = d_project.shape[1]
    wide = (weight.shape[0] - BELOW) // 2
    return pl.pallas_call(
        keep_one_kernel,
        grid=(1,),
        in_specs=[
            pl.BlockSpec((2 * STEP, total), lambda i: (0, 0)),
            pl.BlockSpec((2 * STEP, total // 2), lambda i: (0, 0)),
            pl.BlockSpec((wide, total), lambda i: (number, 0)),
            pl.BlockSpec((wide, total // 2), lambda i: (number, 0)),
            pl.BlockSpec((2 * STEP, wide), lambda i: (0, 0)),
        ],
        out_specs=[pl.BlockSpec((STEP, wide), lambda i: (0, 0))] * 2,
        out_shape=[
            jax.ShapeDtypeStruct((STEP, wide), jnp.float32),
            jax.ShapeDtypeStruct((STEP, wide), jnp.bfloat16),
        ],
        compiler_params=pltpu.CompilerParams(vmem_limit_bytes=VMEM_BYTES),
        cost_estimate=LIGHT,
        name="keep_one",
    )(d_project, through, weight, pick, got)


def stage_lists():
    low = [("narrow", bit) for bit in high_bits("narrow")]
    wide = [("wide", bit) for bit in high_bits("wide")]
    return (low + wide, low + wide[::-1])


def local_block(wide, narrow):
    return (wide // 2) * (lax.axis_size("narrow") // 2) + narrow // 2


def turn(flips, axis, bit):
    return [(fw ^ (bit if axis == "wide" else 0), fn ^ (bit if axis == "narrow" else 0)) for fw, fn in flips]


class Gather:
    def __init__(self, own):
        self.half = own.shape[0] // 2
        self.lists = stage_lists()
        self.rounds = len(self.lists[0])
        self.shared = len(high_bits("narrow"))
        self.number = 0
        self.held = [own]
        self.turns = [[(0, 0)], [(0, 0)]]
        self.got = None

    def send(self, *others):
        if self.got is not None:
            self.take(*others)
        elif others:
            self.held = [after(part, *others) for part in self.held]
        if self.number < self.shared:
            axis, bit = self.lists[0][self.number]
            self.got = [swap(part, axis, bit) for part in self.held]
            return self.held
        if len(self.held) != 2 or self.number == self.shared:
            self.held = [
                jnp.stack([part[n * self.half : (n + 1) * self.half] for part in self.held]) for n in range(2)
            ]
        self.got = [swap(self.held[n], *self.lists[n][self.number]) for n in range(2)]
        return self.held

    def take(self, *others):
        got = [after(part, *others) for part in self.got] if others else self.got
        if self.number < self.shared:
            self.held = self.held + got
        elif self.number < self.rounds - 1:
            self.held = [jnp.concatenate([held, part]) for held, part in zip(self.held, got)]
        else:
            self.last = got
        for n in range(2):
            self.turns[n] = self.turns[n] + turn(self.turns[n], *self.lists[n][self.number])
        self.number += 1
        self.got = None

    def result(self):
        wide, narrow = lax.axis_index("wide"), lax.axis_index("narrow")
        self.take()
        sources, copies, columns = [], [], []
        for n in range(2):
            count = len(self.turns[n]) // 2
            for source, flips in ((self.held[n], self.turns[n][:count]), (self.last[n], self.turns[n][count:])):
                for piece, (fw, fn) in enumerate(flips):
                    copies.append((len(sources), piece, n * self.half))
                    columns.append(local_block(wide ^ fw, narrow ^ fn))
                sources.append(source)
        return sources, copies, jnp.stack(columns).astype(jnp.int32)


def halves(x, outer, bit_value):
    rest = x.shape[-1] // (2 * outer)
    parts = [
        lax.dynamic_slice_in_dim(x, number * 2 * rest + bit_value * rest, rest, x.ndim - 1)
        for number in range(outer)
    ]
    return parts[0] if outer == 1 else jnp.concatenate(parts, axis=-1)


def product(inputs, d_project, number, outer, part, more, got):
    half = inputs.shape[1] // 2
    result = lax.dot_general(
        inputs[:, number * half : (number + 1) * half],
        after(halves(d_project, outer, part)),
        (((0,), (0,)), ((), ())),
        preferred_element_type=jnp.float32,
    )
    if got is None:
        result = result.astype(jnp.bfloat16)
        return result if more is None else jnp.concatenate([result, halves(more, outer, part)])
    if more is None:
        return result + got.astype(jnp.float32)
    below = halves(more, outer, part).astype(jnp.float32) + got[half:].astype(jnp.float32)
    return jnp.concatenate([result + got[:half].astype(jnp.float32), below])


class Scatter:
    def __init__(self, inputs, d_project, more=None):
        self.inputs = inputs
        self.more = more
        self.d_project = d_project
        self.stages = [list(stages[::-1]) for stages in stage_lists()]
        order = [("wide", bit) for bit in high_bits("wide")[::-1]] + [("narrow", bit) for bit in high_bits("narrow")[::-1]]
        self.left = [list(order), list(order)]
        self.total = [None, None]
        self.got = [None, None]
        self.place = [None, None]

    def product(self, n, outer, part, got):
        more = self.more
        if more is not None:
            rows = more.shape[0] // 2
            more = more[n * rows : (n + 1) * rows]
        return product(self.inputs, self.d_project, n, outer, part, more, got)

    def send(self, *which):
        sent = []
        for n in which or range(2):
            axis, bit = self.stages[n].pop(0)
            at = self.left[n].index((axis, bit))
            self.left[n].pop(at)
            outer, mine = 1 << at, side(axis, bit)
            if self.total[n] is None:
                away = self.product(n, outer, 1 - mine, None)
            else:
                away = halves(self.total[n], outer, 1 - mine).astype(jnp.bfloat16)
            self.got[n] = swap(away, axis, bit)
            self.place[n] = (outer, mine)
            sent.append(away)
        return sent

    def add(self, *others):
        for n in range(2):
            outer, mine = self.place[n]
            got = after(self.got[n], *others) if others else self.got[n]
            self.got[n] = None
            if self.total[n] is None:
                self.total[n] = self.product(n, outer, mine, got)
            else:
                self.total[n] = halves(self.total[n], outer, mine) + got.astype(jnp.float32)
        return self.total

    def result(self):
        if self.more is None:
            return jnp.concatenate(self.total)
        rows = self.more.shape[0] // 2
        return jnp.concatenate([part[:-rows] for part in self.total] + [part[-rows:] for part in self.total])


def member_rows(x, count):
    wide, narrow = lax.axis_size("wide"), lax.axis_size("narrow")
    x = x.reshape(wide // 2, 2, narrow // 2, 2, count, x.shape[1]).transpose(1, 3, 0, 2, 4, 5)
    x = jnp.where(side("wide", 1) == 1, x[::-1], x)
    return jnp.where(side("narrow", 1) == 1, x[:, ::-1], x)


def own_rows(x, count, back=False):
    wide, narrow = lax.axis_size("wide"), lax.axis_size("narrow")
    mine = (side("wide", 1), side("narrow", 1))
    if back:
        x = x.reshape(2, 2, wide // 4, narrow // 2, count, x.shape[1])
        x = jnp.where(mine[0] == 1, x[::-1], x)
        x = jnp.where(mine[1] == 1, x[:, ::-1], x)
        return x.transpose(2, 0, 3, 1, 4, 5).reshape(-1, x.shape[5])
    x = x.reshape(wide // 4, 2, narrow // 2, 2, count, x.shape[1]).transpose(1, 3, 0, 2, 4, 5)
    x = jnp.where(mine[0] == 1, x[::-1], x)
    x = jnp.where(mine[1] == 1, x[:, ::-1], x)
    return x.reshape(-1, x.shape[5])


def flip_combinations(bits):
    flips = [0]
    for bit in bits:
        flips = flips + [flip | bit for flip in flips]
    return flips


def scatter_rows(x, axis, bits):
    flips = flip_combinations(bits)
    rows = x.shape[0] // len(flips)
    index = lax.axis_index(axis)

    def share(flip):
        at = sum((((index ^ flip) // bit) % 2) << number for number, bit in enumerate(bits))
        return lax.dynamic_slice_in_dim(x, at * rows, rows, 0)

    got = [swap(share(flip).astype(jnp.bfloat16), axis, flip) for flip in flips[1:]]
    return functools.reduce(jnp.add, [part.astype(jnp.float32) for part in got], share(0))


def join_kernel(at_ref, *refs):
    out_ref = refs[-1]
    for number, part in enumerate(refs[:-1]):
        rows = part.shape[0]
        out_ref[pl.ds(pl.multiple_of(at_ref[number] * rows, 8), rows), :] = part[...]


def gather_rows(x, axis, bits):
    flips = flip_combinations(bits)
    index = lax.axis_index(axis)
    rows = x.shape[0]
    parts = [x] + [swap(x, axis, flip) for flip in flips[1:]]
    at = jnp.stack([sum((((index ^ flip) // bit) % 2) << number for number, bit in enumerate(bits)) for flip in flips])
    if rows % 8:
        out = jnp.zeros((rows * len(flips), x.shape[1]), x.dtype)
        for number, part in enumerate(parts):
            out = lax.dynamic_update_slice_in_dim(out, part, at[number] * rows, 0)
        return out
    return pl.pallas_call(
        join_kernel,
        in_specs=[pl.BlockSpec(memory_space=pltpu.SMEM)] + [NEAR] * len(parts),
        out_specs=NEAR,
        out_shape=jax.ShapeDtypeStruct((rows * len(flips), x.shape[1]), x.dtype),
        compiler_params=pltpu.CompilerParams(vmem_limit_bytes=VMEM_BYTES),
        cost_estimate=LIGHT,
        name="join",
    )(at.astype(jnp.int32), *parts)


def pack_kernel(member_ref, early_ref, late_ref, table_ref, more_table_ref, first_ref, second_ref, given_ref, out_ref):
    at = 0
    for part in (early_ref, late_ref):
        out_ref[at : at + part.shape[0], :] = part[...]
        at += part.shape[0]
    out_ref[at : at + table_ref.shape[0], :] = table_ref[...] + more_table_ref[...]
    at += table_ref.shape[0]
    out_ref[at:, :] = jnp.zeros((out_ref.shape[0] - at, LANES), jnp.float32)
    for part in (first_ref, second_ref):
        rows = part.shape[1] // LANES
        start = pl.multiple_of(at + member_ref[0] * rows, 8)
        for row in range(rows):
            out_ref[pl.ds(start + row, 1), :] = part[0:1, row * LANES : (row + 1) * LANES]
        at += 4 * rows
    out_ref[at : at + given_ref.shape[0], :] = given_ref[...]


def pack(member, early, late, table, more_table, first, second, given, rows):
    return pl.pallas_call(
        pack_kernel,
        in_specs=[pl.BlockSpec(memory_space=pltpu.SMEM)] + [NEAR] * 7,
        out_specs=NEAR,
        out_shape=jax.ShapeDtypeStruct((rows, LANES), jnp.float32),
        compiler_params=pltpu.CompilerParams(vmem_limit_bytes=VMEM_BYTES),
        cost_estimate=LIGHT,
        name="pack",
    )(member.astype(jnp.int32).reshape(1), early, late, table, more_table, first, second, given)


def unpack_kernel(layout, span, table_at, at_ref, summed_ref, *out_refs):
    per = span + 8
    for number, (kernel, leading, filters, natural) in enumerate(layout):
        out_ref = out_refs[kernel - 1]
        height = kernel * 16
        done = 0
        while done < filters:
            block, lane = divmod(natural + done, LANES)
            wide = min(LANES - lane, filters - done)
            out_ref[:, leading + done : leading + done + wide] = summed_ref[
                block * per : block * per + height, lane : lane + wide
            ]
            done += wide
    table_ref, bias_ref = out_refs[7], out_refs[8]
    vocab, emb_width = table_ref.shape
    for number, start in enumerate(range(0, vocab, TABLE_ROWS)):
        rows = min(TABLE_ROWS, vocab - start)
        table_ref[start : start + rows, :] = summed_ref[
            table_at : table_at + rows, number * emb_width : (number + 1) * emb_width
        ]
    for block in range(bias_ref.shape[0]):
        bias_ref[block : block + 1, :] = summed_ref[block * per + span : block * per + span + 1, :]
    for number, out_ref in enumerate(out_refs[9:]):
        out_ref[...] = summed_ref[pl.ds(at_ref[number], 1), :]


def unpack(summed, rows, layout, span, table_at, shapes):
    count = layout[-1][2] + layout[-1][3]
    shapes = shapes + [(count // LANES, LANES)] + [(1, LANES)] * 3
    return pl.pallas_call(
        functools.partial(unpack_kernel, tuple(layout), span, table_at),
        in_specs=[pl.BlockSpec(memory_space=pltpu.SMEM), NEAR],
        out_specs=[NEAR] * len(shapes),
        out_shape=[jax.ShapeDtypeStruct(shape, jnp.float32) for shape in shapes],
        compiler_params=pltpu.CompilerParams(vmem_limit_bytes=VMEM_BYTES),
        cost_estimate=LIGHT,
        name="unpack",
    )(rows.astype(jnp.int32), summed)


def sum_all(x):
    wide = high_bits("wide")
    groups = [wide[i : i + 2] for i in range(0, len(wide), 2)]
    x = scatter_rows(x, "wide", [1])
    for bits in groups:
        x = scatter_rows(x, "wide", bits)
    x = x.astype(jnp.bfloat16)
    sent = x
    parts = [part.astype(jnp.float32) for part in [x] + [swap(x, "narrow", flip) for flip in range(1, lax.axis_size("narrow"))]]
    while len(parts) > 1:
        parts = [parts[i] + parts[i + 1] for i in range(0, len(parts), 2)]
    x = parts[0]
    for bits in groups[::-1]:
        x = gather_rows(x, "wide", bits)
    return gather_rows(x, "wide", [1]), sent


def local(
    char_ids,
    bank_order,
    char_table,
    conv_w1,
    conv_w2,
    conv_w3,
    conv_w4,
    conv_w5,
    conv_w6,
    conv_w7,
    conv_bias,
    highway_w1,
    highway_b1,
    highway_w2,
    highway_b2,
    proj_weight,
    proj_bias,
    cotangent,
):
    feature_count = conv_bias.shape[0]
    tokens, chars = char_ids.shape
    vocab_count, emb_width = char_table.shape
    layout = bank_layout(feature_count // 64)
    weights = (conv_w1, conv_w2, conv_w3, conv_w4, conv_w5, conv_w6, conv_w7)
    wide_size, narrow_size = lax.axis_size("wide"), lax.axis_size("narrow")
    wide, narrow = lax.axis_index("wide"), lax.axis_index("narrow")
    width = highway_w1.shape[1]
    out_part = proj_weight.shape[1]
    members = 4
    blocks = wide_size * narrow_size // members
    own_width = feature_count // members
    mine_wide, mine_narrow = side("wide", 1), side("narrow", 1)
    shape = (members * tokens, feature_count, 2 * own_width)

    starts = bank_starts(bank_order, layout)

    places = column_places(layout, chars)
    low_places = min(places)
    filters = join_filters(weights, layout)
    places_row = jnp.array(places, jnp.float32)
    aux = jnp.pad(
        jnp.stack([conv_bias.astype(jnp.float32) - jnp.log(places_row), places_row]), ((0, 6), (0, 0))
    )
    padded = -(-vocab_count // LANES) * LANES
    table = jnp.pad(
        jnp.tile(char_table, (1, WIDEST)), ((0, padded - vocab_count), (0, LANES - WIDEST * emb_width))
    )
    trips = jnp.array(
        [max(places[start : start + BLOCK]) for start in range(0, feature_count, BLOCK)], jnp.int32
    )
    half_blocks = feature_count // BLOCK // 2
    quarter_blocks = half_blocks // 2
    def conv(blocks_from, count, at, room, onto, *others):
        return conv_forward(
            after(windows, *others) if others else windows,
            filters,
            aux,
            trips,
            low_places,
            places,
            blocks_from,
            count,
            at,
            room,
            onto,
        )

    below = jnp.stack([highway_b1, highway_b2, jnp.pad(proj_bias, (0, width - out_part))])
    below = [jnp.pad(part, ((0, BELOW - part.shape[0]), (0, 0))) for part in (below[:1], below[1:])]
    gather_one = Gather(bank_rows(highway_w1, bank_order, layout, True, below[0]))
    gather_one.send()
    given_along = swap(after(cotangent, gather_one.held), "narrow", 1)
    given_wide = swap(after(cotangent, gather_one.held), "wide", 1)
    gather_two = Gather(jnp.concatenate([own_rows(after(highway_w2, gather_one.held), width), below[1]]))
    windows = make_windows(after(char_ids, gather_one.held), table)
    late = conv(half_blocks, half_blocks, 0, half_blocks, None)
    late_along = swap(late[1], "narrow", 1)
    bundle = after(own_rows(proj_weight, width).T[None], late[1])
    out_stages = list(stage_lists()[0])
    flips = [(0, 0)]

    def out_round(bundle, got, *others):
        if got is not None:
            bundle = jnp.concatenate([bundle, after(got, *others)])
        return bundle, swap(bundle, *out_stages[0])

    bundle, bundle_got = out_round(bundle, None)
    flips = flips + turn(flips, *out_stages.pop(0))
    resolved = list(gather_one.got)
    mark = (late[1],)
    for number in range(1, gather_one.rounds - 1):
        sent = gather_one.send(mark)
        mark = (mark, sent)
    late_wide = swap(late[1], "wide", 1)
    sent_two = gather_two.send(late[1], sent, bundle)
    mid = conv(
        quarter_blocks, half_blocks - quarter_blocks, quarter_blocks, half_blocks, None, late[1], resolved, sent, sent_two, bundle
    )
    resolved = [list(gather_one.got), late_wide, given_along, given_wide]
    bundle, bundle_got = out_round(bundle, bundle_got, mid[1])
    flips = flips + turn(flips, *out_stages.pop(0))
    last = gather_one.send(mid[1], bundle)
    mid_along = swap(mid[1], "narrow", 1)
    late_both = swap(after(late_along, mid[1]), "wide", 1)
    early = conv(0, quarter_blocks, 0, half_blocks, [mid[0], mid[2], mid[3]], mid[1], resolved, last, bundle)
    mark = early[1]
    early_along = swap(early[1], "narrow", 1)
    mid_wide = swap(after(mid[1], mark), "wide", 1)
    early_wide = swap(early[1], "wide", 1)
    late_both = after(late_both, mark)
    mid_both = swap(after(mid_along, mark), "wide", 1)
    while out_stages:
        bundle, bundle_got = out_round(bundle, bundle_got, mark)
        flips = flips + turn(flips, *out_stages.pop(0))
    sent = (mark, last, bundle)
    for number in range(1, gather_two.rounds - 1):
        sent = gather_two.send(sent)
    early_both = swap(after(early_along, mid_both), "wide", 1)
    given_both = swap(after(given_along, mid_both), "wide", 1)

    natural = lax.iota(jnp.int32, feature_count)
    begin = jnp.array([entry[3] for entry in layout], jnp.int32)
    end = jnp.array([entry[3] + entry[2] for entry in layout], jnp.int32)
    inside = (natural[:, None] >= begin[None, :]) & (natural[:, None] < end[None, :])
    shift = jnp.sum(jnp.where(inside, (after(starts, early[1]) - begin)[None, :], 0), axis=1)
    own_at = jnp.arange(own_width, dtype=jnp.int32)
    outer, inner = own_at // (width * (narrow_size // 2)), (own_at // width) % (narrow_size // 2)
    own_feature = ((outer * 2 + mine_wide) * narrow_size + inner * 2 + mine_narrow) * width + own_at % width
    pick = ((natural + shift)[:, None] == own_feature[None, :]).astype(jnp.bfloat16)

    spans = [(half_blocks, half_blocks), (quarter_blocks, half_blocks - quarter_blocks), (0, quarter_blocks)]
    sources = [
        late[1], late_along, late_wide, late_both, mid[1], mid_along, mid_wide, mid_both, early[1], early_along, early_wide, early_both
    ]
    copies = [
        (number * members + by, 0, 0, tokens, count * BLOCK, by * tokens, start * BLOCK)
        for number, (start, count) in enumerate(spans)
        for by in range(members)
    ]
    last_one = list(gather_one.got)
    features, weight_one, proj_one, carried_one, carried_two = layer_one(
        sources, copies, gather_one.result(), after(pick, sent), shape
    )
    hidden_along = swap(carried_two, "narrow", 1)
    resolved = list(gather_two.got)
    sent = gather_two.send(carried_two)
    hidden_wide = swap(carried_two, "wide", 1)
    bundle = jnp.concatenate([bundle, after(bundle_got, carried_two)])
    shares = bundle.reshape(blocks, out_part, members, own_width).transpose(2, 0, 1, 3)
    shares = group_trade([shares[m] for m in range(members)])
    device_at = jnp.stack(
        [
            jnp.stack([(wide ^ (fw | dw)) * narrow_size + (narrow ^ (fn | dn)) for dw, dn in ((0, 0), (0, 1), (1, 0), (1, 1))])
            for fw, fn in flips
        ]
    ).astype(jnp.int32)
    column_at = (device_at[:, :, None] * out_part + lax.iota(jnp.int32, out_part)[None, None, :]).reshape(-1)
    out_order = (column_at[:, None] == lax.iota(jnp.int32, column_at.shape[0])[None, :]).astype(jnp.bfloat16)
    out_weight = jnp.einsum(
        "jn,jf->nf",
        out_order,
        jnp.stack(shares, axis=1).reshape(-1, own_width),
        preferred_element_type=jnp.float32,
    ).astype(jnp.bfloat16)
    givens = [cotangent, given_along, given_wide, given_both]
    hidden_both = swap(hidden_along, "wide", 1)
    copies = [
        (by, (m ^ by) * tokens, 0, tokens, own_width, m * tokens, by * own_width)
        for by in range(members)
        for m in range(members)
    ]
    input_two, weight_two, input_out, d_project, through, sums_two, away = layer_two(
        [carried_two, hidden_along, hidden_wide, hidden_both], copies, gather_two.result(), [out_weight] + givens, shape
    )

    out_bias = weight_two[feature_count + 1].astype(jnp.float32).reshape(wide_size // 2, 1, narrow_size // 2, 1, width)
    out_bias = out_bias[..., :out_part]
    here = (lax.iota(jnp.int32, 2) == mine_wide)[:, None] & (lax.iota(jnp.int32, 2) == mine_narrow)[None, :]
    out_bias = jnp.where(here[None, :, None, :, None], out_bias, 0.0).reshape(-1)

    got = swap(away, "wide", 1)
    scatter_two = Scatter(input_two, d_project)
    sent = scatter_two.send()
    send = keep_two(d_project, weight_two, after(got, sent), 1)
    across = swap(send, "narrow", 1)
    own = keep_two(after(d_project, send), weight_two, got, 0, through)
    input_out = after(input_out, own)
    given = jnp.concatenate(givens)
    grad_out = jnp.einsum("tn,tf->nf", given, input_out, preferred_element_type=jnp.float32).astype(jnp.bfloat16)
    grad_out = member_rows(grad_out, out_part).reshape(members, blocks, out_part, own_width // width, width)
    grad_out = grad_out.transpose(0, 2, 3, 1, 4).reshape(-1, blocks * width)
    encoded = jnp.einsum("tf,nf->tn", input_out, out_weight, preferred_element_type=jnp.float32) + out_bias
    encoded_got = swap(encoded[2 * tokens :].astype(jnp.bfloat16), "wide", 1)
    encoded = encoded[: 2 * tokens]
    scatter_two.add(own, grad_out, encoded)
    sent = scatter_two.send()
    own = after(own, sent, encoded, grad_out)
    d_project, through, sums_one, later, earlier = back_one(own, across, proj_one, carried_one, weight_one, pick)
    later = swap(later, "wide", 1)
    earlier = swap(earlier, "wide", 1)
    scatter_one = Scatter(features, d_project, grad_out)
    sent = scatter_one.send()
    late_own, late_send = keep_one(d_project, through, weight_one, pick, after(later, sent), 1)
    late_got = swap(late_send, "narrow", 1)
    early_own, early_send = keep_one(after(d_project, late_send), through, weight_one, pick, earlier, 0)
    early_got = swap(early_send, "narrow", 1)
    ids_across = jnp.pad(char_ids.T, ((0, -chars % 8), (0, 0)))
    span = WIDEST * emb_width
    resolved = list(scatter_two.got)
    late_filters, late_table = conv_backward(
        [late[0]], [late[2]], [late[3]], late_own, after(late_got, early_send, ids_across, encoded_got, resolved), windows, filters, ids_across, trips, low_places, vocab_count, span, half_blocks
    )
    scatter_one.add(late_table)
    sent = scatter_one.send()
    while scatter_two.stages[0]:
        scatter_two.add(late_table, sent)
        sent_two = scatter_two.send()
    encoded = encoded + after(encoded_got, late_table, sent).astype(jnp.float32)
    encoded_got = swap(encoded[tokens:].astype(jnp.bfloat16), "narrow", 1)
    early_filters, early_table = conv_backward(
        [early[0]], [early[2]], [early[3]], early_own, early_got, after(windows, sent, sent_two, late_table, encoded), filters, ids_across, trips, low_places, vocab_count, span, 0
    )
    resolved = [early_table, list(scatter_one.got), list(scatter_two.got), encoded_got]

    member = mine_wide * 2 + mine_narrow
    own_sums = own_width * 2 // LANES
    ends = [early_filters.shape[0] * early_filters.shape[1]]
    ends.append(ends[-1] + late_filters.shape[0] * late_filters.shape[1])
    ends.append(ends[-1] + TABLE_ROWS)
    ends.append(ends[-1] + members * own_sums)
    ends.append(ends[-1] + members * own_sums)
    unit = 16 * wide_size
    given_sum = jnp.sum(after(cotangent, early[1]).astype(jnp.float32), axis=0).reshape(-1, LANES)
    packed = pack(
        member,
        after(early_filters, resolved).reshape(-1, LANES),
        late_filters.reshape(-1, LANES),
        early_table,
        late_table,
        sums_one,
        sums_two,
        given_sum,
        -(-(ends[-1] + given_sum.shape[0]) // unit) * unit,
    )
    summed, sent = sum_all(packed)
    scatter_one.add(packed)
    scatter_one.total = [after(part, sent) for part in scatter_one.total]
    while scatter_one.stages[0]:
        scatter_one.send()
        scatter_one.add()
    scatter_two.add(sent)
    grad_one_w = scatter_one.result()
    grad_out = grad_one_w[feature_count:].reshape(members, out_part, own_width)
    grad_out = group_trade([grad_out[m] for m in range(members)])
    grad_out = jnp.concatenate(grad_out, axis=1)
    encoded = (encoded[:tokens] + after(encoded_got, packed).astype(jnp.float32)).astype(jnp.bfloat16)
    own_at = (member * blocks + local_block(wide, narrow)) * width
    out_at = (wide * narrow_size + narrow) * out_part
    *grad_weights, d_table, d_bias, own_one, own_two, own_out = unpack(
        summed,
        jnp.stack([ends[2] + own_at // LANES, ends[3] + own_at // LANES, ends[4] + out_at // LANES]),
        layout,
        span,
        ends[1],
        [weight.shape for weight in weights] + [char_table.shape],
    )
    own_one, own_two = (
        lax.dynamic_slice_in_dim(part.reshape(-1), own_at % LANES, width, 0) if width % LANES else part.reshape(-1)
        for part in (own_one, own_two)
    )
    own_out = lax.dynamic_slice_in_dim(own_out.reshape(-1), out_at % LANES, out_part, 0)
    return (
        encoded,
        d_table,
        *grad_weights,
        d_bias.reshape(-1),
        bank_rows(grad_one_w, bank_order, layout, False),
        own_one,
        own_rows(scatter_two.result(), width, True),
        own_two,
        own_rows(grad_out.T, width, True),
        own_out,
    )


def solution(mesh):
    placed = (
        P(("wide", "narrow"), None),
        P(),
        P(),
        P(),
        P(),
        P(),
        P(),
        P(),
        P(),
        P(),
        P(),
        P(None, ("wide", "narrow")),
        P(("wide", "narrow")),
        P(None, ("wide", "narrow")),
        P(("wide", "narrow")),
        P(None, ("wide", "narrow")),
        P(("wide", "narrow")),
        P(("wide", "narrow"), None),
    )
    return jax.shard_map(
        local,
        mesh=mesh,
        in_specs=placed,
        out_specs=(
            P(("wide", "narrow"), None),
            P(),
            P(),
            P(),
            P(),
            P(),
            P(),
            P(),
            P(),
            P(),
            P(None, ("wide", "narrow")),
            P(("wide", "narrow")),
            P(None, ("wide", "narrow")),
            P(("wide", "narrow")),
            P(None, ("wide", "narrow")),
            P(("wide", "narrow")),
        ),
        check_vma=False,
    )
```

time: 923 us -> 440 us (0.48)
  waiting for transfers between devices: 424 us -> 71.2 us
  blocking collectives: 229 us -> 0 us
  Pallas kernels: 105 us -> 192 us
  matrix products: 93.5 us -> 25.1 us
  starting transfers between devices: 0.4 us -> 58.1 us
  other arithmetic: 8.96 us -> 34 us
  local copies, waits for them, and re-layouts: 37.5 us -> 51.9 us
  between operations: 14.7 us -> 2.31 us
    reduce_scatter x4 -> x0, waiting for transfers between devices: 184 us -> none  [local(): part = lax.psum_scatter(part, axis, scatter_dimension=1, tiled=True)]
    all_gather x2 -> x0, blocking collectives: 146 us -> none  [local(): lax.all_gather(part, axes, axis=0, tiled=True)]
    all_gather x3 -> x0, waiting for transfers between devices: 111 us -> none  [local(): lax.all_gather(part, axes, axis=1, tiled=True)]
    unnamed x12 -> x0, waiting for transfers between devices: 88.8 us -> none
    pallas_call x2 -> x19, Pallas kernels: 105 us -> 192 us  [the longest x2 53.1 us: conv_backward(): pl.pallas_call(functools.partial(backward_kernel, chars, low_places, span...]
    ppermute x0 -> x65, waiting for transfers between devices: none -> 71.2 us  [the longest x63 70.7 us: swap(): lax.ppermute(x, axis, [(i, i ^ bit) for i in range(lax.axis_size(axis))])]
    dot_general x10 -> x11, matrix products: 93.5 us -> 25.1 us  [the longest x8 19.5 us: product(): lax.dot_general(inputs[:, number * half:(number + 1) * half], after(halve...]
    ppermute x0 -> x65, starting transfers between devices: none -> 58.1 us  [the longest x63 58 us: swap(): lax.ppermute(x, axis, [(i, i ^ bit) for i in range(lax.axis_size(axis))])]
  transfers between devices with their start and end apart: 10 -> 65, of which waited for: 8 -> 19; matrix products, arithmetic and copies ran while one was open for 14% -> 20% of each run, Pallas kernels for 12% -> 38%
where the time goes in v3:
time: 440 us; the launch traced here: 435 us
  Pallas kernels  192 us (44%)
  waiting for transfers between devices  71.2 us (16%)
  starting transfers between devices  58.1 us (13%)
  local copies, waits for them, and re-layouts  51.9 us (12%)
  other arithmetic  34 us (8%)
  matrix products  25.1 us (6%)
    ppermute x63, waiting for transfers between devices, swap(): lax.ppermute(x, axis, [(i, i ^ bit) for i in range(lax.axis_size(axis))])  70.7 us
    ppermute x63, starting transfers between devices, swap(): lax.ppermute(x, axis, [(i, i ^ bit) for i in range(lax.axis_size(axis))])  58 us
    pallas_call x2, Pallas kernels, conv_backward(): pl.pallas_call(functools.partial(backward_kernel, chars, low_places, span...  53.1 us
    pallas_call x3, Pallas kernels, conv_forward(): pl.pallas_call(functools.partial(kernel, low_places, extras), grid_spec=p...  51.3 us
    pallas_call x2, Pallas kernels, call_layer(): pl.pallas_call(functools.partial(kernel, tuple(x_copies), tuple(w_copies)...  33.7 us
    dot_general x8, matrix products, product(): lax.dot_general(inputs[:, number * half:(number + 1) * half], after(halve...  19.5 us
    unnamed x158, local copies, waits for them, and re-layouts  18.2 us
    pallas_call x2, Pallas kernels, keep_one(): pl.pallas_call(keep_one_kernel, grid=(1,), in_specs=[pl.BlockSpec((2 * ST...  11 us
  transfers between devices with their start and end apart: 65, of which 19 were waited for; matrix products, arithmetic and copies ran while one was open for 20% of the time, Pallas kernels for 38%

profile of v3, /device:TPU:0, one launch (start us, length us, event | category | flops | bytes accessed | tf_op | source)
XLA Modules:
  0.0 435.1 jit_solution(9171715681088945608)
XLA Ops:
  2.0 1.9 bank_rows.2
  4.0 4.0 collective-permute-start.1
  15.5 8.6 %make_windows.1.win_ref.refs_5_ = bf16[50,256,128]{2,1,0:T(8,128)(2,1)} custom-call(s32[256,50]{1,0:T(8,128)} %copy.83.ids_ref, bf16[384,128]{1,0:T(8,128)(2,1)} %pad.56.table_ref), custom_call_target="tpu_custom_call" | custom-call | flops 1 | bytes 1 | tf_op jit(solution)/shard_map/make_windows/pallas_call | solution.py:45
  25.7 21.2 %conv_forward.3 = (bf16[4,50,256,256]{3,2,1,0:T(8,128)(2,1)}, bf16[256,1024]{1,0:T(8,128)(2,1)}, f32[256,1024]{1,0:T(8,128)}, f32[5,256,1024]{2,1,0:T(8,128)}) custom-call(s32[4]{0:T(128)} %broadcast.249.trip_ref, bf16[50,256,128]{2,1,0:T(8,128)(2,1)} %make_windows.1.win_ref.refs_5_, bf16[128,2048]{1,0:T(8,128)(2,1)} %concatenate.80.weight_ref.refs_6_, ...), custom_call_target="tpu_custom_call" | custom-call | flops 1 | bytes 1 | tf_op jit(solution)/shard_map/conv_forward/pallas_call | solution.py:118
  56.6 14.8 %conv_forward.4 = (bf16[4,50,256,256]{3,2,1,0:T(8,128)(2,1)}, bf16[256,512]{1,0:T(8,128)(2,1)}, f32[256,1024]{1,0:T(8,128)}, f32[5,256,1024]{2,1,0:T(8,128)}) custom-call(s32[2]{0:T(128)} %broadcast.250.trip_ref, bf16[50,256,128]{2,1,0:T(8,128)(2,1)} %make_windows.1.win_ref.refs_5_, bf16[128,2048]{1,0:T(8,128)(2,1)} %concatenate.80.weight_ref.refs_6_, ...), custom_call_target="tpu_custom_call" | custom-call | flops 1 | bytes 1 | tf_op jit(solution)/shard_map/conv_forward/pallas_call | solution.py:118
  73.4 2.6 collective-permute-start.9
  80.5 3.2 collective-permute-done.6.refs_1_
  84.5 15.3 %conv_forward.5 = (bf16[4,50,256,256]{3,2,1,0:T(8,128)(2,1)}, bf16[256,512]{1,0:T(8,128)(2,1)}, f32[256,1024]{1,0:T(8,128)}, f32[5,256,1024]{2,1,0:T(8,128)}) custom-call(s32[2]{0:T(128)} %constant.581.trip_ref, bf16[50,256,128]{2,1,0:T(8,128)(2,1)} %make_windows.1.win_ref.refs_5_, ...), custom_call_target="tpu_custom_call", output_to_operand_aliasing={{0}: (4, {}), {2}: (5, {}), {3}: (6, {})} | custom-call | flops 1 | bytes 1 | tf_op jit(solution)/shard_map/conv_forward/pallas_call | solution.py:118
  104.8 4.2 collective-permute-done.15.refs_9_
  115.2 11.8 %collective-permute-done.19.refs_15_ = bf16[4,1040,128]{2,1,0:T(8,128)(2,1)S(1)} collective-permute-done((bf16[4,1040,128]{2,1,0:T(8,128)(2,1)S(1)}, bf16[4,1040,128]{2,1,0:T(8,128)(2,1)S(1)}, u32[]{:S(2)}, u32[]{:S(2)}) %collective-permute-start.19) | collective-permute-done | bytes 1064992 | tf_op jit(solution)/shard_map/ppermute | solution.py:383
  127.9 2.8 collective-permute-done.18.refs_13_
  130.7 16.1 %layer_one.1 = (bf16[1024,2048]{1,0:T(8,128)(2,1)}, bf16[2080,1024]{1,0:T(8,128)(2,1)}, f32[1024,1024]{1,0:T(8,128)}, bf16[1024,512]{1,0:T(8,128)(2,1)}, bf16[1024,512]{1,0:T(8,128)(2,1)}) custom-call(s32[16]{0:T(128)} %stack.312.at_ref, bf16[2048,512]{1,0:T(8,128)(2,1)} %compare_convert_fusion.pick_ref.pick_far, ...), custom_call_target="tpu_custom_call" | custom-call | flops 1 | bytes 1 | tf_op jit(solution)/shard_map/layer_one/pallas_call | solution.py:533
  146.8 1.9 collective-permute-start.24
  153.6 2.0 collective-permute-start.30
  155.7 17.5 %collective-permute-done.24.refs_5_ = bf16[1024,512]{1,0:T(8,128)(2,1)} collective-permute-done((bf16[1024,512]{1,0:T(8,128)(2,1)}, bf16[1024,512]{1,0:T(8,128)(2,1)}, u32[]{:S(2)}, u32[]{:S(2)}) %collective-permute-start.24) | collective-permute-done | bytes 1048608 | tf_op jit(solution)/shard_map/ppermute | solution.py:383
  178.3 3.9 collective-permute-done.20
  185.7 17.5 %layer_two.1 = (bf16[1024,2048]{1,0:T(8,128)(2,1)}, bf16[2080,1024]{1,0:T(8,128)(2,1)}, bf16[1024,512]{1,0:T(8,128)(2,1)}, bf16[1024,1024]{1,0:T(8,128)(2,1)}, f...) custom-call(s32[16]{0:T(128)} %stack.312.at_ref, ...), custom_call_target="tpu_custom_call" | custom-call | flops 1 | bytes 1 | tf_op jit(solution)/shard_map/layer_two/pallas_call | solution.py:533
  209.1 2.3 fusion.27
  211.4 2.0 collective-permute-start.34
  213.6 2.8 fusion.24
  218.2 5.0 %keep_two.2 = bf16[1024,512]{1,0:T(8,128)(2,1)} custom-call(bf16[1024,1024]{1,0:T(8,128)(2,1)} %get-tuple-element.150.d_project_ref, bf16[2080,1024]{1,0:T(8,128)(2,1)} %get-tuple-element.146.w_ref, bf16[1024,1024]{1,0:T(8,128)(2,1)} %copy-done.4), custom_call_target="tpu_custom_call" | custom-call | flops 1 | bytes 1 | tf_op jit(solution)/shard_map/keep_two/pallas_call | solution.py:615
  224.9 5.9 %keep_two.3.own_ref = f32[1024,512]{1,0:T(8,128)} custom-call(bf16[1024,1024]{1,0:T(8,128)(2,1)} %get-tuple-element.150.d_project_ref, bf16[2080,1024]{1,0:T(8,128)(2,1)} %get-tuple-element.146.w_ref, bf16[1024,1024]{1,0:T(8,128)(2,1)} %copy-done.4, f32[1024,512]{1,0:T(8,128)} %get-tuple-element.151.refs_0_), custom_call_target="tpu_custom_call" | custom-call | flops 1 | bytes 1 | tf_op jit(solution)/shard_map/keep_two/pallas_call | solution.py:615
  230.8 2.0 convolution_convert_fusion.1
  233.3 2.2 convolution_add_fusion
  237.7 3.3 convert_add_fusion.2
  243.6 2.5 convert_add_fusion.3
  249.9 10.9 %back_one.1 = (bf16[1024,1024]{1,0:T(8,128)(2,1)}, bf16[1024,512]{1,0:T(8,128)(2,1)}, f32[8,1024]{1,0:T(8,128)}, bf16[512,1024]{1,0:T(8,128)(2,1)}, bf16[512,1024]{1,0:T(8,128)(2,1)}) custom-call(f32[1024,512]{1,0:T(8,128)} %keep_two.3.own_ref, bf16[1024,512]{1,0:T(8,128)(2,1)} %copy-done.28, f32[1024,1024]{1,0:T(8,128)} %get-tuple-element.159.project_ref, ...), custom_call_target="tpu_custom_call" | custom-call | flops 1 | bytes 1 | tf_op jit(solution)/shard_map/back_one/pallas_call | solution.py:663
  261.4 1.8 constant_dynamic-slice_fusion.4
  266.7 2.0 collective-permute-start.42
  271.4 5.5 %keep_one.2 = (f32[256,1024]{1,0:T(8,128)}, bf16[256,1024]{1,0:T(8,128)(2,1)}) custom-call(bf16[1024,1024]{1,0:T(8,128)(2,1)} %get-tuple-element.169.d_project_ref, bf16[1024,512]{1,0:T(8,128)(2,1)} %get-tuple-element.163.through_ref, bf16[2080,1024]{1,0:T(8,128)(2,1)} %get-tuple-element.161.w_far.w_ref, ...), custom_call_target="tpu_custom_call" | custom-call | flops 1 | bytes 1 | tf_op jit(solution)/shard_map/keep_one/pallas_call | solution.py:695
  282.0 5.5 %keep_one.3 = (f32[256,1024]{1,0:T(8,128)}, bf16[256,1024]{1,0:T(8,128)(2,1)}) custom-call(bf16[1024,1024]{1,0:T(8,128)(2,1)} %get-tuple-element.169.d_project_ref, bf16[1024,512]{1,0:T(8,128)(2,1)} %get-tuple-element.163.through_ref, bf16[2080,1024]{1,0:T(8,128)(2,1)} %get-tuple-element.161.w_far.w_ref, ...), custom_call_target="tpu_custom_call" | custom-call | flops 1 | bytes 1 | tf_op jit(solution)/shard_map/keep_one/pallas_call | solution.py:695
  288.2 3.7 collective-permute-done.37.refs_4_
  291.9 25.6 %conv_backward.2 = (f32[8,120,128]{2,1,0:T(8,128)}, f32[40,128]{1,0:T(8,128)}) custom-call(s32[4]{0:T(128)} %broadcast.249.trip_ref, bf16[4,50,256,256]{3,2,1,0:T(8,128)(2,1)} %get-tuple-element.153.refs_0_, f32[256,1024]{1,0:T(8,128)} %get-tuple-element.154.refs_1_, f32[5,256,1024]{2,1,0:T(8,128)} %get-tuple-element.155.refs_2_, ...), custom_call_target="tpu_custom_call" | custom-call | flops 1 | bytes 1 | tf_op jit(solution)/shard_map/conv_backward/pallas_call | solution.py:263
  318.5 3.6 convert_add_fusion
  324.5 2.5 convert_add_fusion.1
  339.2 2.9 collective-permute-start.47
  344.0 27.4 %conv_backward.3 = (f32[8,120,128]{2,1,0:T(8,128)}, f32[40,128]{1,0:T(8,128)}) custom-call(s32[4]{0:T(128)} %constant.583.trip_ref, bf16[4,50,256,256]{3,2,1,0:T(8,128)(2,1)} %get-tuple-element.177.refs_0_, f32[256,1024]{1,0:T(8,128)} %get-tuple-element.178.refs_1_, f32[5,256,1024]{2,1,0:T(8,128)} %get-tuple-element.179.refs_2_, ...), custom_call_target="tpu_custom_call" | custom-call | flops 1 | bytes 1 | tf_op jit(solution)/shard_map/conv_backward/pallas_call | solution.py:263
  372.4 2.3 pack.1
  385.8 2.0 collective-permute-start.54
  391.9 1.9 collective-permute-done.54
  398.6 2.4 collective-permute-done.58.refs_3_
  402.8 1.9 join.2.refs_0_
  404.7 8.4 %collective-permute-done.61 = bf16[1152,128]{1,0:T(8,128)(2,1)S(1)} collective-permute-done((bf16[1152,128]{1,0:T(8,128)(2,1)S(1)}, bf16[1152,128]{1,0:T(8,128)(2,1)S(1)}, u32[]{:S(2)}, u32[]{:S(2)}) %collective-permute-start.61) | collective-permute-done | bytes 294944 | tf_op jit(solution)/shard_map/ppermute | solution.py:383
  413.3 5.6 %collective-permute-done.60 = bf16[1152,128]{1,0:T(8,128)(2,1)} collective-permute-done((bf16[1152,128]{1,0:T(8,128)(2,1)S(1)}, bf16[1152,128]{1,0:T(8,128)(2,1)}, u32[]{:S(2)}, u32[]{:S(2)}) %collective-permute-start.60) | collective-permute-done | bytes 294944 | tf_op jit(solution)/shard_map/ppermute | solution.py:383
  420.1 2.0 collective-permute-start.62
  423.3 2.4 bank_rows.3
  426.9 2.3 join.3.summed_ref
  429.9 2.2 unpack.1
  (415 shorter events, 130.3 us)
Async XLA Ops:
  4.0 48.8 %collective-permute-start.1 = (bf16[2080,128]{1,0:T(8,128)(2,1)}, bf16[2080,128]{1,0:T(8,128)(2,1)S(1)}, u32[]{:S(2)}, u32[]{:S(2)}) collective-permute-start(bf16[2080,128]{1,0:T(8,128)(2,1)} %bank_rows.2), channel_id=1, source_target_pairs={{0,2},{1,3},{2,0},{3,1},{4,6},{5,7},{6,4},{7,5},{8,10},{9,11},{10,... | collective-permute-start | bytes 1597448 | tf_op jit(solution)/shard_map/ppermute | solution.py:383
  8.0 69.8 %collective-permute-start.7 = (bf16[256,512]{1,0:T(8,128)(2,1)}, bf16[256,512]{1,0:T(8,128)(2,1)}, u32[]{:S(2)}, u32[]{:S(2)}) collective-permute-start(bf16[256,512]{1,0:T(8,128)(2,1)} %refs_0_.1), channel_id=1, source_target_pairs={{0,4},{4,0},{8,12},{12,8},{16,20},{20,16},{24,28},{28,24},{1,5},{5... | collective-permute-start | bytes 786440 | tf_op jit(solution)/shard_map/ppermute | solution.py:383
  46.9 24.4 %collective-permute-start.10 = (bf16[256,1024]{1,0:T(8,128)(2,1)}, bf16[256,1024]{1,0:T(8,128)(2,1)}, u32[]{:S(2)}, u32[]{:S(2)}) collective-permute-start(bf16[256,1024]{1,0:T(8,128)(2,1)} %get-tuple-element.114.refs_0_), channel_id=1, source_target_pairs={{0,1},{1,0},{2,3},{3,2},{4,5},{5,4},{6,7},{7,6},{8,9},{9,8},{10,11... | collective-permute-start | bytes 1572872 | tf_op jit(solution)/shard_map/ppermute | solution.py:383
  48.8 23.1 %collective-permute-start = (bf16[1,16,2048]{2,1,0:T(8,128)(2,1)S(1)}, bf16[1,16,2048]{2,1,0:T(8,128)(2,1)}, u32[]{:S(2)}, u32[]{:S(2)}) collective-permute-start(bf16[1,16,2048]{2,1,0:T(8,128)(2,1)S(1)} %bitcast.205), channel_id=1, source_target_pairs={{0,2},{1,3},{2,0},{3,1},{4,6},{5,7},{6,4},{7,5},{8,10},{9,11},{10,... | collective-permute-start | bytes 196616 | tf_op jit(solution)/shard_map/ppermute | solution.py:383
  52.9 20.5 %collective-permute-start.3 = (bf16[2,1040,128]{2,1,0:T(8,128)(2,1)S(1)}, bf16[2,1040,128]{2,1,0:T(8,128)(2,1)S(1)}, u32[]{:S(2)}, u32[]{:S(2)}) collective-permute-start(bf16[2,1040,128]{2,1,0:T(8,128)(2,1)S(1)} %pad_maximum_fusion.11), channel_id=1, source_target_pairs={{0,8},{4,12},{8,0},{12,4},{16,24},{20,28},{24,16},{28,20},{1,9},{5... | collective-permute-start | bytes 1597448 | tf_op jit(solution)/shard_map/ppermute | solution.py:383
  54.5 22.7 %collective-permute-start.4 = (bf16[2,1040,128]{2,1,0:T(8,128)(2,1)S(1)}, bf16[2,1040,128]{2,1,0:T(8,128)(2,1)}, u32[]{:S(2)}, u32[]{:S(2)}) collective-permute-start(bf16[2,1040,128]{2,1,0:T(8,128)(2,1)S(1)} %pad_maximum_fusion.12), channel_id=1, source_target_pairs={{0,16},{4,20},{8,24},{12,28},{16,0},{20,4},{24,8},{28,12},{1,17},{... | collective-permute-start | bytes 1597448 | tf_op jit(solution)/shard_map/ppermute | solution.py:383
  71.4 12.4 %collective-permute-start.6 = (bf16[256,512]{1,0:T(8,128)(2,1)S(1)}, bf16[256,512]{1,0:T(8,128)(2,1)S(1)}, u32[]{:S(2)}, u32[]{:S(2)}) collective-permute-start(bf16[256,512]{1,0:T(8,128)(2,1)S(1)} %copy-done.31), channel_id=1, source_target_pairs={{0,1},{1,0},{2,3},{3,2},{4,5},{5,4},{6,7},{7,6},{8,9},{9,8},{10,11... | collective-permute-start | bytes 786440 | tf_op jit(solution)/shard_map/ppermute | solution.py:383
  71.9 12.6 %collective-permute-start.5 = (bf16[256,1024]{1,0:T(8,128)(2,1)}, bf16[256,1024]{1,0:T(8,128)(2,1)}, u32[]{:S(2)}, u32[]{:S(2)}) collective-permute-start(bf16[256,1024]{1,0:T(8,128)(2,1)} %get-tuple-element.114.refs_0_), channel_id=1, source_target_pairs={{0,4},{4,0},{8,12},{12,8},{16,20},{20,16},{24,28},{28,24},{1,5},{5... | collective-permute-start | bytes 1572872 | tf_op jit(solution)/shard_map/ppermute | solution.py:383
  73.4 28.8 %collective-permute-start.9 = (bf16[2080,128]{1,0:T(8,128)(2,1)S(1)}, bf16[2080,128]{1,0:T(8,128)(2,1)}, u32[]{:S(2)}, u32[]{:S(2)}) collective-permute-start(bf16[2080,128]{1,0:T(8,128)(2,1)S(1)} %pad_maximum_fusion.13), channel_id=1, source_target_pairs={{0,2},{1,3},{2,0},{3,1},{4,6},{5,7},{6,4},{7,5},{8,10},{9,11},{10,... | collective-permute-start | bytes 1597448 | tf_op jit(solution)/shard_map/ppermute | solution.py:383
  77.2 23.4 %collective-permute-start.2 = (bf16[2,16,2048]{2,1,0:T(8,128)(2,1)}, bf16[2,16,2048]{2,1,0:T(8,128)(2,1)}, u32[]{:S(2)}, u32[]{:S(2)}) collective-permute-start(bf16[2,16,2048]{2,1,0:T(8,128)(2,1)} %get-tuple-element.315), channel_id=1, source_target_pairs={{0,8},{4,12},{8,0},{12,4},{16,24},{20,28},{24,16},{28,20},{1,9},{5... | collective-permute-start | bytes 393224 | tf_op jit(solution)/shard_map/ppermute | solution.py:383
  77.8 22.8 %collective-permute-start.12 = (bf16[256,512]{1,0:T(8,128)(2,1)}, bf16[256,512]{1,0:T(8,128)(2,1)}, u32[]{:S(2)}, u32[]{:S(2)}) collective-permute-start(bf16[256,512]{1,0:T(8,128)(2,1)} %get-tuple-element.136.refs_4_), channel_id=1, source_target_pairs={{0,1},{1,0},{2,3},{3,2},{4,5},{5,4},{6,7},{7,6},{8,9},{9,8},{10,11... | collective-permute-start | bytes 786440 | tf_op jit(solution)/shard_map/ppermute | solution.py:383
  84.5 25.5 %collective-permute-start.11 = (bf16[256,1024]{1,0:T(8,128)(2,1)}, bf16[256,1024]{1,0:T(8,128)(2,1)}, u32[]{:S(2)}, u32[]{:S(2)}) collective-permute-start(bf16[256,1024]{1,0:T(8,128)(2,1)} %collective-permute-done.10.refs_1_), channel_id=1, source_target_pairs={{0,4},{4,0},{8,12},{12,8},{16,20},{20,16},{24,28},{28,24},{1,5},{5... | collective-permute-start | bytes 1572872 | tf_op jit(solution)/shard_map/ppermute | solution.py:383
  99.8 11.0 %collective-permute-start.16 = (bf16[256,512]{1,0:T(8,128)(2,1)}, bf16[256,512]{1,0:T(8,128)(2,1)S(1)}, u32[]{:S(2)}, u32[]{:S(2)}) collective-permute-start(bf16[256,512]{1,0:T(8,128)(2,1)} %get-tuple-element.129.refs_8_), channel_id=1, source_target_pairs={{0,4},{4,0},{8,12},{12,8},{16,20},{20,16},{24,28},{28,24},{1,5},{5... | collective-permute-start | bytes 786440 | tf_op jit(solution)/shard_map/ppermute | solution.py:383
  100.5 8.5 %collective-permute-start.15 = (bf16[256,512]{1,0:T(8,128)(2,1)}, bf16[256,512]{1,0:T(8,128)(2,1)S(1)}, u32[]{:S(2)}, u32[]{:S(2)}) collective-permute-start(bf16[256,512]{1,0:T(8,128)(2,1)} %get-tuple-element.129.refs_8_), channel_id=1, source_target_pairs={{0,1},{1,0},{2,3},{3,2},{4,5},{5,4},{6,7},{7,6},{8,9},{9,8},{10,11... | collective-permute-start | bytes 786440 | tf_op jit(solution)/shard_map/ppermute | solution.py:383
  100.5 26.4 %collective-permute-start.19 = (bf16[4,1040,128]{2,1,0:T(8,128)(2,1)S(1)}, bf16[4,1040,128]{2,1,0:T(8,128)(2,1)S(1)}, u32[]{:S(2)}, u32[]{:S(2)}) collective-permute-start(bf16[4,1040,128]{2,1,0:T(8,128)(2,1)S(1)} %pad_maximum_fusion.3.refs_14_), channel_id=1, source_target_pairs={{0,8},{4,12},{8,0},{12,4},{16,24},{20,28},{24,16},{28,20},{1,9},{5... | collective-permute-start | bytes 3194888 | tf_op jit(solution)/shard_map/ppermute | solution.py:383
  104.2 26.5 %collective-permute-start.18 = (bf16[4,1040,128]{2,1,0:T(8,128)(2,1)S(1)}, bf16[4,1040,128]{2,1,0:T(8,128)(2,1)}, u32[]{:S(2)}, u32[]{:S(2)}) collective-permute-start(bf16[4,1040,128]{2,1,0:T(8,128)(2,1)S(1)} %pad_maximum_fusion.2.refs_12_), channel_id=1, source_target_pairs={{0,16},{4,20},{8,24},{12,28},{16,0},{20,4},{24,8},{28,12},{1,17},{... | collective-permute-start | bytes 3194888 | tf_op jit(solution)/shard_map/ppermute | solution.py:383
  110.8 38.0 %collective-permute-start.27 = (bf16[2,1040,128]{2,1,0:T(8,128)(2,1)}, bf16[2,1040,128]{2,1,0:T(8,128)(2,1)}, u32[]{:S(2)}, u32[]{:S(2)}) collective-permute-start(bf16[2,1040,128]{2,1,0:T(8,128)(2,1)} %pad_maximum_fusion.14), channel_id=1, source_target_pairs={{0,8},{4,12},{8,0},{12,4},{16,24},{20,28},{24,16},{28,20},{1,9},{5... | collective-permute-start | bytes 1597448 | tf_op jit(solution)/shard_map/ppermute | solution.py:383
  110.8 38.0 %collective-permute-start.29 = (bf16[2,1040,128]{2,1,0:T(8,128)(2,1)}, bf16[2,1040,128]{2,1,0:T(8,128)(2,1)}, u32[]{:S(2)}, u32[]{:S(2)}) collective-permute-start(bf16[2,1040,128]{2,1,0:T(8,128)(2,1)} %pad_maximum_fusion.15), channel_id=1, source_target_pairs={{0,16},{4,20},{8,24},{12,28},{16,0},{20,4},{24,8},{28,12},{1,17},{... | collective-permute-start | bytes 1597448 | tf_op jit(solution)/shard_map/ppermute | solution.py:383
  112.3 36.5 %collective-permute-start.8 = (bf16[4,16,2048]{2,1,0:T(8,128)(2,1)}, bf16[4,16,2048]{2,1,0:T(8,128)(2,1)S(1)}, u32[]{:S(2)}, u32[]{:S(2)}) collective-permute-start(bf16[4,16,2048]{2,1,0:T(8,128)(2,1)} %constant_dynamic-update-slice_fusion.2), channel_id=1, source_target_pairs={{0,16},{4,20},{8,24},{12,28},{16,0},{20,4},{24,8},{28,12},{1,17},{... | collective-permute-start | bytes 786440 | tf_op jit(solution)/shard_map/ppermute | solution.py:383
  146.8 26.3 %collective-permute-start.24 = (bf16[1024,512]{1,0:T(8,128)(2,1)}, bf16[1024,512]{1,0:T(8,128)(2,1)}, u32[]{:S(2)}, u32[]{:S(2)}) collective-permute-start(bf16[1024,512]{1,0:T(8,128)(2,1)} %get-tuple-element.139.refs_4_), channel_id=1, source_target_pairs={{0,1},{1,0},{2,3},{3,2},{4,5},{5,4},{6,7},{7,6},{8,9},{9,8},{10,11... | collective-permute-start | bytes 3145736 | tf_op jit(solution)/shard_map/ppermute | solution.py:383
  150.6 23.2 %collective-permute-start.22 = (bf16[8,16,512]{2,1,0:T(8,128)(2,1)}, bf16[8,16,512]{2,1,0:T(8,128)(2,1)S(1)}, u32[]{:S(2)}, u32[]{:S(2)}) collective-permute-start(bf16[8,16,512]{2,1,0:T(8,128)(2,1)} %get-tuple-element.306), channel_id=1, source_target_pairs={{0,5},{1,4},{2,7},{3,6},{4,1},{5,0},{6,3},{7,2},{8,13},{9,12},{10,... | collective-permute-start | bytes 393224 | tf_op jit(solution)/shard_map/ppermute | solution.py:389
  151.8 32.9 %collective-permute-start.28 = (bf16[4,1040,128]{2,1,0:T(8,128)(2,1)S(1)}, bf16[4,1040,128]{2,1,0:T(8,128)(2,1)}, u32[]{:S(2)}, u32[]{:S(2)}) collective-permute-start(bf16[4,1040,128]{2,1,0:T(8,128)(2,1)S(1)} %pad_maximum_fusion.4.refs_8_), channel_id=1, source_target_pairs={{0,16},{4,20},{8,24},{12,28},{16,0},{20,4},{24,8},{28,12},{1,17},{... | collective-permute-start | bytes 3194888 | tf_op jit(solution)/shard_map/ppermute | solution.py:383
  153.6 31.1 %collective-permute-start.30 = (bf16[4,1040,128]{2,1,0:T(8,128)(2,1)S(1)}, bf16[4,1040,128]{2,1,0:T(8,128)(2,1)S(1)}, u32[]{:S(2)}, u32[]{:S(2)}) collective-permute-start(bf16[4,1040,128]{2,1,0:T(8,128)(2,1)S(1)} %pad_maximum_fusion.5.refs_10_), channel_id=1, source_target_pairs={{0,8},{4,12},{8,0},{12,4},{16,24},{20,28},{24,16},{28,20},{1,9},{5... | collective-permute-start | bytes 3194888 | tf_op jit(solution)/shard_map/ppermute | solution.py:383
  155.6 29.0 %collective-permute-start.25 = (bf16[1024,512]{1,0:T(8,128)(2,1)}, bf16[1024,512]{1,0:T(8,128)(2,1)}, u32[]{:S(2)}, u32[]{:S(2)}) collective-permute-start(bf16[1024,512]{1,0:T(8,128)(2,1)} %get-tuple-element.139.refs_4_), channel_id=1, source_target_pairs={{0,4},{4,0},{8,12},{12,8},{16,20},{20,16},{24,28},{28,24},{1,5},{5... | collective-permute-start | bytes 3145736 | tf_op jit(solution)/shard_map/ppermute | solution.py:383
  173.2 11.5 %collective-permute-start.26 = (bf16[1024,512]{1,0:T(8,128)(2,1)}, bf16[1024,512]{1,0:T(8,128)(2,1)}, u32[]{:S(2)}, u32[]{:S(2)}) collective-permute-start(bf16[1024,512]{1,0:T(8,128)(2,1)} %collective-permute-done.24.refs_5_), channel_id=1, source_target_pairs={{0,4},{4,0},{8,12},{12,8},{16,20},{20,16},{24,28},{28,24},{1,5},{5... | collective-permute-start | bytes 3145736 | tf_op jit(solution)/shard_map/ppermute | solution.py:383
  203.3 13.6 %collective-permute-start.31 = (bf16[1024,1024]{1,0:T(8,128)(2,1)}, bf16[1024,1024]{1,0:T(8,128)(2,1)S(1)}, u32[]{:S(2)}, u32[]{:S(2)}) collective-permute-start(bf16[1024,1024]{1,0:T(8,128)(2,1)} %get-tuple-element.147), channel_id=1, source_target_pairs={{0,4},{4,0},{8,12},{12,8},{16,20},{20,16},{24,28},{28,24},{1,5},{5... | collective-permute-start | bytes 6291464 | tf_op jit(solution)/shard_map/ppermute | solution.py:383
  211.4 26.4 %collective-permute-start.34 = (bf16[1024,512]{1,0:T(8,128)(2,1)}, bf16[1024,512]{1,0:T(8,128)(2,1)}, u32[]{:S(2)}, u32[]{:S(2)}) collective-permute-start(bf16[1024,512]{1,0:T(8,128)(2,1)} %fusion.27), channel_id=1, source_target_pairs={{0,8},{4,12},{8,0},{12,4},{16,24},{20,28},{24,16},{28,20},{1,9},{5... | collective-permute-start | bytes 3145736 | tf_op jit(solution)/shard_map/ppermute | solution.py:383
  216.3 25.7 %collective-permute-start.33 = (bf16[1024,512]{1,0:T(8,128)(2,1)}, bf16[1024,512]{1,0:T(8,128)(2,1)}, u32[]{:S(2)}, u32[]{:S(2)}) collective-permute-start(bf16[1024,512]{1,0:T(8,128)(2,1)} %fusion.24), channel_id=1, source_target_pairs={{0,16},{4,20},{8,24},{12,28},{16,0},{20,4},{24,8},{28,12},{1,17},{... | collective-permute-start | bytes 3145736 | tf_op jit(solution)/shard_map/ppermute | solution.py:383
  223.2 25.7 %collective-permute-start.35 = (bf16[1024,512]{1,0:T(8,128)(2,1)}, bf16[1024,512]{1,0:T(8,128)(2,1)S(1)}, u32[]{:S(2)}, u32[]{:S(2)}) collective-permute-start(bf16[1024,512]{1,0:T(8,128)(2,1)} %keep_two.2), channel_id=1, source_target_pairs={{0,1},{1,0},{2,3},{3,2},{4,5},{5,4},{6,7},{7,6},{8,9},{9,8},{10,11... | collective-permute-start | bytes 3145736 | tf_op jit(solution)/shard_map/ppermute | solution.py:383
  242.0 34.8 %collective-permute-start.40 = (bf16[1024,256]{1,0:T(8,128)(2,1)}, bf16[1024,256]{1,0:T(8,128)(2,1)}, u32[]{:S(2)}, u32[]{:S(2)}) collective-permute-start(bf16[1024,256]{1,0:T(8,128)(2,1)} %dynamic-slice_convert_fusion), channel_id=1, source_target_pairs={{0,16},{4,20},{8,24},{12,28},{16,0},{20,4},{24,8},{28,12},{1,17},{... | collective-permute-start | bytes 1572872 | tf_op jit(solution)/shard_map/ppermute | solution.py:383
  247.1 40.4 %collective-permute-start.39 = (bf16[1024,256]{1,0:T(8,128)(2,1)}, bf16[1024,256]{1,0:T(8,128)(2,1)}, u32[]{:S(2)}, u32[]{:S(2)}) collective-permute-start(bf16[1024,256]{1,0:T(8,128)(2,1)} %dynamic-slice_convert_fusion.1), channel_id=1, source_target_pairs={{0,8},{4,12},{8,0},{12,4},{16,24},{20,28},{24,16},{28,20},{1,9},{5... | collective-permute-start | bytes 1572872 | tf_op jit(solution)/shard_map/ppermute | solution.py:383
  260.8 10.4 %collective-permute-start.36 = (bf16[512,1024]{1,0:T(8,128)(2,1)}, bf16[512,1024]{1,0:T(8,128)(2,1)}, u32[]{:S(2)}, u32[]{:S(2)}) collective-permute-start(bf16[512,1024]{1,0:T(8,128)(2,1)} %get-tuple-element.164), channel_id=1, source_target_pairs={{0,4},{4,0},{8,12},{12,8},{16,20},{20,16},{24,28},{28,24},{1,5},{5... | collective-permute-start | bytes 3145736 | tf_op jit(solution)/shard_map/ppermute | solution.py:383
  260.9 17.9 %collective-permute-start.38 = (bf16[512,1024]{1,0:T(8,128)(2,1)}, bf16[512,1024]{1,0:T(8,128)(2,1)S(1)}, u32[]{:S(2)}, u32[]{:S(2)}) collective-permute-start(bf16[512,1024]{1,0:T(8,128)(2,1)} %get-tuple-element.170), channel_id=1, source_target_pairs={{0,4},{4,0},{8,12},{12,8},{16,20},{20,16},{24,28},{28,24},{1,5},{5... | collective-permute-start | bytes 3145736 | tf_op jit(solution)/shard_map/ppermute | solution.py:383
  266.7 50.8 %collective-permute-start.42 = (bf16[1152,512]{1,0:T(8,128)(2,1)}, bf16[1152,512]{1,0:T(8,128)(2,1)}, u32[]{:S(2)}, u32[]{:S(2)}) collective-permute-start(bf16[1152,512]{1,0:T(8,128)(2,1)} %maximum_maximum_fusion), channel_id=1, source_target_pairs={{0,8},{4,12},{8,0},{12,4},{16,24},{20,28},{24,16},{28,20},{1,9},{5... | collective-permute-start | bytes 3538952 | tf_op jit(solution)/shard_map/ppermute | solution.py:383
  271.3 16.9 %collective-permute-start.32 = (bf16[512,512]{1,0:T(8,128)(2,1)}, bf16[512,512]{1,0:T(8,128)(2,1)}, u32[]{:S(2)}, u32[]{:S(2)}) collective-permute-start(bf16[512,512]{1,0:T(8,128)(2,1)} %fusion.77), channel_id=1, source_target_pairs={{0,4},{4,0},{8,12},{12,8},{16,20},{20,16},{24,28},{28,24},{1,5},{5... | collective-permute-start | bytes 1572872 | tf_op jit(solution)/shard_map/ppermute | solution.py:383
  276.8 15.0 %collective-permute-start.37 = (bf16[256,1024]{1,0:T(8,128)(2,1)}, bf16[256,1024]{1,0:T(8,128)(2,1)}, u32[]{:S(2)}, u32[]{:S(2)}) collective-permute-start(bf16[256,1024]{1,0:T(8,128)(2,1)} %get-tuple-element.168), channel_id=1, source_target_pairs={{0,1},{1,0},{2,3},{3,2},{4,5},{5,4},{6,7},{7,6},{8,9},{9,8},{10,11... | collective-permute-start | bytes 1572872 | tf_op jit(solution)/shard_map/ppermute | solution.py:383
  278.8 44.8 %collective-permute-start.41 = (bf16[1152,512]{1,0:T(8,128)(2,1)S(1)}, bf16[1152,512]{1,0:T(8,128)(2,1)}, u32[]{:S(2)}, u32[]{:S(2)}) collective-permute-start(bf16[1152,512]{1,0:T(8,128)(2,1)S(1)} %pad_maximum_fusion), channel_id=1, source_target_pairs={{0,16},{4,20},{8,24},{12,28},{16,0},{20,4},{24,8},{28,12},{1,17},{... | collective-permute-start | bytes 3538952 | tf_op jit(solution)/shard_map/ppermute | solution.py:383
  287.5 51.7 %collective-permute-start.44 = (bf16[256,1024]{1,0:T(8,128)(2,1)}, bf16[256,1024]{1,0:T(8,128)(2,1)}, u32[]{:S(2)}, u32[]{:S(2)}) collective-permute-start(bf16[256,1024]{1,0:T(8,128)(2,1)} %get-tuple-element.171), channel_id=1, source_target_pairs={{0,1},{1,0},{2,3},{3,2},{4,5},{5,4},{6,7},{7,6},{8,9},{9,8},{10,11... | collective-permute-start | bytes 1572872 | tf_op jit(solution)/shard_map/ppermute | solution.py:383
  323.0 48.5 %collective-permute-start.46 = (bf16[1152,256]{1,0:T(8,128)(2,1)}, bf16[1152,256]{1,0:T(8,128)(2,1)}, u32[]{:S(2)}, u32[]{:S(2)}) collective-permute-start(bf16[1152,256]{1,0:T(8,128)(2,1)} %fusion.39), channel_id=1, source_target_pairs={{0,16},{4,20},{8,24},{12,28},{16,0},{20,4},{24,8},{28,12},{1,17},{... | collective-permute-start | bytes 1769480 | tf_op jit(solution)/shard_map/ppermute | solution.py:383
  328.0 43.5 %collective-permute-start.45 = (bf16[1152,256]{1,0:T(8,128)(2,1)}, bf16[1152,256]{1,0:T(8,128)(2,1)S(1)}, u32[]{:S(2)}, u32[]{:S(2)}) collective-permute-start(bf16[1152,256]{1,0:T(8,128)(2,1)} %fusion.43), channel_id=1, source_target_pairs={{0,8},{4,12},{8,0},{12,4},{16,24},{20,28},{24,16},{28,20},{1,9},{5... | collective-permute-start | bytes 1769480 | tf_op jit(solution)/shard_map/ppermute | solution.py:383
  331.9 39.5 %collective-permute-start.43 = (bf16[256,512]{1,0:T(8,128)(2,1)}, bf16[256,512]{1,0:T(8,128)(2,1)}, u32[]{:S(2)}, u32[]{:S(2)}) collective-permute-start(bf16[256,512]{1,0:T(8,128)(2,1)} %slice.280), channel_id=1, source_target_pairs={{0,1},{1,0},{2,3},{3,2},{4,5},{5,4},{6,7},{7,6},{8,9},{9,8},{10,11... | collective-permute-start | bytes 786440 | tf_op jit(solution)/shard_map/ppermute | solution.py:383
  336.3 35.2 %collective-permute-start.48 = (bf16[1024,128]{1,0:T(8,128)(2,1)}, bf16[1024,128]{1,0:T(8,128)(2,1)S(1)}, u32[]{:S(2)}, u32[]{:S(2)}) collective-permute-start(bf16[1024,128]{1,0:T(8,128)(2,1)} %dynamic-slice_convert_fusion.5), channel_id=1, source_target_pairs={{0,2},{1,3},{2,0},{3,1},{4,6},{5,7},{6,4},{7,5},{8,10},{9,11},{10,... | collective-permute-start | bytes 786440 | tf_op jit(solution)/shard_map/ppermute | solution.py:383
  339.2 32.3 %collective-permute-start.47 = (bf16[1024,128]{1,0:T(8,128)(2,1)}, bf16[1024,128]{1,0:T(8,128)(2,1)}, u32[]{:S(2)}, u32[]{:S(2)}) collective-permute-start(bf16[1024,128]{1,0:T(8,128)(2,1)} %dynamic-slice_convert_fusion.6), channel_id=1, source_target_pairs={{0,2},{1,3},{2,0},{3,1},{4,6},{5,7},{6,4},{7,5},{8,10},{9,11},{10,... | collective-permute-start | bytes 786440 | tf_op jit(solution)/shard_map/ppermute | solution.py:383
  385.0 7.0 %collective-permute-start.55 = (bf16[256,128]{1,0:T(8,128)(2,1)S(1)}, bf16[256,128]{1,0:T(8,128)(2,1)S(1)}, u32[]{:S(2)}, u32[]{:S(2)}) collective-permute-start(bf16[256,128]{1,0:T(8,128)(2,1)S(1)} %add_convert_fusion), channel_id=1, source_target_pairs={{0,3},{1,2},{2,1},{3,0},{4,7},{5,6},{6,5},{7,4},{8,11},{9,10},{10,... | collective-permute-start | bytes 196616 | tf_op jit(solution)/shard_map/ppermute | solution.py:383
  385.8 8.1 %collective-permute-start.54 = (bf16[256,128]{1,0:T(8,128)(2,1)S(1)}, bf16[256,128]{1,0:T(8,128)(2,1)S(1)}, u32[]{:S(2)}, u32[]{:S(2)}) collective-permute-start(bf16[256,128]{1,0:T(8,128)(2,1)S(1)} %add_convert_fusion), channel_id=1, source_target_pairs={{0,2},{1,3},{2,0},{3,1},{4,6},{5,7},{6,4},{7,5},{8,10},{9,11},{10,... | collective-permute-start | bytes 196616 | tf_op jit(solution)/shard_map/ppermute | solution.py:383
  391.9 21.2 %collective-permute-start.61 = (bf16[1152,128]{1,0:T(8,128)(2,1)S(1)}, bf16[1152,128]{1,0:T(8,128)(2,1)S(1)}, u32[]{:S(2)}, u32[]{:S(2)}) collective-permute-start(bf16[1152,128]{1,0:T(8,128)(2,1)S(1)} %dynamic-slice_convert_fusion.2), channel_id=1, source_target_pairs={{0,2},{1,3},{2,0},{3,1},{4,6},{5,7},{6,4},{7,5},{8,10},{9,11},{10,... | collective-permute-start | bytes 884744 | tf_op jit(solution)/shard_map/ppermute | solution.py:383
  393.9 7.0 %collective-permute-start.58 = (f32[256,128]{1,0:T(8,128)S(1)}, f32[256,128]{1,0:T(8,128)S(1)}, u32[]{:S(2)}, u32[]{:S(2)}) collective-permute-start(f32[256,128]{1,0:T(8,128)S(1)} %add_add_fusion.refs_0_), channel_id=1, source_target_pairs={{0,24},{4,28},{8,16},{12,20},{16,8},{20,12},{24,0},{28,4},{1,25},{... | collective-permute-start | bytes 393224 | tf_op jit(solution)/shard_map/ppermute | solution.py:383
  397.5 21.3 %collective-permute-start.60 = (bf16[1152,128]{1,0:T(8,128)(2,1)S(1)}, bf16[1152,128]{1,0:T(8,128)(2,1)}, u32[]{:S(2)}, u32[]{:S(2)}) collective-permute-start(bf16[1152,128]{1,0:T(8,128)(2,1)S(1)} %dynamic-slice_convert_fusion.3), channel_id=1, source_target_pairs={{0,2},{1,3},{2,0},{3,1},{4,6},{5,7},{6,4},{7,5},{8,10},{9,11},{10,... | collective-permute-start | bytes 884744 | tf_op jit(solution)/shard_map/ppermute | solution.py:383
  (94 other events, 767.3 us)

commit v4 on v3

--- a/solution.py
+++ b/solution.py
@@ -19,13 +19,31 @@
 LIGHT = pl.CostEstimate(flops=1, bytes_accessed=1, transcendentals=0)
 
 
-def window_kernel(chars, ids_ref, table_ref, win_ref, emb_ref):
+def prepare_kernel(chars, layout, ids_ref, chars_ref, bias_ref, *refs):
+    weight_refs, (win_ref, filter_ref, aux_ref, emb_ref, table_ref) = refs[:7], refs[7:]
     tokens = ids_ref.shape[0]
-    vocab = table_ref.shape[0]
-    group = lax.broadcasted_iota(jnp.int32, (tokens, LANES), 1) // 16
-    places = lax.broadcasted_iota(jnp.int32, (tokens, vocab), 1)
+    vocab, emb_width = chars_ref.shape
+    table_ref[...] = jnp.zeros(table_ref.shape, jnp.bfloat16)
+    for k in range(WIDEST):
+        table_ref[:vocab, k * emb_width : (k + 1) * emb_width] = chars_ref[...]
+    filter_ref[...] = jnp.zeros(filter_ref.shape, jnp.bfloat16)
+    column = lax.broadcasted_iota(jnp.int32, (1, filter_ref.shape[1]), 1)
+    places = jnp.zeros(column.shape, jnp.float32)
+    logs = jnp.zeros(column.shape, jnp.float32)
+    for kernel, leading, filters, natural in layout:
+        filter_ref[: kernel * emb_width, natural : natural + filters] = weight_refs[kernel - 1][
+            :, leading : leading + filters
+        ]
+        inside = (column >= natural) & (column < natural + filters)
+        places = jnp.where(inside, float(chars - kernel + 1), places)
+        logs = jnp.where(inside, math.log(chars - kernel + 1), logs)
+    aux_ref[...] = jnp.zeros(aux_ref.shape, jnp.float32)
+    aux_ref[0:1, :] = bias_ref[...].astype(jnp.float32) - logs
+    aux_ref[1:2, :] = places
+    group = lax.broadcasted_iota(jnp.int32, (tokens, LANES), 1) // emb_width
+    numbers = lax.broadcasted_iota(jnp.int32, (tokens, table_ref.shape[0]), 1)
     for c in range(chars):
-        hits = jnp.where(ids_ref[:, c : c + 1] == places, 1.0, 0.0).astype(jnp.bfloat16)
+        hits = jnp.where(ids_ref[:, c : c + 1] == numbers, 1.0, 0.0).astype(jnp.bfloat16)
         emb_ref[c] = jnp.dot(hits, table_ref[...], preferred_element_type=jnp.float32).astype(jnp.bfloat16)
     for c in range(chars, chars + WIDEST - 1):
         emb_ref[c] = jnp.zeros((tokens, LANES), jnp.bfloat16)
@@ -40,16 +58,25 @@
     lax.fori_loop(0, chars, window, 0)
 
 
-def make_windows(ids, table):
+def prepare(ids, char_table, conv_bias, weights, layout):
     tokens, chars = ids.shape
+    count = conv_bias.shape[0]
+    padded = -(-char_table.shape[0] // LANES) * LANES
     return pl.pallas_call(
-        functools.partial(window_kernel, chars),
-        out_shape=jax.ShapeDtypeStruct((chars, tokens, LANES), jnp.bfloat16),
-        scratch_shapes=[pltpu.VMEM((chars + WIDEST - 1, tokens, LANES), jnp.bfloat16)],
+        functools.partial(prepare_kernel, chars, tuple(layout)),
+        out_shape=[
+            jax.ShapeDtypeStruct((chars, tokens, LANES), jnp.bfloat16),
+            jax.ShapeDtypeStruct((LANES, count), jnp.bfloat16),
+            jax.ShapeDtypeStruct((8, count), jnp.float32),
+        ],
+        scratch_shapes=[
+            pltpu.VMEM((chars + WIDEST - 1, tokens, LANES), jnp.bfloat16),
+            pltpu.VMEM((padded, LANES), jnp.bfloat16),
+        ],
         compiler_params=pltpu.CompilerParams(vmem_limit_bytes=VMEM_BYTES),
         cost_estimate=LIGHT,
-        name="make_windows",
-    )(ids, table)
+        name="prepare",
+    )(ids, char_table, conv_bias.reshape(1, count), *weights)
 
 
 def forward_kernel(low_places, extras, trip_ref, win_ref, weight_ref, aux_ref, e_ref, act_ref, x_ref, part_ref, high_ref, total_ref):
@@ -305,14 +332,6 @@
     return layout
 
 
-def join_filters(weights, layout):
-    parts = []
-    for kernel, leading, filters, natural in layout:
-        part = weights[kernel - 1][:, leading : leading + filters]
-        parts.append(jnp.pad(part, ((0, LANES - part.shape[0]), (0, 0))))
-    return jnp.concatenate(parts, axis=1)
-
-
 def column_places(layout, chars):
     return [chars - kernel + 1 for kernel, leading, filters, natural in layout for unused in range(filters)]
 
@@ -1055,15 +1074,6 @@
 
     places = column_places(layout, chars)
     low_places = min(places)
-    filters = join_filters(weights, layout)
-    places_row = jnp.array(places, jnp.float32)
-    aux = jnp.pad(
-        jnp.stack([conv_bias.astype(jnp.float32) - jnp.log(places_row), places_row]), ((0, 6), (0, 0))
-    )
-    padded = -(-vocab_count // LANES) * LANES
-    table = jnp.pad(
-        jnp.tile(char_table, (1, WIDEST)), ((0, padded - vocab_count), (0, LANES - WIDEST * emb_width))
-    )
     trips = jnp.array(
         [max(places[start : start + BLOCK]) for start in range(0, feature_count, BLOCK)], jnp.int32
     )
@@ -1084,58 +1094,66 @@
             onto,
         )
 
+    out_stages = list(stage_lists()[0])
+    flips = [(0, 0)]
+
+    def out_round(bundle, got, *others):
+        if got is not None:
+            bundle = jnp.concatenate([bundle, after(got, *others)])
+        return bundle, swap(bundle, *out_stages[0])
+
+    bundle, bundle_got = out_round(own_rows(proj_weight, width).T[None], None)
+    flips = flips + turn(flips, *out_stages.pop(0))
+    if len(out_stages) > 1:
+        bundle, bundle_got = out_round(bundle, bundle_got)
+        flips = flips + turn(flips, *out_stages.pop(0))
     below = jnp.stack([highway_b1, highway_b2, jnp.pad(proj_bias, (0, width - out_part))])
     below = [jnp.pad(part, ((0, BELOW - part.shape[0]), (0, 0))) for part in (below[:1], below[1:])]
-    gather_one = Gather(bank_rows(highway_w1, bank_order, layout, True, below[0]))
+    gather_one = Gather(bank_rows(after(highway_w1, bundle), bank_order, layout, True, below[0]))
     gather_one.send()
     given_along = swap(after(cotangent, gather_one.held), "narrow", 1)
     given_wide = swap(after(cotangent, gather_one.held), "wide", 1)
     gather_two = Gather(jnp.concatenate([own_rows(after(highway_w2, gather_one.held), width), below[1]]))
-    windows = make_windows(after(char_ids, gather_one.held), table)
+    windows, filters, aux = prepare(after(char_ids, gather_one.held, bundle), char_table, conv_bias, weights, layout)
     late = conv(half_blocks, half_blocks, 0, half_blocks, None)
     late_along = swap(late[1], "narrow", 1)
-    bundle = after(own_rows(proj_weight, width).T[None], late[1])
-    out_stages = list(stage_lists()[0])
-    flips = [(0, 0)]
-
-    def out_round(bundle, got, *others):
-        if got is not None:
-            bundle = jnp.concatenate([bundle, after(got, *others)])
-        return bundle, swap(bundle, *out_stages[0])
-
-    bundle, bundle_got = out_round(bundle, None)
-    flips = flips + turn(flips, *out_stages.pop(0))
+    while out_stages:
+        bundle, bundle_got = out_round(bundle, bundle_got, late[1])
+        flips = flips + turn(flips, *out_stages.pop(0))
     resolved = list(gather_one.got)
-    mark = (late[1],)
+    mark = (late[1], bundle)
     for number in range(1, gather_one.rounds - 1):
         sent = gather_one.send(mark)
         mark = (mark, sent)
-    late_wide = swap(late[1], "wide", 1)
-    sent_two = gather_two.send(late[1], sent, bundle)
+    sent_two = gather_two.send(late[1], sent)
     mid = conv(
-        quarter_blocks, half_blocks - quarter_blocks, quarter_blocks, half_blocks, None, late[1], resolved, sent, sent_two, bundle
+        quarter_blocks, half_blocks - quarter_blocks, quarter_blocks, half_blocks, None, late[1], resolved, sent, sent_two, bundle, given_along, given_wide
     )
-    resolved = [list(gather_one.got), late_wide, given_along, given_wide]
-    bundle, bundle_got = out_round(bundle, bundle_got, mid[1])
-    flips = flips + turn(flips, *out_stages.pop(0))
-    last = gather_one.send(mid[1], bundle)
-    mid_along = swap(mid[1], "narrow", 1)
-    late_both = swap(after(late_along, mid[1]), "wide", 1)
+    resolved = [list(gather_one.got), late_along]
+    last = gather_one.send(mid[1])
+    bundle = jnp.concatenate([bundle, after(bundle_got, mid[1])])
+    shares = bundle.reshape(blocks, out_part, members, own_width).transpose(2, 0, 1, 3)
+    shares = shares.reshape(members, blocks * out_part, own_width)
+    share_rows = blocks * out_part
+    mid_along = swap(jnp.concatenate([mid[1], shares[1], shares[3]]), "narrow", 1)
     early = conv(0, quarter_blocks, 0, half_blocks, [mid[0], mid[2], mid[3]], mid[1], resolved, last, bundle)
     mark = early[1]
     early_along = swap(early[1], "narrow", 1)
-    mid_wide = swap(after(mid[1], mark), "wide", 1)
-    early_wide = swap(early[1], "wide", 1)
-    late_both = after(late_both, mark)
-    mid_both = swap(after(mid_along, mark), "wide", 1)
-    while out_stages:
-        bundle, bundle_got = out_round(bundle, bundle_got, mark)
-        flips = flips + turn(flips, *out_stages.pop(0))
-    sent = (mark, last, bundle)
+    late_across = swap(jnp.concatenate([late[1], after(late_along, mark)]), "wide", 1)
+    mid_along = after(mid_along, mark)
+    mid_across = swap(
+        jnp.concatenate([mid[1], mid_along[:tokens], shares[2], mid_along[tokens + share_rows :]]), "wide", 1
+    )
+    sent = (mark, last)
     for number in range(1, gather_two.rounds - 1):
         sent = gather_two.send(sent)
-    early_both = swap(after(early_along, mid_both), "wide", 1)
-    given_both = swap(after(given_along, mid_both), "wide", 1)
+    early_across = swap(jnp.concatenate([early[1], after(early_along, mid_across)]), "wide", 1)
+    shares = [
+        shares[0],
+        mid_along[tokens : tokens + share_rows],
+        mid_across[2 * tokens : 2 * tokens + share_rows],
+        mid_across[2 * tokens + share_rows :],
+    ]
 
     natural = lax.iota(jnp.int32, feature_count)
     begin = jnp.array([entry[3] for entry in layout], jnp.int32)
@@ -1148,14 +1166,13 @@
     pick = ((natural + shift)[:, None] == own_feature[None, :]).astype(jnp.bfloat16)
 
     spans = [(half_blocks, half_blocks), (quarter_blocks, half_blocks - quarter_blocks), (0, quarter_blocks)]
-    sources = [
-        late[1], late_along, late_wide, late_both, mid[1], mid_along, mid_wide, mid_both, early[1], early_along, early_wide, early_both
-    ]
-    copies = [
-        (number * members + by, 0, 0, tokens, count * BLOCK, by * tokens, start * BLOCK)
-        for number, (start, count) in enumerate(spans)
-        for by in range(members)
-    ]
+    sources, copies = [], []
+    for (start, count), (own, along, across) in zip(
+        spans, ((late[1], late_along, late_across), (mid[1], mid_along, mid_across), (early[1], early_along, early_across))
+    ):
+        for by, (source, row) in enumerate(((0, 0), (1, 0), (2, 0), (2, tokens))):
+            copies.append((len(sources) + source, row, 0, tokens, count * BLOCK, by * tokens, start * BLOCK))
+        sources += [own, along, across]
     last_one = list(gather_one.got)
     features, weight_one, proj_one, carried_one, carried_two = layer_one(
         sources, copies, gather_one.result(), after(pick, sent), shape
@@ -1164,9 +1181,8 @@
     resolved = list(gather_two.got)
     sent = gather_two.send(carried_two)
     hidden_wide = swap(carried_two, "wide", 1)
-    bundle = jnp.concatenate([bundle, after(bundle_got, carried_two)])
-    shares = bundle.reshape(blocks, out_part, members, own_width).transpose(2, 0, 1, 3)
-    shares = group_trade([shares[m] for m in range(members)])
+    given_both = swap(after(given_along, carried_two, sent), "wide", 1)
+    shares = [after(part, carried_two, sent) for part in shares]
     device_at = jnp.stack(
         [
             jnp.stack([(wide ^ (fw | dw)) * narrow_size + (narrow ^ (fn | dn)) for dw, dn in ((0, 0), (0, 1), (1, 0), (1, 1))])
@@ -1178,7 +1194,7 @@
     out_weight = jnp.einsum(
         "jn,jf->nf",
         out_order,
-        jnp.stack(shares, axis=1).reshape(-1, own_width),
+        jnp.stack([part.reshape(blocks, out_part, own_width) for part in shares], axis=1).reshape(-1, own_width),
         preferred_element_type=jnp.float32,
     ).astype(jnp.bfloat16)
     givens = [cotangent, given_along, given_wide, given_both]
@@ -1217,29 +1233,34 @@
     d_project, through, sums_one, later, earlier = back_one(own, across, proj_one, carried_one, weight_one, pick)
     later = swap(later, "wide", 1)
     earlier = swap(earlier, "wide", 1)
-    scatter_one = Scatter(features, d_project, grad_out)
+    resolved = list(scatter_two.got)
+    encoded = encoded + after(encoded_got, sums_one).astype(jnp.float32)
+    scatter_one = Scatter(features, after(d_project, resolved, encoded), grad_out)
     sent = scatter_one.send()
     late_own, late_send = keep_one(d_project, through, weight_one, pick, after(later, sent), 1)
     late_got = swap(late_send, "narrow", 1)
     early_own, early_send = keep_one(after(d_project, late_send), through, weight_one, pick, earlier, 0)
     early_got = swap(early_send, "narrow", 1)
+    scatter_two.add(early_send)
+    sent_two = scatter_two.send()
+    scatter_one.add(early_send, sent_two)
+    sent = scatter_one.send()
+    while scatter_two.stages[0]:
+        scatter_two.add(sent)
+        sent_two = scatter_two.send()
     ids_across = jnp.pad(char_ids.T, ((0, -chars % 8), (0, 0)))
     span = WIDEST * emb_width
-    resolved = list(scatter_two.got)
     late_filters, late_table = conv_backward(
-        [late[0]], [late[2]], [late[3]], late_own, after(late_got, early_send, ids_across, encoded_got, resolved), windows, filters, ids_across, trips, low_places, vocab_count, span, half_blocks
+        [late[0]], [late[2]], [late[3]], late_own, after(late_got, sent, sent_two, ids_across), windows, filters, ids_across, trips, low_places, vocab_count, span, half_blocks
     )
-    scatter_one.add(late_table)
-    sent = scatter_one.send()
-    while scatter_two.stages[0]:
-        scatter_two.add(late_table, sent)
-        sent_two = scatter_two.send()
-    encoded = encoded + after(encoded_got, late_table, sent).astype(jnp.float32)
-    encoded_got = swap(encoded[tokens:].astype(jnp.bfloat16), "narrow", 1)
+    while scatter_one.stages[0]:
+        scatter_one.add(late_table)
+        sent = scatter_one.send()
+    encoded_got = swap(after(encoded[tokens:], late_table).astype(jnp.bfloat16), "narrow", 1)
     early_filters, early_table = conv_backward(
-        [early[0]], [early[2]], [early[3]], early_own, early_got, after(windows, sent, sent_two, late_table, encoded), filters, ids_across, trips, low_places, vocab_count, span, 0
+        [early[0]], [early[2]], [early[3]], early_own, early_got, after(windows, sent, scatter_two.got, late_table, encoded), filters, ids_across, trips, low_places, vocab_count, span, 0
     )
-    resolved = [early_table, list(scatter_one.got), list(scatter_two.got), encoded_got]
+    resolved = [early_table, encoded_got]
 
     member = mine_wide * 2 + mine_narrow
     own_sums = own_width * 2 // LANES
@@ -1262,12 +1283,8 @@
         -(-(ends[-1] + given_sum.shape[0]) // unit) * unit,
     )
     summed, sent = sum_all(packed)
-    scatter_one.add(packed)
-    scatter_one.total = [after(part, sent) for part in scatter_one.total]
-    while scatter_one.stages[0]:
-        scatter_one.send()
-        scatter_one.add()
-    scatter_two.add(sent)
+    scatter_two.add(packed)
+    scatter_one.add(sent)
     grad_one_w = scatter_one.result()
     grad_out = grad_one_w[feature_count:].reshape(members, out_part, own_width)
     grad_out = group_trade([grad_out[m] for m in range(members)])

time: 440 us -> 404 us (0.918)
  waiting for transfers between devices: 71.2 us -> 35.4 us
  other arithmetic: 34 us -> 39.3 us
    ppermute x63 -> x58, waiting for transfers between devices: 70.7 us -> 35.3 us  [swap(): lax.ppermute(x, axis, [(i, i ^ bit) for i in range(lax.axis_size(axis))])]
    pad x9 -> x0, local copies, waits for them, and re-layouts: 5.21 us -> none  [the longest x8 4.54 us: join_filters(): parts.append(jnp.pad(part, ((0, LANES - part.shape[0]), (0, 0))))]
    slice x2 -> x5, local copies, waits for them, and re-layouts: 0.75 us -> 5.92 us  [the longest x1 1.64 us: local(): mid_along[tokens:tokens + share_rows]]
    ppermute x63 -> x58, starting transfers between devices: 58 us -> 54.9 us  [swap(): lax.ppermute(x, axis, [(i, i ^ bit) for i in range(lax.axis_size(axis))])]
    unnamed x158 -> x124, local copies, waits for them, and re-layouts: 18.2 us -> 16.8 us
  transfers between devices with their start and end apart: 65 -> 59, of which waited for: 19 -> 13; matrix products, arithmetic and copies ran while one was open for 20% -> 24% of each run, Pallas kernels for 38% -> 43%
where the time goes in v4:
time: 404 us; the launch traced here: 398 us
  Pallas kernels  193 us (48%)
  starting transfers between devices  55 us (14%)
  local copies, waits for them, and re-layouts  48.4 us (12%)
  other arithmetic  39.3 us (10%)
  waiting for transfers between devices  35.4 us (9%)
  matrix products  24.3 us (6%)
    ppermute x58, starting transfers between devices, swap(): lax.ppermute(x, axis, [(i, i ^ bit) for i in range(lax.axis_size(axis))])  54.9 us
    pallas_call x2, Pallas kernels, conv_backward(): pl.pallas_call(functools.partial(backward_kernel, chars, low_places, span...  52.9 us
    pallas_call x3, Pallas kernels, conv_forward(): pl.pallas_call(functools.partial(kernel, low_places, extras), grid_spec=p...  51.4 us
    ppermute x58, waiting for transfers between devices, swap(): lax.ppermute(x, axis, [(i, i ^ bit) for i in range(lax.axis_size(axis))])  35.3 us
    pallas_call x2, Pallas kernels, call_layer(): pl.pallas_call(functools.partial(kernel, tuple(x_copies), tuple(w_copies)...  33.7 us
    dot_general x8, matrix products, product(): lax.dot_general(inputs[:, number * half:(number + 1) * half], after(halve...  19.1 us
    unnamed x124, local copies, waits for them, and re-layouts  16.8 us
    pallas_call x1, Pallas kernels, back_one(): pl.pallas_call(back_one_kernel, in_specs=[NEAR] * 4 + [ANYWHERE] * 2, out...  11.1 us
  transfers between devices with their start and end apart: 59, of which 13 were waited for; matrix products, arithmetic and copies ran while one was open for 24% of the time, Pallas kernels for 43%

profile of v4, /device:TPU:0, one launch (start us, length us, event | category | flops | bytes accessed | tf_op | source)
XLA Modules:
  0.0 398.0 jit_solution(14980486000830751019)
XLA Ops:
  1.9 4.1 %collective-permute-start = (bf16[1,16,2048]{2,1,0:T(8,128)(2,1)S(1)}, bf16[1,16,2048]{2,1,0:T(8,128)(2,1)S(1)}, u32[]{:S(2)}, u32[]{:S(2)}) collective-permute-start(bf16[1,16,2048]{2,1,0:T(8,128)(2,1)S(1)} %bitcast.195), channel_id=1, source_target_pairs={{0,2},{1,3},{2,0},{3,1},{4,6},{5,7},{6,4},{7,5},{8,10},{9,11},{10,... | collective-permute-start | bytes 196616 | tf_op jit(solution)/shard_map/ppermute | solution.py:402
  15.6 1.9 bank_rows.2
  21.7 9.3 %prepare.1 = (bf16[50,256,128]{2,1,0:T(8,128)(2,1)}, bf16[128,2048]{1,0:T(8,128)(2,1)}, f32[8,2048]{1,0:T(8,128)}) custom-call(s32[256,50]{1,0:T(8,128)} %copy.77.ids_ref, bf16[262,16]{1,0:T(8,128)(2,1)} %copy.78.chars_ref, bf16[1,2048]{1,0:T(2,128)(2,1)} %reshape.351.bias_ref, bf16[16,32]{1,0:T(8,128)(2,1)} %refs_0_.2, bf16[32,32]{1,0:T(8,128)(2,1)} %refs_1_.1, ...), custom_call_target="tpu_custom_call" | custom-call | flops 1 | bytes 1 | tf_op jit(solution)/shard_map/prepare/pallas_call | solution.py:65
  31.5 21.1 %conv_forward.3 = (bf16[4,50,256,256]{3,2,1,0:T(8,128)(2,1)}, bf16[256,1024]{1,0:T(8,128)(2,1)}, f32[256,1024]{1,0:T(8,128)}, f32[5,256,1024]{2,1,0:T(8,128)}) custom-call(s32[4]{0:T(128)} %broadcast.226.trip_ref, bf16[50,256,128]{2,1,0:T(8,128)(2,1)} %get-tuple-element.198.win_ref.refs_5_, bf16[128,2048]{1,0:T(8,128)(2,1)} %get-tuple-element.122.weight_ref.refs_6_, ...), custom_call_target="tpu_custom_call" | custom-call | flops 1 | bytes 1 | tf_op jit(solution)/shard_map/conv_forward/pallas_call | solution.py:145
  53.3 1.6 collective-permute-start.2
  58.6 2.7 collective-permute-start.9
  61.8 14.8 %conv_forward.4 = (bf16[4,50,256,256]{3,2,1,0:T(8,128)(2,1)}, bf16[256,512]{1,0:T(8,128)(2,1)}, f32[256,1024]{1,0:T(8,128)}, f32[5,256,1024]{2,1,0:T(8,128)}) custom-call(s32[2]{0:T(128)} %broadcast.227.trip_ref, bf16[50,256,128]{2,1,0:T(8,128)(2,1)} %get-tuple-element.198.win_ref.refs_5_, bf16[128,2048]{1,0:T(8,128)(2,1)} %get-tuple-element.122.weight_ref.refs_6_, ...), custom_call_target="tpu_custom_call" | custom-call | flops 1 | bytes 1 | tf_op jit(solution)/shard_map/conv_forward/pallas_call | solution.py:145
  77.1 1.6 fusion.82
  87.4 15.5 %conv_forward.5 = (bf16[4,50,256,256]{3,2,1,0:T(8,128)(2,1)}, bf16[256,512]{1,0:T(8,128)(2,1)}, f32[256,1024]{1,0:T(8,128)}, f32[5,256,1024]{2,1,0:T(8,128)}) custom-call(s32[2]{0:T(128)} %constant.555.trip_ref, bf16[50,256,128]{2,1,0:T(8,128)(2,1)} %get-tuple-element.198.win_ref.refs_5_, ...), custom_call_target="tpu_custom_call", output_to_operand_aliasing={{0}: (4, {}), {2}: (5, {}), {3}: (6, {})} | custom-call | flops 1 | bytes 1 | tf_op jit(solution)/shard_map/conv_forward/pallas_call | solution.py:145
  104.4 1.6 fusion.83
  111.5 1.6 compare_convert_fusion.pick_ref.pick_far
  114.1 16.1 %layer_one.1 = (bf16[1024,2048]{1,0:T(8,128)(2,1)}, bf16[2080,1024]{1,0:T(8,128)(2,1)}, f32[1024,1024]{1,0:T(8,128)}, bf16[1024,512]{1,0:T(8,128)(2,1)}, bf16[1024,512]{1,0:T(8,128)(2,1)}) custom-call(s32[16]{0:T(128)} %stack.294.at_ref, bf16[2048,512]{1,0:T(8,128)(2,1)} %compare_convert_fusion.pick_ref.pick_far, ...), custom_call_target="tpu_custom_call" | custom-call | flops 1 | bytes 1 | tf_op jit(solution)/shard_map/layer_one/pallas_call | solution.py:552
  130.3 1.6 collective-permute-start.20
  137.8 18.4 %collective-permute-done.20.refs_5_ = bf16[1024,512]{1,0:T(8,128)(2,1)} collective-permute-done((bf16[1024,512]{1,0:T(8,128)(2,1)}, bf16[1024,512]{1,0:T(8,128)(2,1)}, u32[]{:S(2)}, u32[]{:S(2)}) %collective-permute-start.20) | collective-permute-done | bytes 1048608 | tf_op jit(solution)/shard_map/ppermute | solution.py:402
  162.9 17.6 %layer_two.1 = (bf16[1024,2048]{1,0:T(8,128)(2,1)}, bf16[2080,1024]{1,0:T(8,128)(2,1)}, bf16[1024,512]{1,0:T(8,128)(2,1)}, bf16[1024,1024]{1,0:T(8,128)(2,1)}, f...) custom-call(s32[16]{0:T(128)} %stack.294.at_ref, ...), custom_call_target="tpu_custom_call" | custom-call | flops 1 | bytes 1 | tf_op jit(solution)/shard_map/layer_two/pallas_call | solution.py:552
  183.3 1.7 constant_dynamic-slice_fusion.13
  187.6 2.3 fusion.27
  192.6 2.7 fusion.24
  197.3 5.0 %keep_two.2 = bf16[1024,512]{1,0:T(8,128)(2,1)} custom-call(bf16[1024,1024]{1,0:T(8,128)(2,1)} %get-tuple-element.160.d_project_ref, bf16[2080,1024]{1,0:T(8,128)(2,1)} %get-tuple-element.156.w_ref, bf16[1024,1024]{1,0:T(8,128)(2,1)} %copy-done.4), custom_call_target="tpu_custom_call" | custom-call | flops 1 | bytes 1 | tf_op jit(solution)/shard_map/keep_two/pallas_call | solution.py:634
  203.9 5.9 %keep_two.3.own_ref = f32[1024,512]{1,0:T(8,128)} custom-call(bf16[1024,1024]{1,0:T(8,128)(2,1)} %get-tuple-element.160.d_project_ref, bf16[2080,1024]{1,0:T(8,128)(2,1)} %get-tuple-element.156.w_ref, bf16[1024,1024]{1,0:T(8,128)(2,1)} %copy-done.4, f32[1024,512]{1,0:T(8,128)} %get-tuple-element.161.refs_0_), custom_call_target="tpu_custom_call" | custom-call | flops 1 | bytes 1 | tf_op jit(solution)/shard_map/keep_two/pallas_call | solution.py:634
  209.8 1.8 convolution_convert_fusion.1
  212.6 2.1 convolution_add_fusion
  215.7 3.3 convert_add_fusion.2
  221.6 2.5 convert_add_fusion.3
  227.6 11.1 %back_one.1 = (bf16[1024,1024]{1,0:T(8,128)(2,1)}, bf16[1024,512]{1,0:T(8,128)(2,1)}, f32[8,1024]{1,0:T(8,128)}, bf16[512,1024]{1,0:T(8,128)(2,1)}, bf16[512,1024]{1,0:T(8,128)(2,1)}) custom-call(f32[1024,512]{1,0:T(8,128)} %keep_two.3.own_ref, bf16[1024,512]{1,0:T(8,128)(2,1)} %collective-permute-done.29.got_ref, ...), custom_call_target="tpu_custom_call" | custom-call | flops 1 | bytes 1 | tf_op jit(solution)/shard_map/back_one/pallas_call | solution.py:682
  241.0 1.8 copy-done.52
  251.1 5.5 %keep_one.2 = (f32[256,1024]{1,0:T(8,128)}, bf16[256,1024]{1,0:T(8,128)(2,1)}) custom-call(bf16[1024,1024]{1,0:T(8,128)(2,1)} %get-tuple-element.182.d_project_ref, bf16[1024,512]{1,0:T(8,128)(2,1)} %get-tuple-element.175.through_ref, bf16[2080,1024]{1,0:T(8,128)(2,1)} %get-tuple-element.168.w_far.w_ref, ...), custom_call_target="tpu_custom_call" | custom-call | flops 1 | bytes 1 | tf_op jit(solution)/shard_map/keep_one/pallas_call | solution.py:714
  258.2 5.5 %keep_one.3 = (f32[256,1024]{1,0:T(8,128)}, bf16[256,1024]{1,0:T(8,128)(2,1)}) custom-call(bf16[1024,1024]{1,0:T(8,128)(2,1)} %get-tuple-element.182.d_project_ref, bf16[1024,512]{1,0:T(8,128)(2,1)} %get-tuple-element.175.through_ref, bf16[2080,1024]{1,0:T(8,128)(2,1)} %get-tuple-element.168.w_far.w_ref, ...), custom_call_target="tpu_custom_call" | custom-call | flops 1 | bytes 1 | tf_op jit(solution)/shard_map/keep_one/pallas_call | solution.py:714
  264.1 1.7 convert_add_fusion.4
  268.9 4.3 %collective-permute-done.36 = bf16[1152,512]{1,0:T(8,128)(2,1)} collective-permute-done((bf16[1152,512]{1,0:T(8,128)(2,1)S(1)}, bf16[1152,512]{1,0:T(8,128)(2,1)}, u32[]{:S(2)}, u32[]{:S(2)}) %collective-permute-start.36) | collective-permute-done | bytes 1179680 | tf_op jit(solution)/shard_map/ppermute | solution.py:402
  274.5 3.3 convert_add_fusion
  280.1 2.5 convert_add_fusion.1
  285.9 25.5 %conv_backward.2 = (f32[8,120,128]{2,1,0:T(8,128)}, f32[40,128]{1,0:T(8,128)}) custom-call(s32[4]{0:T(128)} %broadcast.226.trip_ref, bf16[4,50,256,256]{3,2,1,0:T(8,128)(2,1)} %get-tuple-element.171.refs_0_, f32[256,1024]{1,0:T(8,128)} %get-tuple-element.172.refs_1_, f32[5,256,1024]{2,1,0:T(8,128)} %get-tuple-element.173.refs_2_, ...), custom_call_target="tpu_custom_call" | custom-call | flops 1 | bytes 1 | tf_op jit(solution)/shard_map/conv_backward/pallas_call | solution.py:290
  315.1 2.6 collective-permute-start.55
  320.5 27.5 %conv_backward.3 = (f32[8,120,128]{2,1,0:T(8,128)}, f32[40,128]{1,0:T(8,128)}) custom-call(s32[4]{0:T(128)} %constant.557.trip_ref, bf16[4,50,256,256]{3,2,1,0:T(8,128)(2,1)} %get-tuple-element.192.refs_0_, f32[256,1024]{1,0:T(8,128)} %get-tuple-element.193.refs_1_, f32[5,256,1024]{2,1,0:T(8,128)} %get-tuple-element.194.refs_2_, ...), custom_call_target="tpu_custom_call" | custom-call | flops 1 | bytes 1 | tf_op jit(solution)/shard_map/conv_backward/pallas_call | solution.py:290
  348.0 2.4 pack.1
  355.9 1.8 collective-permute-start.46
  358.9 1.7 fusion.52
  362.4 2.8 collective-permute-start.49
  365.2 1.7 collective-permute-start.47
  369.6 1.9 collective-permute-done.48
  375.1 3.6 collective-permute-done.52.refs_3_
  381.1 2.4 bank_rows.3
  384.8 1.9 join.2.refs_0_
  387.1 1.8 collective-permute-done.53.refs_1_
  389.7 2.3 join.3.summed_ref
  392.7 2.2 unpack.1
  394.9 1.6 copy.90
  (365 shorter events, 120.0 us)
Async XLA Ops:
  1.9 12.2 %collective-permute-start = (bf16[1,16,2048]{2,1,0:T(8,128)(2,1)S(1)}, bf16[1,16,2048]{2,1,0:T(8,128)(2,1)S(1)}, u32[]{:S(2)}, u32[]{:S(2)}) collective-permute-start(bf16[1,16,2048]{2,1,0:T(8,128)(2,1)S(1)} %bitcast.195), channel_id=1, source_target_pairs={{0,2},{1,3},{2,0},{3,1},{4,6},{5,7},{6,4},{7,5},{8,10},{9,11},{10,... | collective-permute-start | bytes 196616 | tf_op jit(solution)/shard_map/ppermute | solution.py:402
  14.1 39.1 %collective-permute-start.1 = (bf16[2,16,2048]{2,1,0:T(8,128)(2,1)S(1)}, bf16[2,16,2048]{2,1,0:T(8,128)(2,1)S(1)}, u32[]{:S(2)}, u32[]{:S(2)}) collective-permute-start(bf16[2,16,2048]{2,1,0:T(8,128)(2,1)S(1)} %pad_maximum_fusion.22), channel_id=1, source_target_pairs={{0,8},{4,12},{8,0},{12,4},{16,24},{20,28},{24,16},{28,20},{1,9},{5... | collective-permute-start | bytes 393224 | tf_op jit(solution)/shard_map/ppermute | solution.py:402
  17.6 40.6 %collective-permute-start.5 = (bf16[256,512]{1,0:T(8,128)(2,1)S(1)}, bf16[256,512]{1,0:T(8,128)(2,1)}, u32[]{:S(2)}, u32[]{:S(2)}) collective-permute-start(bf16[256,512]{1,0:T(8,128)(2,1)S(1)} %copy-done.28), channel_id=1, source_target_pairs={{0,4},{4,0},{8,12},{12,8},{16,20},{20,16},{24,28},{28,24},{1,5},{5... | collective-permute-start | bytes 786440 | tf_op jit(solution)/shard_map/ppermute | solution.py:402
  17.6 41.0 %collective-permute-start.4 = (bf16[256,512]{1,0:T(8,128)(2,1)S(1)}, bf16[256,512]{1,0:T(8,128)(2,1)}, u32[]{:S(2)}, u32[]{:S(2)}) collective-permute-start(bf16[256,512]{1,0:T(8,128)(2,1)S(1)} %copy-done.28), channel_id=1, source_target_pairs={{0,1},{1,0},{2,3},{3,2},{4,5},{5,4},{6,7},{7,6},{8,9},{9,8},{10,11... | collective-permute-start | bytes 786440 | tf_op jit(solution)/shard_map/ppermute | solution.py:402
  20.2 34.6 %collective-permute-start.3 = (bf16[2080,128]{1,0:T(8,128)(2,1)}, bf16[2080,128]{1,0:T(8,128)(2,1)}, u32[]{:S(2)}, u32[]{:S(2)}) collective-permute-start(bf16[2080,128]{1,0:T(8,128)(2,1)} %bank_rows.2), channel_id=1, source_target_pairs={{0,2},{1,3},{2,0},{3,1},{4,6},{5,7},{6,4},{7,5},{8,10},{9,11},{10,... | collective-permute-start | bytes 1597448 | tf_op jit(solution)/shard_map/ppermute | solution.py:402
  52.6 34.8 %collective-permute-start.8 = (bf16[256,1024]{1,0:T(8,128)(2,1)}, bf16[256,1024]{1,0:T(8,128)(2,1)}, u32[]{:S(2)}, u32[]{:S(2)}) collective-permute-start(bf16[256,1024]{1,0:T(8,128)(2,1)} %get-tuple-element.124.refs_0_), channel_id=1, source_target_pairs={{0,1},{1,0},{2,3},{3,2},{4,5},{5,4},{6,7},{7,6},{8,9},{9,8},{10,11... | collective-permute-start | bytes 1572872 | tf_op jit(solution)/shard_map/ppermute | solution.py:402
  53.3 23.3 %collective-permute-start.2 = (bf16[4,16,2048]{2,1,0:T(8,128)(2,1)S(1)}, bf16[4,16,2048]{2,1,0:T(8,128)(2,1)S(1)}, u32[]{:S(2)}, u32[]{:S(2)}) collective-permute-start(bf16[4,16,2048]{2,1,0:T(8,128)(2,1)S(1)} %pad_maximum_fusion.21), channel_id=1, source_target_pairs={{0,16},{4,20},{8,24},{12,28},{16,0},{20,4},{24,8},{28,12},{1,17},{... | collective-permute-start | bytes 786440 | tf_op jit(solution)/shard_map/ppermute | solution.py:402
  56.8 26.3 %collective-permute-start.6 = (bf16[2,1040,128]{2,1,0:T(8,128)(2,1)}, bf16[2,1040,128]{2,1,0:T(8,128)(2,1)}, u32[]{:S(2)}, u32[]{:S(2)}) collective-permute-start(bf16[2,1040,128]{2,1,0:T(8,128)(2,1)} %pad_maximum_fusion.13), channel_id=1, source_target_pairs={{0,8},{4,12},{8,0},{12,4},{16,24},{20,28},{24,16},{28,20},{1,9},{5... | collective-permute-start | bytes 1597448 | tf_op jit(solution)/shard_map/ppermute | solution.py:402
  58.2 23.7 %collective-permute-start.7 = (bf16[2,1040,128]{2,1,0:T(8,128)(2,1)}, bf16[2,1040,128]{2,1,0:T(8,128)(2,1)}, u32[]{:S(2)}, u32[]{:S(2)}) collective-permute-start(bf16[2,1040,128]{2,1,0:T(8,128)(2,1)} %pad_maximum_fusion.14), channel_id=1, source_target_pairs={{0,16},{4,20},{8,24},{12,28},{16,0},{20,4},{24,8},{28,12},{1,17},{... | collective-permute-start | bytes 1597448 | tf_op jit(solution)/shard_map/ppermute | solution.py:402
  58.6 47.5 %collective-permute-start.9 = (bf16[2080,128]{1,0:T(8,128)(2,1)S(1)}, bf16[2080,128]{1,0:T(8,128)(2,1)}, u32[]{:S(2)}, u32[]{:S(2)}) collective-permute-start(bf16[2080,128]{1,0:T(8,128)(2,1)S(1)} %pad_maximum_fusion.15), channel_id=1, source_target_pairs={{0,2},{1,3},{2,0},{3,1},{4,6},{5,7},{6,4},{7,5},{8,10},{9,11},{10,... | collective-permute-start | bytes 1597448 | tf_op jit(solution)/shard_map/ppermute | solution.py:402
  80.3 23.2 %collective-permute-start.11 = (bf16[512,512]{1,0:T(8,128)(2,1)}, bf16[512,512]{1,0:T(8,128)(2,1)}, u32[]{:S(2)}, u32[]{:S(2)}) collective-permute-start(bf16[512,512]{1,0:T(8,128)(2,1)} %pad_maximum_fusion.18), channel_id=1, source_target_pairs={{0,1},{1,0},{2,3},{3,2},{4,5},{5,4},{6,7},{7,6},{8,9},{9,8},{10,11... | collective-permute-start | bytes 1572872 | tf_op jit(solution)/shard_map/ppermute | solution.py:402
  83.1 30.5 %collective-permute-start.16 = (bf16[4,1040,128]{2,1,0:T(8,128)(2,1)S(1)}, bf16[4,1040,128]{2,1,0:T(8,128)(2,1)}, u32[]{:S(2)}, u32[]{:S(2)}) collective-permute-start(bf16[4,1040,128]{2,1,0:T(8,128)(2,1)S(1)} %pad_maximum_fusion.3.refs_11_), channel_id=1, source_target_pairs={{0,8},{4,12},{8,0},{12,4},{16,24},{20,28},{24,16},{28,20},{1,9},{5... | collective-permute-start | bytes 3194888 | tf_op jit(solution)/shard_map/ppermute | solution.py:402
  85.8 27.8 %collective-permute-start.15 = (bf16[4,1040,128]{2,1,0:T(8,128)(2,1)S(1)}, bf16[4,1040,128]{2,1,0:T(8,128)(2,1)}, u32[]{:S(2)}, u32[]{:S(2)}) collective-permute-start(bf16[4,1040,128]{2,1,0:T(8,128)(2,1)S(1)} %pad_maximum_fusion.2.refs_9_), channel_id=1, source_target_pairs={{0,16},{4,20},{8,24},{12,28},{16,0},{20,4},{24,8},{28,12},{1,17},{... | collective-permute-start | bytes 3194888 | tf_op jit(solution)/shard_map/ppermute | solution.py:402
  102.9 7.9 %collective-permute-start.13 = (bf16[256,512]{1,0:T(8,128)(2,1)}, bf16[256,512]{1,0:T(8,128)(2,1)S(1)}, u32[]{:S(2)}, u32[]{:S(2)}) collective-permute-start(bf16[256,512]{1,0:T(8,128)(2,1)} %get-tuple-element.139.refs_6_), channel_id=1, source_target_pairs={{0,1},{1,0},{2,3},{3,2},{4,5},{5,4},{6,7},{7,6},{8,9},{9,8},{10,11... | collective-permute-start | bytes 786440 | tf_op jit(solution)/shard_map/ppermute | solution.py:402
  110.9 21.8 %collective-permute-start.17 = (bf16[2,1040,128]{2,1,0:T(8,128)(2,1)}, bf16[2,1040,128]{2,1,0:T(8,128)(2,1)}, u32[]{:S(2)}, u32[]{:S(2)}) collective-permute-start(bf16[2,1040,128]{2,1,0:T(8,128)(2,1)} %pad_maximum_fusion.16), channel_id=1, source_target_pairs={{0,8},{4,12},{8,0},{12,4},{16,24},{20,28},{24,16},{28,20},{1,9},{5... | collective-permute-start | bytes 1597448 | tf_op jit(solution)/shard_map/ppermute | solution.py:402
  113.1 19.5 %collective-permute-start.18 = (bf16[2,1040,128]{2,1,0:T(8,128)(2,1)}, bf16[2,1040,128]{2,1,0:T(8,128)(2,1)}, u32[]{:S(2)}, u32[]{:S(2)}) collective-permute-start(bf16[2,1040,128]{2,1,0:T(8,128)(2,1)} %pad_maximum_fusion.17), channel_id=1, source_target_pairs={{0,16},{4,20},{8,24},{12,28},{16,0},{20,4},{24,8},{28,12},{1,17},{... | collective-permute-start | bytes 1597448 | tf_op jit(solution)/shard_map/ppermute | solution.py:402
  130.3 25.9 %collective-permute-start.20 = (bf16[1024,512]{1,0:T(8,128)(2,1)}, bf16[1024,512]{1,0:T(8,128)(2,1)}, u32[]{:S(2)}, u32[]{:S(2)}) collective-permute-start(bf16[1024,512]{1,0:T(8,128)(2,1)} %get-tuple-element.146.refs_4_), channel_id=1, source_target_pairs={{0,1},{1,0},{2,3},{3,2},{4,5},{5,4},{6,7},{7,6},{8,9},{9,8},{10,11... | collective-permute-start | bytes 3145736 | tf_op jit(solution)/shard_map/ppermute | solution.py:402
  133.9 27.0 %collective-permute-start.23 = (bf16[4,1040,128]{2,1,0:T(8,128)(2,1)S(1)}, bf16[4,1040,128]{2,1,0:T(8,128)(2,1)}, u32[]{:S(2)}, u32[]{:S(2)}) collective-permute-start(bf16[4,1040,128]{2,1,0:T(8,128)(2,1)S(1)} %pad_maximum_fusion.4.refs_8_), channel_id=1, source_target_pairs={{0,16},{4,20},{8,24},{12,28},{16,0},{20,4},{24,8},{28,12},{1,17},{... | collective-permute-start | bytes 3194888 | tf_op jit(solution)/shard_map/ppermute | solution.py:402
  136.1 25.1 %collective-permute-start.24 = (bf16[4,1040,128]{2,1,0:T(8,128)(2,1)S(1)}, bf16[4,1040,128]{2,1,0:T(8,128)(2,1)S(1)}, u32[]{:S(2)}, u32[]{:S(2)}) collective-permute-start(bf16[4,1040,128]{2,1,0:T(8,128)(2,1)S(1)} %pad_maximum_fusion.5.refs_10_), channel_id=1, source_target_pairs={{0,8},{4,12},{8,0},{12,4},{16,24},{20,28},{24,16},{28,20},{1,9},{5... | collective-permute-start | bytes 3194888 | tf_op jit(solution)/shard_map/ppermute | solution.py:402
  137.8 23.1 %collective-permute-start.21 = (bf16[1024,512]{1,0:T(8,128)(2,1)}, bf16[1024,512]{1,0:T(8,128)(2,1)S(1)}, u32[]{:S(2)}, u32[]{:S(2)}) collective-permute-start(bf16[1024,512]{1,0:T(8,128)(2,1)} %get-tuple-element.146.refs_4_), channel_id=1, source_target_pairs={{0,4},{4,0},{8,12},{12,8},{16,20},{20,16},{24,28},{28,24},{1,5},{5... | collective-permute-start | bytes 3145736 | tf_op jit(solution)/shard_map/ppermute | solution.py:402
  180.5 15.5 %collective-permute-start.25 = (bf16[1024,1024]{1,0:T(8,128)(2,1)}, bf16[1024,1024]{1,0:T(8,128)(2,1)S(1)}, u32[]{:S(2)}, u32[]{:S(2)}) collective-permute-start(bf16[1024,1024]{1,0:T(8,128)(2,1)} %get-tuple-element.157), channel_id=1, source_target_pairs={{0,4},{4,0},{8,12},{12,8},{16,20},{20,16},{24,28},{28,24},{1,5},{5... | collective-permute-start | bytes 6291464 | tf_op jit(solution)/shard_map/ppermute | solution.py:402
  189.9 25.9 %collective-permute-start.28 = (bf16[1024,512]{1,0:T(8,128)(2,1)}, bf16[1024,512]{1,0:T(8,128)(2,1)}, u32[]{:S(2)}, u32[]{:S(2)}) collective-permute-start(bf16[1024,512]{1,0:T(8,128)(2,1)} %fusion.27), channel_id=1, source_target_pairs={{0,8},{4,12},{8,0},{12,4},{16,24},{20,28},{24,16},{28,20},{1,9},{5... | collective-permute-start | bytes 3145736 | tf_op jit(solution)/shard_map/ppermute | solution.py:402
  195.2 25.6 %collective-permute-start.27 = (bf16[1024,512]{1,0:T(8,128)(2,1)}, bf16[1024,512]{1,0:T(8,128)(2,1)}, u32[]{:S(2)}, u32[]{:S(2)}) collective-permute-start(bf16[1024,512]{1,0:T(8,128)(2,1)} %fusion.24), channel_id=1, source_target_pairs={{0,16},{4,20},{8,24},{12,28},{16,0},{20,4},{24,8},{28,12},{1,17},{... | collective-permute-start | bytes 3145736 | tf_op jit(solution)/shard_map/ppermute | solution.py:402
  202.3 25.3 %collective-permute-start.29 = (bf16[1024,512]{1,0:T(8,128)(2,1)}, bf16[1024,512]{1,0:T(8,128)(2,1)}, u32[]{:S(2)}, u32[]{:S(2)}) collective-permute-start(bf16[1024,512]{1,0:T(8,128)(2,1)} %keep_two.2), channel_id=1, source_target_pairs={{0,1},{1,0},{2,3},{3,2},{4,5},{5,4},{6,7},{7,6},{8,9},{9,8},{10,11... | collective-permute-start | bytes 3145736 | tf_op jit(solution)/shard_map/ppermute | solution.py:402
  220.8 18.0 %collective-permute-start.32 = (bf16[1024,256]{1,0:T(8,128)(2,1)}, bf16[1024,256]{1,0:T(8,128)(2,1)}, u32[]{:S(2)}, u32[]{:S(2)}) collective-permute-start(bf16[1024,256]{1,0:T(8,128)(2,1)} %dynamic-slice_convert_fusion), channel_id=1, source_target_pairs={{0,16},{4,20},{8,24},{12,28},{16,0},{20,4},{24,8},{28,12},{1,17},{... | collective-permute-start | bytes 1572872 | tf_op jit(solution)/shard_map/ppermute | solution.py:402
  221.6 17.1 %collective-permute-start.26 = (bf16[512,512]{1,0:T(8,128)(2,1)}, bf16[512,512]{1,0:T(8,128)(2,1)S(1)}, u32[]{:S(2)}, u32[]{:S(2)}) collective-permute-start(bf16[512,512]{1,0:T(8,128)(2,1)} %fusion.77), channel_id=1, source_target_pairs={{0,4},{4,0},{8,12},{12,8},{16,20},{20,16},{24,28},{28,24},{1,5},{5... | collective-permute-start | bytes 1572872 | tf_op jit(solution)/shard_map/ppermute | solution.py:402
  225.1 14.7 %collective-permute-start.31 = (bf16[1024,256]{1,0:T(8,128)(2,1)}, bf16[1024,256]{1,0:T(8,128)(2,1)}, u32[]{:S(2)}, u32[]{:S(2)}) collective-permute-start(bf16[1024,256]{1,0:T(8,128)(2,1)} %dynamic-slice_convert_fusion.1), channel_id=1, source_target_pairs={{0,8},{4,12},{8,0},{12,4},{16,24},{20,28},{24,16},{28,20},{1,9},{5... | collective-permute-start | bytes 1572872 | tf_op jit(solution)/shard_map/ppermute | solution.py:402
  239.8 11.3 %collective-permute-start.30 = (bf16[512,1024]{1,0:T(8,128)(2,1)}, bf16[512,1024]{1,0:T(8,128)(2,1)}, u32[]{:S(2)}, u32[]{:S(2)}) collective-permute-start(bf16[512,1024]{1,0:T(8,128)(2,1)} %get-tuple-element.176), channel_id=1, source_target_pairs={{0,4},{4,0},{8,12},{12,8},{16,20},{20,16},{24,28},{28,24},{1,5},{5... | collective-permute-start | bytes 3145736 | tf_op jit(solution)/shard_map/ppermute | solution.py:402
  239.8 18.4 %collective-permute-start.35 = (bf16[512,1024]{1,0:T(8,128)(2,1)}, bf16[512,1024]{1,0:T(8,128)(2,1)}, u32[]{:S(2)}, u32[]{:S(2)}) collective-permute-start(bf16[512,1024]{1,0:T(8,128)(2,1)} %get-tuple-element.183), channel_id=1, source_target_pairs={{0,4},{4,0},{8,12},{12,8},{16,20},{20,16},{24,28},{28,24},{1,5},{5... | collective-permute-start | bytes 3145736 | tf_op jit(solution)/shard_map/ppermute | solution.py:402
  245.0 28.2 %collective-permute-start.36 = (bf16[1152,512]{1,0:T(8,128)(2,1)S(1)}, bf16[1152,512]{1,0:T(8,128)(2,1)}, u32[]{:S(2)}, u32[]{:S(2)}) collective-permute-start(bf16[1152,512]{1,0:T(8,128)(2,1)S(1)} %maximum_maximum_fusion), channel_id=1, source_target_pairs={{0,8},{4,12},{8,0},{12,4},{16,24},{20,28},{24,16},{28,20},{1,9},{5... | collective-permute-start | bytes 3538952 | tf_op jit(solution)/shard_map/ppermute | solution.py:402
  249.8 28.9 %collective-permute-start.34 = (bf16[1152,512]{1,0:T(8,128)(2,1)S(1)}, bf16[1152,512]{1,0:T(8,128)(2,1)}, u32[]{:S(2)}, u32[]{:S(2)}) collective-permute-start(bf16[1152,512]{1,0:T(8,128)(2,1)S(1)} %pad_maximum_fusion), channel_id=1, source_target_pairs={{0,16},{4,20},{8,24},{12,28},{16,0},{20,4},{24,8},{28,12},{1,17},{... | collective-permute-start | bytes 3538952 | tf_op jit(solution)/shard_map/ppermute | solution.py:402
  256.6 28.2 %collective-permute-start.33 = (bf16[256,1024]{1,0:T(8,128)(2,1)}, bf16[256,1024]{1,0:T(8,128)(2,1)}, u32[]{:S(2)}, u32[]{:S(2)}) collective-permute-start(bf16[256,1024]{1,0:T(8,128)(2,1)} %get-tuple-element.181), channel_id=1, source_target_pairs={{0,1},{1,0},{2,3},{3,2},{4,5},{5,4},{6,7},{7,6},{8,9},{9,8},{10,11... | collective-permute-start | bytes 1572872 | tf_op jit(solution)/shard_map/ppermute | solution.py:402
  263.7 56.8 %collective-permute-start.38 = (bf16[256,1024]{1,0:T(8,128)(2,1)}, bf16[256,1024]{1,0:T(8,128)(2,1)}, u32[]{:S(2)}, u32[]{:S(2)}) collective-permute-start(bf16[256,1024]{1,0:T(8,128)(2,1)} %get-tuple-element.184), channel_id=1, source_target_pairs={{0,1},{1,0},{2,3},{3,2},{4,5},{5,4},{6,7},{7,6},{8,9},{9,8},{10,11... | collective-permute-start | bytes 1572872 | tf_op jit(solution)/shard_map/ppermute | solution.py:402
  266.6 53.5 %collective-permute-start.42 = (bf16[1024,128]{1,0:T(8,128)(2,1)}, bf16[1024,128]{1,0:T(8,128)(2,1)}, u32[]{:S(2)}, u32[]{:S(2)}) collective-permute-start(bf16[1024,128]{1,0:T(8,128)(2,1)} %dynamic-slice_convert_fusion.5), channel_id=1, source_target_pairs={{0,2},{1,3},{2,0},{3,1},{4,6},{5,7},{6,4},{7,5},{8,10},{9,11},{10,... | collective-permute-start | bytes 786440 | tf_op jit(solution)/shard_map/ppermute | solution.py:402
  273.2 47.3 %collective-permute-start.41 = (bf16[1024,128]{1,0:T(8,128)(2,1)}, bf16[1024,128]{1,0:T(8,128)(2,1)}, u32[]{:S(2)}, u32[]{:S(2)}) collective-permute-start(bf16[1024,128]{1,0:T(8,128)(2,1)} %dynamic-slice_convert_fusion.6), channel_id=1, source_target_pairs={{0,2},{1,3},{2,0},{3,1},{4,6},{5,7},{6,4},{7,5},{8,10},{9,11},{10,... | collective-permute-start | bytes 786440 | tf_op jit(solution)/shard_map/ppermute | solution.py:402
  278.7 32.7 %collective-permute-start.40 = (bf16[1152,256]{1,0:T(8,128)(2,1)}, bf16[1152,256]{1,0:T(8,128)(2,1)S(1)}, u32[]{:S(2)}, u32[]{:S(2)}) collective-permute-start(bf16[1152,256]{1,0:T(8,128)(2,1)} %fusion.39), channel_id=1, source_target_pairs={{0,16},{4,20},{8,24},{12,28},{16,0},{20,4},{24,8},{28,12},{1,17},{... | collective-permute-start | bytes 1769480 | tf_op jit(solution)/shard_map/ppermute | solution.py:402
  284.8 30.2 %collective-permute-start.39 = (bf16[1152,256]{1,0:T(8,128)(2,1)}, bf16[1152,256]{1,0:T(8,128)(2,1)}, u32[]{:S(2)}, u32[]{:S(2)}) collective-permute-start(bf16[1152,256]{1,0:T(8,128)(2,1)} %fusion.43), channel_id=1, source_target_pairs={{0,8},{4,12},{8,0},{12,4},{16,24},{20,28},{24,16},{28,20},{1,9},{5... | collective-permute-start | bytes 1769480 | tf_op jit(solution)/shard_map/ppermute | solution.py:402
  312.2 35.8 %collective-permute-start.37 = (bf16[256,512]{1,0:T(8,128)(2,1)}, bf16[256,512]{1,0:T(8,128)(2,1)}, u32[]{:S(2)}, u32[]{:S(2)}) collective-permute-start(bf16[256,512]{1,0:T(8,128)(2,1)} %slice.227), channel_id=1, source_target_pairs={{0,1},{1,0},{2,3},{3,2},{4,5},{5,4},{6,7},{7,6},{8,9},{9,8},{10,11... | collective-permute-start | bytes 786440 | tf_op jit(solution)/shard_map/ppermute | solution.py:402
  315.1 51.8 %collective-permute-start.55 = (bf16[1152,128]{1,0:T(8,128)(2,1)S(1)}, bf16[1152,128]{1,0:T(8,128)(2,1)}, u32[]{:S(2)}, u32[]{:S(2)}) collective-permute-start(bf16[1152,128]{1,0:T(8,128)(2,1)S(1)} %dynamic-slice_convert_fusion.2), channel_id=1, source_target_pairs={{0,2},{1,3},{2,0},{3,1},{4,6},{5,7},{6,4},{7,5},{8,10},{9,11},{10,... | collective-permute-start | bytes 884744 | tf_op jit(solution)/shard_map/ppermute | solution.py:402
  320.1 47.8 %collective-permute-start.54 = (bf16[1152,128]{1,0:T(8,128)(2,1)S(1)}, bf16[1152,128]{1,0:T(8,128)(2,1)}, u32[]{:S(2)}, u32[]{:S(2)}) collective-permute-start(bf16[1152,128]{1,0:T(8,128)(2,1)S(1)} %dynamic-slice_convert_fusion.3), channel_id=1, source_target_pairs={{0,2},{1,3},{2,0},{3,1},{4,6},{5,7},{6,4},{7,5},{8,10},{9,11},{10,... | collective-permute-start | bytes 884744 | tf_op jit(solution)/shard_map/ppermute | solution.py:402
  362.4 7.2 %collective-permute-start.49 = (bf16[256,128]{1,0:T(8,128)(2,1)S(1)}, bf16[256,128]{1,0:T(8,128)(2,1)}, u32[]{:S(2)}, u32[]{:S(2)}) collective-permute-start(bf16[256,128]{1,0:T(8,128)(2,1)S(1)} %add_convert_fusion), channel_id=1, source_target_pairs={{0,3},{1,2},{2,1},{3,0},{4,7},{5,6},{6,5},{7,4},{8,11},{9,10},{10,... | collective-permute-start | bytes 196616 | tf_op jit(solution)/shard_map/ppermute | solution.py:402
  365.2 6.3 %collective-permute-start.48 = (bf16[256,128]{1,0:T(8,128)(2,1)S(1)}, bf16[256,128]{1,0:T(8,128)(2,1)}, u32[]{:S(2)}, u32[]{:S(2)}) collective-permute-start(bf16[256,128]{1,0:T(8,128)(2,1)S(1)} %add_convert_fusion), channel_id=1, source_target_pairs={{0,2},{1,3},{2,0},{3,1},{4,6},{5,7},{6,4},{7,5},{8,10},{9,11},{10,... | collective-permute-start | bytes 196616 | tf_op jit(solution)/shard_map/ppermute | solution.py:402
  365.2 6.3 %collective-permute-start.47 = (bf16[256,128]{1,0:T(8,128)(2,1)S(1)}, bf16[256,128]{1,0:T(8,128)(2,1)}, u32[]{:S(2)}, u32[]{:S(2)}) collective-permute-start(bf16[256,128]{1,0:T(8,128)(2,1)S(1)} %add_convert_fusion), channel_id=1, source_target_pairs={{0,1},{1,0},{2,3},{3,2},{4,5},{5,4},{6,7},{7,6},{8,9},{9,8},{10,11... | collective-permute-start | bytes 196616 | tf_op jit(solution)/shard_map/ppermute | solution.py:402
  369.1 17.6 %collective-permute-start.58 = (f32[16,512]{1,0:T(8,128)S(1)}, f32[16,512]{1,0:T(8,128)S(1)}, u32[]{:S(2)}, u32[]{:S(2)}) collective-permute-start(f32[16,512]{1,0:T(8,128)S(1)} %squeeze.32), channel_id=1, source_target_pairs={{0,5},{1,4},{2,7},{3,6},{4,1},{5,0},{6,3},{7,2},{8,13},{9,12},{10,... | collective-permute-start | bytes 98312 | tf_op jit(solution)/shard_map/ppermute | solution.py:408
  369.2 17.6 %collective-permute-start.57 = (f32[16,512]{1,0:T(8,128)S(1)}, f32[16,512]{1,0:T(8,128)S(1)}, u32[]{:S(2)}, u32[]{:S(2)}) collective-permute-start(f32[16,512]{1,0:T(8,128)S(1)} %squeeze.31), channel_id=1, source_target_pairs={{0,4},{4,0},{8,12},{12,8},{16,20},{20,16},{24,28},{28,24},{1,5},{5... | collective-permute-start | bytes 98312 | tf_op jit(solution)/shard_map/ppermute | solution.py:402
  372.5 6.1 %collective-permute-start.52 = (f32[256,128]{1,0:T(8,128)S(1)}, f32[256,128]{1,0:T(8,128)S(1)}, u32[]{:S(2)}, u32[]{:S(2)}) collective-permute-start(f32[256,128]{1,0:T(8,128)S(1)} %add_add_fusion.refs_0_), channel_id=1, source_target_pairs={{0,24},{4,28},{8,16},{12,20},{16,8},{20,12},{24,0},{28,4},{1,25},{... | collective-permute-start | bytes 393224 | tf_op jit(solution)/shard_map/ppermute | solution.py:402
  374.0 12.7 %collective-permute-start.56 = (f32[16,512]{1,0:T(8,128)S(1)}, f32[16,512]{1,0:T(8,128)S(1)}, u32[]{:S(2)}, u32[]{:S(2)}) collective-permute-start(f32[16,512]{1,0:T(8,128)S(1)} %squeeze.30), channel_id=1, source_target_pairs={{0,1},{1,0},{2,3},{3,2},{4,5},{5,4},{6,7},{7,6},{8,9},{9,8},{10,11... | collective-permute-start | bytes 98312 | tf_op jit(solution)/shard_map/ppermute | solution.py:402
  374.4 9.1 %collective-permute-start.51 = (f32[256,128]{1,0:T(8,128)S(1)}, f32[256,128]{1,0:T(8,128)S(1)}, u32[]{:S(2)}, u32[]{:S(2)}) collective-permute-start(f32[256,128]{1,0:T(8,128)S(1)} %add_add_fusion.refs_0_), channel_id=1, source_target_pairs={{0,16},{4,20},{8,24},{12,28},{16,0},{20,4},{24,8},{28,12},{1,17},{... | collective-permute-start | bytes 393224 | tf_op jit(solution)/shard_map/ppermute | solution.py:402
  (69 other events, 437.4 us)

commit v5 on v4

--- a/solution.py
+++ b/solution.py
@@ -615,27 +615,31 @@
 
 
 def keep_two_kernel(d_project_ref, w_ref, got_ref, *refs):
-    result = turned_dot(d_project_ref[...], w_ref[...]) + got_ref[...].astype(jnp.float32)
-    if len(refs) == 2:
-        result = result + refs[0][...]
-    refs[-1][...] = result.astype(refs[-1].dtype)
+    result = turned_dot(d_project_ref[...], w_ref[...])
+    half = result.shape[0] // 2
+    for to, start in ((0, half), (half, 0)):
+        part = result[to : to + half] + got_ref[start : start + half, :].astype(jnp.float32)
+        if len(refs) == 2:
+            part = part + refs[0][to : to + half, :]
+        refs[-1][to : to + half, :] = part.astype(refs[-1].dtype)
 
 
 def keep_two(d_project, weight, got, number, through=None):
     count, total = d_project.shape
     wide = (weight.shape[0] - BELOW) // 4
+    per = wide // STEP
     specs = [
-        pl.BlockSpec((STEP, total), lambda i: (i, 0)),
-        pl.BlockSpec((wide, total), lambda i: (number, 0)),
-        pl.BlockSpec((STEP, wide), lambda i: (jnp.bitwise_xor(i, 2), number)),
+        pl.BlockSpec((count, total), lambda j: (0, 0)),
+        pl.BlockSpec((STEP, total), lambda j: (number * per + j, 0)),
+        pl.BlockSpec((count, STEP), lambda j: (0, number * per + j)),
     ]
     if through is not None:
-        specs.append(pl.BlockSpec((STEP, wide), lambda i: (i, 0)))
+        specs.append(pl.BlockSpec((count, STEP), lambda j: (0, j)))
     return pl.pallas_call(
         keep_two_kernel,
-        grid=(count // STEP,),
+        grid=(per,),
         in_specs=specs,
-        out_specs=pl.BlockSpec((STEP, wide), lambda i: (i, 0)),
+        out_specs=pl.BlockSpec((count, STEP), lambda j: (0, j)),
         out_shape=jax.ShapeDtypeStruct((count, wide), jnp.bfloat16 if through is None else jnp.float32),
         compiler_params=pltpu.CompilerParams(vmem_limit_bytes=VMEM_BYTES),
         cost_estimate=LIGHT,
@@ -978,44 +982,57 @@
     )(member.astype(jnp.int32).reshape(1), early, late, table, more_table, first, second, given)
 
 
-def unpack_kernel(layout, span, table_at, at_ref, summed_ref, *out_refs):
-    per = span + 8
-    for number, (kernel, leading, filters, natural) in enumerate(layout):
-        out_ref = out_refs[kernel - 1]
-        height = kernel * 16
-        done = 0
-        while done < filters:
-            block, lane = divmod(natural + done, LANES)
-            wide = min(LANES - lane, filters - done)
-            out_ref[:, leading + done : leading + done + wide] = summed_ref[
-                block * per : block * per + height, lane : lane + wide
-            ]
-            done += wide
-    table_ref, bias_ref = out_refs[7], out_refs[8]
-    vocab, emb_width = table_ref.shape
-    for number, start in enumerate(range(0, vocab, TABLE_ROWS)):
-        rows = min(TABLE_ROWS, vocab - start)
-        table_ref[start : start + rows, :] = summed_ref[
-            table_at : table_at + rows, number * emb_width : (number + 1) * emb_width
-        ]
-    for block in range(bias_ref.shape[0]):
-        bias_ref[block : block + 1, :] = summed_ref[block * per + span : block * per + span + 1, :]
-    for number, out_ref in enumerate(out_refs[9:]):
-        out_ref[...] = summed_ref[pl.ds(at_ref[number], 1), :]
-
-
-def unpack(summed, rows, layout, span, table_at, shapes):
+def unpack_kernel(layout, span, table_at, side_ref, at_ref, own_ref, got_ref, *out_refs):
+    half = own_ref.shape[0]
+
+    def copy(first_ref, second_ref):
+        def move(out_ref, to, lanes_to, start, count, lanes):
+            for source, low in ((first_ref, 0), (second_ref, half)):
+                begin, end = max(start, low), min(start + count, low + half)
+                if begin < end:
+                    out_ref[to + begin - start : to + end - start, lanes_to] = source[begin - low : end - low, lanes]
+
+        per = span + 8
+        for number, (kernel, leading, filters, natural) in enumerate(layout):
+            done = 0
+            while done < filters:
+                block, lane = divmod(natural + done, LANES)
+                wide = min(LANES - lane, filters - done)
+                to = slice(leading + done, leading + done + wide)
+                move(out_refs[kernel - 1], 0, to, block * per, kernel * 16, slice(lane, lane + wide))
+                done += wide
+        table_ref, bias_ref = out_refs[7], out_refs[8]
+        vocab, emb_width = table_ref.shape
+        for number, start in enumerate(range(0, vocab, TABLE_ROWS)):
+            rows = min(TABLE_ROWS, vocab - start)
+            lanes = slice(number * emb_width, (number + 1) * emb_width)
+            move(table_ref, start, slice(0, emb_width), table_at, rows, lanes)
+        for block in range(bias_ref.shape[0]):
+            move(bias_ref, block, slice(0, LANES), block * per + span, 1, slice(0, LANES))
+        for number, out_ref in enumerate(out_refs[9:]):
+            out_ref[...] = second_ref[pl.ds(at_ref[number] - half, 1), :]
+
+    @pl.when(side_ref[0] == 0)
+    def lower():
+        copy(own_ref, got_ref)
+
+    @pl.when(side_ref[0] == 1)
+    def upper():
+        copy(got_ref, own_ref)
+
+
+def unpack(own, got, mine, rows, layout, span, table_at, shapes):
     count = layout[-1][2] + layout[-1][3]
     shapes = shapes + [(count // LANES, LANES)] + [(1, LANES)] * 3
     return pl.pallas_call(
         functools.partial(unpack_kernel, tuple(layout), span, table_at),
-        in_specs=[pl.BlockSpec(memory_space=pltpu.SMEM), NEAR],
+        in_specs=[pl.BlockSpec(memory_space=pltpu.SMEM)] * 2 + [NEAR] * 2,
         out_specs=[NEAR] * len(shapes),
         out_shape=[jax.ShapeDtypeStruct(shape, jnp.float32) for shape in shapes],
         compiler_params=pltpu.CompilerParams(vmem_limit_bytes=VMEM_BYTES),
         cost_estimate=LIGHT,
         name="unpack",
-    )(rows.astype(jnp.int32), summed)
+    )(mine.astype(jnp.int32).reshape(1), rows.astype(jnp.int32), own, got)
 
 
 def sum_all(x):
@@ -1032,7 +1049,7 @@
     x = parts[0]
     for bits in groups[::-1]:
         x = gather_rows(x, "wide", bits)
-    return gather_rows(x, "wide", [1]), sent
+    return x, swap(x, "wide", 1), sent
 
 
 def local(
@@ -1208,11 +1225,6 @@
         [carried_two, hidden_along, hidden_wide, hidden_both], copies, gather_two.result(), [out_weight] + givens, shape
     )
 
-    out_bias = weight_two[feature_count + 1].astype(jnp.float32).reshape(wide_size // 2, 1, narrow_size // 2, 1, width)
-    out_bias = out_bias[..., :out_part]
-    here = (lax.iota(jnp.int32, 2) == mine_wide)[:, None] & (lax.iota(jnp.int32, 2) == mine_narrow)[None, :]
-    out_bias = jnp.where(here[None, :, None, :, None], out_bias, 0.0).reshape(-1)
-
     got = swap(away, "wide", 1)
     scatter_two = Scatter(input_two, d_project)
     sent = scatter_two.send()
@@ -1224,6 +1236,10 @@
     grad_out = jnp.einsum("tn,tf->nf", given, input_out, preferred_element_type=jnp.float32).astype(jnp.bfloat16)
     grad_out = member_rows(grad_out, out_part).reshape(members, blocks, out_part, own_width // width, width)
     grad_out = grad_out.transpose(0, 2, 3, 1, 4).reshape(-1, blocks * width)
+    out_bias = after(weight_two, own)[feature_count + 1].astype(jnp.float32).reshape(wide_size // 2, 1, narrow_size // 2, 1, width)
+    out_bias = out_bias[..., :out_part]
+    here = (lax.iota(jnp.int32, 2) == mine_wide)[:, None] & (lax.iota(jnp.int32, 2) == mine_narrow)[None, :]
+    out_bias = jnp.where(here[None, :, None, :, None], out_bias, 0.0).reshape(-1)
     encoded = jnp.einsum("tf,nf->tn", input_out, out_weight, preferred_element_type=jnp.float32) + out_bias
     encoded_got = swap(encoded[2 * tokens :].astype(jnp.bfloat16), "wide", 1)
     encoded = encoded[: 2 * tokens]
@@ -1248,7 +1264,7 @@
     while scatter_two.stages[0]:
         scatter_two.add(sent)
         sent_two = scatter_two.send()
-    ids_across = jnp.pad(char_ids.T, ((0, -chars % 8), (0, 0)))
+    ids_across = jnp.pad(after(char_ids, late_send).T, ((0, -chars % 8), (0, 0)))
     span = WIDEST * emb_width
     late_filters, late_table = conv_backward(
         [late[0]], [late[2]], [late[3]], late_own, after(late_got, sent, sent_two, ids_across), windows, filters, ids_across, trips, low_places, vocab_count, span, half_blocks
@@ -1270,7 +1286,7 @@
     ends.append(ends[-1] + members * own_sums)
     ends.append(ends[-1] + members * own_sums)
     unit = 16 * wide_size
-    given_sum = jnp.sum(after(cotangent, early[1]).astype(jnp.float32), axis=0).reshape(-1, LANES)
+    given_sum = jnp.sum(after(cotangent, late_send).astype(jnp.float32), axis=0).reshape(-1, LANES)
     packed = pack(
         member,
         after(early_filters, resolved).reshape(-1, LANES),
@@ -1282,7 +1298,7 @@
         given_sum,
         -(-(ends[-1] + given_sum.shape[0]) // unit) * unit,
     )
-    summed, sent = sum_all(packed)
+    summed, summed_got, sent = sum_all(packed)
     scatter_two.add(packed)
     scatter_one.add(sent)
     grad_one_w = scatter_one.result()
@@ -1294,6 +1310,8 @@
     out_at = (wide * narrow_size + narrow) * out_part
     *grad_weights, d_table, d_bias, own_one, own_two, own_out = unpack(
         summed,
+        summed_got,
+        mine_wide,
         jnp.stack([ends[2] + own_at // LANES, ends[3] + own_at // LANES, ends[4] + out_at // LANES]),
         layout,
         span,

time: 404 us -> 402 us (level)
    unnamed x124 -> x130, local copies, waits for them, and re-layouts: 16.8 us -> 14.6 us
  transfers between devices with their start and end apart: 59 -> 59, of which waited for: 13 -> 11; matrix products, arithmetic and copies ran while one was open for 24% -> 23% of each run, Pallas kernels for 43% -> 43%
where the time goes in v5:
time: 402 us; the launch traced here: 396 us
  Pallas kernels  190 us (47%)
  starting transfers between devices  56.2 us (14%)
  local copies, waits for them, and re-layouts  48.4 us (12%)
  waiting for transfers between devices  38.7 us (10%)
  other arithmetic  36.6 us (9%)
  matrix products  24.2 us (6%)
    ppermute x58, starting transfers between devices, swap(): lax.ppermute(x, axis, [(i, i ^ bit) for i in range(lax.axis_size(axis))])  54.9 us
    pallas_call x2, Pallas kernels, conv_backward(): pl.pallas_call(functools.partial(backward_kernel, chars, low_places, span...  53 us
    pallas_call x3, Pallas kernels, conv_forward(): pl.pallas_call(functools.partial(kernel, low_places, extras), grid_spec=p...  51.3 us
    ppermute x58, waiting for transfers between devices, swap(): lax.ppermute(x, axis, [(i, i ^ bit) for i in range(lax.axis_size(axis))])  38.7 us
    pallas_call x2, Pallas kernels, call_layer(): pl.pallas_call(functools.partial(kernel, tuple(x_copies), tuple(w_copies)...  33.7 us
    dot_general x8, matrix products, product(): lax.dot_general(inputs[:, number * half:(number + 1) * half], after(halve...  19 us
    unnamed x130, local copies, waits for them, and re-layouts  14.6 us
    pallas_call x1, Pallas kernels, back_one(): pl.pallas_call(back_one_kernel, in_specs=[NEAR] * 4 + [ANYWHERE] * 2, out...  11.1 us
  transfers between devices with their start and end apart: 59, of which 11 were waited for; matrix products, arithmetic and copies ran while one was open for 23% of the time, Pallas kernels for 43%

profile of v5, /device:TPU:0, one launch (start us, length us, event | category | flops | bytes accessed | tf_op | source)
XLA Modules:
  0.0 396.5 jit_solution(16880246014106134191)
XLA Ops:
  1.9 4.1 %collective-permute-start = (bf16[1,16,2048]{2,1,0:T(8,128)(2,1)S(1)}, bf16[1,16,2048]{2,1,0:T(8,128)(2,1)S(1)}, u32[]{:S(2)}, u32[]{:S(2)}) collective-permute-start(bf16[1,16,2048]{2,1,0:T(8,128)(2,1)S(1)} %bitcast.194), channel_id=1, source_target_pairs={{0,2},{1,3},{2,0},{3,1},{4,6},{5,7},{6,4},{7,5},{8,10},{9,11},{10,... | collective-permute-start | bytes 196616 | tf_op jit(solution)/shard_map/ppermute | solution.py:402
  15.3 1.9 bank_rows.2
  18.7 1.6 collective-permute-start.4
  21.4 9.4 %prepare.1 = (bf16[50,256,128]{2,1,0:T(8,128)(2,1)}, bf16[128,2048]{1,0:T(8,128)(2,1)}, f32[8,2048]{1,0:T(8,128)}) custom-call(s32[256,50]{1,0:T(8,128)} %copy.77.ids_ref, bf16[262,16]{1,0:T(8,128)(2,1)} %copy.78.chars_ref, bf16[1,2048]{1,0:T(2,128)(2,1)} %reshape.354.bias_ref, bf16[16,32]{1,0:T(8,128)(2,1)} %refs_0_.2, bf16[32,32]{1,0:T(8,128)(2,1)} %refs_1_.1, ...), custom_call_target="tpu_custom_call" | custom-call | flops 1 | bytes 1 | tf_op jit(solution)/shard_map/prepare/pallas_call | solution.py:65
  31.4 21.1 %conv_forward.3 = (bf16[4,50,256,256]{3,2,1,0:T(8,128)(2,1)}, bf16[256,1024]{1,0:T(8,128)(2,1)}, f32[256,1024]{1,0:T(8,128)}, f32[5,256,1024]{2,1,0:T(8,128)}) custom-call(s32[4]{0:T(128)} %broadcast.226.trip_ref, bf16[50,256,128]{2,1,0:T(8,128)(2,1)} %get-tuple-element.202.win_ref.refs_5_, bf16[128,2048]{1,0:T(8,128)(2,1)} %get-tuple-element.124.weight_ref.refs_6_, ...), custom_call_target="tpu_custom_call" | custom-call | flops 1 | bytes 1 | tf_op jit(solution)/shard_map/conv_forward/pallas_call | solution.py:145
  54.0 1.6 collective-permute-start.2
  56.7 2.8 collective-permute-start.9
  60.0 14.7 %conv_forward.4 = (bf16[4,50,256,256]{3,2,1,0:T(8,128)(2,1)}, bf16[256,512]{1,0:T(8,128)(2,1)}, f32[256,1024]{1,0:T(8,128)}, f32[5,256,1024]{2,1,0:T(8,128)}) custom-call(s32[2]{0:T(128)} %broadcast.227.trip_ref, bf16[50,256,128]{2,1,0:T(8,128)(2,1)} %get-tuple-element.202.win_ref.refs_5_, bf16[128,2048]{1,0:T(8,128)(2,1)} %get-tuple-element.124.weight_ref.refs_6_, ...), custom_call_target="tpu_custom_call" | custom-call | flops 1 | bytes 1 | tf_op jit(solution)/shard_map/conv_forward/pallas_call | solution.py:145
  79.4 1.6 collective-permute-start.11
  88.5 15.5 %conv_forward.5 = (bf16[4,50,256,256]{3,2,1,0:T(8,128)(2,1)}, bf16[256,512]{1,0:T(8,128)(2,1)}, f32[256,1024]{1,0:T(8,128)}, f32[5,256,1024]{2,1,0:T(8,128)}) custom-call(s32[2]{0:T(128)} %constant.547.trip_ref, bf16[50,256,128]{2,1,0:T(8,128)(2,1)} %get-tuple-element.202.win_ref.refs_5_, ...), custom_call_target="tpu_custom_call", output_to_operand_aliasing={{0}: (4, {}), {2}: (5, {}), {3}: (6, {})} | custom-call | flops 1 | bytes 1 | tf_op jit(solution)/shard_map/conv_forward/pallas_call | solution.py:145
  114.1 16.1 %layer_one.1 = (bf16[1024,2048]{1,0:T(8,128)(2,1)}, bf16[2080,1024]{1,0:T(8,128)(2,1)}, f32[1024,1024]{1,0:T(8,128)}, bf16[1024,512]{1,0:T(8,128)(2,1)}, bf16[1024,512]{1,0:T(8,128)(2,1)}) custom-call(s32[16]{0:T(128)} %stack.285.at_ref, bf16[2048,512]{1,0:T(8,128)(2,1)} %compare_convert_fusion.pick_ref.pick_far, ...), custom_call_target="tpu_custom_call" | custom-call | flops 1 | bytes 1 | tf_op jit(solution)/shard_map/layer_one/pallas_call | solution.py:552
  130.3 1.7 collective-permute-start.20
  137.8 18.1 %collective-permute-done.20.refs_5_ = bf16[1024,512]{1,0:T(8,128)(2,1)} collective-permute-done((bf16[1024,512]{1,0:T(8,128)(2,1)}, bf16[1024,512]{1,0:T(8,128)(2,1)}, u32[]{:S(2)}, u32[]{:S(2)}) %collective-permute-start.20) | collective-permute-done | bytes 1048608 | tf_op jit(solution)/shard_map/ppermute | solution.py:402
  159.2 2.1 collective-permute-done.23.refs_9_
  161.3 17.6 %layer_two.1 = (bf16[1024,2048]{1,0:T(8,128)(2,1)}, bf16[2080,1024]{1,0:T(8,128)(2,1)}, bf16[1024,512]{1,0:T(8,128)(2,1)}, bf16[1024,1024]{1,0:T(8,128)(2,1)}, f...) custom-call(s32[16]{0:T(128)} %stack.285.at_ref, ...), custom_call_target="tpu_custom_call" | custom-call | flops 1 | bytes 1 | tf_op jit(solution)/shard_map/layer_two/pallas_call | solution.py:552
  180.7 1.7 constant_dynamic-slice_fusion.13
  186.9 2.3 fusion.27
  189.8 2.7 fusion.24
  194.0 4.3 %keep_two.2 = bf16[1024,512]{1,0:T(8,128)(2,1)} custom-call(bf16[1024,1024]{1,0:T(8,128)(2,1)} %get-tuple-element.162.d_project_ref, bf16[2080,1024]{1,0:T(8,128)(2,1)} %get-tuple-element.165.w_ref, bf16[1024,1024]{1,0:T(8,128)(2,1)} %collective-permute-done.25.got_ref), custom_call_target="tpu_custom_call" | custom-call | flops 1 | bytes 1 | tf_op jit(solution)/shard_map/keep_two/pallas_call | solution.py:638
  199.3 4.9 %keep_two.3.own_ref = f32[1024,512]{1,0:T(8,128)} custom-call(bf16[1024,1024]{1,0:T(8,128)(2,1)} %get-tuple-element.162.d_project_ref, bf16[2080,1024]{1,0:T(8,128)(2,1)} %get-tuple-element.165.w_ref, bf16[1024,1024]{1,0:T(8,128)(2,1)} %collective-permute-done.25.got_ref, f32[1024,512]{1,0:T(8,128)} %get-tuple-element.163.refs_0_), custom_call_target="tpu_custom_call" | custom-call | flops 1 | bytes 1 | tf_op jit(solution)/shard_map/keep_two/pallas_call | solution.py:638
  204.3 1.8 convolution_convert_fusion.1
  207.4 2.1 convolution_add_fusion
  210.4 4.3 %collective-permute-done.28 = bf16[1024,512]{1,0:T(8,128)(2,1)} collective-permute-done((bf16[1024,512]{1,0:T(8,128)(2,1)}, bf16[1024,512]{1,0:T(8,128)(2,1)}, u32[]{:S(2)}, u32[]{:S(2)}) %collective-permute-start.28) | collective-permute-done | bytes 1048608 | tf_op jit(solution)/shard_map/ppermute | solution.py:402
  214.7 3.0 collective-permute-done.27
  217.7 3.2 convert_add_fusion.2
  223.4 2.5 convert_add_fusion.3
  230.7 11.1 %back_one.1 = (bf16[1024,1024]{1,0:T(8,128)(2,1)}, bf16[1024,512]{1,0:T(8,128)(2,1)}, f32[8,1024]{1,0:T(8,128)}, bf16[512,1024]{1,0:T(8,128)(2,1)}, bf16[512,1024]{1,0:T(8,128)(2,1)}) custom-call(f32[1024,512]{1,0:T(8,128)} %keep_two.3.own_ref, bf16[1024,512]{1,0:T(8,128)(2,1)} %collective-permute-done.29.got_ref, ...), custom_call_target="tpu_custom_call" | custom-call | flops 1 | bytes 1 | tf_op jit(solution)/shard_map/back_one/pallas_call | solution.py:686
  242.0 1.8 copy-done
  252.6 5.5 %keep_one.2 = (f32[256,1024]{1,0:T(8,128)}, bf16[256,1024]{1,0:T(8,128)(2,1)}) custom-call(bf16[1024,1024]{1,0:T(8,128)(2,1)} %get-tuple-element.185.d_project_ref, bf16[1024,512]{1,0:T(8,128)(2,1)} %get-tuple-element.178.through_ref, bf16[2080,1024]{1,0:T(8,128)(2,1)} %get-tuple-element.171.w_far.w_ref, ...), custom_call_target="tpu_custom_call" | custom-call | flops 1 | bytes 1 | tf_op jit(solution)/shard_map/keep_one/pallas_call | solution.py:718
  260.3 5.5 %keep_one.3 = (f32[256,1024]{1,0:T(8,128)}, bf16[256,1024]{1,0:T(8,128)(2,1)}) custom-call(bf16[1024,1024]{1,0:T(8,128)(2,1)} %get-tuple-element.185.d_project_ref, bf16[1024,512]{1,0:T(8,128)(2,1)} %get-tuple-element.178.through_ref, bf16[2080,1024]{1,0:T(8,128)(2,1)} %get-tuple-element.171.w_far.w_ref, ...), custom_call_target="tpu_custom_call" | custom-call | flops 1 | bytes 1 | tf_op jit(solution)/shard_map/keep_one/pallas_call | solution.py:718
  265.8 1.6 convert_add_fusion.4
  270.6 2.6 collective-permute-start.41
  273.2 3.7 collective-permute-done.36
  277.9 3.3 convert_add_fusion
  282.7 2.5 convert_add_fusion.1
  290.5 25.5 %conv_backward.2 = (f32[8,120,128]{2,1,0:T(8,128)}, f32[40,128]{1,0:T(8,128)}) custom-call(s32[4]{0:T(128)} %broadcast.226.trip_ref, bf16[4,50,256,256]{3,2,1,0:T(8,128)(2,1)} %get-tuple-element.174.refs_0_, f32[256,1024]{1,0:T(8,128)} %get-tuple-element.175.refs_1_, f32[5,256,1024]{2,1,0:T(8,128)} %get-tuple-element.176.refs_2_, ...), custom_call_target="tpu_custom_call" | custom-call | flops 1 | bytes 1 | tf_op jit(solution)/shard_map/conv_backward/pallas_call | solution.py:290
  321.0 2.7 collective-permute-start.55
  323.7 27.4 %conv_backward.3 = (f32[8,120,128]{2,1,0:T(8,128)}, f32[40,128]{1,0:T(8,128)}) custom-call(s32[4]{0:T(128)} %constant.549.trip_ref, bf16[4,50,256,256]{3,2,1,0:T(8,128)(2,1)} %get-tuple-element.196.refs_0_, f32[256,1024]{1,0:T(8,128)} %get-tuple-element.197.refs_1_, f32[5,256,1024]{2,1,0:T(8,128)} %get-tuple-element.198.refs_2_, ...), custom_call_target="tpu_custom_call" | custom-call | flops 1 | bytes 1 | tf_op jit(solution)/shard_map/conv_backward/pallas_call | solution.py:290
  351.1 2.4 pack.1
  359.6 1.6 collective-permute-start.45
  361.7 1.7 fusion.52
  363.9 2.5 collective-permute-done.46
  367.4 3.5 collective-permute-start.49
  377.3 2.0 collective-permute-done.50.refs_1_
  382.5 2.4 bank_rows.3
  386.2 1.9 join.1.own_ref
  391.1 2.3 unpack.1
  393.4 1.6 copy.90
  (369 shorter events, 116.0 us)
Async XLA Ops:
  1.9 11.9 %collective-permute-start = (bf16[1,16,2048]{2,1,0:T(8,128)(2,1)S(1)}, bf16[1,16,2048]{2,1,0:T(8,128)(2,1)S(1)}, u32[]{:S(2)}, u32[]{:S(2)}) collective-permute-start(bf16[1,16,2048]{2,1,0:T(8,128)(2,1)S(1)} %bitcast.194), channel_id=1, source_target_pairs={{0,2},{1,3},{2,0},{3,1},{4,6},{5,7},{6,4},{7,5},{8,10},{9,11},{10,... | collective-permute-start | bytes 196616 | tf_op jit(solution)/shard_map/ppermute | solution.py:402
  13.8 40.1 %collective-permute-start.1 = (bf16[2,16,2048]{2,1,0:T(8,128)(2,1)S(1)}, bf16[2,16,2048]{2,1,0:T(8,128)(2,1)S(1)}, u32[]{:S(2)}, u32[]{:S(2)}) collective-permute-start(bf16[2,16,2048]{2,1,0:T(8,128)(2,1)S(1)} %pad_maximum_fusion.22), channel_id=1, source_target_pairs={{0,8},{4,12},{8,0},{12,4},{16,24},{20,28},{24,16},{28,20},{1,9},{5... | collective-permute-start | bytes 393224 | tf_op jit(solution)/shard_map/ppermute | solution.py:402
  17.3 38.3 %collective-permute-start.3 = (bf16[2080,128]{1,0:T(8,128)(2,1)}, bf16[2080,128]{1,0:T(8,128)(2,1)S(1)}, u32[]{:S(2)}, u32[]{:S(2)}) collective-permute-start(bf16[2080,128]{1,0:T(8,128)(2,1)} %bank_rows.2), channel_id=1, source_target_pairs={{0,2},{1,3},{2,0},{3,1},{4,6},{5,7},{6,4},{7,5},{8,10},{9,11},{10,... | collective-permute-start | bytes 1597448 | tf_op jit(solution)/shard_map/ppermute | solution.py:402
  18.7 37.6 %collective-permute-start.4 = (bf16[256,512]{1,0:T(8,128)(2,1)S(1)}, bf16[256,512]{1,0:T(8,128)(2,1)}, u32[]{:S(2)}, u32[]{:S(2)}) collective-permute-start(bf16[256,512]{1,0:T(8,128)(2,1)S(1)} %copy-done.26), channel_id=1, source_target_pairs={{0,1},{1,0},{2,3},{3,2},{4,5},{5,4},{6,7},{7,6},{8,9},{9,8},{10,11... | collective-permute-start | bytes 786440 | tf_op jit(solution)/shard_map/ppermute | solution.py:402
  20.3 36.4 %collective-permute-start.5 = (bf16[256,512]{1,0:T(8,128)(2,1)S(1)}, bf16[256,512]{1,0:T(8,128)(2,1)}, u32[]{:S(2)}, u32[]{:S(2)}) collective-permute-start(bf16[256,512]{1,0:T(8,128)(2,1)S(1)} %copy-done.26), channel_id=1, source_target_pairs={{0,4},{4,0},{8,12},{12,8},{16,20},{20,16},{24,28},{28,24},{1,5},{5... | collective-permute-start | bytes 786440 | tf_op jit(solution)/shard_map/ppermute | solution.py:402
  52.5 36.1 %collective-permute-start.8 = (bf16[256,1024]{1,0:T(8,128)(2,1)}, bf16[256,1024]{1,0:T(8,128)(2,1)}, u32[]{:S(2)}, u32[]{:S(2)}) collective-permute-start(bf16[256,1024]{1,0:T(8,128)(2,1)} %get-tuple-element.126.refs_0_), channel_id=1, source_target_pairs={{0,1},{1,0},{2,3},{3,2},{4,5},{5,4},{6,7},{7,6},{8,9},{9,8},{10,11... | collective-permute-start | bytes 1572872 | tf_op jit(solution)/shard_map/ppermute | solution.py:402
  54.0 20.8 %collective-permute-start.2 = (bf16[4,16,2048]{2,1,0:T(8,128)(2,1)S(1)}, bf16[4,16,2048]{2,1,0:T(8,128)(2,1)S(1)}, u32[]{:S(2)}, u32[]{:S(2)}) collective-permute-start(bf16[4,16,2048]{2,1,0:T(8,128)(2,1)S(1)} %pad_maximum_fusion.21), channel_id=1, source_target_pairs={{0,16},{4,20},{8,24},{12,28},{16,0},{20,4},{24,8},{28,12},{1,17},{... | collective-permute-start | bytes 786440 | tf_op jit(solution)/shard_map/ppermute | solution.py:402
  55.6 27.1 %collective-permute-start.7 = (bf16[2,1040,128]{2,1,0:T(8,128)(2,1)S(1)}, bf16[2,1040,128]{2,1,0:T(8,128)(2,1)}, u32[]{:S(2)}, u32[]{:S(2)}) collective-permute-start(bf16[2,1040,128]{2,1,0:T(8,128)(2,1)S(1)} %pad_maximum_fusion.14), channel_id=1, source_target_pairs={{0,16},{4,20},{8,24},{12,28},{16,0},{20,4},{24,8},{28,12},{1,17},{... | collective-permute-start | bytes 1597448 | tf_op jit(solution)/shard_map/ppermute | solution.py:402
  56.3 26.5 %collective-permute-start.6 = (bf16[2,1040,128]{2,1,0:T(8,128)(2,1)S(1)}, bf16[2,1040,128]{2,1,0:T(8,128)(2,1)}, u32[]{:S(2)}, u32[]{:S(2)}) collective-permute-start(bf16[2,1040,128]{2,1,0:T(8,128)(2,1)S(1)} %pad_maximum_fusion.13), channel_id=1, source_target_pairs={{0,8},{4,12},{8,0},{12,4},{16,24},{20,28},{24,16},{28,20},{1,9},{5... | collective-permute-start | bytes 1597448 | tf_op jit(solution)/shard_map/ppermute | solution.py:402
  56.7 51.1 %collective-permute-start.9 = (bf16[2080,128]{1,0:T(8,128)(2,1)}, bf16[2080,128]{1,0:T(8,128)(2,1)}, u32[]{:S(2)}, u32[]{:S(2)}) collective-permute-start(bf16[2080,128]{1,0:T(8,128)(2,1)} %pad_maximum_fusion.15), channel_id=1, source_target_pairs={{0,2},{1,3},{2,0},{3,1},{4,6},{5,7},{6,4},{7,5},{8,10},{9,11},{10,... | collective-permute-start | bytes 1597448 | tf_op jit(solution)/shard_map/ppermute | solution.py:402
  79.4 25.1 %collective-permute-start.11 = (bf16[512,512]{1,0:T(8,128)(2,1)}, bf16[512,512]{1,0:T(8,128)(2,1)}, u32[]{:S(2)}, u32[]{:S(2)}) collective-permute-start(bf16[512,512]{1,0:T(8,128)(2,1)} %pad_maximum_fusion.18), channel_id=1, source_target_pairs={{0,1},{1,0},{2,3},{3,2},{4,5},{5,4},{6,7},{7,6},{8,9},{9,8},{10,11... | collective-permute-start | bytes 1572872 | tf_op jit(solution)/shard_map/ppermute | solution.py:402
  85.5 28.7 %collective-permute-start.16 = (bf16[4,1040,128]{2,1,0:T(8,128)(2,1)S(1)}, bf16[4,1040,128]{2,1,0:T(8,128)(2,1)}, u32[]{:S(2)}, u32[]{:S(2)}) collective-permute-start(bf16[4,1040,128]{2,1,0:T(8,128)(2,1)S(1)} %pad_maximum_fusion.3.refs_11_), channel_id=1, source_target_pairs={{0,8},{4,12},{8,0},{12,4},{16,24},{20,28},{24,16},{28,20},{1,9},{5... | collective-permute-start | bytes 3194888 | tf_op jit(solution)/shard_map/ppermute | solution.py:402
  87.0 27.1 %collective-permute-start.15 = (bf16[4,1040,128]{2,1,0:T(8,128)(2,1)S(1)}, bf16[4,1040,128]{2,1,0:T(8,128)(2,1)}, u32[]{:S(2)}, u32[]{:S(2)}) collective-permute-start(bf16[4,1040,128]{2,1,0:T(8,128)(2,1)S(1)} %pad_maximum_fusion.2.refs_9_), channel_id=1, source_target_pairs={{0,16},{4,20},{8,24},{12,28},{16,0},{20,4},{24,8},{28,12},{1,17},{... | collective-permute-start | bytes 3194888 | tf_op jit(solution)/shard_map/ppermute | solution.py:402
  104.0 7.3 %collective-permute-start.13 = (bf16[256,512]{1,0:T(8,128)(2,1)}, bf16[256,512]{1,0:T(8,128)(2,1)S(1)}, u32[]{:S(2)}, u32[]{:S(2)}) collective-permute-start(bf16[256,512]{1,0:T(8,128)(2,1)} %get-tuple-element.141.refs_6_), channel_id=1, source_target_pairs={{0,1},{1,0},{2,3},{3,2},{4,5},{5,4},{6,7},{7,6},{8,9},{9,8},{10,11... | collective-permute-start | bytes 786440 | tf_op jit(solution)/shard_map/ppermute | solution.py:402
  111.3 20.9 %collective-permute-start.18 = (bf16[2,1040,128]{2,1,0:T(8,128)(2,1)}, bf16[2,1040,128]{2,1,0:T(8,128)(2,1)}, u32[]{:S(2)}, u32[]{:S(2)}) collective-permute-start(bf16[2,1040,128]{2,1,0:T(8,128)(2,1)} %pad_maximum_fusion.17), channel_id=1, source_target_pairs={{0,16},{4,20},{8,24},{12,28},{16,0},{20,4},{24,8},{28,12},{1,17},{... | collective-permute-start | bytes 1597448 | tf_op jit(solution)/shard_map/ppermute | solution.py:402
  112.0 20.2 %collective-permute-start.17 = (bf16[2,1040,128]{2,1,0:T(8,128)(2,1)}, bf16[2,1040,128]{2,1,0:T(8,128)(2,1)}, u32[]{:S(2)}, u32[]{:S(2)}) collective-permute-start(bf16[2,1040,128]{2,1,0:T(8,128)(2,1)} %pad_maximum_fusion.16), channel_id=1, source_target_pairs={{0,8},{4,12},{8,0},{12,4},{16,24},{20,28},{24,16},{28,20},{1,9},{5... | collective-permute-start | bytes 1597448 | tf_op jit(solution)/shard_map/ppermute | solution.py:402
  130.3 25.6 %collective-permute-start.20 = (bf16[1024,512]{1,0:T(8,128)(2,1)}, bf16[1024,512]{1,0:T(8,128)(2,1)}, u32[]{:S(2)}, u32[]{:S(2)}) collective-permute-start(bf16[1024,512]{1,0:T(8,128)(2,1)} %get-tuple-element.148.refs_4_), channel_id=1, source_target_pairs={{0,1},{1,0},{2,3},{3,2},{4,5},{5,4},{6,7},{7,6},{8,9},{9,8},{10,11... | collective-permute-start | bytes 3145736 | tf_op jit(solution)/shard_map/ppermute | solution.py:402
  133.4 25.8 %collective-permute-start.24 = (bf16[4,1040,128]{2,1,0:T(8,128)(2,1)S(1)}, bf16[4,1040,128]{2,1,0:T(8,128)(2,1)}, u32[]{:S(2)}, u32[]{:S(2)}) collective-permute-start(bf16[4,1040,128]{2,1,0:T(8,128)(2,1)S(1)} %pad_maximum_fusion.5.refs_10_), channel_id=1, source_target_pairs={{0,8},{4,12},{8,0},{12,4},{16,24},{20,28},{24,16},{28,20},{1,9},{5... | collective-permute-start | bytes 3194888 | tf_op jit(solution)/shard_map/ppermute | solution.py:402
  136.1 25.2 %collective-permute-start.23 = (bf16[4,1040,128]{2,1,0:T(8,128)(2,1)S(1)}, bf16[4,1040,128]{2,1,0:T(8,128)(2,1)}, u32[]{:S(2)}, u32[]{:S(2)}) collective-permute-start(bf16[4,1040,128]{2,1,0:T(8,128)(2,1)S(1)} %pad_maximum_fusion.4.refs_8_), channel_id=1, source_target_pairs={{0,16},{4,20},{8,24},{12,28},{16,0},{20,4},{24,8},{28,12},{1,17},{... | collective-permute-start | bytes 3194888 | tf_op jit(solution)/shard_map/ppermute | solution.py:402
  137.8 21.4 %collective-permute-start.21 = (bf16[1024,512]{1,0:T(8,128)(2,1)}, bf16[1024,512]{1,0:T(8,128)(2,1)}, u32[]{:S(2)}, u32[]{:S(2)}) collective-permute-start(bf16[1024,512]{1,0:T(8,128)(2,1)} %get-tuple-element.148.refs_4_), channel_id=1, source_target_pairs={{0,4},{4,0},{8,12},{12,8},{16,20},{20,16},{24,28},{28,24},{1,5},{5... | collective-permute-start | bytes 3145736 | tf_op jit(solution)/shard_map/ppermute | solution.py:402
  178.9 15.1 %collective-permute-start.25 = (bf16[1024,1024]{1,0:T(8,128)(2,1)}, bf16[1024,1024]{1,0:T(8,128)(2,1)}, u32[]{:S(2)}, u32[]{:S(2)}) collective-permute-start(bf16[1024,1024]{1,0:T(8,128)(2,1)} %get-tuple-element.159), channel_id=1, source_target_pairs={{0,4},{4,0},{8,12},{12,8},{16,20},{20,16},{24,28},{28,24},{1,5},{5... | collective-permute-start | bytes 6291464 | tf_op jit(solution)/shard_map/ppermute | solution.py:402
  189.2 25.5 %collective-permute-start.28 = (bf16[1024,512]{1,0:T(8,128)(2,1)}, bf16[1024,512]{1,0:T(8,128)(2,1)}, u32[]{:S(2)}, u32[]{:S(2)}) collective-permute-start(bf16[1024,512]{1,0:T(8,128)(2,1)} %fusion.27), channel_id=1, source_target_pairs={{0,8},{4,12},{8,0},{12,4},{16,24},{20,28},{24,16},{28,20},{1,9},{5... | collective-permute-start | bytes 3145736 | tf_op jit(solution)/shard_map/ppermute | solution.py:402
  192.5 25.2 %collective-permute-start.27 = (bf16[1024,512]{1,0:T(8,128)(2,1)}, bf16[1024,512]{1,0:T(8,128)(2,1)}, u32[]{:S(2)}, u32[]{:S(2)}) collective-permute-start(bf16[1024,512]{1,0:T(8,128)(2,1)} %fusion.24), channel_id=1, source_target_pairs={{0,16},{4,20},{8,24},{12,28},{16,0},{20,4},{24,8},{28,12},{1,17},{... | collective-permute-start | bytes 3145736 | tf_op jit(solution)/shard_map/ppermute | solution.py:402
  198.3 32.4 %collective-permute-start.29 = (bf16[1024,512]{1,0:T(8,128)(2,1)}, bf16[1024,512]{1,0:T(8,128)(2,1)}, u32[]{:S(2)}, u32[]{:S(2)}) collective-permute-start(bf16[1024,512]{1,0:T(8,128)(2,1)} %keep_two.2), channel_id=1, source_target_pairs={{0,1},{1,0},{2,3},{3,2},{4,5},{5,4},{6,7},{7,6},{8,9},{9,8},{10,11... | collective-permute-start | bytes 3145736 | tf_op jit(solution)/shard_map/ppermute | solution.py:402
  217.7 24.1 %collective-permute-start.26 = (bf16[512,512]{1,0:T(8,128)(2,1)}, bf16[512,512]{1,0:T(8,128)(2,1)S(1)}, u32[]{:S(2)}, u32[]{:S(2)}) collective-permute-start(bf16[512,512]{1,0:T(8,128)(2,1)} %fusion.77), channel_id=1, source_target_pairs={{0,4},{4,0},{8,12},{12,8},{16,20},{20,16},{24,28},{28,24},{1,5},{5... | collective-permute-start | bytes 1572872 | tf_op jit(solution)/shard_map/ppermute | solution.py:402
  221.9 20.1 %collective-permute-start.32 = (bf16[1024,256]{1,0:T(8,128)(2,1)}, bf16[1024,256]{1,0:T(8,128)(2,1)}, u32[]{:S(2)}, u32[]{:S(2)}) collective-permute-start(bf16[1024,256]{1,0:T(8,128)(2,1)} %dynamic-slice_convert_fusion), channel_id=1, source_target_pairs={{0,16},{4,20},{8,24},{12,28},{16,0},{20,4},{24,8},{28,12},{1,17},{... | collective-permute-start | bytes 1572872 | tf_op jit(solution)/shard_map/ppermute | solution.py:402
  226.9 15.1 %collective-permute-start.31 = (bf16[1024,256]{1,0:T(8,128)(2,1)}, bf16[1024,256]{1,0:T(8,128)(2,1)}, u32[]{:S(2)}, u32[]{:S(2)}) collective-permute-start(bf16[1024,256]{1,0:T(8,128)(2,1)} %dynamic-slice_convert_fusion.1), channel_id=1, source_target_pairs={{0,8},{4,12},{8,0},{12,4},{16,24},{20,28},{24,16},{28,20},{1,9},{5... | collective-permute-start | bytes 1572872 | tf_op jit(solution)/shard_map/ppermute | solution.py:402
  247.0 5.6 %collective-permute-start.30 = (bf16[512,1024]{1,0:T(8,128)(2,1)S(1)}, bf16[512,1024]{1,0:T(8,128)(2,1)}, u32[]{:S(2)}, u32[]{:S(2)}) collective-permute-start(bf16[512,1024]{1,0:T(8,128)(2,1)S(1)} %copy-done.59), channel_id=1, source_target_pairs={{0,4},{4,0},{8,12},{12,8},{16,20},{20,16},{24,28},{28,24},{1,5},{5... | collective-permute-start | bytes 3145736 | tf_op jit(solution)/shard_map/ppermute | solution.py:402
  247.0 12.3 %collective-permute-start.35 = (bf16[512,1024]{1,0:T(8,128)(2,1)}, bf16[512,1024]{1,0:T(8,128)(2,1)S(1)}, u32[]{:S(2)}, u32[]{:S(2)}) collective-permute-start(bf16[512,1024]{1,0:T(8,128)(2,1)} %get-tuple-element.186), channel_id=1, source_target_pairs={{0,4},{4,0},{8,12},{12,8},{16,20},{20,16},{24,28},{28,24},{1,5},{5... | collective-permute-start | bytes 3145736 | tf_op jit(solution)/shard_map/ppermute | solution.py:402
  248.9 28.0 %collective-permute-start.36 = (bf16[1152,512]{1,0:T(8,128)(2,1)S(1)}, bf16[1152,512]{1,0:T(8,128)(2,1)}, u32[]{:S(2)}, u32[]{:S(2)}) collective-permute-start(bf16[1152,512]{1,0:T(8,128)(2,1)S(1)} %maximum_maximum_fusion), channel_id=1, source_target_pairs={{0,8},{4,12},{8,0},{12,4},{16,24},{20,28},{24,16},{28,20},{1,9},{5... | collective-permute-start | bytes 3538952 | tf_op jit(solution)/shard_map/ppermute | solution.py:402
  252.0 30.7 %collective-permute-start.34 = (bf16[1152,512]{1,0:T(8,128)(2,1)S(1)}, bf16[1152,512]{1,0:T(8,128)(2,1)}, u32[]{:S(2)}, u32[]{:S(2)}) collective-permute-start(bf16[1152,512]{1,0:T(8,128)(2,1)S(1)} %pad_maximum_fusion), channel_id=1, source_target_pairs={{0,16},{4,20},{8,24},{12,28},{16,0},{20,4},{24,8},{28,12},{1,17},{... | collective-permute-start | bytes 3538952 | tf_op jit(solution)/shard_map/ppermute | solution.py:402
  258.1 31.2 %collective-permute-start.33 = (bf16[256,1024]{1,0:T(8,128)(2,1)}, bf16[256,1024]{1,0:T(8,128)(2,1)}, u32[]{:S(2)}, u32[]{:S(2)}) collective-permute-start(bf16[256,1024]{1,0:T(8,128)(2,1)} %get-tuple-element.184), channel_id=1, source_target_pairs={{0,1},{1,0},{2,3},{3,2},{4,5},{5,4},{6,7},{7,6},{8,9},{9,8},{10,11... | collective-permute-start | bytes 1572872 | tf_op jit(solution)/shard_map/ppermute | solution.py:402
  268.3 52.7 %collective-permute-start.42 = (bf16[1024,128]{1,0:T(8,128)(2,1)}, bf16[1024,128]{1,0:T(8,128)(2,1)}, u32[]{:S(2)}, u32[]{:S(2)}) collective-permute-start(bf16[1024,128]{1,0:T(8,128)(2,1)} %dynamic-slice_convert_fusion.5), channel_id=1, source_target_pairs={{0,2},{1,3},{2,0},{3,1},{4,6},{5,7},{6,4},{7,5},{8,10},{9,11},{10,... | collective-permute-start | bytes 786440 | tf_op jit(solution)/shard_map/ppermute | solution.py:402
  270.6 53.0 %collective-permute-start.41 = (bf16[1024,128]{1,0:T(8,128)(2,1)}, bf16[1024,128]{1,0:T(8,128)(2,1)}, u32[]{:S(2)}, u32[]{:S(2)}) collective-permute-start(bf16[1024,128]{1,0:T(8,128)(2,1)} %dynamic-slice_convert_fusion.6), channel_id=1, source_target_pairs={{0,2},{1,3},{2,0},{3,1},{4,6},{5,7},{6,4},{7,5},{8,10},{9,11},{10,... | collective-permute-start | bytes 786440 | tf_op jit(solution)/shard_map/ppermute | solution.py:402
  282.1 33.9 %collective-permute-start.40 = (bf16[1152,256]{1,0:T(8,128)(2,1)}, bf16[1152,256]{1,0:T(8,128)(2,1)}, u32[]{:S(2)}, u32[]{:S(2)}) collective-permute-start(bf16[1152,256]{1,0:T(8,128)(2,1)} %fusion.39), channel_id=1, source_target_pairs={{0,16},{4,20},{8,24},{12,28},{16,0},{20,4},{24,8},{28,12},{1,17},{... | collective-permute-start | bytes 1769480 | tf_op jit(solution)/shard_map/ppermute | solution.py:402
  287.4 30.8 %collective-permute-start.39 = (bf16[1152,256]{1,0:T(8,128)(2,1)}, bf16[1152,256]{1,0:T(8,128)(2,1)}, u32[]{:S(2)}, u32[]{:S(2)}) collective-permute-start(bf16[1152,256]{1,0:T(8,128)(2,1)} %fusion.43), channel_id=1, source_target_pairs={{0,8},{4,12},{8,0},{12,4},{16,24},{20,28},{24,16},{28,20},{1,9},{5... | collective-permute-start | bytes 1769480 | tf_op jit(solution)/shard_map/ppermute | solution.py:402
  289.3 34.4 %collective-permute-start.38 = (bf16[256,1024]{1,0:T(8,128)(2,1)}, bf16[256,1024]{1,0:T(8,128)(2,1)}, u32[]{:S(2)}, u32[]{:S(2)}) collective-permute-start(bf16[256,1024]{1,0:T(8,128)(2,1)} %get-tuple-element.187), channel_id=1, source_target_pairs={{0,1},{1,0},{2,3},{3,2},{4,5},{5,4},{6,7},{7,6},{8,9},{9,8},{10,11... | collective-permute-start | bytes 1572872 | tf_op jit(solution)/shard_map/ppermute | solution.py:402
  316.1 35.1 %collective-permute-start.37 = (bf16[256,512]{1,0:T(8,128)(2,1)S(1)}, bf16[256,512]{1,0:T(8,128)(2,1)}, u32[]{:S(2)}, u32[]{:S(2)}) collective-permute-start(bf16[256,512]{1,0:T(8,128)(2,1)S(1)} %copy-done.44), channel_id=1, source_target_pairs={{0,1},{1,0},{2,3},{3,2},{4,5},{5,4},{6,7},{7,6},{8,9},{9,8},{10,11... | collective-permute-start | bytes 786440 | tf_op jit(solution)/shard_map/ppermute | solution.py:402
  320.6 50.3 %collective-permute-start.54 = (bf16[1152,128]{1,0:T(8,128)(2,1)S(1)}, bf16[1152,128]{1,0:T(8,128)(2,1)}, u32[]{:S(2)}, u32[]{:S(2)}) collective-permute-start(bf16[1152,128]{1,0:T(8,128)(2,1)S(1)} %dynamic-slice_convert_fusion.3), channel_id=1, source_target_pairs={{0,2},{1,3},{2,0},{3,1},{4,6},{5,7},{6,4},{7,5},{8,10},{9,11},{10,... | collective-permute-start | bytes 884744 | tf_op jit(solution)/shard_map/ppermute | solution.py:402
  321.0 50.9 %collective-permute-start.55 = (bf16[1152,128]{1,0:T(8,128)(2,1)S(1)}, bf16[1152,128]{1,0:T(8,128)(2,1)}, u32[]{:S(2)}, u32[]{:S(2)}) collective-permute-start(bf16[1152,128]{1,0:T(8,128)(2,1)S(1)} %dynamic-slice_convert_fusion.2), channel_id=1, source_target_pairs={{0,2},{1,3},{2,0},{3,1},{4,6},{5,7},{6,4},{7,5},{8,10},{9,11},{10,... | collective-permute-start | bytes 884744 | tf_op jit(solution)/shard_map/ppermute | solution.py:402
  366.4 6.8 %collective-permute-start.47 = (bf16[256,128]{1,0:T(8,128)(2,1)S(1)}, bf16[256,128]{1,0:T(8,128)(2,1)S(1)}, u32[]{:S(2)}, u32[]{:S(2)}) collective-permute-start(bf16[256,128]{1,0:T(8,128)(2,1)S(1)} %add_convert_fusion), channel_id=1, source_target_pairs={{0,1},{1,0},{2,3},{3,2},{4,5},{5,4},{6,7},{7,6},{8,9},{9,8},{10,11... | collective-permute-start | bytes 196616 | tf_op jit(solution)/shard_map/ppermute | solution.py:402
  367.0 6.2 %collective-permute-start.48 = (bf16[256,128]{1,0:T(8,128)(2,1)S(1)}, bf16[256,128]{1,0:T(8,128)(2,1)S(1)}, u32[]{:S(2)}, u32[]{:S(2)}) collective-permute-start(bf16[256,128]{1,0:T(8,128)(2,1)S(1)} %add_convert_fusion), channel_id=1, source_target_pairs={{0,2},{1,3},{2,0},{3,1},{4,6},{5,7},{6,4},{7,5},{8,10},{9,11},{10,... | collective-permute-start | bytes 196616 | tf_op jit(solution)/shard_map/ppermute | solution.py:402
  367.4 6.9 %collective-permute-start.49 = (bf16[256,128]{1,0:T(8,128)(2,1)S(1)}, bf16[256,128]{1,0:T(8,128)(2,1)S(1)}, u32[]{:S(2)}, u32[]{:S(2)}) collective-permute-start(bf16[256,128]{1,0:T(8,128)(2,1)S(1)} %add_convert_fusion), channel_id=1, source_target_pairs={{0,3},{1,2},{2,1},{3,0},{4,7},{5,6},{6,5},{7,4},{8,11},{9,10},{10,... | collective-permute-start | bytes 196616 | tf_op jit(solution)/shard_map/ppermute | solution.py:402
  373.1 15.1 %collective-permute-start.56 = (f32[16,512]{1,0:T(8,128)S(1)}, f32[16,512]{1,0:T(8,128)S(1)}, u32[]{:S(2)}, u32[]{:S(2)}) collective-permute-start(f32[16,512]{1,0:T(8,128)S(1)} %squeeze.30), channel_id=1, source_target_pairs={{0,1},{1,0},{2,3},{3,2},{4,5},{5,4},{6,7},{7,6},{8,9},{9,8},{10,11... | collective-permute-start | bytes 98312 | tf_op jit(solution)/shard_map/ppermute | solution.py:402
  375.4 12.8 %collective-permute-start.57 = (f32[16,512]{1,0:T(8,128)S(1)}, f32[16,512]{1,0:T(8,128)S(1)}, u32[]{:S(2)}, u32[]{:S(2)}) collective-permute-start(f32[16,512]{1,0:T(8,128)S(1)} %squeeze.31), channel_id=1, source_target_pairs={{0,4},{4,0},{8,12},{12,8},{16,20},{20,16},{24,28},{28,24},{1,5},{5... | collective-permute-start | bytes 98312 | tf_op jit(solution)/shard_map/ppermute | solution.py:402
  375.5 12.7 %collective-permute-start.58 = (f32[16,512]{1,0:T(8,128)S(1)}, f32[16,512]{1,0:T(8,128)S(1)}, u32[]{:S(2)}, u32[]{:S(2)}) collective-permute-start(f32[16,512]{1,0:T(8,128)S(1)} %squeeze.32), channel_id=1, source_target_pairs={{0,5},{1,4},{2,7},{3,6},{4,1},{5,0},{6,3},{7,2},{8,13},{9,12},{10,... | collective-permute-start | bytes 98312 | tf_op jit(solution)/shard_map/ppermute | solution.py:408
  376.7 8.2 %collective-permute-start.51 = (f32[256,128]{1,0:T(8,128)S(1)}, f32[256,128]{1,0:T(8,128)S(1)}, u32[]{:S(2)}, u32[]{:S(2)}) collective-permute-start(f32[256,128]{1,0:T(8,128)S(1)} %add_add_fusion.refs_0_), channel_id=1, source_target_pairs={{0,16},{4,20},{8,24},{12,28},{16,0},{20,4},{24,8},{28,12},{1,17},{... | collective-permute-start | bytes 393224 | tf_op jit(solution)/shard_map/ppermute | solution.py:402
  379.3 5.9 %collective-permute-start.52 = (f32[256,128]{1,0:T(8,128)S(1)}, f32[256,128]{1,0:T(8,128)S(1)}, u32[]{:S(2)}, u32[]{:S(2)}) collective-permute-start(f32[256,128]{1,0:T(8,128)S(1)} %add_add_fusion.refs_0_), channel_id=1, source_target_pairs={{0,24},{4,28},{8,16},{12,20},{16,8},{20,12},{24,0},{28,4},{1,25},{... | collective-permute-start | bytes 393224 | tf_op jit(solution)/shard_map/ppermute | solution.py:402
  (72 other events, 475.1 us)

commit v6 on v5

--- a/solution.py
+++ b/solution.py
@@ -109,16 +109,15 @@
 
         @pl.when(trip_ref[step] == low_places + count)
         def tail(count=count):
-            @pl.loop(0, tokens // ROWS)
-            def rows(i):
-                pool(PARTS - 1, low_places, count, pl.multiple_of(i * ROWS, ROWS))
+            for r in range(0, tokens, ROWS):
+                pool(PARTS - 1, low_places, count, r)
 
     @pl.when(trip_ref[step] == low_places)
     def no_tail():
         high_ref[PARTS - 1] = high_ref[0]
         total_ref[PARTS - 1] = jnp.zeros(total_ref.shape[1:], jnp.float32)
 
-    @pl.loop(0, tokens // 32)
+    @pl.loop(0, tokens // 32, unroll=4)
     def finish(i):
         r = pl.ds(pl.multiple_of(i * 32, 32), 32)
         highs = [high_ref[number, r, :] for number in range(PARTS)]

time: 402 us -> 399 us (level)
  transfers between devices with their start and end apart: 59 -> 59, of which waited for: 11 -> 11; matrix products, arithmetic and copies ran while one was open for 23% -> 23% of each run, Pallas kernels for 43% -> 42%
where the time goes in v6:
time: 399 us; the launch traced here: 394 us
  Pallas kernels  187 us (47%)
  starting transfers between devices  56.4 us (14%)
  local copies, waits for them, and re-layouts  48.5 us (12%)
  waiting for transfers between devices  38.5 us (10%)
  other arithmetic  36.6 us (9%)
  matrix products  24 us (6%)
    ppermute x58, starting transfers between devices, swap(): lax.ppermute(x, axis, [(i, i ^ bit) for i in range(lax.axis_size(axis))])  55.1 us
    pallas_call x2, Pallas kernels, conv_backward(): pl.pallas_call(functools.partial(backward_kernel, chars, low_places, span...  53.1 us
    pallas_call x3, Pallas kernels, conv_forward(): pl.pallas_call(functools.partial(kernel, low_places, extras), grid_spec=p...  48.7 us
    ppermute x58, waiting for transfers between devices, swap(): lax.ppermute(x, axis, [(i, i ^ bit) for i in range(lax.axis_size(axis))])  38.5 us
    pallas_call x2, Pallas kernels, call_layer(): pl.pallas_call(functools.partial(kernel, tuple(x_copies), tuple(w_copies)...  33.9 us
    dot_general x8, matrix products, product(): lax.dot_general(inputs[:, number * half:(number + 1) * half], after(halve...  18.8 us
    unnamed x130, local copies, waits for them, and re-layouts  14.7 us
    pallas_call x1, Pallas kernels, back_one(): pl.pallas_call(back_one_kernel, in_specs=[NEAR] * 4 + [ANYWHERE] * 2, out...  11.1 us
  transfers between devices with their start and end apart: 59, of which 11 were waited for; matrix products, arithmetic and copies ran while one was open for 23% of the time, Pallas kernels for 42%

profile of v6, /device:TPU:0, one launch (start us, length us, event | category | flops | bytes accessed | tf_op | source)
XLA Modules:
  0.0 393.5 jit_solution(17131141578034139947)
XLA Ops:
  1.9 4.1 %collective-permute-start = (bf16[1,16,2048]{2,1,0:T(8,128)(2,1)S(1)}, bf16[1,16,2048]{2,1,0:T(8,128)(2,1)S(1)}, u32[]{:S(2)}, u32[]{:S(2)}) collective-permute-start(bf16[1,16,2048]{2,1,0:T(8,128)(2,1)S(1)} %bitcast.194), channel_id=1, source_target_pairs={{0,2},{1,3},{2,0},{3,1},{4,6},{5,7},{6,4},{7,5},{8,10},{9,11},{10,... | collective-permute-start | bytes 196616 | tf_op jit(solution)/shard_map/ppermute | solution.py:401
  15.3 1.9 bank_rows.2
  18.7 1.6 collective-permute-start.4
  21.4 9.0 %prepare.1 = (bf16[50,256,128]{2,1,0:T(8,128)(2,1)}, bf16[128,2048]{1,0:T(8,128)(2,1)}, f32[8,2048]{1,0:T(8,128)}) custom-call(s32[256,50]{1,0:T(8,128)} %copy.77.ids_ref, bf16[262,16]{1,0:T(8,128)(2,1)} %copy.78.chars_ref, bf16[1,2048]{1,0:T(2,128)(2,1)} %reshape.354.bias_ref, bf16[16,32]{1,0:T(8,128)(2,1)} %refs_0_.2, bf16[32,32]{1,0:T(8,128)(2,1)} %refs_1_.1, ...), custom_call_target="tpu_custom_call" | custom-call | flops 1 | bytes 1 | tf_op jit(solution)/shard_map/prepare/pallas_call | solution.py:65
  31.0 20.6 %conv_forward.3 = (bf16[4,50,256,256]{3,2,1,0:T(8,128)(2,1)}, bf16[256,1024]{1,0:T(8,128)(2,1)}, f32[256,1024]{1,0:T(8,128)}, f32[5,256,1024]{2,1,0:T(8,128)}) custom-call(s32[4]{0:T(128)} %broadcast.226.trip_ref, bf16[50,256,128]{2,1,0:T(8,128)(2,1)} %get-tuple-element.202.win_ref.refs_5_, bf16[128,2048]{1,0:T(8,128)(2,1)} %get-tuple-element.124.weight_ref.refs_6_, ...), custom_call_target="tpu_custom_call" | custom-call | flops 1 | bytes 1 | tf_op jit(solution)/shard_map/conv_forward/pallas_call | solution.py:144
  53.1 1.6 collective-permute-start.2
  55.9 2.8 collective-permute-start.9
  59.1 13.8 %conv_forward.4 = (bf16[4,50,256,256]{3,2,1,0:T(8,128)(2,1)}, bf16[256,512]{1,0:T(8,128)(2,1)}, f32[256,1024]{1,0:T(8,128)}, f32[5,256,1024]{2,1,0:T(8,128)}) custom-call(s32[2]{0:T(128)} %broadcast.227.trip_ref, bf16[50,256,128]{2,1,0:T(8,128)(2,1)} %get-tuple-element.202.win_ref.refs_5_, bf16[128,2048]{1,0:T(8,128)(2,1)} %get-tuple-element.124.weight_ref.refs_6_, ...), custom_call_target="tpu_custom_call" | custom-call | flops 1 | bytes 1 | tf_op jit(solution)/shard_map/conv_forward/pallas_call | solution.py:144
  77.7 1.6 collective-permute-start.11
  86.8 14.2 %conv_forward.5 = (bf16[4,50,256,256]{3,2,1,0:T(8,128)(2,1)}, bf16[256,512]{1,0:T(8,128)(2,1)}, f32[256,1024]{1,0:T(8,128)}, f32[5,256,1024]{2,1,0:T(8,128)}) custom-call(s32[2]{0:T(128)} %constant.547.trip_ref, bf16[50,256,128]{2,1,0:T(8,128)(2,1)} %get-tuple-element.202.win_ref.refs_5_, ...), custom_call_target="tpu_custom_call", output_to_operand_aliasing={{0}: (4, {}), {2}: (5, {}), {3}: (6, {})} | custom-call | flops 1 | bytes 1 | tf_op jit(solution)/shard_map/conv_forward/pallas_call | solution.py:144
  111.2 16.3 %layer_one.1 = (bf16[1024,2048]{1,0:T(8,128)(2,1)}, bf16[2080,1024]{1,0:T(8,128)(2,1)}, f32[1024,1024]{1,0:T(8,128)}, bf16[1024,512]{1,0:T(8,128)(2,1)}, bf16[1024,512]{1,0:T(8,128)(2,1)}) custom-call(s32[16]{0:T(128)} %stack.285.at_ref, bf16[2048,512]{1,0:T(8,128)(2,1)} %compare_convert_fusion.pick_ref.pick_far, ...), custom_call_target="tpu_custom_call" | custom-call | flops 1 | bytes 1 | tf_op jit(solution)/shard_map/layer_one/pallas_call | solution.py:551
  127.5 1.6 collective-permute-start.20
  133.3 1.6 collective-permute-start.23
  135.1 18.1 %collective-permute-done.20.refs_5_ = bf16[1024,512]{1,0:T(8,128)(2,1)} collective-permute-done((bf16[1024,512]{1,0:T(8,128)(2,1)}, bf16[1024,512]{1,0:T(8,128)(2,1)}, u32[]{:S(2)}, u32[]{:S(2)}) %collective-permute-start.20) | collective-permute-done | bytes 1048608 | tf_op jit(solution)/shard_map/ppermute | solution.py:401
  156.4 2.1 collective-permute-done.23.refs_9_
  158.5 17.6 %layer_two.1 = (bf16[1024,2048]{1,0:T(8,128)(2,1)}, bf16[2080,1024]{1,0:T(8,128)(2,1)}, bf16[1024,512]{1,0:T(8,128)(2,1)}, bf16[1024,1024]{1,0:T(8,128)(2,1)}, f...) custom-call(s32[16]{0:T(128)} %stack.285.at_ref, ...), custom_call_target="tpu_custom_call" | custom-call | flops 1 | bytes 1 | tf_op jit(solution)/shard_map/layer_two/pallas_call | solution.py:551
  177.9 1.7 constant_dynamic-slice_fusion.13
  184.1 2.3 fusion.27
  187.0 2.5 fusion.24
  191.0 4.3 %keep_two.2 = bf16[1024,512]{1,0:T(8,128)(2,1)} custom-call(bf16[1024,1024]{1,0:T(8,128)(2,1)} %get-tuple-element.162.d_project_ref, bf16[2080,1024]{1,0:T(8,128)(2,1)} %get-tuple-element.165.w_ref, bf16[1024,1024]{1,0:T(8,128)(2,1)} %collective-permute-done.25.got_ref), custom_call_target="tpu_custom_call" | custom-call | flops 1 | bytes 1 | tf_op jit(solution)/shard_map/keep_two/pallas_call | solution.py:637
  196.3 4.9 %keep_two.3.own_ref = f32[1024,512]{1,0:T(8,128)} custom-call(bf16[1024,1024]{1,0:T(8,128)(2,1)} %get-tuple-element.162.d_project_ref, bf16[2080,1024]{1,0:T(8,128)(2,1)} %get-tuple-element.165.w_ref, bf16[1024,1024]{1,0:T(8,128)(2,1)} %collective-permute-done.25.got_ref, f32[1024,512]{1,0:T(8,128)} %get-tuple-element.163.refs_0_), custom_call_target="tpu_custom_call" | custom-call | flops 1 | bytes 1 | tf_op jit(solution)/shard_map/keep_two/pallas_call | solution.py:637
  201.3 1.8 convolution_convert_fusion.1
  204.4 2.1 convolution_add_fusion
  207.3 4.6 %collective-permute-done.28 = bf16[1024,512]{1,0:T(8,128)(2,1)} collective-permute-done((bf16[1024,512]{1,0:T(8,128)(2,1)}, bf16[1024,512]{1,0:T(8,128)(2,1)}, u32[]{:S(2)}, u32[]{:S(2)}) %collective-permute-start.28) | collective-permute-done | bytes 1048608 | tf_op jit(solution)/shard_map/ppermute | solution.py:401
  211.9 2.8 collective-permute-done.27
  214.7 3.2 convert_add_fusion.2
  220.4 2.5 convert_add_fusion.3
  227.7 11.1 %back_one.1 = (bf16[1024,1024]{1,0:T(8,128)(2,1)}, bf16[1024,512]{1,0:T(8,128)(2,1)}, f32[8,1024]{1,0:T(8,128)}, bf16[512,1024]{1,0:T(8,128)(2,1)}, bf16[512,1024]{1,0:T(8,128)(2,1)}) custom-call(f32[1024,512]{1,0:T(8,128)} %keep_two.3.own_ref, bf16[1024,512]{1,0:T(8,128)(2,1)} %collective-permute-done.29.got_ref, ...), custom_call_target="tpu_custom_call" | custom-call | flops 1 | bytes 1 | tf_op jit(solution)/shard_map/back_one/pallas_call | solution.py:685
  239.0 1.8 copy-done
  249.6 5.5 %keep_one.2 = (f32[256,1024]{1,0:T(8,128)}, bf16[256,1024]{1,0:T(8,128)(2,1)}) custom-call(bf16[1024,1024]{1,0:T(8,128)(2,1)} %get-tuple-element.185.d_project_ref, bf16[1024,512]{1,0:T(8,128)(2,1)} %get-tuple-element.178.through_ref, bf16[2080,1024]{1,0:T(8,128)(2,1)} %get-tuple-element.171.w_far.w_ref, ...), custom_call_target="tpu_custom_call" | custom-call | flops 1 | bytes 1 | tf_op jit(solution)/shard_map/keep_one/pallas_call | solution.py:717
  257.3 5.5 %keep_one.3 = (f32[256,1024]{1,0:T(8,128)}, bf16[256,1024]{1,0:T(8,128)(2,1)}) custom-call(bf16[1024,1024]{1,0:T(8,128)(2,1)} %get-tuple-element.185.d_project_ref, bf16[1024,512]{1,0:T(8,128)(2,1)} %get-tuple-element.178.through_ref, bf16[2080,1024]{1,0:T(8,128)(2,1)} %get-tuple-element.171.w_far.w_ref, ...), custom_call_target="tpu_custom_call" | custom-call | flops 1 | bytes 1 | tf_op jit(solution)/shard_map/keep_one/pallas_call | solution.py:717
  262.8 1.6 convert_add_fusion.4
  267.6 2.6 collective-permute-start.41
  270.2 3.7 collective-permute-done.36
  274.9 3.3 convert_add_fusion
  279.7 2.5 convert_add_fusion.1
  287.5 25.7 %conv_backward.2 = (f32[8,120,128]{2,1,0:T(8,128)}, f32[40,128]{1,0:T(8,128)}) custom-call(s32[4]{0:T(128)} %broadcast.226.trip_ref, bf16[4,50,256,256]{3,2,1,0:T(8,128)(2,1)} %get-tuple-element.174.refs_0_, f32[256,1024]{1,0:T(8,128)} %get-tuple-element.175.refs_1_, f32[5,256,1024]{2,1,0:T(8,128)} %get-tuple-element.176.refs_2_, ...), custom_call_target="tpu_custom_call" | custom-call | flops 1 | bytes 1 | tf_op jit(solution)/shard_map/conv_backward/pallas_call | solution.py:289
  318.2 2.7 collective-permute-start.55
  320.9 27.4 %conv_backward.3 = (f32[8,120,128]{2,1,0:T(8,128)}, f32[40,128]{1,0:T(8,128)}) custom-call(s32[4]{0:T(128)} %constant.549.trip_ref, bf16[4,50,256,256]{3,2,1,0:T(8,128)(2,1)} %get-tuple-element.196.refs_0_, f32[256,1024]{1,0:T(8,128)} %get-tuple-element.197.refs_1_, f32[5,256,1024]{2,1,0:T(8,128)} %get-tuple-element.198.refs_2_, ...), custom_call_target="tpu_custom_call" | custom-call | flops 1 | bytes 1 | tf_op jit(solution)/shard_map/conv_backward/pallas_call | solution.py:289
  348.3 2.4 pack.1
  358.8 1.7 fusion.52
  361.0 2.4 collective-permute-done.46
  364.4 3.5 collective-permute-start.49
  374.4 1.9 collective-permute-done.50.refs_1_
  379.6 2.4 bank_rows.3
  383.4 1.9 join.1.own_ref
  388.2 2.3 unpack.1
  390.5 1.6 copy.90
  (369 shorter events, 116.2 us)
Async XLA Ops:
  1.9 11.9 %collective-permute-start = (bf16[1,16,2048]{2,1,0:T(8,128)(2,1)S(1)}, bf16[1,16,2048]{2,1,0:T(8,128)(2,1)S(1)}, u32[]{:S(2)}, u32[]{:S(2)}) collective-permute-start(bf16[1,16,2048]{2,1,0:T(8,128)(2,1)S(1)} %bitcast.194), channel_id=1, source_target_pairs={{0,2},{1,3},{2,0},{3,1},{4,6},{5,7},{6,4},{7,5},{8,10},{9,11},{10,... | collective-permute-start | bytes 196616 | tf_op jit(solution)/shard_map/ppermute | solution.py:401
  13.8 39.2 %collective-permute-start.1 = (bf16[2,16,2048]{2,1,0:T(8,128)(2,1)S(1)}, bf16[2,16,2048]{2,1,0:T(8,128)(2,1)S(1)}, u32[]{:S(2)}, u32[]{:S(2)}) collective-permute-start(bf16[2,16,2048]{2,1,0:T(8,128)(2,1)S(1)} %pad_maximum_fusion.22), channel_id=1, source_target_pairs={{0,8},{4,12},{8,0},{12,4},{16,24},{20,28},{24,16},{28,20},{1,9},{5... | collective-permute-start | bytes 393224 | tf_op jit(solution)/shard_map/ppermute | solution.py:401
  17.3 37.4 %collective-permute-start.3 = (bf16[2080,128]{1,0:T(8,128)(2,1)}, bf16[2080,128]{1,0:T(8,128)(2,1)S(1)}, u32[]{:S(2)}, u32[]{:S(2)}) collective-permute-start(bf16[2080,128]{1,0:T(8,128)(2,1)} %bank_rows.2), channel_id=1, source_target_pairs={{0,2},{1,3},{2,0},{3,1},{4,6},{5,7},{6,4},{7,5},{8,10},{9,11},{10,... | collective-permute-start | bytes 1597448 | tf_op jit(solution)/shard_map/ppermute | solution.py:401
  18.7 36.7 %collective-permute-start.4 = (bf16[256,512]{1,0:T(8,128)(2,1)S(1)}, bf16[256,512]{1,0:T(8,128)(2,1)}, u32[]{:S(2)}, u32[]{:S(2)}) collective-permute-start(bf16[256,512]{1,0:T(8,128)(2,1)S(1)} %copy-done.26), channel_id=1, source_target_pairs={{0,1},{1,0},{2,3},{3,2},{4,5},{5,4},{6,7},{7,6},{8,9},{9,8},{10,11... | collective-permute-start | bytes 786440 | tf_op jit(solution)/shard_map/ppermute | solution.py:401
  20.3 35.5 %collective-permute-start.5 = (bf16[256,512]{1,0:T(8,128)(2,1)S(1)}, bf16[256,512]{1,0:T(8,128)(2,1)}, u32[]{:S(2)}, u32[]{:S(2)}) collective-permute-start(bf16[256,512]{1,0:T(8,128)(2,1)S(1)} %copy-done.26), channel_id=1, source_target_pairs={{0,4},{4,0},{8,12},{12,8},{16,20},{20,16},{24,28},{28,24},{1,5},{5... | collective-permute-start | bytes 786440 | tf_op jit(solution)/shard_map/ppermute | solution.py:401
  51.6 35.2 %collective-permute-start.8 = (bf16[256,1024]{1,0:T(8,128)(2,1)}, bf16[256,1024]{1,0:T(8,128)(2,1)}, u32[]{:S(2)}, u32[]{:S(2)}) collective-permute-start(bf16[256,1024]{1,0:T(8,128)(2,1)} %get-tuple-element.126.refs_0_), channel_id=1, source_target_pairs={{0,1},{1,0},{2,3},{3,2},{4,5},{5,4},{6,7},{7,6},{8,9},{9,8},{10,11... | collective-permute-start | bytes 1572872 | tf_op jit(solution)/shard_map/ppermute | solution.py:401
  53.1 19.9 %collective-permute-start.2 = (bf16[4,16,2048]{2,1,0:T(8,128)(2,1)S(1)}, bf16[4,16,2048]{2,1,0:T(8,128)(2,1)S(1)}, u32[]{:S(2)}, u32[]{:S(2)}) collective-permute-start(bf16[4,16,2048]{2,1,0:T(8,128)(2,1)S(1)} %pad_maximum_fusion.21), channel_id=1, source_target_pairs={{0,16},{4,20},{8,24},{12,28},{16,0},{20,4},{24,8},{28,12},{1,17},{... | collective-permute-start | bytes 786440 | tf_op jit(solution)/shard_map/ppermute | solution.py:401
  54.8 26.2 %collective-permute-start.7 = (bf16[2,1040,128]{2,1,0:T(8,128)(2,1)S(1)}, bf16[2,1040,128]{2,1,0:T(8,128)(2,1)}, u32[]{:S(2)}, u32[]{:S(2)}) collective-permute-start(bf16[2,1040,128]{2,1,0:T(8,128)(2,1)S(1)} %pad_maximum_fusion.14), channel_id=1, source_target_pairs={{0,16},{4,20},{8,24},{12,28},{16,0},{20,4},{24,8},{28,12},{1,17},{... | collective-permute-start | bytes 1597448 | tf_op jit(solution)/shard_map/ppermute | solution.py:401
  55.4 25.6 %collective-permute-start.6 = (bf16[2,1040,128]{2,1,0:T(8,128)(2,1)S(1)}, bf16[2,1040,128]{2,1,0:T(8,128)(2,1)}, u32[]{:S(2)}, u32[]{:S(2)}) collective-permute-start(bf16[2,1040,128]{2,1,0:T(8,128)(2,1)S(1)} %pad_maximum_fusion.13), channel_id=1, source_target_pairs={{0,8},{4,12},{8,0},{12,4},{16,24},{20,28},{24,16},{28,20},{1,9},{5... | collective-permute-start | bytes 1597448 | tf_op jit(solution)/shard_map/ppermute | solution.py:401
  55.9 49.0 %collective-permute-start.9 = (bf16[2080,128]{1,0:T(8,128)(2,1)}, bf16[2080,128]{1,0:T(8,128)(2,1)}, u32[]{:S(2)}, u32[]{:S(2)}) collective-permute-start(bf16[2080,128]{1,0:T(8,128)(2,1)} %pad_maximum_fusion.15), channel_id=1, source_target_pairs={{0,2},{1,3},{2,0},{3,1},{4,6},{5,7},{6,4},{7,5},{8,10},{9,11},{10,... | collective-permute-start | bytes 1597448 | tf_op jit(solution)/shard_map/ppermute | solution.py:401
  77.7 23.9 %collective-permute-start.11 = (bf16[512,512]{1,0:T(8,128)(2,1)}, bf16[512,512]{1,0:T(8,128)(2,1)}, u32[]{:S(2)}, u32[]{:S(2)}) collective-permute-start(bf16[512,512]{1,0:T(8,128)(2,1)} %pad_maximum_fusion.18), channel_id=1, source_target_pairs={{0,1},{1,0},{2,3},{3,2},{4,5},{5,4},{6,7},{7,6},{8,9},{9,8},{10,11... | collective-permute-start | bytes 1572872 | tf_op jit(solution)/shard_map/ppermute | solution.py:401
  83.7 27.4 %collective-permute-start.16 = (bf16[4,1040,128]{2,1,0:T(8,128)(2,1)S(1)}, bf16[4,1040,128]{2,1,0:T(8,128)(2,1)}, u32[]{:S(2)}, u32[]{:S(2)}) collective-permute-start(bf16[4,1040,128]{2,1,0:T(8,128)(2,1)S(1)} %pad_maximum_fusion.3.refs_11_), channel_id=1, source_target_pairs={{0,8},{4,12},{8,0},{12,4},{16,24},{20,28},{24,16},{28,20},{1,9},{5... | collective-permute-start | bytes 3194888 | tf_op jit(solution)/shard_map/ppermute | solution.py:401
  85.3 25.8 %collective-permute-start.15 = (bf16[4,1040,128]{2,1,0:T(8,128)(2,1)S(1)}, bf16[4,1040,128]{2,1,0:T(8,128)(2,1)}, u32[]{:S(2)}, u32[]{:S(2)}) collective-permute-start(bf16[4,1040,128]{2,1,0:T(8,128)(2,1)S(1)} %pad_maximum_fusion.2.refs_9_), channel_id=1, source_target_pairs={{0,16},{4,20},{8,24},{12,28},{16,0},{20,4},{24,8},{28,12},{1,17},{... | collective-permute-start | bytes 3194888 | tf_op jit(solution)/shard_map/ppermute | solution.py:401
  101.0 7.3 %collective-permute-start.13 = (bf16[256,512]{1,0:T(8,128)(2,1)}, bf16[256,512]{1,0:T(8,128)(2,1)S(1)}, u32[]{:S(2)}, u32[]{:S(2)}) collective-permute-start(bf16[256,512]{1,0:T(8,128)(2,1)} %get-tuple-element.141.refs_6_), channel_id=1, source_target_pairs={{0,1},{1,0},{2,3},{3,2},{4,5},{5,4},{6,7},{7,6},{8,9},{9,8},{10,11... | collective-permute-start | bytes 786440 | tf_op jit(solution)/shard_map/ppermute | solution.py:401
  108.3 21.0 %collective-permute-start.18 = (bf16[2,1040,128]{2,1,0:T(8,128)(2,1)}, bf16[2,1040,128]{2,1,0:T(8,128)(2,1)}, u32[]{:S(2)}, u32[]{:S(2)}) collective-permute-start(bf16[2,1040,128]{2,1,0:T(8,128)(2,1)} %pad_maximum_fusion.17), channel_id=1, source_target_pairs={{0,16},{4,20},{8,24},{12,28},{16,0},{20,4},{24,8},{28,12},{1,17},{... | collective-permute-start | bytes 1597448 | tf_op jit(solution)/shard_map/ppermute | solution.py:401
  109.0 20.4 %collective-permute-start.17 = (bf16[2,1040,128]{2,1,0:T(8,128)(2,1)}, bf16[2,1040,128]{2,1,0:T(8,128)(2,1)}, u32[]{:S(2)}, u32[]{:S(2)}) collective-permute-start(bf16[2,1040,128]{2,1,0:T(8,128)(2,1)} %pad_maximum_fusion.16), channel_id=1, source_target_pairs={{0,8},{4,12},{8,0},{12,4},{16,24},{20,28},{24,16},{28,20},{1,9},{5... | collective-permute-start | bytes 1597448 | tf_op jit(solution)/shard_map/ppermute | solution.py:401
  127.5 25.6 %collective-permute-start.20 = (bf16[1024,512]{1,0:T(8,128)(2,1)}, bf16[1024,512]{1,0:T(8,128)(2,1)}, u32[]{:S(2)}, u32[]{:S(2)}) collective-permute-start(bf16[1024,512]{1,0:T(8,128)(2,1)} %get-tuple-element.148.refs_4_), channel_id=1, source_target_pairs={{0,1},{1,0},{2,3},{3,2},{4,5},{5,4},{6,7},{7,6},{8,9},{9,8},{10,11... | collective-permute-start | bytes 3145736 | tf_op jit(solution)/shard_map/ppermute | solution.py:401
  130.6 25.8 %collective-permute-start.24 = (bf16[4,1040,128]{2,1,0:T(8,128)(2,1)S(1)}, bf16[4,1040,128]{2,1,0:T(8,128)(2,1)}, u32[]{:S(2)}, u32[]{:S(2)}) collective-permute-start(bf16[4,1040,128]{2,1,0:T(8,128)(2,1)S(1)} %pad_maximum_fusion.5.refs_10_), channel_id=1, source_target_pairs={{0,8},{4,12},{8,0},{12,4},{16,24},{20,28},{24,16},{28,20},{1,9},{5... | collective-permute-start | bytes 3194888 | tf_op jit(solution)/shard_map/ppermute | solution.py:401
  133.3 25.2 %collective-permute-start.23 = (bf16[4,1040,128]{2,1,0:T(8,128)(2,1)S(1)}, bf16[4,1040,128]{2,1,0:T(8,128)(2,1)}, u32[]{:S(2)}, u32[]{:S(2)}) collective-permute-start(bf16[4,1040,128]{2,1,0:T(8,128)(2,1)S(1)} %pad_maximum_fusion.4.refs_8_), channel_id=1, source_target_pairs={{0,16},{4,20},{8,24},{12,28},{16,0},{20,4},{24,8},{28,12},{1,17},{... | collective-permute-start | bytes 3194888 | tf_op jit(solution)/shard_map/ppermute | solution.py:401
  135.0 21.4 %collective-permute-start.21 = (bf16[1024,512]{1,0:T(8,128)(2,1)}, bf16[1024,512]{1,0:T(8,128)(2,1)}, u32[]{:S(2)}, u32[]{:S(2)}) collective-permute-start(bf16[1024,512]{1,0:T(8,128)(2,1)} %get-tuple-element.148.refs_4_), channel_id=1, source_target_pairs={{0,4},{4,0},{8,12},{12,8},{16,20},{20,16},{24,28},{28,24},{1,5},{5... | collective-permute-start | bytes 3145736 | tf_op jit(solution)/shard_map/ppermute | solution.py:401
  176.1 14.9 %collective-permute-start.25 = (bf16[1024,1024]{1,0:T(8,128)(2,1)}, bf16[1024,1024]{1,0:T(8,128)(2,1)}, u32[]{:S(2)}, u32[]{:S(2)}) collective-permute-start(bf16[1024,1024]{1,0:T(8,128)(2,1)} %get-tuple-element.159), channel_id=1, source_target_pairs={{0,4},{4,0},{8,12},{12,8},{16,20},{20,16},{24,28},{28,24},{1,5},{5... | collective-permute-start | bytes 6291464 | tf_op jit(solution)/shard_map/ppermute | solution.py:401
  186.4 25.5 %collective-permute-start.28 = (bf16[1024,512]{1,0:T(8,128)(2,1)}, bf16[1024,512]{1,0:T(8,128)(2,1)}, u32[]{:S(2)}, u32[]{:S(2)}) collective-permute-start(bf16[1024,512]{1,0:T(8,128)(2,1)} %fusion.27), channel_id=1, source_target_pairs={{0,8},{4,12},{8,0},{12,4},{16,24},{20,28},{24,16},{28,20},{1,9},{5... | collective-permute-start | bytes 3145736 | tf_op jit(solution)/shard_map/ppermute | solution.py:401
  189.5 25.2 %collective-permute-start.27 = (bf16[1024,512]{1,0:T(8,128)(2,1)}, bf16[1024,512]{1,0:T(8,128)(2,1)}, u32[]{:S(2)}, u32[]{:S(2)}) collective-permute-start(bf16[1024,512]{1,0:T(8,128)(2,1)} %fusion.24), channel_id=1, source_target_pairs={{0,16},{4,20},{8,24},{12,28},{16,0},{20,4},{24,8},{28,12},{1,17},{... | collective-permute-start | bytes 3145736 | tf_op jit(solution)/shard_map/ppermute | solution.py:401
  195.3 32.4 %collective-permute-start.29 = (bf16[1024,512]{1,0:T(8,128)(2,1)}, bf16[1024,512]{1,0:T(8,128)(2,1)}, u32[]{:S(2)}, u32[]{:S(2)}) collective-permute-start(bf16[1024,512]{1,0:T(8,128)(2,1)} %keep_two.2), channel_id=1, source_target_pairs={{0,1},{1,0},{2,3},{3,2},{4,5},{5,4},{6,7},{7,6},{8,9},{9,8},{10,11... | collective-permute-start | bytes 3145736 | tf_op jit(solution)/shard_map/ppermute | solution.py:401
  214.7 24.2 %collective-permute-start.26 = (bf16[512,512]{1,0:T(8,128)(2,1)}, bf16[512,512]{1,0:T(8,128)(2,1)S(1)}, u32[]{:S(2)}, u32[]{:S(2)}) collective-permute-start(bf16[512,512]{1,0:T(8,128)(2,1)} %fusion.77), channel_id=1, source_target_pairs={{0,4},{4,0},{8,12},{12,8},{16,20},{20,16},{24,28},{28,24},{1,5},{5... | collective-permute-start | bytes 1572872 | tf_op jit(solution)/shard_map/ppermute | solution.py:401
  218.9 20.1 %collective-permute-start.32 = (bf16[1024,256]{1,0:T(8,128)(2,1)}, bf16[1024,256]{1,0:T(8,128)(2,1)}, u32[]{:S(2)}, u32[]{:S(2)}) collective-permute-start(bf16[1024,256]{1,0:T(8,128)(2,1)} %dynamic-slice_convert_fusion), channel_id=1, source_target_pairs={{0,16},{4,20},{8,24},{12,28},{16,0},{20,4},{24,8},{28,12},{1,17},{... | collective-permute-start | bytes 1572872 | tf_op jit(solution)/shard_map/ppermute | solution.py:401
  223.9 15.1 %collective-permute-start.31 = (bf16[1024,256]{1,0:T(8,128)(2,1)}, bf16[1024,256]{1,0:T(8,128)(2,1)}, u32[]{:S(2)}, u32[]{:S(2)}) collective-permute-start(bf16[1024,256]{1,0:T(8,128)(2,1)} %dynamic-slice_convert_fusion.1), channel_id=1, source_target_pairs={{0,8},{4,12},{8,0},{12,4},{16,24},{20,28},{24,16},{28,20},{1,9},{5... | collective-permute-start | bytes 1572872 | tf_op jit(solution)/shard_map/ppermute | solution.py:401
  244.0 5.6 %collective-permute-start.30 = (bf16[512,1024]{1,0:T(8,128)(2,1)S(1)}, bf16[512,1024]{1,0:T(8,128)(2,1)}, u32[]{:S(2)}, u32[]{:S(2)}) collective-permute-start(bf16[512,1024]{1,0:T(8,128)(2,1)S(1)} %copy-done.59), channel_id=1, source_target_pairs={{0,4},{4,0},{8,12},{12,8},{16,20},{20,16},{24,28},{28,24},{1,5},{5... | collective-permute-start | bytes 3145736 | tf_op jit(solution)/shard_map/ppermute | solution.py:401
  244.0 12.3 %collective-permute-start.35 = (bf16[512,1024]{1,0:T(8,128)(2,1)}, bf16[512,1024]{1,0:T(8,128)(2,1)S(1)}, u32[]{:S(2)}, u32[]{:S(2)}) collective-permute-start(bf16[512,1024]{1,0:T(8,128)(2,1)} %get-tuple-element.186), channel_id=1, source_target_pairs={{0,4},{4,0},{8,12},{12,8},{16,20},{20,16},{24,28},{28,24},{1,5},{5... | collective-permute-start | bytes 3145736 | tf_op jit(solution)/shard_map/ppermute | solution.py:401
  245.9 28.1 %collective-permute-start.36 = (bf16[1152,512]{1,0:T(8,128)(2,1)S(1)}, bf16[1152,512]{1,0:T(8,128)(2,1)}, u32[]{:S(2)}, u32[]{:S(2)}) collective-permute-start(bf16[1152,512]{1,0:T(8,128)(2,1)S(1)} %maximum_maximum_fusion), channel_id=1, source_target_pairs={{0,8},{4,12},{8,0},{12,4},{16,24},{20,28},{24,16},{28,20},{1,9},{5... | collective-permute-start | bytes 3538952 | tf_op jit(solution)/shard_map/ppermute | solution.py:401
  249.0 30.6 %collective-permute-start.34 = (bf16[1152,512]{1,0:T(8,128)(2,1)S(1)}, bf16[1152,512]{1,0:T(8,128)(2,1)}, u32[]{:S(2)}, u32[]{:S(2)}) collective-permute-start(bf16[1152,512]{1,0:T(8,128)(2,1)S(1)} %pad_maximum_fusion), channel_id=1, source_target_pairs={{0,16},{4,20},{8,24},{12,28},{16,0},{20,4},{24,8},{28,12},{1,17},{... | collective-permute-start | bytes 3538952 | tf_op jit(solution)/shard_map/ppermute | solution.py:401
  255.1 31.2 %collective-permute-start.33 = (bf16[256,1024]{1,0:T(8,128)(2,1)}, bf16[256,1024]{1,0:T(8,128)(2,1)}, u32[]{:S(2)}, u32[]{:S(2)}) collective-permute-start(bf16[256,1024]{1,0:T(8,128)(2,1)} %get-tuple-element.184), channel_id=1, source_target_pairs={{0,1},{1,0},{2,3},{3,2},{4,5},{5,4},{6,7},{7,6},{8,9},{9,8},{10,11... | collective-permute-start | bytes 1572872 | tf_op jit(solution)/shard_map/ppermute | solution.py:401
  265.3 52.9 %collective-permute-start.42 = (bf16[1024,128]{1,0:T(8,128)(2,1)}, bf16[1024,128]{1,0:T(8,128)(2,1)}, u32[]{:S(2)}, u32[]{:S(2)}) collective-permute-start(bf16[1024,128]{1,0:T(8,128)(2,1)} %dynamic-slice_convert_fusion.5), channel_id=1, source_target_pairs={{0,2},{1,3},{2,0},{3,1},{4,6},{5,7},{6,4},{7,5},{8,10},{9,11},{10,... | collective-permute-start | bytes 786440 | tf_op jit(solution)/shard_map/ppermute | solution.py:401
  267.6 53.2 %collective-permute-start.41 = (bf16[1024,128]{1,0:T(8,128)(2,1)}, bf16[1024,128]{1,0:T(8,128)(2,1)}, u32[]{:S(2)}, u32[]{:S(2)}) collective-permute-start(bf16[1024,128]{1,0:T(8,128)(2,1)} %dynamic-slice_convert_fusion.6), channel_id=1, source_target_pairs={{0,2},{1,3},{2,0},{3,1},{4,6},{5,7},{6,4},{7,5},{8,10},{9,11},{10,... | collective-permute-start | bytes 786440 | tf_op jit(solution)/shard_map/ppermute | solution.py:401
  279.2 34.1 %collective-permute-start.40 = (bf16[1152,256]{1,0:T(8,128)(2,1)}, bf16[1152,256]{1,0:T(8,128)(2,1)}, u32[]{:S(2)}, u32[]{:S(2)}) collective-permute-start(bf16[1152,256]{1,0:T(8,128)(2,1)} %fusion.39), channel_id=1, source_target_pairs={{0,16},{4,20},{8,24},{12,28},{16,0},{20,4},{24,8},{28,12},{1,17},{... | collective-permute-start | bytes 1769480 | tf_op jit(solution)/shard_map/ppermute | solution.py:401
  284.4 31.0 %collective-permute-start.39 = (bf16[1152,256]{1,0:T(8,128)(2,1)}, bf16[1152,256]{1,0:T(8,128)(2,1)}, u32[]{:S(2)}, u32[]{:S(2)}) collective-permute-start(bf16[1152,256]{1,0:T(8,128)(2,1)} %fusion.43), channel_id=1, source_target_pairs={{0,8},{4,12},{8,0},{12,4},{16,24},{20,28},{24,16},{28,20},{1,9},{5... | collective-permute-start | bytes 1769480 | tf_op jit(solution)/shard_map/ppermute | solution.py:401
  286.3 34.6 %collective-permute-start.38 = (bf16[256,1024]{1,0:T(8,128)(2,1)}, bf16[256,1024]{1,0:T(8,128)(2,1)}, u32[]{:S(2)}, u32[]{:S(2)}) collective-permute-start(bf16[256,1024]{1,0:T(8,128)(2,1)} %get-tuple-element.187), channel_id=1, source_target_pairs={{0,1},{1,0},{2,3},{3,2},{4,5},{5,4},{6,7},{7,6},{8,9},{9,8},{10,11... | collective-permute-start | bytes 1572872 | tf_op jit(solution)/shard_map/ppermute | solution.py:401
  313.2 35.0 %collective-permute-start.37 = (bf16[256,512]{1,0:T(8,128)(2,1)S(1)}, bf16[256,512]{1,0:T(8,128)(2,1)}, u32[]{:S(2)}, u32[]{:S(2)}) collective-permute-start(bf16[256,512]{1,0:T(8,128)(2,1)S(1)} %copy-done.44), channel_id=1, source_target_pairs={{0,1},{1,0},{2,3},{3,2},{4,5},{5,4},{6,7},{7,6},{8,9},{9,8},{10,11... | collective-permute-start | bytes 786440 | tf_op jit(solution)/shard_map/ppermute | solution.py:401
  317.8 50.2 %collective-permute-start.54 = (bf16[1152,128]{1,0:T(8,128)(2,1)S(1)}, bf16[1152,128]{1,0:T(8,128)(2,1)}, u32[]{:S(2)}, u32[]{:S(2)}) collective-permute-start(bf16[1152,128]{1,0:T(8,128)(2,1)S(1)} %dynamic-slice_convert_fusion.3), channel_id=1, source_target_pairs={{0,2},{1,3},{2,0},{3,1},{4,6},{5,7},{6,4},{7,5},{8,10},{9,11},{10,... | collective-permute-start | bytes 884744 | tf_op jit(solution)/shard_map/ppermute | solution.py:401
  318.2 50.7 %collective-permute-start.55 = (bf16[1152,128]{1,0:T(8,128)(2,1)S(1)}, bf16[1152,128]{1,0:T(8,128)(2,1)}, u32[]{:S(2)}, u32[]{:S(2)}) collective-permute-start(bf16[1152,128]{1,0:T(8,128)(2,1)S(1)} %dynamic-slice_convert_fusion.2), channel_id=1, source_target_pairs={{0,2},{1,3},{2,0},{3,1},{4,6},{5,7},{6,4},{7,5},{8,10},{9,11},{10,... | collective-permute-start | bytes 884744 | tf_op jit(solution)/shard_map/ppermute | solution.py:401
  363.5 6.8 %collective-permute-start.47 = (bf16[256,128]{1,0:T(8,128)(2,1)S(1)}, bf16[256,128]{1,0:T(8,128)(2,1)S(1)}, u32[]{:S(2)}, u32[]{:S(2)}) collective-permute-start(bf16[256,128]{1,0:T(8,128)(2,1)S(1)} %add_convert_fusion), channel_id=1, source_target_pairs={{0,1},{1,0},{2,3},{3,2},{4,5},{5,4},{6,7},{7,6},{8,9},{9,8},{10,11... | collective-permute-start | bytes 196616 | tf_op jit(solution)/shard_map/ppermute | solution.py:401
  364.1 6.2 %collective-permute-start.48 = (bf16[256,128]{1,0:T(8,128)(2,1)S(1)}, bf16[256,128]{1,0:T(8,128)(2,1)S(1)}, u32[]{:S(2)}, u32[]{:S(2)}) collective-permute-start(bf16[256,128]{1,0:T(8,128)(2,1)S(1)} %add_convert_fusion), channel_id=1, source_target_pairs={{0,2},{1,3},{2,0},{3,1},{4,6},{5,7},{6,4},{7,5},{8,10},{9,11},{10,... | collective-permute-start | bytes 196616 | tf_op jit(solution)/shard_map/ppermute | solution.py:401
  364.4 6.9 %collective-permute-start.49 = (bf16[256,128]{1,0:T(8,128)(2,1)S(1)}, bf16[256,128]{1,0:T(8,128)(2,1)S(1)}, u32[]{:S(2)}, u32[]{:S(2)}) collective-permute-start(bf16[256,128]{1,0:T(8,128)(2,1)S(1)} %add_convert_fusion), channel_id=1, source_target_pairs={{0,3},{1,2},{2,1},{3,0},{4,7},{5,6},{6,5},{7,4},{8,11},{9,10},{10,... | collective-permute-start | bytes 196616 | tf_op jit(solution)/shard_map/ppermute | solution.py:401
  370.1 15.2 %collective-permute-start.56 = (f32[16,512]{1,0:T(8,128)S(1)}, f32[16,512]{1,0:T(8,128)S(1)}, u32[]{:S(2)}, u32[]{:S(2)}) collective-permute-start(f32[16,512]{1,0:T(8,128)S(1)} %squeeze.30), channel_id=1, source_target_pairs={{0,1},{1,0},{2,3},{3,2},{4,5},{5,4},{6,7},{7,6},{8,9},{9,8},{10,11... | collective-permute-start | bytes 98312 | tf_op jit(solution)/shard_map/ppermute | solution.py:401
  372.5 12.8 %collective-permute-start.57 = (f32[16,512]{1,0:T(8,128)S(1)}, f32[16,512]{1,0:T(8,128)S(1)}, u32[]{:S(2)}, u32[]{:S(2)}) collective-permute-start(f32[16,512]{1,0:T(8,128)S(1)} %squeeze.31), channel_id=1, source_target_pairs={{0,4},{4,0},{8,12},{12,8},{16,20},{20,16},{24,28},{28,24},{1,5},{5... | collective-permute-start | bytes 98312 | tf_op jit(solution)/shard_map/ppermute | solution.py:401
  372.6 12.7 %collective-permute-start.58 = (f32[16,512]{1,0:T(8,128)S(1)}, f32[16,512]{1,0:T(8,128)S(1)}, u32[]{:S(2)}, u32[]{:S(2)}) collective-permute-start(f32[16,512]{1,0:T(8,128)S(1)} %squeeze.32), channel_id=1, source_target_pairs={{0,5},{1,4},{2,7},{3,6},{4,1},{5,0},{6,3},{7,2},{8,13},{9,12},{10,... | collective-permute-start | bytes 98312 | tf_op jit(solution)/shard_map/ppermute | solution.py:407
  373.9 8.2 %collective-permute-start.51 = (f32[256,128]{1,0:T(8,128)S(1)}, f32[256,128]{1,0:T(8,128)S(1)}, u32[]{:S(2)}, u32[]{:S(2)}) collective-permute-start(f32[256,128]{1,0:T(8,128)S(1)} %add_add_fusion.refs_0_), channel_id=1, source_target_pairs={{0,16},{4,20},{8,24},{12,28},{16,0},{20,4},{24,8},{28,12},{1,17},{... | collective-permute-start | bytes 393224 | tf_op jit(solution)/shard_map/ppermute | solution.py:401
  376.4 5.9 %collective-permute-start.52 = (f32[256,128]{1,0:T(8,128)S(1)}, f32[256,128]{1,0:T(8,128)S(1)}, u32[]{:S(2)}, u32[]{:S(2)}) collective-permute-start(f32[256,128]{1,0:T(8,128)S(1)} %add_add_fusion.refs_0_), channel_id=1, source_target_pairs={{0,24},{4,28},{8,16},{12,20},{16,8},{20,12},{24,0},{28,4},{1,25},{... | collective-permute-start | bytes 393224 | tf_op jit(solution)/shard_map/ppermute | solution.py:401
  (72 other events, 471.6 us)

commit v7 on v6

--- a/solution.py
+++ b/solution.py
@@ -714,17 +714,19 @@
 def keep_one(d_project, through, weight, pick, got, number):
     total = d_project.shape[1]
     wide = (weight.shape[0] - BELOW) // 2
+    block = 2 * STEP
+    per = wide // block
     return pl.pallas_call(
         keep_one_kernel,
-        grid=(1,),
+        grid=(per,),
         in_specs=[
-            pl.BlockSpec((2 * STEP, total), lambda i: (0, 0)),
-            pl.BlockSpec((2 * STEP, total // 2), lambda i: (0, 0)),
-            pl.BlockSpec((wide, total), lambda i: (number, 0)),
-            pl.BlockSpec((wide, total // 2), lambda i: (number, 0)),
-            pl.BlockSpec((2 * STEP, wide), lambda i: (0, 0)),
+            pl.BlockSpec((2 * STEP, total), lambda j: (0, 0)),
+            pl.BlockSpec((2 * STEP, total // 2), lambda j: (0, 0)),
+            pl.BlockSpec((block, total), lambda j: (number * per + j, 0)),
+            pl.BlockSpec((block, total // 2), lambda j: (number * per + j, 0)),
+            pl.BlockSpec((2 * STEP, block), lambda j: (0, j)),
         ],
-        out_specs=[pl.BlockSpec((STEP, wide), lambda i: (0, 0))] * 2,
+        out_specs=[pl.BlockSpec((STEP, block), lambda j: (0, j))] * 2,
         out_shape=[
             jax.ShapeDtypeStruct((STEP, wide), jnp.float32),
             jax.ShapeDtypeStruct((STEP, wide), jnp.bfloat16),

time: 399 us -> 399 us (level)
  no operation moved by 1% of the time
where the time goes in v7:
time: 399 us; the launch traced here: 394 us
  Pallas kernels  186 us (47%)
  starting transfers between devices  56.2 us (14%)
  local copies, waits for them, and re-layouts  48.4 us (12%)
  waiting for transfers between devices  40 us (10%)
  other arithmetic  36.6 us (9%)
  matrix products  24 us (6%)
    ppermute x58, starting transfers between devices, swap(): lax.ppermute(x, axis, [(i, i ^ bit) for i in range(lax.axis_size(axis))])  54.9 us
    pallas_call x2, Pallas kernels, conv_backward(): pl.pallas_call(functools.partial(backward_kernel, chars, low_places, span...  53 us
    pallas_call x3, Pallas kernels, conv_forward(): pl.pallas_call(functools.partial(kernel, low_places, extras), grid_spec=p...  48.7 us
    ppermute x58, waiting for transfers between devices, swap(): lax.ppermute(x, axis, [(i, i ^ bit) for i in range(lax.axis_size(axis))])  40 us
    pallas_call x2, Pallas kernels, call_layer(): pl.pallas_call(functools.partial(kernel, tuple(x_copies), tuple(w_copies)...  33.9 us
    dot_general x8, matrix products, product(): lax.dot_general(inputs[:, number * half:(number + 1) * half], after(halve...  18.8 us
    unnamed x130, local copies, waits for them, and re-layouts  14.6 us
    pallas_call x1, Pallas kernels, back_one(): pl.pallas_call(back_one_kernel, in_specs=[NEAR] * 4 + [ANYWHERE] * 2, out...  11.1 us
  transfers between devices with their start and end apart: 59, of which 11 were waited for; matrix products, arithmetic and copies ran while one was open for 23% of the time, Pallas kernels for 42%

profile of v7, /device:TPU:0, one launch (start us, length us, event | category | flops | bytes accessed | tf_op | source)
XLA Modules:
  0.0 393.8 jit_solution(2942863098636866446)
XLA Ops:
  1.9 4.1 %collective-permute-start = (bf16[1,16,2048]{2,1,0:T(8,128)(2,1)S(1)}, bf16[1,16,2048]{2,1,0:T(8,128)(2,1)S(1)}, u32[]{:S(2)}, u32[]{:S(2)}) collective-permute-start(bf16[1,16,2048]{2,1,0:T(8,128)(2,1)S(1)} %bitcast.194), channel_id=1, source_target_pairs={{0,2},{1,3},{2,0},{3,1},{4,6},{5,7},{6,4},{7,5},{8,10},{9,11},{10,... | collective-permute-start | bytes 196616 | tf_op jit(solution)/shard_map/ppermute | solution.py:401
  15.3 1.9 bank_rows.2
  18.7 1.6 collective-permute-start.4
  21.4 9.0 %prepare.1 = (bf16[50,256,128]{2,1,0:T(8,128)(2,1)}, bf16[128,2048]{1,0:T(8,128)(2,1)}, f32[8,2048]{1,0:T(8,128)}) custom-call(s32[256,50]{1,0:T(8,128)} %copy.77.ids_ref, bf16[262,16]{1,0:T(8,128)(2,1)} %copy.78.chars_ref, bf16[1,2048]{1,0:T(2,128)(2,1)} %reshape.354.bias_ref, bf16[16,32]{1,0:T(8,128)(2,1)} %refs_0_.2, bf16[32,32]{1,0:T(8,128)(2,1)} %refs_1_.1, ...), custom_call_target="tpu_custom_call" | custom-call | flops 1 | bytes 1 | tf_op jit(solution)/shard_map/prepare/pallas_call | solution.py:65
  31.0 20.6 %conv_forward.3 = (bf16[4,50,256,256]{3,2,1,0:T(8,128)(2,1)}, bf16[256,1024]{1,0:T(8,128)(2,1)}, f32[256,1024]{1,0:T(8,128)}, f32[5,256,1024]{2,1,0:T(8,128)}) custom-call(s32[4]{0:T(128)} %broadcast.226.trip_ref, bf16[50,256,128]{2,1,0:T(8,128)(2,1)} %get-tuple-element.202.win_ref.refs_5_, bf16[128,2048]{1,0:T(8,128)(2,1)} %get-tuple-element.124.weight_ref.refs_6_, ...), custom_call_target="tpu_custom_call" | custom-call | flops 1 | bytes 1 | tf_op jit(solution)/shard_map/conv_forward/pallas_call | solution.py:144
  53.1 1.6 collective-permute-start.2
  55.9 2.7 collective-permute-start.9
  59.1 13.8 %conv_forward.4 = (bf16[4,50,256,256]{3,2,1,0:T(8,128)(2,1)}, bf16[256,512]{1,0:T(8,128)(2,1)}, f32[256,1024]{1,0:T(8,128)}, f32[5,256,1024]{2,1,0:T(8,128)}) custom-call(s32[2]{0:T(128)} %broadcast.227.trip_ref, bf16[50,256,128]{2,1,0:T(8,128)(2,1)} %get-tuple-element.202.win_ref.refs_5_, bf16[128,2048]{1,0:T(8,128)(2,1)} %get-tuple-element.124.weight_ref.refs_6_, ...), custom_call_target="tpu_custom_call" | custom-call | flops 1 | bytes 1 | tf_op jit(solution)/shard_map/conv_forward/pallas_call | solution.py:144
  77.7 1.6 collective-permute-start.11
  86.8 14.2 %conv_forward.5 = (bf16[4,50,256,256]{3,2,1,0:T(8,128)(2,1)}, bf16[256,512]{1,0:T(8,128)(2,1)}, f32[256,1024]{1,0:T(8,128)}, f32[5,256,1024]{2,1,0:T(8,128)}) custom-call(s32[2]{0:T(128)} %constant.547.trip_ref, bf16[50,256,128]{2,1,0:T(8,128)(2,1)} %get-tuple-element.202.win_ref.refs_5_, ...), custom_call_target="tpu_custom_call", output_to_operand_aliasing={{0}: (4, {}), {2}: (5, {}), {3}: (6, {})} | custom-call | flops 1 | bytes 1 | tf_op jit(solution)/shard_map/conv_forward/pallas_call | solution.py:144
  111.2 16.3 %layer_one.1 = (bf16[1024,2048]{1,0:T(8,128)(2,1)}, bf16[2080,1024]{1,0:T(8,128)(2,1)}, f32[1024,1024]{1,0:T(8,128)}, bf16[1024,512]{1,0:T(8,128)(2,1)}, bf16[1024,512]{1,0:T(8,128)(2,1)}) custom-call(s32[16]{0:T(128)} %stack.285.at_ref, bf16[2048,512]{1,0:T(8,128)(2,1)} %compare_convert_fusion.pick_ref.pick_far, ...), custom_call_target="tpu_custom_call" | custom-call | flops 1 | bytes 1 | tf_op jit(solution)/shard_map/layer_one/pallas_call | solution.py:551
  127.5 1.6 collective-permute-start.20
  133.3 1.6 collective-permute-start.23
  135.1 18.0 %collective-permute-done.20.refs_5_ = bf16[1024,512]{1,0:T(8,128)(2,1)} collective-permute-done((bf16[1024,512]{1,0:T(8,128)(2,1)}, bf16[1024,512]{1,0:T(8,128)(2,1)}, u32[]{:S(2)}, u32[]{:S(2)}) %collective-permute-start.20) | collective-permute-done | bytes 1048608 | tf_op jit(solution)/shard_map/ppermute | solution.py:401
  156.4 2.1 collective-permute-done.23.refs_9_
  158.5 17.6 %layer_two.1 = (bf16[1024,2048]{1,0:T(8,128)(2,1)}, bf16[2080,1024]{1,0:T(8,128)(2,1)}, bf16[1024,512]{1,0:T(8,128)(2,1)}, bf16[1024,1024]{1,0:T(8,128)(2,1)}, f...) custom-call(s32[16]{0:T(128)} %stack.285.at_ref, ...), custom_call_target="tpu_custom_call" | custom-call | flops 1 | bytes 1 | tf_op jit(solution)/shard_map/layer_two/pallas_call | solution.py:551
  177.9 1.7 constant_dynamic-slice_fusion.13
  184.1 2.3 fusion.27
  187.0 2.5 fusion.24
  191.0 4.3 %keep_two.2 = bf16[1024,512]{1,0:T(8,128)(2,1)} custom-call(bf16[1024,1024]{1,0:T(8,128)(2,1)} %get-tuple-element.162.d_project_ref, bf16[2080,1024]{1,0:T(8,128)(2,1)} %get-tuple-element.165.w_ref, bf16[1024,1024]{1,0:T(8,128)(2,1)} %collective-permute-done.25.got_ref), custom_call_target="tpu_custom_call" | custom-call | flops 1 | bytes 1 | tf_op jit(solution)/shard_map/keep_two/pallas_call | solution.py:637
  196.3 4.9 %keep_two.3.own_ref = f32[1024,512]{1,0:T(8,128)} custom-call(bf16[1024,1024]{1,0:T(8,128)(2,1)} %get-tuple-element.162.d_project_ref, bf16[2080,1024]{1,0:T(8,128)(2,1)} %get-tuple-element.165.w_ref, bf16[1024,1024]{1,0:T(8,128)(2,1)} %collective-permute-done.25.got_ref, f32[1024,512]{1,0:T(8,128)} %get-tuple-element.163.refs_0_), custom_call_target="tpu_custom_call" | custom-call | flops 1 | bytes 1 | tf_op jit(solution)/shard_map/keep_two/pallas_call | solution.py:637
  201.3 1.8 convolution_convert_fusion.1
  204.4 2.1 convolution_add_fusion
  207.3 4.5 %collective-permute-done.28 = bf16[1024,512]{1,0:T(8,128)(2,1)} collective-permute-done((bf16[1024,512]{1,0:T(8,128)(2,1)}, bf16[1024,512]{1,0:T(8,128)(2,1)}, u32[]{:S(2)}, u32[]{:S(2)}) %collective-permute-start.28) | collective-permute-done | bytes 1048608 | tf_op jit(solution)/shard_map/ppermute | solution.py:401
  211.9 2.8 collective-permute-done.27
  214.7 3.2 convert_add_fusion.2
  220.4 2.5 convert_add_fusion.3
  227.7 11.1 %back_one.1 = (bf16[1024,1024]{1,0:T(8,128)(2,1)}, bf16[1024,512]{1,0:T(8,128)(2,1)}, f32[8,1024]{1,0:T(8,128)}, bf16[512,1024]{1,0:T(8,128)(2,1)}, bf16[512,1024]{1,0:T(8,128)(2,1)}) custom-call(f32[1024,512]{1,0:T(8,128)} %keep_two.3.own_ref, bf16[1024,512]{1,0:T(8,128)(2,1)} %collective-permute-done.29.got_ref, ...), custom_call_target="tpu_custom_call" | custom-call | flops 1 | bytes 1 | tf_op jit(solution)/shard_map/back_one/pallas_call | solution.py:685
  239.0 1.8 copy-done
  249.6 4.9 %keep_one.2 = (f32[256,1024]{1,0:T(8,128)}, bf16[256,1024]{1,0:T(8,128)(2,1)}) custom-call(bf16[1024,1024]{1,0:T(8,128)(2,1)} %get-tuple-element.185.d_project_ref, bf16[1024,512]{1,0:T(8,128)(2,1)} %get-tuple-element.178.through_ref, bf16[2080,1024]{1,0:T(8,128)(2,1)} %get-tuple-element.171.w_far.w_ref, ...), custom_call_target="tpu_custom_call" | custom-call | flops 1 | bytes 1 | tf_op jit(solution)/shard_map/keep_one/pallas_call | solution.py:719
  256.7 4.9 %keep_one.3 = (f32[256,1024]{1,0:T(8,128)}, bf16[256,1024]{1,0:T(8,128)(2,1)}) custom-call(bf16[1024,1024]{1,0:T(8,128)(2,1)} %get-tuple-element.185.d_project_ref, bf16[1024,512]{1,0:T(8,128)(2,1)} %get-tuple-element.178.through_ref, bf16[2080,1024]{1,0:T(8,128)(2,1)} %get-tuple-element.171.w_far.w_ref, ...), custom_call_target="tpu_custom_call" | custom-call | flops 1 | bytes 1 | tf_op jit(solution)/shard_map/keep_one/pallas_call | solution.py:719
  261.6 1.6 convert_add_fusion.4
  266.4 2.6 collective-permute-start.41
  269.0 5.0 %collective-permute-done.36 = bf16[1152,512]{1,0:T(8,128)(2,1)} collective-permute-done((bf16[1152,512]{1,0:T(8,128)(2,1)S(1)}, bf16[1152,512]{1,0:T(8,128)(2,1)}, u32[]{:S(2)}, u32[]{:S(2)}) %collective-permute-start.36) | collective-permute-done | bytes 1179680 | tf_op jit(solution)/shard_map/ppermute | solution.py:401
  274.9 3.3 convert_add_fusion
  279.7 2.5 convert_add_fusion.1
  287.5 25.6 %conv_backward.2 = (f32[8,120,128]{2,1,0:T(8,128)}, f32[40,128]{1,0:T(8,128)}) custom-call(s32[4]{0:T(128)} %broadcast.226.trip_ref, bf16[4,50,256,256]{3,2,1,0:T(8,128)(2,1)} %get-tuple-element.174.refs_0_, f32[256,1024]{1,0:T(8,128)} %get-tuple-element.175.refs_1_, f32[5,256,1024]{2,1,0:T(8,128)} %get-tuple-element.176.refs_2_, ...), custom_call_target="tpu_custom_call" | custom-call | flops 1 | bytes 1 | tf_op jit(solution)/shard_map/conv_backward/pallas_call | solution.py:289
  318.1 2.6 collective-permute-start.55
  320.7 27.4 %conv_backward.3 = (f32[8,120,128]{2,1,0:T(8,128)}, f32[40,128]{1,0:T(8,128)}) custom-call(s32[4]{0:T(128)} %constant.549.trip_ref, bf16[4,50,256,256]{3,2,1,0:T(8,128)(2,1)} %get-tuple-element.196.refs_0_, f32[256,1024]{1,0:T(8,128)} %get-tuple-element.197.refs_1_, f32[5,256,1024]{2,1,0:T(8,128)} %get-tuple-element.198.refs_2_, ...), custom_call_target="tpu_custom_call" | custom-call | flops 1 | bytes 1 | tf_op jit(solution)/shard_map/conv_backward/pallas_call | solution.py:289
  348.2 2.4 pack.1
  358.8 1.7 fusion.52
  361.0 2.4 collective-permute-done.46
  364.4 3.5 collective-permute-start.49
  374.4 2.0 collective-permute-done.50.refs_1_
  379.5 2.4 bank_rows.3
  383.3 1.9 join.1.own_ref
  388.1 2.3 unpack.1
  390.4 1.6 copy.90
  (369 shorter events, 116.1 us)
Async XLA Ops:
  1.9 11.9 %collective-permute-start = (bf16[1,16,2048]{2,1,0:T(8,128)(2,1)S(1)}, bf16[1,16,2048]{2,1,0:T(8,128)(2,1)S(1)}, u32[]{:S(2)}, u32[]{:S(2)}) collective-permute-start(bf16[1,16,2048]{2,1,0:T(8,128)(2,1)S(1)} %bitcast.194), channel_id=1, source_target_pairs={{0,2},{1,3},{2,0},{3,1},{4,6},{5,7},{6,4},{7,5},{8,10},{9,11},{10,... | collective-permute-start | bytes 196616 | tf_op jit(solution)/shard_map/ppermute | solution.py:401
  13.8 39.2 %collective-permute-start.1 = (bf16[2,16,2048]{2,1,0:T(8,128)(2,1)S(1)}, bf16[2,16,2048]{2,1,0:T(8,128)(2,1)S(1)}, u32[]{:S(2)}, u32[]{:S(2)}) collective-permute-start(bf16[2,16,2048]{2,1,0:T(8,128)(2,1)S(1)} %pad_maximum_fusion.22), channel_id=1, source_target_pairs={{0,8},{4,12},{8,0},{12,4},{16,24},{20,28},{24,16},{28,20},{1,9},{5... | collective-permute-start | bytes 393224 | tf_op jit(solution)/shard_map/ppermute | solution.py:401
  17.3 37.4 %collective-permute-start.3 = (bf16[2080,128]{1,0:T(8,128)(2,1)}, bf16[2080,128]{1,0:T(8,128)(2,1)S(1)}, u32[]{:S(2)}, u32[]{:S(2)}) collective-permute-start(bf16[2080,128]{1,0:T(8,128)(2,1)} %bank_rows.2), channel_id=1, source_target_pairs={{0,2},{1,3},{2,0},{3,1},{4,6},{5,7},{6,4},{7,5},{8,10},{9,11},{10,... | collective-permute-start | bytes 1597448 | tf_op jit(solution)/shard_map/ppermute | solution.py:401
  18.7 36.7 %collective-permute-start.4 = (bf16[256,512]{1,0:T(8,128)(2,1)S(1)}, bf16[256,512]{1,0:T(8,128)(2,1)}, u32[]{:S(2)}, u32[]{:S(2)}) collective-permute-start(bf16[256,512]{1,0:T(8,128)(2,1)S(1)} %copy-done.26), channel_id=1, source_target_pairs={{0,1},{1,0},{2,3},{3,2},{4,5},{5,4},{6,7},{7,6},{8,9},{9,8},{10,11... | collective-permute-start | bytes 786440 | tf_op jit(solution)/shard_map/ppermute | solution.py:401
  20.3 35.5 %collective-permute-start.5 = (bf16[256,512]{1,0:T(8,128)(2,1)S(1)}, bf16[256,512]{1,0:T(8,128)(2,1)}, u32[]{:S(2)}, u32[]{:S(2)}) collective-permute-start(bf16[256,512]{1,0:T(8,128)(2,1)S(1)} %copy-done.26), channel_id=1, source_target_pairs={{0,4},{4,0},{8,12},{12,8},{16,20},{20,16},{24,28},{28,24},{1,5},{5... | collective-permute-start | bytes 786440 | tf_op jit(solution)/shard_map/ppermute | solution.py:401
  51.6 35.2 %collective-permute-start.8 = (bf16[256,1024]{1,0:T(8,128)(2,1)}, bf16[256,1024]{1,0:T(8,128)(2,1)}, u32[]{:S(2)}, u32[]{:S(2)}) collective-permute-start(bf16[256,1024]{1,0:T(8,128)(2,1)} %get-tuple-element.126.refs_0_), channel_id=1, source_target_pairs={{0,1},{1,0},{2,3},{3,2},{4,5},{5,4},{6,7},{7,6},{8,9},{9,8},{10,11... | collective-permute-start | bytes 1572872 | tf_op jit(solution)/shard_map/ppermute | solution.py:401
  53.1 19.9 %collective-permute-start.2 = (bf16[4,16,2048]{2,1,0:T(8,128)(2,1)S(1)}, bf16[4,16,2048]{2,1,0:T(8,128)(2,1)S(1)}, u32[]{:S(2)}, u32[]{:S(2)}) collective-permute-start(bf16[4,16,2048]{2,1,0:T(8,128)(2,1)S(1)} %pad_maximum_fusion.21), channel_id=1, source_target_pairs={{0,16},{4,20},{8,24},{12,28},{16,0},{20,4},{24,8},{28,12},{1,17},{... | collective-permute-start | bytes 786440 | tf_op jit(solution)/shard_map/ppermute | solution.py:401
  54.8 26.2 %collective-permute-start.7 = (bf16[2,1040,128]{2,1,0:T(8,128)(2,1)S(1)}, bf16[2,1040,128]{2,1,0:T(8,128)(2,1)}, u32[]{:S(2)}, u32[]{:S(2)}) collective-permute-start(bf16[2,1040,128]{2,1,0:T(8,128)(2,1)S(1)} %pad_maximum_fusion.14), channel_id=1, source_target_pairs={{0,16},{4,20},{8,24},{12,28},{16,0},{20,4},{24,8},{28,12},{1,17},{... | collective-permute-start | bytes 1597448 | tf_op jit(solution)/shard_map/ppermute | solution.py:401
  55.4 25.6 %collective-permute-start.6 = (bf16[2,1040,128]{2,1,0:T(8,128)(2,1)S(1)}, bf16[2,1040,128]{2,1,0:T(8,128)(2,1)}, u32[]{:S(2)}, u32[]{:S(2)}) collective-permute-start(bf16[2,1040,128]{2,1,0:T(8,128)(2,1)S(1)} %pad_maximum_fusion.13), channel_id=1, source_target_pairs={{0,8},{4,12},{8,0},{12,4},{16,24},{20,28},{24,16},{28,20},{1,9},{5... | collective-permute-start | bytes 1597448 | tf_op jit(solution)/shard_map/ppermute | solution.py:401
  55.9 48.9 %collective-permute-start.9 = (bf16[2080,128]{1,0:T(8,128)(2,1)}, bf16[2080,128]{1,0:T(8,128)(2,1)}, u32[]{:S(2)}, u32[]{:S(2)}) collective-permute-start(bf16[2080,128]{1,0:T(8,128)(2,1)} %pad_maximum_fusion.15), channel_id=1, source_target_pairs={{0,2},{1,3},{2,0},{3,1},{4,6},{5,7},{6,4},{7,5},{8,10},{9,11},{10,... | collective-permute-start | bytes 1597448 | tf_op jit(solution)/shard_map/ppermute | solution.py:401
  77.7 23.9 %collective-permute-start.11 = (bf16[512,512]{1,0:T(8,128)(2,1)}, bf16[512,512]{1,0:T(8,128)(2,1)}, u32[]{:S(2)}, u32[]{:S(2)}) collective-permute-start(bf16[512,512]{1,0:T(8,128)(2,1)} %pad_maximum_fusion.18), channel_id=1, source_target_pairs={{0,1},{1,0},{2,3},{3,2},{4,5},{5,4},{6,7},{7,6},{8,9},{9,8},{10,11... | collective-permute-start | bytes 1572872 | tf_op jit(solution)/shard_map/ppermute | solution.py:401
  83.7 27.4 %collective-permute-start.16 = (bf16[4,1040,128]{2,1,0:T(8,128)(2,1)S(1)}, bf16[4,1040,128]{2,1,0:T(8,128)(2,1)}, u32[]{:S(2)}, u32[]{:S(2)}) collective-permute-start(bf16[4,1040,128]{2,1,0:T(8,128)(2,1)S(1)} %pad_maximum_fusion.3.refs_11_), channel_id=1, source_target_pairs={{0,8},{4,12},{8,0},{12,4},{16,24},{20,28},{24,16},{28,20},{1,9},{5... | collective-permute-start | bytes 3194888 | tf_op jit(solution)/shard_map/ppermute | solution.py:401
  85.3 25.8 %collective-permute-start.15 = (bf16[4,1040,128]{2,1,0:T(8,128)(2,1)S(1)}, bf16[4,1040,128]{2,1,0:T(8,128)(2,1)}, u32[]{:S(2)}, u32[]{:S(2)}) collective-permute-start(bf16[4,1040,128]{2,1,0:T(8,128)(2,1)S(1)} %pad_maximum_fusion.2.refs_9_), channel_id=1, source_target_pairs={{0,16},{4,20},{8,24},{12,28},{16,0},{20,4},{24,8},{28,12},{1,17},{... | collective-permute-start | bytes 3194888 | tf_op jit(solution)/shard_map/ppermute | solution.py:401
  101.0 7.3 %collective-permute-start.13 = (bf16[256,512]{1,0:T(8,128)(2,1)}, bf16[256,512]{1,0:T(8,128)(2,1)S(1)}, u32[]{:S(2)}, u32[]{:S(2)}) collective-permute-start(bf16[256,512]{1,0:T(8,128)(2,1)} %get-tuple-element.141.refs_6_), channel_id=1, source_target_pairs={{0,1},{1,0},{2,3},{3,2},{4,5},{5,4},{6,7},{7,6},{8,9},{9,8},{10,11... | collective-permute-start | bytes 786440 | tf_op jit(solution)/shard_map/ppermute | solution.py:401
  108.3 21.0 %collective-permute-start.18 = (bf16[2,1040,128]{2,1,0:T(8,128)(2,1)}, bf16[2,1040,128]{2,1,0:T(8,128)(2,1)}, u32[]{:S(2)}, u32[]{:S(2)}) collective-permute-start(bf16[2,1040,128]{2,1,0:T(8,128)(2,1)} %pad_maximum_fusion.17), channel_id=1, source_target_pairs={{0,16},{4,20},{8,24},{12,28},{16,0},{20,4},{24,8},{28,12},{1,17},{... | collective-permute-start | bytes 1597448 | tf_op jit(solution)/shard_map/ppermute | solution.py:401
  109.0 20.4 %collective-permute-start.17 = (bf16[2,1040,128]{2,1,0:T(8,128)(2,1)}, bf16[2,1040,128]{2,1,0:T(8,128)(2,1)}, u32[]{:S(2)}, u32[]{:S(2)}) collective-permute-start(bf16[2,1040,128]{2,1,0:T(8,128)(2,1)} %pad_maximum_fusion.16), channel_id=1, source_target_pairs={{0,8},{4,12},{8,0},{12,4},{16,24},{20,28},{24,16},{28,20},{1,9},{5... | collective-permute-start | bytes 1597448 | tf_op jit(solution)/shard_map/ppermute | solution.py:401
  127.5 25.6 %collective-permute-start.20 = (bf16[1024,512]{1,0:T(8,128)(2,1)}, bf16[1024,512]{1,0:T(8,128)(2,1)}, u32[]{:S(2)}, u32[]{:S(2)}) collective-permute-start(bf16[1024,512]{1,0:T(8,128)(2,1)} %get-tuple-element.148.refs_4_), channel_id=1, source_target_pairs={{0,1},{1,0},{2,3},{3,2},{4,5},{5,4},{6,7},{7,6},{8,9},{9,8},{10,11... | collective-permute-start | bytes 3145736 | tf_op jit(solution)/shard_map/ppermute | solution.py:401
  130.6 25.8 %collective-permute-start.24 = (bf16[4,1040,128]{2,1,0:T(8,128)(2,1)S(1)}, bf16[4,1040,128]{2,1,0:T(8,128)(2,1)}, u32[]{:S(2)}, u32[]{:S(2)}) collective-permute-start(bf16[4,1040,128]{2,1,0:T(8,128)(2,1)S(1)} %pad_maximum_fusion.5.refs_10_), channel_id=1, source_target_pairs={{0,8},{4,12},{8,0},{12,4},{16,24},{20,28},{24,16},{28,20},{1,9},{5... | collective-permute-start | bytes 3194888 | tf_op jit(solution)/shard_map/ppermute | solution.py:401
  133.3 25.2 %collective-permute-start.23 = (bf16[4,1040,128]{2,1,0:T(8,128)(2,1)S(1)}, bf16[4,1040,128]{2,1,0:T(8,128)(2,1)}, u32[]{:S(2)}, u32[]{:S(2)}) collective-permute-start(bf16[4,1040,128]{2,1,0:T(8,128)(2,1)S(1)} %pad_maximum_fusion.4.refs_8_), channel_id=1, source_target_pairs={{0,16},{4,20},{8,24},{12,28},{16,0},{20,4},{24,8},{28,12},{1,17},{... | collective-permute-start | bytes 3194888 | tf_op jit(solution)/shard_map/ppermute | solution.py:401
  135.0 21.4 %collective-permute-start.21 = (bf16[1024,512]{1,0:T(8,128)(2,1)}, bf16[1024,512]{1,0:T(8,128)(2,1)}, u32[]{:S(2)}, u32[]{:S(2)}) collective-permute-start(bf16[1024,512]{1,0:T(8,128)(2,1)} %get-tuple-element.148.refs_4_), channel_id=1, source_target_pairs={{0,4},{4,0},{8,12},{12,8},{16,20},{20,16},{24,28},{28,24},{1,5},{5... | collective-permute-start | bytes 3145736 | tf_op jit(solution)/shard_map/ppermute | solution.py:401
  176.1 14.9 %collective-permute-start.25 = (bf16[1024,1024]{1,0:T(8,128)(2,1)}, bf16[1024,1024]{1,0:T(8,128)(2,1)}, u32[]{:S(2)}, u32[]{:S(2)}) collective-permute-start(bf16[1024,1024]{1,0:T(8,128)(2,1)} %get-tuple-element.159), channel_id=1, source_target_pairs={{0,4},{4,0},{8,12},{12,8},{16,20},{20,16},{24,28},{28,24},{1,5},{5... | collective-permute-start | bytes 6291464 | tf_op jit(solution)/shard_map/ppermute | solution.py:401
  186.4 25.5 %collective-permute-start.28 = (bf16[1024,512]{1,0:T(8,128)(2,1)}, bf16[1024,512]{1,0:T(8,128)(2,1)}, u32[]{:S(2)}, u32[]{:S(2)}) collective-permute-start(bf16[1024,512]{1,0:T(8,128)(2,1)} %fusion.27), channel_id=1, source_target_pairs={{0,8},{4,12},{8,0},{12,4},{16,24},{20,28},{24,16},{28,20},{1,9},{5... | collective-permute-start | bytes 3145736 | tf_op jit(solution)/shard_map/ppermute | solution.py:401
  189.5 25.2 %collective-permute-start.27 = (bf16[1024,512]{1,0:T(8,128)(2,1)}, bf16[1024,512]{1,0:T(8,128)(2,1)}, u32[]{:S(2)}, u32[]{:S(2)}) collective-permute-start(bf16[1024,512]{1,0:T(8,128)(2,1)} %fusion.24), channel_id=1, source_target_pairs={{0,16},{4,20},{8,24},{12,28},{16,0},{20,4},{24,8},{28,12},{1,17},{... | collective-permute-start | bytes 3145736 | tf_op jit(solution)/shard_map/ppermute | solution.py:401
  195.3 32.4 %collective-permute-start.29 = (bf16[1024,512]{1,0:T(8,128)(2,1)}, bf16[1024,512]{1,0:T(8,128)(2,1)}, u32[]{:S(2)}, u32[]{:S(2)}) collective-permute-start(bf16[1024,512]{1,0:T(8,128)(2,1)} %keep_two.2), channel_id=1, source_target_pairs={{0,1},{1,0},{2,3},{3,2},{4,5},{5,4},{6,7},{7,6},{8,9},{9,8},{10,11... | collective-permute-start | bytes 3145736 | tf_op jit(solution)/shard_map/ppermute | solution.py:401
  214.7 24.2 %collective-permute-start.26 = (bf16[512,512]{1,0:T(8,128)(2,1)}, bf16[512,512]{1,0:T(8,128)(2,1)S(1)}, u32[]{:S(2)}, u32[]{:S(2)}) collective-permute-start(bf16[512,512]{1,0:T(8,128)(2,1)} %fusion.77), channel_id=1, source_target_pairs={{0,4},{4,0},{8,12},{12,8},{16,20},{20,16},{24,28},{28,24},{1,5},{5... | collective-permute-start | bytes 1572872 | tf_op jit(solution)/shard_map/ppermute | solution.py:401
  218.9 20.1 %collective-permute-start.32 = (bf16[1024,256]{1,0:T(8,128)(2,1)}, bf16[1024,256]{1,0:T(8,128)(2,1)}, u32[]{:S(2)}, u32[]{:S(2)}) collective-permute-start(bf16[1024,256]{1,0:T(8,128)(2,1)} %dynamic-slice_convert_fusion), channel_id=1, source_target_pairs={{0,16},{4,20},{8,24},{12,28},{16,0},{20,4},{24,8},{28,12},{1,17},{... | collective-permute-start | bytes 1572872 | tf_op jit(solution)/shard_map/ppermute | solution.py:401
  223.9 15.1 %collective-permute-start.31 = (bf16[1024,256]{1,0:T(8,128)(2,1)}, bf16[1024,256]{1,0:T(8,128)(2,1)}, u32[]{:S(2)}, u32[]{:S(2)}) collective-permute-start(bf16[1024,256]{1,0:T(8,128)(2,1)} %dynamic-slice_convert_fusion.1), channel_id=1, source_target_pairs={{0,8},{4,12},{8,0},{12,4},{16,24},{20,28},{24,16},{28,20},{1,9},{5... | collective-permute-start | bytes 1572872 | tf_op jit(solution)/shard_map/ppermute | solution.py:401
  244.0 5.6 %collective-permute-start.30 = (bf16[512,1024]{1,0:T(8,128)(2,1)S(1)}, bf16[512,1024]{1,0:T(8,128)(2,1)}, u32[]{:S(2)}, u32[]{:S(2)}) collective-permute-start(bf16[512,1024]{1,0:T(8,128)(2,1)S(1)} %copy-done.59), channel_id=1, source_target_pairs={{0,4},{4,0},{8,12},{12,8},{16,20},{20,16},{24,28},{28,24},{1,5},{5... | collective-permute-start | bytes 3145736 | tf_op jit(solution)/shard_map/ppermute | solution.py:401
  244.0 11.7 %collective-permute-start.35 = (bf16[512,1024]{1,0:T(8,128)(2,1)}, bf16[512,1024]{1,0:T(8,128)(2,1)S(1)}, u32[]{:S(2)}, u32[]{:S(2)}) collective-permute-start(bf16[512,1024]{1,0:T(8,128)(2,1)} %get-tuple-element.186), channel_id=1, source_target_pairs={{0,4},{4,0},{8,12},{12,8},{16,20},{20,16},{24,28},{28,24},{1,5},{5... | collective-permute-start | bytes 3145736 | tf_op jit(solution)/shard_map/ppermute | solution.py:401
  245.9 28.1 %collective-permute-start.36 = (bf16[1152,512]{1,0:T(8,128)(2,1)S(1)}, bf16[1152,512]{1,0:T(8,128)(2,1)}, u32[]{:S(2)}, u32[]{:S(2)}) collective-permute-start(bf16[1152,512]{1,0:T(8,128)(2,1)S(1)} %maximum_maximum_fusion), channel_id=1, source_target_pairs={{0,8},{4,12},{8,0},{12,4},{16,24},{20,28},{24,16},{28,20},{1,9},{5... | collective-permute-start | bytes 3538952 | tf_op jit(solution)/shard_map/ppermute | solution.py:401
  249.0 30.6 %collective-permute-start.34 = (bf16[1152,512]{1,0:T(8,128)(2,1)S(1)}, bf16[1152,512]{1,0:T(8,128)(2,1)}, u32[]{:S(2)}, u32[]{:S(2)}) collective-permute-start(bf16[1152,512]{1,0:T(8,128)(2,1)S(1)} %pad_maximum_fusion), channel_id=1, source_target_pairs={{0,16},{4,20},{8,24},{12,28},{16,0},{20,4},{24,8},{28,12},{1,17},{... | collective-permute-start | bytes 3538952 | tf_op jit(solution)/shard_map/ppermute | solution.py:401
  254.5 31.8 %collective-permute-start.33 = (bf16[256,1024]{1,0:T(8,128)(2,1)}, bf16[256,1024]{1,0:T(8,128)(2,1)}, u32[]{:S(2)}, u32[]{:S(2)}) collective-permute-start(bf16[256,1024]{1,0:T(8,128)(2,1)} %get-tuple-element.184), channel_id=1, source_target_pairs={{0,1},{1,0},{2,3},{3,2},{4,5},{5,4},{6,7},{7,6},{8,9},{9,8},{10,11... | collective-permute-start | bytes 1572872 | tf_op jit(solution)/shard_map/ppermute | solution.py:401
  264.0 54.0 %collective-permute-start.42 = (bf16[1024,128]{1,0:T(8,128)(2,1)}, bf16[1024,128]{1,0:T(8,128)(2,1)}, u32[]{:S(2)}, u32[]{:S(2)}) collective-permute-start(bf16[1024,128]{1,0:T(8,128)(2,1)} %dynamic-slice_convert_fusion.5), channel_id=1, source_target_pairs={{0,2},{1,3},{2,0},{3,1},{4,6},{5,7},{6,4},{7,5},{8,10},{9,11},{10,... | collective-permute-start | bytes 786440 | tf_op jit(solution)/shard_map/ppermute | solution.py:401
  266.4 54.3 %collective-permute-start.41 = (bf16[1024,128]{1,0:T(8,128)(2,1)}, bf16[1024,128]{1,0:T(8,128)(2,1)}, u32[]{:S(2)}, u32[]{:S(2)}) collective-permute-start(bf16[1024,128]{1,0:T(8,128)(2,1)} %dynamic-slice_convert_fusion.6), channel_id=1, source_target_pairs={{0,2},{1,3},{2,0},{3,1},{4,6},{5,7},{6,4},{7,5},{8,10},{9,11},{10,... | collective-permute-start | bytes 786440 | tf_op jit(solution)/shard_map/ppermute | solution.py:401
  279.2 33.9 %collective-permute-start.40 = (bf16[1152,256]{1,0:T(8,128)(2,1)}, bf16[1152,256]{1,0:T(8,128)(2,1)}, u32[]{:S(2)}, u32[]{:S(2)}) collective-permute-start(bf16[1152,256]{1,0:T(8,128)(2,1)} %fusion.39), channel_id=1, source_target_pairs={{0,16},{4,20},{8,24},{12,28},{16,0},{20,4},{24,8},{28,12},{1,17},{... | collective-permute-start | bytes 1769480 | tf_op jit(solution)/shard_map/ppermute | solution.py:401
  284.4 30.8 %collective-permute-start.39 = (bf16[1152,256]{1,0:T(8,128)(2,1)}, bf16[1152,256]{1,0:T(8,128)(2,1)}, u32[]{:S(2)}, u32[]{:S(2)}) collective-permute-start(bf16[1152,256]{1,0:T(8,128)(2,1)} %fusion.43), channel_id=1, source_target_pairs={{0,8},{4,12},{8,0},{12,4},{16,24},{20,28},{24,16},{28,20},{1,9},{5... | collective-permute-start | bytes 1769480 | tf_op jit(solution)/shard_map/ppermute | solution.py:401
  286.3 34.4 %collective-permute-start.38 = (bf16[256,1024]{1,0:T(8,128)(2,1)}, bf16[256,1024]{1,0:T(8,128)(2,1)}, u32[]{:S(2)}, u32[]{:S(2)}) collective-permute-start(bf16[256,1024]{1,0:T(8,128)(2,1)} %get-tuple-element.187), channel_id=1, source_target_pairs={{0,1},{1,0},{2,3},{3,2},{4,5},{5,4},{6,7},{7,6},{8,9},{9,8},{10,11... | collective-permute-start | bytes 1572872 | tf_op jit(solution)/shard_map/ppermute | solution.py:401
  313.1 35.1 %collective-permute-start.37 = (bf16[256,512]{1,0:T(8,128)(2,1)S(1)}, bf16[256,512]{1,0:T(8,128)(2,1)}, u32[]{:S(2)}, u32[]{:S(2)}) collective-permute-start(bf16[256,512]{1,0:T(8,128)(2,1)S(1)} %copy-done.44), channel_id=1, source_target_pairs={{0,1},{1,0},{2,3},{3,2},{4,5},{5,4},{6,7},{7,6},{8,9},{9,8},{10,11... | collective-permute-start | bytes 786440 | tf_op jit(solution)/shard_map/ppermute | solution.py:401
  317.6 50.3 %collective-permute-start.54 = (bf16[1152,128]{1,0:T(8,128)(2,1)S(1)}, bf16[1152,128]{1,0:T(8,128)(2,1)}, u32[]{:S(2)}, u32[]{:S(2)}) collective-permute-start(bf16[1152,128]{1,0:T(8,128)(2,1)S(1)} %dynamic-slice_convert_fusion.3), channel_id=1, source_target_pairs={{0,2},{1,3},{2,0},{3,1},{4,6},{5,7},{6,4},{7,5},{8,10},{9,11},{10,... | collective-permute-start | bytes 884744 | tf_op jit(solution)/shard_map/ppermute | solution.py:401
  318.1 50.9 %collective-permute-start.55 = (bf16[1152,128]{1,0:T(8,128)(2,1)S(1)}, bf16[1152,128]{1,0:T(8,128)(2,1)}, u32[]{:S(2)}, u32[]{:S(2)}) collective-permute-start(bf16[1152,128]{1,0:T(8,128)(2,1)S(1)} %dynamic-slice_convert_fusion.2), channel_id=1, source_target_pairs={{0,2},{1,3},{2,0},{3,1},{4,6},{5,7},{6,4},{7,5},{8,10},{9,11},{10,... | collective-permute-start | bytes 884744 | tf_op jit(solution)/shard_map/ppermute | solution.py:401
  363.5 6.8 %collective-permute-start.47 = (bf16[256,128]{1,0:T(8,128)(2,1)S(1)}, bf16[256,128]{1,0:T(8,128)(2,1)S(1)}, u32[]{:S(2)}, u32[]{:S(2)}) collective-permute-start(bf16[256,128]{1,0:T(8,128)(2,1)S(1)} %add_convert_fusion), channel_id=1, source_target_pairs={{0,1},{1,0},{2,3},{3,2},{4,5},{5,4},{6,7},{7,6},{8,9},{9,8},{10,11... | collective-permute-start | bytes 196616 | tf_op jit(solution)/shard_map/ppermute | solution.py:401
  364.1 6.2 %collective-permute-start.48 = (bf16[256,128]{1,0:T(8,128)(2,1)S(1)}, bf16[256,128]{1,0:T(8,128)(2,1)S(1)}, u32[]{:S(2)}, u32[]{:S(2)}) collective-permute-start(bf16[256,128]{1,0:T(8,128)(2,1)S(1)} %add_convert_fusion), channel_id=1, source_target_pairs={{0,2},{1,3},{2,0},{3,1},{4,6},{5,7},{6,4},{7,5},{8,10},{9,11},{10,... | collective-permute-start | bytes 196616 | tf_op jit(solution)/shard_map/ppermute | solution.py:401
  364.4 6.9 %collective-permute-start.49 = (bf16[256,128]{1,0:T(8,128)(2,1)S(1)}, bf16[256,128]{1,0:T(8,128)(2,1)S(1)}, u32[]{:S(2)}, u32[]{:S(2)}) collective-permute-start(bf16[256,128]{1,0:T(8,128)(2,1)S(1)} %add_convert_fusion), channel_id=1, source_target_pairs={{0,3},{1,2},{2,1},{3,0},{4,7},{5,6},{6,5},{7,4},{8,11},{9,10},{10,... | collective-permute-start | bytes 196616 | tf_op jit(solution)/shard_map/ppermute | solution.py:401
  370.2 15.1 %collective-permute-start.56 = (f32[16,512]{1,0:T(8,128)S(1)}, f32[16,512]{1,0:T(8,128)S(1)}, u32[]{:S(2)}, u32[]{:S(2)}) collective-permute-start(f32[16,512]{1,0:T(8,128)S(1)} %squeeze.30), channel_id=1, source_target_pairs={{0,1},{1,0},{2,3},{3,2},{4,5},{5,4},{6,7},{7,6},{8,9},{9,8},{10,11... | collective-permute-start | bytes 98312 | tf_op jit(solution)/shard_map/ppermute | solution.py:401
  372.4 12.8 %collective-permute-start.57 = (f32[16,512]{1,0:T(8,128)S(1)}, f32[16,512]{1,0:T(8,128)S(1)}, u32[]{:S(2)}, u32[]{:S(2)}) collective-permute-start(f32[16,512]{1,0:T(8,128)S(1)} %squeeze.31), channel_id=1, source_target_pairs={{0,4},{4,0},{8,12},{12,8},{16,20},{20,16},{24,28},{28,24},{1,5},{5... | collective-permute-start | bytes 98312 | tf_op jit(solution)/shard_map/ppermute | solution.py:401
  372.5 12.7 %collective-permute-start.58 = (f32[16,512]{1,0:T(8,128)S(1)}, f32[16,512]{1,0:T(8,128)S(1)}, u32[]{:S(2)}, u32[]{:S(2)}) collective-permute-start(f32[16,512]{1,0:T(8,128)S(1)} %squeeze.32), channel_id=1, source_target_pairs={{0,5},{1,4},{2,7},{3,6},{4,1},{5,0},{6,3},{7,2},{8,13},{9,12},{10,... | collective-permute-start | bytes 98312 | tf_op jit(solution)/shard_map/ppermute | solution.py:407
  373.8 8.2 %collective-permute-start.51 = (f32[256,128]{1,0:T(8,128)S(1)}, f32[256,128]{1,0:T(8,128)S(1)}, u32[]{:S(2)}, u32[]{:S(2)}) collective-permute-start(f32[256,128]{1,0:T(8,128)S(1)} %add_add_fusion.refs_0_), channel_id=1, source_target_pairs={{0,16},{4,20},{8,24},{12,28},{16,0},{20,4},{24,8},{28,12},{1,17},{... | collective-permute-start | bytes 393224 | tf_op jit(solution)/shard_map/ppermute | solution.py:401
  376.4 5.9 %collective-permute-start.52 = (f32[256,128]{1,0:T(8,128)S(1)}, f32[256,128]{1,0:T(8,128)S(1)}, u32[]{:S(2)}, u32[]{:S(2)}) collective-permute-start(f32[256,128]{1,0:T(8,128)S(1)} %add_add_fusion.refs_0_), channel_id=1, source_target_pairs={{0,24},{4,28},{8,16},{12,20},{16,8},{20,12},{24,0},{28,4},{1,25},{... | collective-permute-start | bytes 393224 | tf_op jit(solution)/shard_map/ppermute | solution.py:401
  (72 other events, 476.3 us)
